TPU v7x, 32 devices: a whole 2x2x4 slice. The times are simulated.
32 devices in a mesh: grp: 2 (over y), dev: 8 (over z, core), pair: 2 (over x), sub: 1.
Axes of the slice: x: 2, y: 2, z: 4, core: 2. Of those that a mesh axis runs over, the one named last changes fastest.
Arguments:
- queries: bfloat16 [256, 4096], P(('grp', 'dev', 'sub'), 'pair'), parts along dimension 0, may hold values from -6 to 6
- key_rows: bfloat16 [256, 4096], P(('grp', 'dev', 'sub'), 'pair'), parts along dimension 0, may hold values from -6 to 6
- value_rows: bfloat16 [256, 4096], P(('grp', 'dev', 'sub'), 'pair'), parts along dimension 0, may hold values from -6 to 6
- states: float32 [64, 32, 128, 128], P(('grp', 'dev', 'sub'), 'pair'), parts along dimension 0, may hold values from -6 to 6
- decay_rates: float32 [32], P('pair'), may hold values from 0.02 to 2
- head_gain: float32 [4096], P('pair'), may hold values from 0.5 to 1.5
- out_weight: bfloat16 [4096, 6144], P('pair', ('dev', 'sub')), may hold values from -0.09375 to 0.09375
- residual: bfloat16 [256, 6144], P(('grp', 'dev', 'pair', 'sub')), parts along dimension 0, may hold values from -6 to 6
- norm_gain: float32 [6144], replicated, may hold values from 0.5 to 1.5
- expert_ids: int32 [256, 2], P(('grp', 'dev', 'pair', 'sub')), parts along dimension 0, may hold values from 0 to 3, all different within a row; in each aligned block of 8 rows (0 to 7, 8 to 15, ...) at most 4 rows name the same one
- gate_weights: float32 [256, 2], P(('grp', 'dev', 'pair', 'sub')), parts along dimension 0, may hold values from 0.1 to 1
- expert_gate: bfloat16 [18432, 6144], P(('dev', 'pair', 'sub')), may hold values from -0.078125 to 0.078125
- expert_up: bfloat16 [18432, 6144], P(('dev', 'pair', 'sub')), may hold values from -0.078125 to 0.078125
- expert_down: bfloat16 [18432, 6144], P(('dev', 'pair', 'sub')), may hold values from -0.09375 to 0.09375
Outputs:
- layer_out: bfloat16 [256, 6144], P(('grp', 'dev', 'pair', 'sub')), parts along dimension 0
There are 2 independent parts, one for each index of `grp`. A program takes and returns all parts, laid end to end along the dimension named above; an argument that names none is the same for every part. Nothing has to cross between parts.
Inputs may be any that keep to these rules, and one draw needn't show every extreme that they name: `expert_ids`: each row names 2 different experts. In each aligned block of 8 rows (the rows of one device) no expert is named by more than 4 rows, and in every draw some block has an expert named by exactly 4 rows.
All inputs are finite; a program needn't handle non-finite values.
Results may differ from a plain program's by a relative error of at most 0.0048.
Values may be sent and summed in bfloat16 or wider, within the bound.
No kernel may reach another device: no remote copies, remote signals or barrier semaphores. Data moves between devices by JAX's collectives and lax.ppermute only.
A program may use at most 128 MiB of HBM per device.

v0:
```python
import jax
import jax.numpy as jnp
from jax import lax
from jax.sharding import PartitionSpec as P

EPSILON = 1e-06
HIGHEST = lax.Precision.HIGHEST


def attend(queries, key_rows, value_rows, states, decay_rates, head_gain):
    requests = states.shape[0]
    head_count = states.shape[1]
    head_size = states.shape[2]
    positions = queries.shape[0] // requests
    layout = (requests, positions, head_count, head_size)
    query_plain = queries.reshape(layout)
    key_plain = key_rows.reshape(layout)
    query_float = query_plain.astype(jnp.float32)
    value_float = value_rows.reshape(layout).astype(jnp.float32)
    offsets = jnp.arange(positions, dtype=jnp.float32)
    carried = jnp.exp(-decay_rates[None, :] * (offsets[:, None] + 1.0))
    from_state = jnp.einsum("rphk,rhkv->rphv", query_float, states, precision=HIGHEST)
    from_state = from_state * carried[None, :, :, None]
    scores = jnp.einsum(
        "rthk,rjhk->rhtj", query_plain, key_plain, preferred_element_type=jnp.float32
    )
    distance = offsets[:, None] - offsets[None, :]
    fading = jnp.exp(-decay_rates[:, None, None] * jnp.maximum(distance, 0.0)[None, :, :])
    fading = jnp.where(distance[None, :, :] >= 0.0, fading, 0.0)
    scores = scores * fading[None]
    within = jnp.einsum("rhtj,rjhv->rthv", scores, value_float, precision=HIGHEST)
    mixed_heads = from_state + within
    spread = jnp.mean(mixed_heads * mixed_heads, axis=3, keepdims=True)
    normal = (
        mixed_heads
        * lax.rsqrt(spread + EPSILON)
        * head_gain.reshape(head_count, head_size)[None, None]
    )
    return normal.astype(jnp.bfloat16).reshape(requests * positions, head_count * head_size)


def expert_apply(picked, gate_part, up_part, down_part):
    leading = picked.shape
    flattened = picked.reshape(-1, leading[-1])
    contract = (((1,), (1,)), ((), ()))
    gate_value = lax.dot_general(flattened, gate_part, contract, preferred_element_type=jnp.float32)
    lifted = lax.dot_general(flattened, up_part, contract, preferred_element_type=jnp.float32)
    hidden = (jax.nn.silu(gate_value) * lifted).astype(jnp.bfloat16)
    output = jnp.dot(hidden, down_part, preferred_element_type=jnp.float32)
    return output.reshape(leading)


def on_device(
    queries,
    key_rows,
    value_rows,
    states,
    decay_rates,
    head_gain,
    out_weight,
    residual,
    norm_gain,
    expert_ids,
    gate_weights,
    expert_gate,
    expert_up,
    expert_down,
):
    outer_count = lax.axis_size("dev")
    pair_count = lax.axis_size("pair")
    core_count = lax.axis_size("sub")
    attended = attend(queries, key_rows, value_rows, states, decay_rates, head_gain)
    partial_value = jnp.dot(
        lax.all_gather(attended, ("dev", "sub"), axis=0, tiled=True),
        out_weight,
        preferred_element_type=jnp.float32,
    )
    local_rows = residual.shape[0]
    columns = partial_value.shape[1]
    blocks = partial_value.reshape(outer_count, pair_count, core_count, local_rows, columns)
    ordered = jnp.transpose(blocks, (1, 0, 2, 3, 4)).reshape(
        pair_count, outer_count * core_count * local_rows, columns
    )
    shared = lax.psum_scatter(ordered, "pair", scatter_dimension=0, tiled=True)
    shared = shared.reshape(outer_count * core_count, local_rows, columns)
    regrouped = lax.all_to_all(shared, ("dev", "sub"), split_axis=0, concat_axis=2, tiled=True)
    own_rows = regrouped[0]
    combined = residual.astype(jnp.float32) + own_rows
    spread = jnp.mean(combined * combined, axis=-1, keepdims=True)
    normed = (combined * lax.rsqrt(spread + EPSILON) * norm_gain).astype(jnp.bfloat16)
    width = normed.shape[1]
    top_count = expert_ids.shape[1]
    expert_count = outer_count // 2
    capacity = max(2, local_rows * top_count // expert_count)
    chosen_ids = expert_ids.reshape(-1)
    choose = (chosen_ids[:, None] == jnp.arange(expert_count, dtype=jnp.int32)[None, :]).astype(
        jnp.int32
    )
    before = jnp.cumsum(choose, axis=0) - choose
    position = jnp.sum(before * choose, axis=1)
    target = chosen_ids * capacity + position
    placing = (
        target[None, :] == jnp.arange(expert_count * capacity, dtype=jnp.int32)[:, None]
    ).astype(jnp.bfloat16)
    repeated = jnp.repeat(normed, top_count, axis=0)
    packed = jnp.dot(placing, repeated, preferred_element_type=jnp.float32).astype(jnp.bfloat16)
    slot_rows = packed.reshape(expert_count, 1, capacity, width)
    outgoing = jnp.broadcast_to(slot_rows, (expert_count, 2, capacity, width)).reshape(
        outer_count, capacity, width
    )
    partials = expert_apply(
        lax.all_gather(
            lax.all_to_all(outgoing, "dev", split_axis=0, concat_axis=0, tiled=True)[None],
            ("pair", "sub"),
            axis=0,
            tiled=True,
        ),
        expert_gate,
        expert_up,
        expert_down,
    )
    summed_terms = lax.psum_scatter(partials, ("pair", "sub"), scatter_dimension=0, tiled=True)
    returned = lax.all_to_all(summed_terms[0], "dev", split_axis=0, concat_axis=0, tiled=True)
    halves = jnp.sum(returned.reshape(expert_count, -1, capacity, width), axis=1).reshape(
        expert_count * capacity, width
    )
    weighting = placing.astype(jnp.float32) * gate_weights.reshape(-1)[None, :]
    per_slot = lax.dot_general(
        weighting,
        halves,
        (((0,), (0,)), ((), ())),
        precision=HIGHEST,
        preferred_element_type=jnp.float32,
    )
    mixture = jnp.sum(per_slot.reshape(local_rows, top_count, width), axis=1)
    return (combined + mixture).astype(jnp.bfloat16)


def solution(mesh):
    return jax.shard_map(
        on_device,
        mesh=mesh,
        in_specs=(
            P(("grp", "dev", "sub"), "pair"),
            P(("grp", "dev", "sub"), "pair"),
            P(("grp", "dev", "sub"), "pair"),
            P(("grp", "dev", "sub"), "pair", None, None),
            P("pair"),
            P("pair"),
            P("pair", ("dev", "sub")),
            P(("grp", "dev", "pair", "sub"), None),
            P(),
            P(("grp", "dev", "pair", "sub"), None),
            P(("grp", "dev", "pair", "sub"), None),
            P(("dev", "pair", "sub"), None),
            P(("dev", "pair", "sub"), None),
            P(("dev", "pair", "sub"), None),
        ),
        out_specs=P(("grp", "dev", "pair", "sub"), None),
        check_vma=False,
    )
```

profile of v0, /device:TPU:0, one launch (start us, length us, event | category | flops | bytes accessed | tf_op | source)
XLA Modules:
  0.0 199.2 jit_solution(17931602684695852897)
XLA Ops:
  6.5 0.0 copy-start
  6.5 0.0 reduce-scatter.3.cloned.1.call-start
  6.6 0.8 neg.10
  7.4 1.0 copy.63
  8.3 0.9 copy.64
  9.2 0.9 copy.65
  10.1 0.1 multiply_exponential_fusion
  10.1 0.1 exponential_select_fusion
  10.2 0.2 convolution_multiply_fusion.1
  10.4 4.2 %fusion.2 = f32[4,4,16,128]{3,1,2,0:T(4,128)S(1)} fusion(f32[4,16,128,128]{3,2,1,0:T(8,128)} %param.17, f32[4,16]{0,1:T(8,128)S(1)} %multiply_exponential_fusion, bf16[4,4,16,128]{3,2,1,0:T(8,128)(2,1)S(1)} %bitcast.61), kind=kOutput, calls=%fused_computation.8 | convolution fusion | flops 50364416 | bytes 4391168 | tf_op jit(solution)/shard_map/rphk,rhkv->rphv/dot_general | solution.py:22
  14.6 0.4 multiply_reduce_fusion.1
  15.1 0.8 multiply_convert_fusion.1
  16.0 16.6 %all_gather.6 = bf16[128,2048]{1,0:T(8,128)(2,1)S(1)} all-gather(bf16[16,2048]{1,0:T(8,128)(2,1)S(1)} %bitcast.63), channel_id=1, replica_groups=mesh['grp'=2,'dev'=8,'pair'=2,'sub'=1] {'dev','sub'}, dimensions={0}, use_global_device_ids=true | all-gather | bytes 589824 | tf_op jit(solution)/shard_map/all_gather | solution.py:74
  32.6 0.0 copy-done
  32.6 0.6 fusion.26
  33.1 0.8 copy.79
  33.9 0.0 reduce-scatter.3.cloned.1.call-update
  33.9 0.8 copy.55
  34.7 0.1 reshape.175
  34.8 13.5 %reduce-scatter.3.cloned.1.call-done = f32[1,64,768]{2,1,0:T(8,128)} async-done(((f32[2,64,768]{2,1,0:T(8,128)}), f32[1,64,768]{2,1,0:T(8,128)}) %reduce-scatter.3.cloned.1.call-update) | async-done | bytes 196624 | tf_op jit(solution)/shard_map/reduce_scatter | solution.py:84
  48.2 4.6 %all-to-all-start = ((f32[8,8,768]{2,1,0:T(8,128)}), f32[8,8,768]{2,1,0:T(8,128)S(1)}, u32[]{:S(2)}, u32[]{:S(2)}) async-start(f32[8,8,768]{2,1,0:T(8,128)} %bitcast.65), calls=%async_computation.1 | async-start | bytes 393216 | tf_op jit(solution)/shard_map/all_to_all | solution.py:86
  52.8 0.0 reduce-scatter.5.cloned.1.call-start
  52.9 0.1 fusion.17
  53.0 0.2 select_reduce_fusion
  53.2 8.0 %all-to-all-done = f32[8,8,768]{2,1,0:T(8,128)S(1)} async-done(((f32[8,8,768]{2,1,0:T(8,128)}), f32[8,8,768]{2,1,0:T(8,128)S(1)}, u32[]{:S(2)}, u32[]{:S(2)}) %all-to-all-start) | async-done | bytes 196640 | tf_op jit(solution)/shard_map/all_to_all | solution.py:86
  61.2 1.1 multiply_reduce_fusion
  62.3 1.0 multiply_convert_fusion
  63.3 0.8 broadcast_in_dim.22
  64.0 1.0 reshape.176
  65.0 0.9 convolution_convert_fusion
  65.9 1.0 broadcast_in_dim.23
  66.9 0.1 broadcast_in_dim.24
  67.0 14.9 %all_to_all.25 = bf16[8,4,6144]{2,1,0:T(4,128)(2,1)S(1)} all-to-all(bf16[8,4,6144]{2,1,0:T(4,128)(2,1)S(1)} %bitcast.57), channel_id=1, replica_groups=mesh['grp'=2,'dev'=8,'pair'=2,'sub'=1] {'dev'}, dimensions={0} | all-to-all | bytes 786432 | tf_op jit(solution)/shard_map/all_to_all | solution.py:113
  82.0 11.6 %all-gather = bf16[16,4,6144]{2,1,0:T(4,128)(2,1)} all-gather(bf16[8,4,6144]{2,1,0:T(4,128)(2,1)S(1)} %all_to_all.25), channel_id=2, replica_groups=mesh['grp'=2,'dev'=8,'pair'=2,'sub'=1] {'pair','sub'}, dimensions={0}, use_global_device_ids=true | all-gather | bytes 1179648 | tf_op jit(solution)/shard_map/all_gather | solution.py:112
  93.6 2.3 %reshape.178 = bf16[64,6144]{1,0:T(8,128)(2,1)} reshape(bf16[16,4,6144]{2,1,0:T(4,128)(2,1)} %all-gather) | data formatting | bytes 1572864 | tf_op jit(solution)/shard_map/reshape | solution.py:44
  95.9 10.4 %fusion.27 = f32[64,1152]{1,0:T(8,128)} fusion(bf16[64,6144]{1,0:T(8,128)(2,1)} %reshape.178, bf16[1152,6144]{1,0:T(8,128)(2,1)} %param.25), kind=kOutput, calls=%fused_computation.53 | convolution fusion | flops 905969664 | bytes 15237120 | tf_op jit(solution)/shard_map/dot_general | solution.py:46
  106.3 0.0 copy-start.2
  106.3 0.0 copy-start.1
  106.3 20.7 %fusion.3 = f32[64,6144]{1,0:T(8,128)} fusion(bf16[1152,6144]{1,0:T(8,128)(2,1)} %param.27, bf16[64,6144]{1,0:T(8,128)(2,1)} %reshape.178, bf16[1152,6144]{1,0:T(8,128)(2,1)} %param.26, f32[64,1152]{1,0:T(8,128)} %fusion.27), kind=kOutput, calls=%fused_computation.10 | convolution fusion | flops 1812381696 | bytes 30965760 | tf_op jit(solution)/shard_map/dot_general | solution.py:49
  127.0 2.8 %reshape.179 = f32[2,8,4,6144]{3,2,1,0:T(4,128)} reshape(f32[64,6144]{1,0:T(8,128)} %fusion.3) | data formatting | bytes 3145728 | tf_op jit(solution)/shard_map/reshape | solution.py:50
  129.8 3.5 %copy.58 = f32[2,8,4,6144]{3,1,2,0:T(8,128)} copy(f32[2,8,4,6144]{3,2,1,0:T(4,128)} %reshape.179) | data formatting | bytes 3145728 | tf_op jit(solution)/shard_map/reshape | solution.py:50
  133.2 0.0 reduce-scatter.5.cloned.1.call-update
  133.3 24.6 %reduce-scatter.5.cloned.1.call-done = f32[1,8,4,6144]{3,1,2,0:T(8,128)} async-done(((f32[2,8,4,6144]{3,1,2,0:T(8,128)}), f32[1,8,4,6144]{3,1,2,0:T(8,128)}) %reduce-scatter.5.cloned.1.call-update) | async-done | bytes 786448 | tf_op jit(solution)/shard_map/reduce_scatter | solution.py:122
  157.8 2.5 %copy.59 = f32[8,4,6144]{2,1,0:T(4,128)} copy(f32[8,4,6144]{2,0,1:T(8,128)} %bitcast.59) | data formatting | bytes 1572864 | tf_op jit(solution)/shard_map/squeeze | solution.py:123
  160.4 4.6 %all-to-all-start.2 = ((f32[8,4,6144]{2,1,0:T(4,128)}), f32[8,4,6144]{2,1,0:T(4,128)}, u32[]{:S(2)}, u32[]{:S(2)}) async-start(f32[8,4,6144]{2,1,0:T(4,128)} %copy.59), calls=%async_computation.4 | async-start | bytes 1572864 | tf_op jit(solution)/shard_map/all_to_all | solution.py:123
  165.0 0.1 reduce_sum.49
  165.1 0.1 copy.57
  165.2 20.9 %all-to-all-done.2 = f32[8,4,6144]{2,1,0:T(4,128)} async-done(((f32[8,4,6144]{2,1,0:T(4,128)}), f32[8,4,6144]{2,1,0:T(4,128)}, u32[]{:S(2)}, u32[]{:S(2)}) %all-to-all-start.2) | async-done | bytes 786464 | tf_op jit(solution)/shard_map/all_to_all | solution.py:123
  186.1 2.1 %bitcast_reduce_fusion = f32[4,4,6144]{2,1,0:T(4,128)} fusion(f32[8,4,6144]{2,1,0:T(4,128)} %all-to-all-done.2), kind=kLoop, calls=%fused_computation.9 | loop fusion | flops 98304 | bytes 1179648 | tf_op jit(solution)/shard_map/reduce_sum | solution.py:124
  188.2 1.9 reshape.184
  190.1 0.0 copy-done.2
  190.1 1.6 convolution_reduce_fusion
  191.7 0.0 copy-done.1
  191.7 0.7 add_convert_fusion
  (10 shorter events, 0.1 us)
Async XLA Ops:
  6.5 26.0 %copy-start = (bf16[2048,768]{1,0:T(8,128)(2,1)S(1)}, bf16[2048,768]{1,0:T(8,128)(2,1)}, u32[]{:S(2)}) copy-start(bf16[2048,768]{1,0:T(8,128)(2,1)} %param.20) | copy-start | bytes 9437188
  6.5 41.7 %reduce-scatter.3.cloned.1.call-start = ((), (), s32[]{:S(2)}) async-start(), calls=%async_computation.5 | async-start | bytes 589824 | tf_op jit(solution)/shard_map/reduce_scatter | solution.py:84
  48.2 12.9 %all-to-all-start = ((f32[8,8,768]{2,1,0:T(8,128)}), f32[8,8,768]{2,1,0:T(8,128)S(1)}, u32[]{:S(2)}, u32[]{:S(2)}) async-start(f32[8,8,768]{2,1,0:T(8,128)} %bitcast.65), calls=%async_computation.1 | async-start | bytes 393216 | tf_op jit(solution)/shard_map/all_to_all | solution.py:86
  52.8 105.0 %reduce-scatter.5.cloned.1.call-start = ((), (), s32[]{:S(2)}) async-start(), calls=%async_computation.6 | async-start | bytes 2359296 | tf_op jit(solution)/shard_map/reduce_scatter | solution.py:122
  106.3 83.8 %copy-start.2 = (f32[8,2]{0,1:T(2,128)S(1)}, f32[8,2]{0,1:T(2,128)}, u32[]{:S(2)}) copy-start(f32[8,2]{0,1:T(2,128)} %param.24) | copy-start | bytes 196
  106.3 85.4 %copy-start.1 = (bf16[8,6144]{1,0:T(8,128)(2,1)S(1)}, bf16[8,6144]{1,0:T(8,128)(2,1)}, u32[]{:S(2)}) copy-start(bf16[8,6144]{1,0:T(8,128)(2,1)} %param.21) | copy-start | bytes 294916
  160.4 25.7 %all-to-all-start.2 = ((f32[8,4,6144]{2,1,0:T(4,128)}), f32[8,4,6144]{2,1,0:T(4,128)}, u32[]{:S(2)}, u32[]{:S(2)}) async-start(f32[8,4,6144]{2,1,0:T(4,128)} %copy.59), calls=%async_computation.4 | async-start | bytes 1572864 | tf_op jit(solution)/shard_map/all_to_all | solution.py:123
Sparse Core Ops, SparseCore 0:
  34.0 14.1 reduce-scatter.2
  133.4 24.4 reduce-scatter.4
where the time goes:
time: 200 us; the launch traced here: 199 us
  waiting for transfers between devices  67 us (34%)
  blocking collectives  43.1 us (22%)
  matrix products  38.9 us (19%)
  local copies, waits for them, and re-layouts  20.3 us (10%)
  between operations  13.5 us (7%)
  starting transfers between devices  9.27 us (5%)
  other arithmetic  7.04 us (4%)
    reduce_scatter x1, waiting for transfers between devices, on_device(): lax.psum_scatter(partials, ('pair', 'sub'), scatter_dimension=0, tiled=True)  24.6 us
    all_to_all x1, waiting for transfers between devices, on_device(): lax.all_to_all(summed_terms[0], 'dev', split_axis=0, concat_axis=0, tiled...  20.9 us
    dot_general x1, matrix products, expert_apply(): output = jnp.dot(hidden, down_part, preferred_element_type=jnp.float32)  20.7 us
    all_gather x1, blocking collectives, on_device(): lax.all_gather(attended, ('dev', 'sub'), axis=0, tiled=True)  16.6 us
    all_to_all x1, blocking collectives, on_device(): lax.all_to_all(outgoing, 'dev', split_axis=0, concat_axis=0, tiled=True)  14.9 us
    reduce_scatter x1, waiting for transfers between devices, on_device(): shared = lax.psum_scatter(ordered, 'pair', scatter_dimension=0, tiled=True)  13.5 us
    all_gather x1, blocking collectives, on_device(): lax.all_gather(lax.all_to_all(outgoing, 'dev', split_axis=0, concat_axis=...  11.6 us
    dot_general x1, matrix products, expert_apply(): lax.dot_general(flattened, gate_part, contract, preferred_element_type=jn...  10.4 us
  transfers between devices with their start and end apart: 4, of which 4 were waited for; matrix products, arithmetic and copies ran while one was open for 1% of the time, Pallas kernels for 0%

commit v1 on v0

v1 whole, which is shorter than its diff:
```python
import functools

import jax
import jax.numpy as jnp
from jax import lax
from jax.experimental import pallas as pl
from jax.experimental.pallas import tpu as pltpu
from jax.sharding import Mesh
from jax.sharding import PartitionSpec as P

EPSILON = 1e-06
F32 = jnp.float32
BF16 = jnp.bfloat16
MIB = 1 << 20
VMEM = pl.BlockSpec(memory_space=pltpu.VMEM)
SMEM = pl.BlockSpec(memory_space=pltpu.SMEM)
ANY = pl.BlockSpec(memory_space=pl.ANY)


def dot(a, b):
    return jnp.dot(a, b, preferred_element_type=F32)


def dot_t(a, b):
    return lax.dot_general(a, b, (((1,), (1,)), ((), ())), preferred_element_type=F32)


def halves_of(x):
    high = x.astype(BF16)
    return high, (x - high.astype(F32)).astype(BF16)


def attend_kernel(positions, decay_ref, q_ref, k_ref, v_ref, gain_ref, s_ref, o_ref):
    requests, heads, size, _ = s_ref.shape
    rows = q_ref.shape[0]
    first = pl.program_id(0) * heads
    row = lax.broadcasted_iota(jnp.int32, (rows, rows), 0)
    col = lax.broadcasted_iota(jnp.int32, (rows, rows), 1)
    seen = (row // positions == col // positions) & (row >= col)
    distance = jnp.maximum(row - col, 0).astype(F32)
    owner = lax.broadcasted_iota(jnp.int32, (rows, size), 0)
    age = (owner % positions + 1).astype(F32)
    for i in range(heads):
        rate = decay_ref[first + i]
        at = slice(i * size, (i + 1) * size)
        q = q_ref[:, at]
        spread_q = jnp.concatenate(
            [jnp.where(owner // positions == r, q, jnp.zeros_like(q)) for r in range(requests)],
            axis=1,
        )
        high, low = halves_of(s_ref[:, i].reshape(requests * size, size))
        from_state = (dot(spread_q, high) + dot(spread_q, low)) * jnp.exp(-rate * age)
        scores = jnp.where(seen, dot_t(q, k_ref[:, at]) * jnp.exp(-rate * distance), 0.0)
        score_high, score_low = halves_of(scores)
        v = v_ref[:, at]
        mixed = from_state + dot(score_high, v) + dot(score_low, v)
        spread = jnp.mean(mixed * mixed, axis=1, keepdims=True)
        normal = mixed * lax.rsqrt(spread + EPSILON) * gain_ref[:, at]
        o_ref[:, at] = normal.astype(BF16)


def attend(queries, key_rows, value_rows, states, decay_rates, head_gain):
    requests, heads, size, _ = states.shape
    rows = queries.shape[0]
    step = 4 if heads % 4 == 0 else 1
    wide = pl.BlockSpec((rows, step * size), lambda i: (0, i))
    return pl.pallas_call(
        functools.partial(attend_kernel, rows // requests),
        grid=(heads // step,),
        in_specs=[
            SMEM,
            wide,
            wide,
            wide,
            pl.BlockSpec((1, step * size), lambda i: (0, i)),
            pl.BlockSpec((requests, step, size, size), lambda i: (0, i, 0, 0)),
        ],
        out_specs=wide,
        out_shape=jax.ShapeDtypeStruct(queries.shape, BF16),
        compiler_params=pltpu.CompilerParams(vmem_limit_bytes=16 * MIB),
        name="attention",
    )(decay_rates, queries, key_rows, value_rows, head_gain.reshape(1, -1), states)


def project_kernel(count, chunk, base_ref, *refs):
    pieces, weight_ref, out_ref = refs[:count], refs[count], refs[count + 1]
    rows = pieces[0].shape[0]
    per = rows // chunk
    for i in range(count):
        product = dot(pieces[i][...], weight_ref[...]).astype(BF16)
        for j in range(per):
            out_ref[base_ref[i] * per + j] = product[j * chunk : (j + 1) * chunk]


def project(pieces, bases, weight, chunk):
    count = len(pieces)
    rows = pieces[0].shape[0]
    columns = weight.shape[1]
    return pl.pallas_call(
        functools.partial(project_kernel, count, chunk),
        in_specs=[SMEM] + [VMEM] * (count + 1),
        out_specs=VMEM,
        out_shape=jax.ShapeDtypeStruct((count * rows // chunk, chunk, columns), BF16),
        compiler_params=pltpu.CompilerParams(vmem_limit_bytes=16 * MIB),
        name="projection",
    )(bases, *pieces, weight)


def slots_of(ids_ref, experts, capacity):
    top, rows = ids_ref.shape
    order = [(t, k) for t in range(rows) for k in range(top)]
    named = [ids_ref[k, t] for t, k in order]
    slots = {}
    for j, at in enumerate(order):
        rank = jnp.int32(0)
        for i in range(j):
            rank = rank + jnp.where(named[i] == named[j], 1, 0)
        slots[at] = named[j] * capacity + rank
    return slots


def pack_kernel(
    experts, capacity, pairs, subs, ids_ref, got_ref, residual_ref, gain_ref, combined_ref, out_ref
):
    rows, width = residual_ref.shape
    if got_ref.ndim == 2:
        combined = residual_ref[...].astype(F32) + got_ref[...]
    else:
        sources, _, columns = got_ref.shape
        blocks = []
        for b in range(sources // pairs):
            total = residual_ref[:, b * columns : (b + 1) * columns].astype(F32)
            for p in range(pairs):
                source = (b // subs * pairs + p) * subs + b % subs
                total = total + got_ref[source].astype(F32)
            blocks.append(total)
        combined = jnp.concatenate(blocks, axis=1)
    combined_ref[...] = combined
    spread = jnp.mean(combined * combined, axis=1, keepdims=True)
    normed = (combined * lax.rsqrt(spread + EPSILON) * gain_ref[...]).astype(BF16)
    count = experts * capacity
    slot = lax.broadcasted_iota(jnp.int32, (count, rows), 0)
    row = lax.broadcasted_iota(jnp.int32, (count, rows), 1)
    placing = jnp.zeros((count, rows), F32)
    for (t, k), at in slots_of(ids_ref, experts, capacity).items():
        placing = jnp.where((slot == at) & (row == t), 1.0, placing)
    packed = dot(placing.astype(BF16), normed)
    copies = out_ref.shape[0] // experts
    parts = out_ref.shape[1] // capacity
    part = width // parts
    for e in range(experts):
        mine = packed[e * capacity : (e + 1) * capacity]
        folded = jnp.concatenate(
            [mine[:, h * part : (h + 1) * part] for h in range(parts)], axis=0
        ).astype(BF16)
        for c in range(copies):
            out_ref[e * copies + c] = folded


def pack(ids, got, residual, gain, experts, capacity, copies, pairs, subs):
    rows, width = residual.shape
    parts = 8 // capacity
    return pl.pallas_call(
        functools.partial(pack_kernel, experts, capacity, pairs, subs),
        in_specs=[SMEM, VMEM, VMEM, VMEM],
        out_specs=(VMEM, VMEM),
        out_shape=(
            jax.ShapeDtypeStruct((rows, width), F32),
            jax.ShapeDtypeStruct((experts * copies, 8, width // parts), BF16),
        ),
        compiler_params=pltpu.CompilerParams(vmem_limit_bytes=16 * MIB),
        name="pack",
    )(ids, got, residual, gain.reshape(1, -1))


def expert_kernel(capacity, block, wide, count, *refs):
    pieces = refs[:count]
    gate_hbm, up_hbm, down_hbm = refs[count : count + 3]
    own_ref, other_ref = refs[count + 3], refs[count + 4 : -8]
    other_ref = other_ref[0] if other_ref else None
    x_ref, hidden_ref, gate_ref, up_ref, down_ref, gate_sem, up_sem, down_sem = refs[-8:]
    units, width = gate_hbm.shape
    chunks = pieces[0].shape[0]
    parts = 8 // capacity
    part = width // parts
    blocks = units // block
    panels = width // wide

    def gate_copy(t):
        at = pl.ds(t * block, block)
        return pltpu.make_async_copy(gate_hbm.at[at], gate_ref.at[at], gate_sem.at[t])

    def up_copy(t):
        at = pl.ds(t * block, block)
        return pltpu.make_async_copy(up_hbm.at[at], up_ref.at[at], up_sem.at[t])

    def down_copy(n):
        at = pl.ds(n * wide, wide)
        return pltpu.make_async_copy(down_hbm.at[:, at], down_ref.at[:, at], down_sem.at[n])

    for t in range(blocks):
        gate_copy(t).start()
        up_copy(t).start()
    for n in range(panels):
        down_copy(n).start()

    piece_rows = chunks * capacity
    in_part = lax.broadcasted_iota(jnp.int32, (8, part), 0) // capacity
    for i in range(count):
        for h in range(parts):
            tiles = []
            for group in range(chunks // parts):
                tile = jnp.zeros((8, part), F32)
                for p in range(parts):
                    chunk = pieces[i][group * parts + p].astype(F32)
                    shift = (p - h) * capacity % 8
                    chunk = pltpu.roll(chunk, shift, 0) if shift else chunk
                    tile = jnp.where(in_part == p, chunk, tile)
                tiles.append(tile)
            x_ref[i * piece_rows : (i + 1) * piece_rows, h * part : (h + 1) * part] = (
                jnp.concatenate(tiles, axis=0).astype(BF16)
            )

    def hidden_step(t, carry):
        at = pl.ds(pl.multiple_of(t * block, block), block)
        gate_copy(t).wait()
        gate_value = dot_t(gate_ref[at], x_ref[...])
        up_copy(t).wait()
        lifted = dot_t(up_ref[at], x_ref[...])
        hidden_ref[at] = gate_value / (1.0 + jnp.exp(-gate_value)) * lifted
        return carry

    lax.fori_loop(0, blocks, hidden_step, 0)
    hidden = hidden_ref[...].T.astype(BF16)

    for n in range(panels):
        down_copy(n).wait()
        at = slice(n * wide, (n + 1) * wide)
        x_ref[:, at] = dot(hidden, down_ref[:, at]).astype(BF16)

    for i in range(count):
        for group in range(chunks // parts):
            first = i * piece_rows + group * 8
            for p in range(parts):
                tile = jnp.zeros((8, part), F32)
                for h in range(parts):
                    rows = x_ref[first : first + 8, h * part : (h + 1) * part].astype(F32)
                    shift = (h - p) * capacity % 8
                    rows = pltpu.roll(rows, shift, 0) if shift else rows
                    tile = jnp.where(in_part == h, rows, tile)
                if i == 0:
                    own_ref[group * parts + p] = tile.astype(BF16)
                else:
                    other_ref[i - 1, group * parts + p] = tile.astype(BF16)


def expert_apply(pieces, gate_part, up_part, down_part, capacity):
    count = len(pieces)
    units, width = gate_part.shape
    block = next(b for b in (128, 96, 64, 32, 16) if units % b == 0)
    wide = 512
    rows = count * pieces[0].shape[0] * capacity
    return pl.pallas_call(
        functools.partial(expert_kernel, capacity, block, wide, count),
        in_specs=[VMEM] * count + [ANY] * 3,
        out_specs=(VMEM, VMEM),
        out_shape=(
            jax.ShapeDtypeStruct(pieces[0].shape, BF16),
            jax.ShapeDtypeStruct((count - 1,) + pieces[0].shape, BF16),
        ),
        scratch_shapes=[
            pltpu.VMEM((rows, width), BF16),
            pltpu.VMEM((units, rows), F32),
            pltpu.VMEM((units, width), BF16),
            pltpu.VMEM((units, width), BF16),
            pltpu.VMEM((units, width), BF16),
            pltpu.SemaphoreType.DMA((units // block,)),
            pltpu.SemaphoreType.DMA((units // block,)),
            pltpu.SemaphoreType.DMA((width // wide,)),
        ],
        compiler_params=pltpu.CompilerParams(vmem_limit_bytes=56 * MIB),
        name="experts",
    )(*pieces, gate_part, up_part, down_part)


def finish_kernel(experts, capacity, ids_ref, weights_ref, got_ref, combined_ref, out_ref):
    sources, tall, part = got_ref.shape
    copies = sources // experts
    parts = tall // capacity
    rows = combined_ref.shape[0]
    row = lax.broadcasted_iota(jnp.int32, (rows, sources * tall), 0)
    place = lax.broadcasted_iota(jnp.int32, (rows, sources * tall), 1)
    slot = place // (copies * tall) * capacity + place % capacity
    in_part = place % tall // capacity
    weighting = jnp.zeros((rows, sources * tall), F32)
    for (t, k), at in slots_of(ids_ref, experts, capacity).items():
        weighting = jnp.where((slot == at) & (row == t), weights_ref[k, t], weighting)
    got = got_ref[...].reshape(sources * tall, part)
    for h in range(parts):
        at = slice(h * part, (h + 1) * part)
        high, low = halves_of(jnp.where(in_part == h, weighting, 0.0))
        mixture = dot(high, got) + dot(low, got)
        out_ref[:, at] = (combined_ref[:, at] + mixture).astype(BF16)


def finish(ids, weights, got, combined, experts, capacity):
    return pl.pallas_call(
        functools.partial(finish_kernel, experts, capacity),
        in_specs=[SMEM, SMEM, VMEM, VMEM],
        out_specs=VMEM,
        out_shape=jax.ShapeDtypeStruct(combined.shape, BF16),
        compiler_params=pltpu.CompilerParams(vmem_limit_bytes=16 * MIB),
        name="finish",
    )(ids, weights, got, combined)


def shift_along(x, axes, size, by):
    return lax.ppermute(x, axes, [(i, (i + by) % size) for i in range(size)])


def on_device(
    queries,
    key_rows,
    value_rows,
    states,
    decay_rates,
    head_gain,
    out_weight,
    residual,
    norm_gain,
    expert_ids,
    gate_weights,
    expert_gate,
    expert_up,
    expert_down,
):
    experts = lax.axis_size("expert")
    pairs = lax.axis_size("pair")
    subs = lax.axis_size("sub")
    inner = ("half", "sub")
    inners = lax.axis_size("half") * subs
    local_rows, width = residual.shape
    capacity = max(2, local_rows * expert_ids.shape[1] // experts)
    ids, weights = expert_ids.T, gate_weights.T

    attended = attend(queries, key_rows, value_rows, states, decay_rates, head_gain)
    my_expert, my_inner = lax.axis_index("expert"), lax.axis_index(inner)
    pieces, bases = [], []
    for d in range(experts):
        piece = shift_along(attended, "expert", experts, d) if d else attended
        for c in range(inners):
            pieces.append(shift_along(piece, inner, inners, c) if c else piece)
            bases.append(
                (my_expert - d + experts) % experts * inners + (my_inner - c + inners) % inners
            )
    blocks = project(pieces, jnp.stack(bases).astype(jnp.int32), out_weight, local_rows)

    columns = out_weight.shape[1]
    got = lax.all_to_all(
        blocks, ("expert", "half", "pair", "sub"), split_axis=0, concat_axis=0, tiled=True
    )
    if columns % 128:
        got = got.reshape(experts * 2, pairs, subs, local_rows, columns).astype(F32)
        got = jnp.transpose(got.sum(axis=1), (2, 0, 1, 3)).reshape(local_rows, width)
    combined, outgoing = pack(
        ids, got, residual, norm_gain, experts, capacity, pairs, pairs, subs
    )

    plane = ("expert", "pair")
    routed = lax.all_to_all(outgoing, plane, split_axis=0, concat_axis=0, tiled=True)
    routed = [shift_along(routed, inner, inners, c) if c else routed for c in range(inners)]
    own, others = expert_apply(routed, expert_gate, expert_up, expert_down, capacity)

    total = own.astype(F32)
    for c in range(1, inners):
        total = total + shift_along(others[c - 1], inner, inners, inners - c).astype(F32)
    back = lax.all_to_all(total.astype(BF16), plane, split_axis=0, concat_axis=0, tiled=True)
    return finish(ids, weights, back, combined, experts, capacity)


def solution(mesh):
    sizes = dict(mesh.shape)
    experts = sizes["dev"] // 2
    cut = Mesh(
        mesh.devices.reshape(sizes["grp"], experts, 2, sizes["pair"], sizes["sub"]),
        ("grp", "expert", "half", "pair", "sub"),
    )
    dev = ("expert", "half")
    requests = P(("grp",) + dev + ("sub",), "pair")
    tokens = P(("grp",) + dev + ("pair", "sub"), None)
    units = P(dev + ("pair", "sub"), None)
    return jax.shard_map(
        on_device,
        mesh=cut,
        in_specs=(
            requests,
            requests,
            requests,
            P(("grp",) + dev + ("sub",), "pair", None, None),
            P("pair"),
            P("pair"),
            P("pair", dev + ("sub",)),
            tokens,
            P(),
            tokens,
            tokens,
            units,
            units,
            units,
        ),
        out_specs=tokens,
        check_vma=False,
    )
```

time: 200 us -> 109 us (0.55)
  waiting for transfers between devices: 67 us -> 9.77 us
  matrix products: 38.9 us -> 0 us
  Pallas kernels: 0 us -> 35.7 us
  between operations: 13.5 us -> 0.07 us
  local copies, waits for them, and re-layouts: 20.3 us -> 11.1 us
  other arithmetic: 7.04 us -> 1.1 us
  starting transfers between devices: 9.27 us -> 6.84 us
    dot_general x8 -> x0, matrix products: 38.9 us -> none  [the longest x1 20.7 us: expert_apply(): output = jnp.dot(hidden, down_part, preferred_element_type=jnp.float32)]
    reduce_scatter x2 -> x0, waiting for transfers between devices: 38.1 us -> none  [the longest x1 24.6 us: on_device(): lax.psum_scatter(partials, ('pair', 'sub'), scatter_dimension=0, tiled=True)]
    pallas_call x0 -> x5, Pallas kernels: none -> 35.7 us  [the longest x1 25.9 us: expert_apply(): pl.pallas_call(functools.partial(expert_kernel, capacity, block, wide, co...]
    all_to_all x2 -> x0, waiting for transfers between devices: 28.9 us -> none  [the longest x1 20.9 us: on_device(): lax.all_to_all(summed_terms[0], 'dev', split_axis=0, concat_axis=0, tiled...]
    all_to_all x1 -> x3, blocking collectives: 14.9 us -> 43.3 us  [the longest x1 15.4 us: on_device(): lax.all_to_all(total.astype(BF16), plane, split_axis=0, concat_axis=0, ti...]
    all_gather x2 -> x0, blocking collectives: 28.2 us -> none  [the longest x1 16.6 us: on_device(): lax.all_gather(attended, ('dev', 'sub'), axis=0, tiled=True)]
    reshape x7 -> x0, local copies, waits for them, and re-layouts: 12.3 us -> none  [the longest x2 6.26 us: expert_apply(): return output.reshape(leading)]
    ppermute x0 -> x9, waiting for transfers between devices: none -> 9.77 us  [shift_along(): return lax.ppermute(x, axes, [(i, (i + by) % size) for i in range(size)])]
  transfers between devices with their start and end apart: 4 -> 9, of which waited for: 4 -> 6; matrix products, arithmetic and copies ran while one was open for 1% -> 0% of each run, Pallas kernels for 0% -> 0%
where the time goes in v1:
time: 109 us; the launch traced here: 108 us
  blocking collectives  43.3 us (40%)
  Pallas kernels  35.7 us (33%)
  local copies, waits for them, and re-layouts  11.1 us (10%)
  waiting for transfers between devices  9.77 us (9%)
  starting transfers between devices  6.84 us (6%)
  other arithmetic  1.1 us (1%)
    pallas_call x1, Pallas kernels, expert_apply(): pl.pallas_call(functools.partial(expert_kernel, capacity, block, wide, co...  25.9 us
    all_to_all x1, blocking collectives, on_device(): lax.all_to_all(total.astype(BF16), plane, split_axis=0, concat_axis=0, ti...  15.4 us
    all_to_all x1, blocking collectives, on_device(): lax.all_to_all(outgoing, plane, split_axis=0, concat_axis=0, tiled=True)  15.1 us
    all_to_all x1, blocking collectives, on_device(): lax.all_to_all(blocks, ('expert', 'half', 'pair', 'sub'), split_axis=0, c...  12.7 us
    unnamed x28, local copies, waits for them, and re-layouts  11 us
    ppermute x9, waiting for transfers between devices, shift_along(): return lax.ppermute(x, axes, [(i, (i + by) % size) for i in range(size)])  9.77 us
    ppermute x9, starting transfers between devices, shift_along(): return lax.ppermute(x, axes, [(i, (i + by) % size) for i in range(size)])  6.84 us
    pallas_call x1, Pallas kernels, project(): pl.pallas_call(functools.partial(project_kernel, count, chunk), in_specs=...  3.9 us
  transfers between devices with their start and end apart: 9, of which 6 were waited for; matrix products, arithmetic and copies ran while one was open for 0% of the time, Pallas kernels for 0%

profile of v1, /device:TPU:0, one launch (start us, length us, event | category | flops | bytes accessed | tf_op | source)
XLA Modules:
  0.0 107.9 jit_solution(10680988853200655163)
XLA Ops:
  0.0 0.0 copy-start
  0.0 2.2 %copy-done = f32[4,16,128,128]{3,2,1,0:T(8,128)S(1)} copy-done((f32[4,16,128,128]{3,2,1,0:T(8,128)S(1)}, f32[4,16,128,128]{3,2,1,0:T(8,128)}, u32[]{:S(2)}) %copy-start) | copy-done | bytes 4194328
  2.2 0.0 copy-start.3
  2.2 0.8 copy-done.3
  3.0 0.0 copy-start.4
  3.0 0.8 copy-done.4
  3.9 0.0 copy-start.5
  3.9 0.8 copy-done.5
  4.7 0.0 copy-start.7
  4.7 0.7 copy-done.7
  5.4 0.0 copy-start.11
  5.4 0.7 copy-done.11
  6.1 3.3 %attention.1.refs_0_ = bf16[16,2048]{1,0:T(8,128)(2,1)S(1)} custom-call(f32[16]{0:T(128)S(1)} %copy-done.11, bf16[16,2048]{1,0:T(8,128)(2,1)S(1)} %copy-done.3, bf16[16,2048]{1,0:T(8,128)(2,1)S(1)} %copy-done.4, bf16[16,2048]{1,0:T(8,128)(2,1)S(1)} %copy-done.5, f32[1,2048]{1,0:T(1,128)S(1)} %bitcast.14, f32[4,16,128,128]{3,2,1,0:T(8,128)S(1)} %copy-done), custom_call_target="tpu_custom_call" | custom-call | tf_op jit(solution)/shard_map/attention/pallas_call | solution.py:67
  9.4 5.1 %collective-permute-start.5 = (bf16[16,2048]{1,0:T(8,128)(2,1)S(1)}, bf16[16,2048]{1,0:T(8,128)(2,1)S(1)}, u32[]{:S(2)}, u32[]{:S(2)}) collective-permute-start(bf16[16,2048]{1,0:T(8,128)(2,1)S(1)} %attention.1.refs_0_), channel_id=1, source_target_pairs={{0,12},{4,0},{8,4},{12,8},{1,13},{5,1},{9,5},{13,9},{2,14},{6,2},{... | collective-permute-start | bytes 196616 | tf_op jit(solution)/shard_map/ppermute | solution.py:318
  14.5 0.0 collective-permute-start.3
  14.5 1.0 collective-permute-start.1
  15.5 0.0 collective-permute-start
  15.5 1.5 %collective-permute-done.5.refs_6_ = bf16[16,2048]{1,0:T(8,128)(2,1)S(1)} collective-permute-done((bf16[16,2048]{1,0:T(8,128)(2,1)S(1)}, bf16[16,2048]{1,0:T(8,128)(2,1)S(1)}, u32[]{:S(2)}, u32[]{:S(2)}) %collective-permute-start.5) | collective-permute-done | bytes 65568 | tf_op jit(solution)/shard_map/ppermute | solution.py:318
  17.0 0.0 collective-permute-start.6
  17.0 4.0 %collective-permute-done.3.refs_4_ = bf16[16,2048]{1,0:T(8,128)(2,1)S(1)} collective-permute-done((bf16[16,2048]{1,0:T(8,128)(2,1)S(1)}, bf16[16,2048]{1,0:T(8,128)(2,1)S(1)}, u32[]{:S(2)}, u32[]{:S(2)}) %collective-permute-start.3) | collective-permute-done | bytes 65568 | tf_op jit(solution)/shard_map/ppermute | solution.py:318
  20.9 0.0 collective-permute-start.4
  20.9 0.0 collective-permute-done.1.refs_2_
  20.9 0.5 collective-permute-start.2
  21.4 0.1 stack.35.base_ref
  21.5 0.0 collective-permute-done.refs_1_
  21.5 0.0 collective-permute-done.6.refs_7_
  21.5 0.6 collective-permute-done.4.refs_5_
  22.2 0.2 collective-permute-done.2.refs_3_
  22.3 0.0 copy-start.1
  22.3 1.9 %copy-done.1 = bf16[2048,768]{1,0:T(8,128)(2,1)S(1)} copy-done((bf16[2048,768]{1,0:T(8,128)(2,1)S(1)}, bf16[2048,768]{1,0:T(8,128)(2,1)}, u32[]{:S(2)}) %copy-start.1) | copy-done | bytes 3145752
  24.2 3.9 %projection.1 = bf16[16,8,768]{2,1,0:T(8,128)(2,1)S(1)} custom-call(s32[8]{0:T(128)S(1)} %stack.35.base_ref, bf16[16,2048]{1,0:T(8,128)(2,1)S(1)} %attention.1.refs_0_, bf16[16,2048]{1,0:T(8,128)(2,1)S(1)} %collective-permute-done.refs_1_, bf16[16,2048]{1,0:T(8,128)(2,1)S(1)} %collective-permute-done.1.refs_2_, ...), custom_call_target="tpu_custom_call" | custom-call | tf_op jit(solution)/shard_map/projection/pallas_call | solution.py:99
  28.1 12.7 %all_to_all.15.got_ref = bf16[16,8,768]{2,1,0:T(8,128)(2,1)S(1)} all-to-all(bf16[16,8,768]{2,1,0:T(8,128)(2,1)S(1)} %projection.1), channel_id=1, replica_groups=mesh['grp'=2,'expert'=4,'half'=2,'pair'=2,'sub'=1] {'expert','half','pai..., dimensions={0} | all-to-all | bytes 393216 | tf_op jit(solution)/shard_map/all_to_all | solution.py:359
  40.9 0.0 copy-start.2
  40.9 0.9 copy-done.2
  41.8 0.0 copy-start.6
  41.8 0.7 copy-done.6
  42.5 0.0 copy-start.8
  42.5 0.7 copy-done.8
  43.2 0.9 pack.1
  44.1 15.1 %all_to_all.16.refs_0_ = bf16[8,8,3072]{2,1,0:T(8,128)(2,1)S(1)} all-to-all(bf16[8,8,3072]{2,1,0:T(8,128)(2,1)S(1)} %get-tuple-element.9), channel_id=1, replica_groups=mesh['grp'=2,'expert'=4,'half'=2,'pair'=2,'sub'=1] {'expert','pair'}, dimensions={0} | all-to-all | bytes 786432 | tf_op jit(solution)/shard_map/all_to_all | solution.py:370
  59.2 0.0 copy-start.12
  59.3 0.0 copy-start.9
  59.3 0.0 copy-start.10
  59.3 0.0 collective-permute-start.7
  59.3 1.7 %collective-permute-done.7.refs_1_ = bf16[8,8,3072]{2,1,0:T(8,128)(2,1)S(1)} collective-permute-done((bf16[8,8,3072]{2,1,0:T(8,128)(2,1)S(1)}, bf16[8,8,3072]{2,1,0:T(8,128)(2,1)S(1)}, u32[]{:S(2)}, u32[]{:S(2)}) %collective-permute-start.7) | collective-permute-done | bytes 393248 | tf_op jit(solution)/shard_map/ppermute | solution.py:318
  61.0 0.0 copy-done.12
  61.0 0.0 copy-start.13
  61.0 0.7 copy-done.13
  61.7 25.9 %experts.1 = (bf16[8,8,3072]{2,1,0:T(8,128)(2,1)}, bf16[1,8,8,3072]{3,2,1,0:T(8,128)(2,1)}) custom-call(bf16[8,8,3072]{2,1,0:T(8,128)(2,1)} %copy-done.12, bf16[8,8,3072]{2,1,0:T(8,128)(2,1)} %copy-done.13, bf16[1152,6144]{1,0:T(8,128)(2,1)} %refs_2_.1, bf16[1152,6144]{1,0:T(8,128)(2,1)} %refs_3_.1, bf16[1152,6144]{1,0:T(8,128)(2,1)} %refs_4_.1), custom_call_target="tpu_custom_call" | custom-call | tf_op jit(solution)/shard_map/experts/pallas_call | solution.py:263
  87.6 0.2 collective-permute-start.8
  87.8 1.8 %collective-permute-done.8 = bf16[8,8,3072]{2,1,0:T(8,128)(2,1)S(1)} collective-permute-done((bf16[8,8,3072]{2,1,0:T(8,128)(2,1)}, bf16[8,8,3072]{2,1,0:T(8,128)(2,1)S(1)}, u32[]{:S(2)}, u32[]{:S(2)}) %collective-permute-start.8) | collective-permute-done | bytes 393248 | tf_op jit(solution)/shard_map/ppermute | solution.py:318
  89.6 1.1 %add_convert_fusion = bf16[8,8,3072]{2,1,0:T(8,128)(2,1)S(1)} fusion(bf16[8,8,3072]{2,1,0:T(8,128)(2,1)S(1)} %collective-permute-done.8, bf16[8,8,3072]{2,1,0:T(8,128)(2,1)} %get-tuple-element.10), kind=kLoop, calls=%fused_computation | loop fusion | flops 786432 | bytes 1179648 | tf_op jit(solution)/shard_map/convert_element_type | solution.py:377
  90.7 15.4 %all_to_all.17.got_ref = bf16[8,8,3072]{2,1,0:T(8,128)(2,1)S(1)} all-to-all(bf16[8,8,3072]{2,1,0:T(8,128)(2,1)S(1)} %add_convert_fusion), channel_id=1, replica_groups=mesh['grp'=2,'expert'=4,'half'=2,'pair'=2,'sub'=1] {'expert','pair'}, dimensions={0} | all-to-all | bytes 786432 | tf_op jit(solution)/shard_map/all_to_all | solution.py:377
  106.2 0.0 copy-done.9
  106.2 0.0 copy-done.10
  106.2 1.7 %finish.1 = bf16[8,6144]{1,0:T(8,128)(2,1)} custom-call(s32[2,8]{1,0:T(2,128)S(1)} %bitcast.16, f32[2,8]{1,0:T(2,128)S(1)} %bitcast.17, bf16[8,8,3072]{2,1,0:T(8,128)(2,1)S(1)} %all_to_all.17.got_ref, f32[8,6144]{1,0:T(8,128)S(1)} %get-tuple-element.12.combined_ref), custom_call_target="tpu_custom_call" | custom-call | tf_op jit(solution)/shard_map/finish/pallas_call | solution.py:307
Async XLA Ops:
  0.0 2.2 %copy-start = (f32[4,16,128,128]{3,2,1,0:T(8,128)S(1)}, f32[4,16,128,128]{3,2,1,0:T(8,128)}, u32[]{:S(2)}) copy-start(f32[4,16,128,128]{3,2,1,0:T(8,128)} %s_ref.1) | copy-start | bytes 12582916
  2.2 0.8 copy-start.3
  3.0 0.8 copy-start.4
  3.9 0.8 copy-start.5
  4.7 0.7 copy-start.7
  5.4 0.7 copy-start.11
  9.4 7.6 %collective-permute-start.5 = (bf16[16,2048]{1,0:T(8,128)(2,1)S(1)}, bf16[16,2048]{1,0:T(8,128)(2,1)S(1)}, u32[]{:S(2)}, u32[]{:S(2)}) collective-permute-start(bf16[16,2048]{1,0:T(8,128)(2,1)S(1)} %attention.1.refs_0_), channel_id=1, source_target_pairs={{0,12},{4,0},{8,4},{12,8},{1,13},{5,1},{9,5},{13,9},{2,14},{6,2},{... | collective-permute-start | bytes 196616 | tf_op jit(solution)/shard_map/ppermute | solution.py:318
  14.5 6.5 %collective-permute-start.3 = (bf16[16,2048]{1,0:T(8,128)(2,1)S(1)}, bf16[16,2048]{1,0:T(8,128)(2,1)S(1)}, u32[]{:S(2)}, u32[]{:S(2)}) collective-permute-start(bf16[16,2048]{1,0:T(8,128)(2,1)S(1)} %attention.1.refs_0_), channel_id=1, source_target_pairs={{0,8},{4,12},{8,0},{12,4},{1,9},{5,13},{9,1},{13,5},{2,10},{6,14},... | collective-permute-start | bytes 196616 | tf_op jit(solution)/shard_map/ppermute | solution.py:318
  14.5 6.5 %collective-permute-start.1 = (bf16[16,2048]{1,0:T(8,128)(2,1)S(1)}, bf16[16,2048]{1,0:T(8,128)(2,1)S(1)}, u32[]{:S(2)}, u32[]{:S(2)}) collective-permute-start(bf16[16,2048]{1,0:T(8,128)(2,1)S(1)} %attention.1.refs_0_), channel_id=1, source_target_pairs={{0,4},{4,8},{8,12},{12,0},{1,5},{5,9},{9,13},{13,1},{2,6},{6,10},{... | collective-permute-start | bytes 196616 | tf_op jit(solution)/shard_map/ppermute | solution.py:318
  15.5 6.1 %collective-permute-start = (bf16[16,2048]{1,0:T(8,128)(2,1)S(1)}, bf16[16,2048]{1,0:T(8,128)(2,1)S(1)}, u32[]{:S(2)}, u32[]{:S(2)}) collective-permute-start(bf16[16,2048]{1,0:T(8,128)(2,1)S(1)} %attention.1.refs_0_), channel_id=1, source_target_pairs={{0,2},{2,0},{1,3},{3,1},{4,6},{6,4},{5,7},{7,5},{8,10},{10,8},{9,1... | collective-permute-start | bytes 196616 | tf_op jit(solution)/shard_map/ppermute | solution.py:318
  17.0 4.6 %collective-permute-start.6 = (bf16[16,2048]{1,0:T(8,128)(2,1)S(1)}, bf16[16,2048]{1,0:T(8,128)(2,1)S(1)}, u32[]{:S(2)}, u32[]{:S(2)}) collective-permute-start(bf16[16,2048]{1,0:T(8,128)(2,1)S(1)} %collective-permute-done.5.refs_6_), channel_id=1, source_target_pairs={{0,2},{2,0},{1,3},{3,1},{4,6},{6,4},{5,7},{7,5},{8,10},{10,8},{9,1... | collective-permute-start | bytes 196616 | tf_op jit(solution)/shard_map/ppermute | solution.py:318
  20.9 1.3 %collective-permute-start.4 = (bf16[16,2048]{1,0:T(8,128)(2,1)S(1)}, bf16[16,2048]{1,0:T(8,128)(2,1)S(1)}, u32[]{:S(2)}, u32[]{:S(2)}) collective-permute-start(bf16[16,2048]{1,0:T(8,128)(2,1)S(1)} %collective-permute-done.3.refs_4_), channel_id=1, source_target_pairs={{0,2},{2,0},{1,3},{3,1},{4,6},{6,4},{5,7},{7,5},{8,10},{10,8},{9,1... | collective-permute-start | bytes 196616 | tf_op jit(solution)/shard_map/ppermute | solution.py:318
  20.9 1.4 %collective-permute-start.2 = (bf16[16,2048]{1,0:T(8,128)(2,1)S(1)}, bf16[16,2048]{1,0:T(8,128)(2,1)S(1)}, u32[]{:S(2)}, u32[]{:S(2)}) collective-permute-start(bf16[16,2048]{1,0:T(8,128)(2,1)S(1)} %collective-permute-done.1.refs_2_), channel_id=1, source_target_pairs={{0,2},{2,0},{1,3},{3,1},{4,6},{6,4},{5,7},{7,5},{8,10},{10,8},{9,1... | collective-permute-start | bytes 196616 | tf_op jit(solution)/shard_map/ppermute | solution.py:318
  22.3 1.9 %copy-start.1 = (bf16[2048,768]{1,0:T(8,128)(2,1)S(1)}, bf16[2048,768]{1,0:T(8,128)(2,1)}, u32[]{:S(2)}) copy-start(bf16[2048,768]{1,0:T(8,128)(2,1)} %refs_8_.1) | copy-start | bytes 9437188
  40.9 0.9 copy-start.2
  41.8 0.7 copy-start.6
  42.5 0.7 copy-start.8
  59.2 1.7 %copy-start.12 = (bf16[8,8,3072]{2,1,0:T(8,128)(2,1)}, bf16[8,8,3072]{2,1,0:T(8,128)(2,1)S(1)}, u32[]{:S(2)}) copy-start(bf16[8,8,3072]{2,1,0:T(8,128)(2,1)S(1)} %all_to_all.16.refs_0_) | copy-start | bytes 1179652
  59.3 46.9 %copy-start.9 = (s32[8,2]{0,1:T(2,128)S(1)}, s32[8,2]{0,1:T(2,128)}, u32[]{:S(2)}) copy-start(s32[8,2]{0,1:T(2,128)} %param.23) | copy-start | bytes 196
  59.3 46.9 %copy-start.10 = (f32[8,2]{0,1:T(2,128)S(1)}, f32[8,2]{0,1:T(2,128)}, u32[]{:S(2)}) copy-start(f32[8,2]{0,1:T(2,128)} %param.24) | copy-start | bytes 196
  59.3 1.7 %collective-permute-start.7 = (bf16[8,8,3072]{2,1,0:T(8,128)(2,1)S(1)}, bf16[8,8,3072]{2,1,0:T(8,128)(2,1)S(1)}, u32[]{:S(2)}, u32[]{:S(2)}) collective-permute-start(bf16[8,8,3072]{2,1,0:T(8,128)(2,1)S(1)} %all_to_all.16.refs_0_), channel_id=1, source_target_pairs={{0,2},{2,0},{1,3},{3,1},{4,6},{6,4},{5,7},{7,5},{8,10},{10,8},{9,1... | collective-permute-start | bytes 1179656 | tf_op jit(solution)/shard_map/ppermute | solution.py:318
  61.0 0.7 copy-start.13
  87.6 2.0 %collective-permute-start.8 = (bf16[8,8,3072]{2,1,0:T(8,128)(2,1)}, bf16[8,8,3072]{2,1,0:T(8,128)(2,1)S(1)}, u32[]{:S(2)}, u32[]{:S(2)}) collective-permute-start(bf16[8,8,3072]{2,1,0:T(8,128)(2,1)} %bitcast.18), channel_id=1, source_target_pairs={{0,2},{2,0},{1,3},{3,1},{4,6},{6,4},{5,7},{7,5},{8,10},{10,8},{9,1... | collective-permute-start | bytes 1179656 | tf_op jit(solution)/shard_map/ppermute | solution.py:318

commit v2 on v1

v2 whole, which is shorter than its diff:
```python
import functools

import jax
import jax.numpy as jnp
from jax import lax
from jax.experimental import pallas as pl
from jax.experimental.pallas import tpu as pltpu
from jax.sharding import Mesh
from jax.sharding import PartitionSpec as P

EPSILON = 1e-06
F32 = jnp.float32
BF16 = jnp.bfloat16
MIB = 1 << 20
VMEM = pl.BlockSpec(memory_space=pltpu.VMEM)
SMEM = pl.BlockSpec(memory_space=pltpu.SMEM)
ANY = pl.BlockSpec(memory_space=pl.ANY)


def in_hbm(*arrays):
    return [pltpu.with_memory_space_constraint(a, pltpu.HBM) for a in arrays]


def limits(mib):
    return pltpu.CompilerParams(vmem_limit_bytes=mib * MIB)


def here():
    inner = lax.axis_index("half") * lax.axis_size("sub") + lax.axis_index("sub")
    return lax.axis_index("expert"), inner, lax.axis_index("pair")


def dot(a, b):
    return jnp.dot(a, b, preferred_element_type=F32)


def dot_t(a, b):
    return lax.dot_general(a, b, (((1,), (1,)), ((), ())), preferred_element_type=F32)


def halves_of(x):
    high = x.astype(BF16)
    return high, (x - high.astype(F32)).astype(BF16)


def attend_kernel(positions, decay_ref, q_ref, k_ref, v_ref, gain_ref, s_ref, o_ref):
    requests, heads, size, _ = s_ref.shape
    rows = q_ref.shape[0]
    first = pl.program_id(0) * heads
    row = lax.broadcasted_iota(jnp.int32, (rows, rows), 0)
    col = lax.broadcasted_iota(jnp.int32, (rows, rows), 1)
    seen = (row // positions == col // positions) & (row >= col)
    distance = jnp.maximum(row - col, 0).astype(F32)
    owner = lax.broadcasted_iota(jnp.int32, (rows, size), 0)
    age = (owner % positions + 1).astype(F32)
    for i in range(heads):
        rate = decay_ref[first + i]
        at = slice(i * size, (i + 1) * size)
        q = q_ref[:, at]
        spread_q = jnp.concatenate(
            [jnp.where(owner // positions == r, q, jnp.zeros_like(q)) for r in range(requests)],
            axis=1,
        )
        high, low = halves_of(s_ref[:, i].reshape(requests * size, size))
        from_state = (dot(spread_q, high) + dot(spread_q, low)) * jnp.exp(-rate * age)
        scores = jnp.where(seen, dot_t(q, k_ref[:, at]) * jnp.exp(-rate * distance), 0.0)
        score_high, score_low = halves_of(scores)
        v = v_ref[:, at]
        mixed = from_state + dot(score_high, v) + dot(score_low, v)
        spread = jnp.mean(mixed * mixed, axis=1, keepdims=True)
        normal = mixed * lax.rsqrt(spread + EPSILON) * gain_ref[:, at]
        o_ref[:, at] = normal.astype(BF16)


def attend(queries, key_rows, value_rows, states, decay_rates, head_gain):
    requests, heads, size, _ = states.shape
    rows = queries.shape[0]
    step = 4 if heads % 4 == 0 else 1
    wide = pl.BlockSpec((rows, step * size), lambda i: (0, i))
    return pl.pallas_call(
        functools.partial(attend_kernel, rows // requests),
        grid=(heads // step,),
        in_specs=[
            SMEM,
            wide,
            wide,
            wide,
            pl.BlockSpec((1, step * size), lambda i: (0, i)),
            pl.BlockSpec((requests, step, size, size), lambda i: (0, i, 0, 0)),
        ],
        out_specs=wide,
        out_shape=jax.ShapeDtypeStruct(queries.shape, BF16),
        compiler_params=limits(8),
        name="attention",
    )(*in_hbm(decay_rates, queries, key_rows, value_rows, head_gain.reshape(1, -1), states))


def load_kernel(count, *refs):
    sources, targets, sems = refs[:count], refs[count + 1 : -1], refs[-1]
    copies = [
        pltpu.make_async_copy(source, target, sems.at[i])
        for i, (source, target) in enumerate(zip(sources, targets))
    ]
    for copy in copies:
        copy.start()
    for copy in copies:
        copy.wait()


def load(arrays, after, name):
    count = len(arrays)
    size = sum(a.size * a.dtype.itemsize for a in arrays)
    return pl.pallas_call(
        functools.partial(load_kernel, count),
        in_specs=[ANY] * (count + 1),
        out_specs=[VMEM] * count,
        out_shape=[pltpu.VMEM(a.shape, a.dtype) for a in arrays],
        scratch_shapes=[pltpu.SemaphoreType.DMA((count,))],
        compiler_params=limits(1),
        cost_estimate=pl.CostEstimate(flops=0, bytes_accessed=2 * size, transcendentals=0),
        name=name,
    )(*in_hbm(*arrays), after)


def project_kernel(chunk, experts, inners, relative, *refs):
    count = experts * inners
    pieces, weight_ref = refs[:count], refs[count]
    outs, x_ref, product_ref = refs[count + 1 : -2], refs[-2], refs[-1]
    rows = pieces[0].shape[0]
    expert, inner, pair = here()
    for d in range(experts):
        for c in range(inners):
            base = (expert ^ d) * inners + (inner ^ c)
            x_ref[pl.ds(pl.multiple_of(base * rows, rows), rows)] = pieces[d * inners + c][...]
    product_ref[...] = dot(x_ref[...], weight_ref[...])
    if relative:
        me = lax.axis_index(("expert", "half", "pair", "sub"))
        for d, out in enumerate(outs):
            at = pl.ds(pl.multiple_of((me ^ d) * chunk, chunk), chunk)
            out[...] = product_ref[at].astype(BF16)
    else:
        for d in range(outs[0].shape[0]):
            outs[0][d] = product_ref[d * chunk : (d + 1) * chunk].astype(BF16)


def project(pieces, weight, chunk, experts, inners, relative):
    rows = pieces[0].shape[0] * len(pieces)
    depth, columns = weight.shape
    chunks = rows // chunk
    if relative:
        out_shape = [jax.ShapeDtypeStruct((chunk, columns), BF16)] * chunks
    else:
        out_shape = [jax.ShapeDtypeStruct((chunks, chunk, columns), BF16)]
    return pl.pallas_call(
        functools.partial(project_kernel, chunk, experts, inners, relative),
        in_specs=[VMEM] * (len(pieces) + 1),
        out_specs=[VMEM] * len(out_shape),
        out_shape=out_shape,
        scratch_shapes=[pltpu.VMEM((rows, depth), BF16), pltpu.VMEM((rows, columns), F32)],
        compiler_params=limits(8),
        name="projection",
    )(*pieces, weight)


def slots_of(ids_ref, capacity, me):
    top, rows = ids_ref.shape
    order = [(t, k) for t in range(rows) for k in range(top)]
    named = [ids_ref[k, t] for t, k in order]
    slots = {}
    for j, at in enumerate(order):
        rank = jnp.int32(0)
        for i in range(j):
            rank = rank + jnp.where(named[i] == named[j], 1, 0)
        slots[at] = (named[j] ^ me) * capacity + rank
    return slots


def pack_kernel(capacity, pairs, subs, relative, count, ids_ref, residual_ref, gain_ref, *refs):
    got, combined_ref, outs = refs[:count], refs[count], refs[count + 1 :]
    rows, width = residual_ref.shape
    experts = lax.axis_size("expert")
    if count == 1:
        combined_ref[...] = residual_ref[...].astype(F32) + got[0][...]
    else:
        combined_ref[...] = residual_ref[...].astype(F32)
        columns = got[0].shape[1]
        me = lax.axis_index(("expert", "half", "pair", "sub"))
        for d in range(count):
            source = me ^ d
            block = source // (pairs * subs) * subs + source % subs
            at = pl.ds(pl.multiple_of(block * columns, columns), columns)
            combined_ref[:, at] += got[d][...].astype(F32)
    combined = combined_ref[...]
    spread = jnp.mean(combined * combined, axis=1, keepdims=True)
    normed = (combined * lax.rsqrt(spread + EPSILON) * gain_ref[...]).astype(BF16)
    slot = lax.broadcasted_iota(jnp.int32, (experts * capacity, rows), 0)
    row = lax.broadcasted_iota(jnp.int32, (experts * capacity, rows), 1)
    placing = jnp.zeros((experts * capacity, rows), F32)
    me = lax.axis_index("expert") if relative else 0
    for (t, k), at in slots_of(ids_ref, capacity, me).items():
        placing = jnp.where((slot == at) & (row == t), 1.0, placing)
    packed = dot(placing.astype(BF16), normed)
    parts = outs[0].shape[1] // capacity
    part = width // parts
    for e in range(experts):
        mine = packed[e * capacity : (e + 1) * capacity]
        folded = jnp.concatenate(
            [mine[:, h * part : (h + 1) * part] for h in range(parts)], axis=0
        ).astype(BF16)
        if relative:
            outs[e][0] = folded
        else:
            for c in range(pairs):
                outs[0][e * pairs + c] = folded


def pack(ids, residual, gain, got, capacity, experts, pairs, subs, relative):
    rows, width = residual.shape
    parts = 8 // capacity
    if relative:
        out_shape = [jax.ShapeDtypeStruct((1, 8, width // parts), BF16)] * experts
    else:
        out_shape = [jax.ShapeDtypeStruct((experts * pairs, 8, width // parts), BF16)]
    return pl.pallas_call(
        functools.partial(pack_kernel, capacity, pairs, subs, relative, len(got)),
        in_specs=[SMEM, VMEM, VMEM] + [VMEM] * len(got),
        out_specs=[VMEM] * (1 + len(out_shape)),
        out_shape=[jax.ShapeDtypeStruct((rows, width), F32)] + out_shape,
        compiler_params=limits(8),
        name="pack",
    )(*in_hbm(ids), residual, gain, *got)


def expert_kernel(capacity, block, wide, own, count, *refs):
    pieces, gate_ref, up_ref, down_hbm = refs[:count], *refs[count : count + 3]
    own_ref, others_ref = refs[count + 3 : count + 5]
    x_ref, hidden_ref, down_ref, down_sem = refs[count + 5 :]
    units, width = gate_ref.shape
    parts = 8 // capacity
    part = width // parts
    rows = x_ref.shape[0]

    def down_copy(n):
        at = pl.ds(n * wide, wide)
        return pltpu.make_async_copy(down_hbm.at[:, at], down_ref.at[:, at], down_sem.at[n])

    panels = [[(h * part) // wide + n for h in range(parts)] for n in range(part // wide)]
    for panel in panels:
        for n in panel:
            down_copy(n).start()

    first = 0
    for piece in pieces:
        tall = piece.shape[0] * 8
        x_ref[first : first + tall] = piece[...].astype(F32).reshape(tall, part)
        first += tall
    x = x_ref[...].T.astype(BF16)

    part_of = lax.broadcasted_iota(jnp.int32, (block, rows), 1) % 8 // capacity

    def product(weight_ref, at):
        total = jnp.zeros((block, rows), F32)
        for h in range(parts):
            term = dot(weight_ref[at, h * part : (h + 1) * part], x)
            total = jnp.where(part_of == h, term, total)
        step = 1
        while step < parts:
            odd = part_of // step % 2 == 1
            by = step * capacity
            total = total + jnp.where(
                odd, pltpu.roll(total, by, 1), pltpu.roll(total, rows - by, 1)
            )
            step *= 2
        return total

    for t in range(units // block):
        at = slice(t * block, (t + 1) * block)
        gate_value = product(gate_ref, at)
        lifted = product(up_ref, at)
        hidden = gate_value / (1.0 + jnp.exp(-gate_value)) * lifted
        hidden_ref[:, at] = hidden.T.astype(BF16)

    row_part = lax.broadcasted_iota(jnp.int32, (rows, wide), 0) % 8 // capacity
    for i, panel in enumerate(panels):
        total = jnp.zeros((rows, wide), F32)
        for h, n in enumerate(panel):
            down_copy(n).wait()
            term = dot(hidden_ref[...], down_ref[:, n * wide : (n + 1) * wide])
            total = jnp.where(row_part == h, term, total)
        at = slice(i * wide, (i + 1) * wide)
        total = total.reshape(rows // 8, 8, wide)
        own_ref[:, :, at] = total[:own]
        for j in range(others_ref.shape[0]):
            others_ref[j, :, :, at] = total[(j + 1) * own : (j + 2) * own].astype(BF16)


def expert_apply(pieces, gate_part, up_part, down_part, capacity, inners):
    units, width = gate_part.shape
    block = next(b for b in (384, 288, 256, 128, 96, 64, 32, 16) if units % b == 0)
    wide = 512
    chunks = sum(piece.shape[0] for piece in pieces)
    own = chunks // inners
    part = pieces[0].shape[2]
    return pl.pallas_call(
        functools.partial(expert_kernel, capacity, block, wide, own, len(pieces)),
        in_specs=[VMEM] * (len(pieces) + 2) + [ANY],
        out_specs=(VMEM, VMEM),
        out_shape=(
            jax.ShapeDtypeStruct((own, 8, part), F32),
            jax.ShapeDtypeStruct((inners - 1, own, 8, part), BF16),
        ),
        scratch_shapes=[
            pltpu.VMEM((chunks * 8, part), F32),
            pltpu.VMEM((chunks * 8, units), BF16),
            pltpu.VMEM((units, width), BF16),
            pltpu.SemaphoreType.DMA((width // wide,)),
        ],
        compiler_params=limits(24),
        name="experts",
    )(*pieces, gate_part, up_part, *in_hbm(down_part))


def add_kernel(own_ref, *refs):
    count = refs[0].shape[0]
    others = [ref for ref in refs if len(ref.shape) == 4]
    outs = refs[len(others) :]
    total = own_ref[...]
    for other in others:
        total = total + other[0].astype(F32)
    for i, out in enumerate(outs):
        each = out.shape[0]
        out[...] = total[i * each : (i + 1) * each].astype(BF16)


def add_terms(own, others, count):
    chunks, tall, part = own.shape
    each = (chunks // count, tall, part)
    return pl.pallas_call(
        add_kernel,
        in_specs=[VMEM] * (1 + len(others)),
        out_specs=[VMEM] * count,
        out_shape=[jax.ShapeDtypeStruct(each, BF16)] * count,
        compiler_params=limits(8),
        name="terms",
    )(own, *others)


def finish_kernel(capacity, pairs, relative, count, ids_ref, weights_ref, combined_ref, *refs):
    got, out_ref = refs[:count], refs[count]
    rows = combined_ref.shape[0]
    part = got[0].shape[2]
    parts = 8 // capacity
    places = sum(piece.shape[0] for piece in got) * 8
    row = lax.broadcasted_iota(jnp.int32, (rows, places), 0)
    place = lax.broadcasted_iota(jnp.int32, (rows, places), 1)
    slot = place // (pairs * 8) * capacity + place % capacity
    in_part = place % 8 // capacity
    weighting = jnp.zeros((rows, places), F32)
    me = lax.axis_index("expert") if relative else 0
    for (t, k), at in slots_of(ids_ref, capacity, me).items():
        weighting = jnp.where((slot == at) & (row == t), weights_ref[k, t], weighting)
    terms = jnp.concatenate([piece[...].reshape(-1, part) for piece in got], axis=0)
    for h in range(parts):
        at = slice(h * part, (h + 1) * part)
        high, low = halves_of(jnp.where(in_part == h, weighting, 0.0))
        mixture = dot(high, terms) + dot(low, terms)
        out_ref[:, at] = (combined_ref[:, at] + mixture).astype(BF16)


def finish(ids, weights, combined, got, capacity, pairs, relative):
    return pl.pallas_call(
        functools.partial(finish_kernel, capacity, pairs, relative, len(got)),
        in_specs=[SMEM, SMEM, VMEM] + [VMEM] * len(got),
        out_specs=VMEM,
        out_shape=jax.ShapeDtypeStruct(combined.shape, BF16),
        compiler_params=limits(8),
        name="finish",
    )(*in_hbm(ids, weights), combined, *got)


def swap(x, axes, by):
    return lax.ppermute(x, axes, [(i, i ^ by) for i in range(lax.axis_size(axes))]) if by else x


def on_device(
    queries,
    key_rows,
    value_rows,
    states,
    decay_rates,
    head_gain,
    out_weight,
    residual,
    norm_gain,
    expert_ids,
    gate_weights,
    expert_gate,
    expert_up,
    expert_down,
):
    experts = lax.axis_size("expert")
    pairs = lax.axis_size("pair")
    subs = lax.axis_size("sub")
    inner = ("half", "sub")
    everyone = ("expert", "half", "pair", "sub")
    plane = ("expert", "pair")
    inners = lax.axis_size(inner)
    local_rows, width = residual.shape
    columns = out_weight.shape[1]
    capacity = max(2, local_rows * expert_ids.shape[1] // experts)
    ids, weights = expert_ids.T, gate_weights.T
    relative = experts * pairs * inners <= 16 and columns % 128 == 0

    attended = attend(queries, key_rows, value_rows, states, decay_rates, head_gain)
    out_here, gate_here = load([out_weight, expert_gate], attended, "load_first")
    pieces = []
    for d in range(experts):
        piece = swap(attended, "expert", d)
        pieces += [swap(piece, inner, c) for c in range(inners)]
    blocks = project(pieces, out_here, local_rows, experts, inners, relative)

    up_here, residual_here, gain_here = load(
        [expert_up, residual, norm_gain.reshape(1, -1)], blocks[0], "load_second"
    )
    if relative:
        got = [swap(block, everyone, d) for d, block in enumerate(blocks)]
    else:
        got = lax.all_to_all(blocks[0], everyone, split_axis=0, concat_axis=0, tiled=True)
        got = got.reshape(experts * 2, pairs, subs, local_rows, columns).astype(F32)
        got = [jnp.transpose(got.sum(axis=1), (2, 0, 1, 3)).reshape(local_rows, width)]
    combined, *outgoing = pack(
        ids, residual_here, gain_here, got, capacity, experts, pairs, subs, relative
    )

    if relative:
        routed = []
        for d, rows in enumerate(outgoing):
            rows = swap(rows, "expert", d)
            routed += [swap(rows, "pair", p) for p in range(pairs)]
    else:
        routed = [lax.all_to_all(outgoing[0], plane, split_axis=0, concat_axis=0, tiled=True)]
    routed = [swap(rows, inner, c) for c in range(inners) for rows in routed]
    own, others = expert_apply(routed, gate_here, up_here, expert_down, capacity, inners)

    others = [swap(others[c - 1 : c], inner, c) for c in range(1, inners)]
    terms = add_terms(own, others, len(routed) // inners)
    if relative:
        back = [swap(term, plane, d) for d, term in enumerate(terms)]
    else:
        back = [lax.all_to_all(terms[0], plane, split_axis=0, concat_axis=0, tiled=True)]
    return finish(ids, weights, combined, back, capacity, pairs, relative)


def solution(mesh):
    sizes = dict(mesh.shape)
    experts = sizes["dev"] // 2
    cut = Mesh(
        mesh.devices.reshape(sizes["grp"], experts, 2, sizes["pair"], sizes["sub"]),
        ("grp", "expert", "half", "pair", "sub"),
    )
    dev = ("expert", "half")
    requests = P(("grp",) + dev + ("sub",), "pair")
    tokens = P(("grp",) + dev + ("pair", "sub"), None)
    units = P(dev + ("pair", "sub"), None)
    return jax.shard_map(
        on_device,
        mesh=cut,
        in_specs=(
            requests,
            requests,
            requests,
            P(("grp",) + dev + ("sub",), "pair", None, None),
            P("pair"),
            P("pair"),
            P("pair", dev + ("sub",)),
            tokens,
            P(),
            tokens,
            tokens,
            units,
            units,
            units,
        ),
        out_specs=tokens,
        check_vma=False,
    )
```

time: 109 us -> 98.9 us (0.907)
  blocking collectives: 43.3 us -> 0 us
  starting transfers between devices: 6.84 us -> 48.1 us
  local copies, waits for them, and re-layouts: 11.1 us -> 0 us
  waiting for transfers between devices: 9.77 us -> 17.7 us
  Pallas kernels: 35.7 us -> 32.6 us
  other arithmetic: 1.1 us -> 0 us
    all_to_all x3 -> x0, blocking collectives: 43.3 us -> none  [the longest x1 15.4 us: on_device(): lax.all_to_all(total.astype(BF16), plane, split_axis=0, concat_axis=0, ti...]
    ppermute x9 -> x45, starting transfers between devices: 6.84 us -> 48.1 us  [swap(): lax.ppermute(x, axes, [(i, i ^ by) for i in range(lax.axis_size(axes))])]
    unnamed x28 -> x0, local copies, waits for them, and re-layouts: 11 us -> none
    ppermute x9 -> x45, waiting for transfers between devices: 9.77 us -> 17.7 us  [swap(): lax.ppermute(x, axes, [(i, i ^ by) for i in range(lax.axis_size(axes))])]
    pallas_call x4 -> x7, Pallas kernels: 32.4 us -> 28 us  [the longest x1 13.2 us: expert_apply(): pl.pallas_call(functools.partial(expert_kernel, capacity, block, wide, ow...]
    pallas_call x1, Pallas kernels: 3.28 us -> 4.57 us  [attend(): pl.pallas_call(functools.partial(attend_kernel, rows // requests), grid=(...]
    convert_element_type x1 -> x0, other arithmetic: 1.1 us -> none  [on_device(): total.astype(BF16)]
  transfers between devices with their start and end apart: 9 -> 45, of which waited for: 6 -> 10; matrix products, arithmetic and copies ran while one was open for 0% -> 0% of each run, Pallas kernels for 0% -> 11%
where the time goes in v2:
time: 98.9 us; the launch traced here: 98.7 us
  starting transfers between devices  48.1 us (49%)
  Pallas kernels  32.6 us (33%)
  waiting for transfers between devices  17.7 us (18%)
    ppermute x45, starting transfers between devices, swap(): lax.ppermute(x, axes, [(i, i ^ by) for i in range(lax.axis_size(axes))])  48.1 us
    ppermute x45, waiting for transfers between devices, swap(): lax.ppermute(x, axes, [(i, i ^ by) for i in range(lax.axis_size(axes))])  17.7 us
    pallas_call x1, Pallas kernels, expert_apply(): pl.pallas_call(functools.partial(expert_kernel, capacity, block, wide, ow...  13.2 us
    pallas_call x2, Pallas kernels, load(): pl.pallas_call(functools.partial(load_kernel, count), in_specs=[ANY] * (c...  11.1 us
    pallas_call x1, Pallas kernels, attend(): pl.pallas_call(functools.partial(attend_kernel, rows // requests), grid=(...  4.57 us
  transfers between devices with their start and end apart: 45, of which 10 were waited for; matrix products, arithmetic and copies ran while one was open for 0% of the time, Pallas kernels for 11%

profile of v2, /device:TPU:0, one launch (start us, length us, event | category | flops | bytes accessed | tf_op | source)
XLA Modules:
  0.0 98.7 jit_solution(8590445291371849513)
XLA Ops:
  0.0 4.6 %attention.1.refs_2_.refs_0_ = bf16[16,2048]{1,0:T(8,128)(2,1)S(1)} custom-call(f32[16]{0:T(128)} %decay_ref.1, bf16[16,2048]{1,0:T(8,128)(2,1)} %q_ref.1, bf16[16,2048]{1,0:T(8,128)(2,1)} %k_ref.1, bf16[16,2048]{1,0:T(8,128)(2,1)} %v_ref.1, f32[1,2048]{1,0:T(1,128)} %bitcast.5, f32[4,16,128,128]{3,2,1,0:T(8,128)} %s_ref.1), custom_call_target="tpu_custom_call" | custom-call | tf_op jit(solution)/shard_map/attention/pallas_call | solution.py:80
  4.6 5.1 %collective-permute-start.5 = (bf16[16,2048]{1,0:T(8,128)(2,1)S(1)}, bf16[16,2048]{1,0:T(8,128)(2,1)S(1)}, u32[]{:S(2)}, u32[]{:S(2)}) collective-permute-start(bf16[16,2048]{1,0:T(8,128)(2,1)S(1)} %attention.1.refs_2_.refs_0_), channel_id=1, source_target_pairs={{0,12},{4,8},{8,4},{12,0},{1,13},{5,9},{9,5},{13,1},{2,14},{6,10},... | collective-permute-start | bytes 196616 | tf_op jit(solution)/shard_map/ppermute | solution.py:382
  9.7 0.6 collective-permute-start.1
  10.3 1.9 %collective-permute-done.5.refs_6_ = bf16[16,2048]{1,0:T(8,128)(2,1)S(1)} collective-permute-done((bf16[16,2048]{1,0:T(8,128)(2,1)S(1)}, bf16[16,2048]{1,0:T(8,128)(2,1)S(1)}, u32[]{:S(2)}, u32[]{:S(2)}) %collective-permute-start.5) | collective-permute-done | bytes 65568 | tf_op jit(solution)/shard_map/ppermute | solution.py:382
  12.3 3.0 %collective-permute-done.3.refs_4_ = bf16[16,2048]{1,0:T(8,128)(2,1)S(1)} collective-permute-done((bf16[16,2048]{1,0:T(8,128)(2,1)S(1)}, bf16[16,2048]{1,0:T(8,128)(2,1)S(1)}, u32[]{:S(2)}, u32[]{:S(2)}) %collective-permute-start.3) | collective-permute-done | bytes 65568 | tf_op jit(solution)/shard_map/ppermute | solution.py:382
  15.3 0.5 collective-permute-start.2
  15.8 6.0 %load_first.1 = (bf16[2048,768]{1,0:T(8,128)(2,1)S(1)}, bf16[1152,6144]{1,0:T(8,128)(2,1)S(1)}) custom-call(bf16[2048,768]{1,0:T(8,128)(2,1)} %refs_0_.2, bf16[1152,6144]{1,0:T(8,128)(2,1)} %refs_1_.2, bf16[16,2048]{1,0:T(8,128)(2,1)S(1)} %attention.1.refs_2_.refs_0_), custom_call_target="tpu_custom_call" | custom-call | bytes 34603008 | tf_op jit(solution)/shard_map/load_first/pallas_call | solution.py:113
  21.8 0.0 collective-permute-done.4.refs_5_
  21.9 0.0 collective-permute-done.2.refs_3_
  21.9 0.6 projection.1
  22.5 1.6 %collective-permute-start.7 = (bf16[8,768]{1,0:T(8,128)(2,1)S(1)}, bf16[8,768]{1,0:T(8,128)(2,1)S(1)}, u32[]{:S(2)}, u32[]{:S(2)}) collective-permute-start(bf16[8,768]{1,0:T(8,128)(2,1)S(1)} %get-tuple-element.45), channel_id=1, source_target_pairs={{0,1},{1,0},{2,3},{3,2},{4,5},{5,4},{6,7},{7,6},{8,9},{9,8},{10,11... | collective-permute-start | bytes 36872 | tf_op jit(solution)/shard_map/ppermute | solution.py:382
  24.1 0.0 collective-permute-start.8
  24.1 0.6 collective-permute-start.9
  24.7 0.6 collective-permute-start.10
  25.3 2.4 %collective-permute-start.11 = (bf16[8,768]{1,0:T(8,128)(2,1)S(1)}, bf16[8,768]{1,0:T(8,128)(2,1)S(1)}, u32[]{:S(2)}, u32[]{:S(2)}) collective-permute-start(bf16[8,768]{1,0:T(8,128)(2,1)S(1)} %get-tuple-element.49), channel_id=1, source_target_pairs={{0,5},{1,4},{2,7},{3,6},{4,1},{5,0},{6,3},{7,2},{8,13},{9,12},{10,... | collective-permute-start | bytes 36872 | tf_op jit(solution)/shard_map/ppermute | solution.py:382
  27.7 0.0 collective-permute-done.7.refs_1_
  27.7 0.0 collective-permute-start.12
  27.7 0.0 collective-permute-done.8.refs_2_
  27.7 1.7 %collective-permute-start.13 = (bf16[8,768]{1,0:T(8,128)(2,1)S(1)}, bf16[8,768]{1,0:T(8,128)(2,1)S(1)}, u32[]{:S(2)}, u32[]{:S(2)}) collective-permute-start(bf16[8,768]{1,0:T(8,128)(2,1)S(1)} %get-tuple-element.51), channel_id=1, source_target_pairs={{0,7},{1,6},{2,5},{3,4},{4,3},{5,2},{6,1},{7,0},{8,15},{9,14},{10,... | collective-permute-start | bytes 36872 | tf_op jit(solution)/shard_map/ppermute | solution.py:382
  29.4 0.0 collective-permute-done.9.refs_3_
  29.4 1.3 %collective-permute-start.14 = (bf16[8,768]{1,0:T(8,128)(2,1)S(1)}, bf16[8,768]{1,0:T(8,128)(2,1)S(1)}, u32[]{:S(2)}, u32[]{:S(2)}) collective-permute-start(bf16[8,768]{1,0:T(8,128)(2,1)S(1)} %get-tuple-element.52), channel_id=1, source_target_pairs={{0,8},{1,9},{2,10},{3,11},{4,12},{5,13},{6,14},{7,15},{8,0},{9,1},... | collective-permute-start | bytes 36872 | tf_op jit(solution)/shard_map/ppermute | solution.py:382
  30.7 0.0 collective-permute-done.10.refs_4_
  30.7 2.6 %collective-permute-start.15 = (bf16[8,768]{1,0:T(8,128)(2,1)S(1)}, bf16[8,768]{1,0:T(8,128)(2,1)S(1)}, u32[]{:S(2)}, u32[]{:S(2)}) collective-permute-start(bf16[8,768]{1,0:T(8,128)(2,1)S(1)} %get-tuple-element.53), channel_id=1, source_target_pairs={{0,9},{1,8},{2,11},{3,10},{4,13},{5,12},{6,15},{7,14},{8,1},{9,0},... | collective-permute-start | bytes 36872 | tf_op jit(solution)/shard_map/ppermute | solution.py:382
  33.3 0.0 collective-permute-done.11.refs_5_
  33.3 0.8 collective-permute-start.16
  34.0 0.0 collective-permute-done.12.refs_6_
  34.0 1.8 %collective-permute-start.17 = (bf16[8,768]{1,0:T(8,128)(2,1)S(1)}, bf16[8,768]{1,0:T(8,128)(2,1)S(1)}, u32[]{:S(2)}, u32[]{:S(2)}) collective-permute-start(bf16[8,768]{1,0:T(8,128)(2,1)S(1)} %get-tuple-element.55), channel_id=1, source_target_pairs={{0,11},{1,10},{2,9},{3,8},{4,15},{5,14},{6,13},{7,12},{8,3},{9,2},... | collective-permute-start | bytes 36872 | tf_op jit(solution)/shard_map/ppermute | solution.py:382
  35.9 0.0 collective-permute-done.13.refs_7_
  35.9 2.7 %collective-permute-start.18 = (bf16[8,768]{1,0:T(8,128)(2,1)S(1)}, bf16[8,768]{1,0:T(8,128)(2,1)S(1)}, u32[]{:S(2)}, u32[]{:S(2)}) collective-permute-start(bf16[8,768]{1,0:T(8,128)(2,1)S(1)} %get-tuple-element.56), channel_id=1, source_target_pairs={{0,12},{1,13},{2,14},{3,15},{4,8},{5,9},{6,10},{7,11},{8,4},{9,5},... | collective-permute-start | bytes 36872 | tf_op jit(solution)/shard_map/ppermute | solution.py:382
  38.6 0.0 collective-permute-done.14.refs_8_
  38.6 2.0 %collective-permute-start.19 = (bf16[8,768]{1,0:T(8,128)(2,1)S(1)}, bf16[8,768]{1,0:T(8,128)(2,1)S(1)}, u32[]{:S(2)}, u32[]{:S(2)}) collective-permute-start(bf16[8,768]{1,0:T(8,128)(2,1)S(1)} %get-tuple-element.57), channel_id=1, source_target_pairs={{0,13},{1,12},{2,15},{3,14},{4,9},{5,8},{6,11},{7,10},{8,5},{9,4},... | collective-permute-start | bytes 36872 | tf_op jit(solution)/shard_map/ppermute | solution.py:382
  40.6 0.6 collective-permute-start.20
  41.3 0.0 collective-permute-done.16.refs_10_
  41.3 2.9 %collective-permute-start.21 = (bf16[8,768]{1,0:T(8,128)(2,1)S(1)}, bf16[8,768]{1,0:T(8,128)(2,1)S(1)}, u32[]{:S(2)}, u32[]{:S(2)}) collective-permute-start(bf16[8,768]{1,0:T(8,128)(2,1)S(1)} %get-tuple-element.59), channel_id=1, source_target_pairs={{0,15},{1,14},{2,13},{3,12},{4,11},{5,10},{6,9},{7,8},{8,7},{9,6},... | collective-permute-start | bytes 36872 | tf_op jit(solution)/shard_map/ppermute | solution.py:382
  44.2 5.1 %load_second.1 = (bf16[1152,6144]{1,0:T(8,128)(2,1)S(1)}, bf16[8,6144]{1,0:T(8,128)(2,1)S(1)}, f32[1,6144]{1,0:T(1,128)S(1)}) custom-call(bf16[1152,6144]{1,0:T(8,128)(2,1)} %refs_0_.3, bf16[8,6144]{1,0:T(8,128)(2,1)} %refs_1_.3, f32[1,6144]{1,0:T(1,128)} %bitcast.4, bf16[8,768]{1,0:T(8,128)(2,1)S(1)} %get-tuple-element.42.refs_3_.refs_0_), custom_call_target="tpu_custom_call" | custom-call | bytes 28557312 | tf_op jit(solution)/shard_map/load_second/pallas_call | solution.py:113
  49.3 1.2 %pack.1 = (f32[8,6144]{1,0:T(8,128)S(1)}, bf16[1,8,3072]{2,1,0:T(8,128)(2,1)S(1)}, bf16[1,8,3072]{2,1,0:T(8,128)(2,1)S(1)}, bf16[1,8,3072]{2,1,0:T(8,128)(2,1)S(1)}, bf16[1,8,3072]{2,1,0:T(8,128)(2,1)S(1)}) custom-call(s32[2,8]{1,0:T(2,128)} %bitcast.6, bf16[8,6144]{1,0:T(8,128)(2,1)S(1)} %get-tuple-element.43.residual_ref, ...), custom_call_target="tpu_custom_call" | custom-call | tf_op jit(solution)/shard_map/pack/pallas_call | solution.py:224
  50.5 0.1 collective-permute-start.23
  50.5 3.3 %collective-permute-start.25 = (bf16[1,8,3072]{2,1,0:T(8,128)(2,1)S(1)}, bf16[1,8,3072]{2,1,0:T(8,128)(2,1)S(1)}, u32[]{:S(2)}, u32[]{:S(2)}) collective-permute-start(bf16[1,8,3072]{2,1,0:T(8,128)(2,1)S(1)} %get-tuple-element.63), channel_id=1, source_target_pairs={{0,8},{4,12},{8,0},{12,4},{1,9},{5,13},{9,1},{13,5},{2,10},{6,14},... | collective-permute-start | bytes 147464 | tf_op jit(solution)/shard_map/ppermute | solution.py:382
  53.8 1.1 %collective-permute-start.27 = (bf16[1,8,3072]{2,1,0:T(8,128)(2,1)S(1)}, bf16[1,8,3072]{2,1,0:T(8,128)(2,1)S(1)}, u32[]{:S(2)}, u32[]{:S(2)}) collective-permute-start(bf16[1,8,3072]{2,1,0:T(8,128)(2,1)S(1)} %get-tuple-element.64), channel_id=1, source_target_pairs={{0,12},{4,8},{8,4},{12,0},{1,13},{5,9},{9,5},{13,1},{2,14},{6,10},... | collective-permute-start | bytes 147464 | tf_op jit(solution)/shard_map/ppermute | solution.py:382
  54.9 1.5 %collective-permute-start.22 = (bf16[1,8,3072]{2,1,0:T(8,128)(2,1)S(1)}, bf16[1,8,3072]{2,1,0:T(8,128)(2,1)S(1)}, u32[]{:S(2)}, u32[]{:S(2)}) collective-permute-start(bf16[1,8,3072]{2,1,0:T(8,128)(2,1)S(1)} %get-tuple-element.61.refs_0_), channel_id=1, source_target_pairs={{0,1},{1,0},{2,3},{3,2},{4,5},{5,4},{6,7},{7,6},{8,9},{9,8},{10,11... | collective-permute-start | bytes 147464 | tf_op jit(solution)/shard_map/ppermute | solution.py:382
  56.4 0.2 collective-permute-start.31
  56.6 0.7 collective-permute-done.25.refs_4_
  57.3 0.0 collective-permute-start.24
  57.4 2.3 %collective-permute-done.27.refs_6_ = bf16[1,8,3072]{2,1,0:T(8,128)(2,1)S(1)} collective-permute-done((bf16[1,8,3072]{2,1,0:T(8,128)(2,1)S(1)}, bf16[1,8,3072]{2,1,0:T(8,128)(2,1)S(1)}, u32[]{:S(2)}, u32[]{:S(2)}) %collective-permute-start.27) | collective-permute-done | bytes 49184 | tf_op jit(solution)/shard_map/ppermute | solution.py:382
  59.7 1.5 %collective-permute-start.26 = (bf16[1,8,3072]{2,1,0:T(8,128)(2,1)S(1)}, bf16[1,8,3072]{2,1,0:T(8,128)(2,1)S(1)}, u32[]{:S(2)}, u32[]{:S(2)}) collective-permute-start(bf16[1,8,3072]{2,1,0:T(8,128)(2,1)S(1)} %collective-permute-done.25.refs_4_), channel_id=1, source_target_pairs={{0,1},{1,0},{2,3},{3,2},{4,5},{5,4},{6,7},{7,6},{8,9},{9,8},{10,11... | collective-permute-start | bytes 147464 | tf_op jit(solution)/shard_map/ppermute | solution.py:382
  61.2 0.5 collective-permute-start.28
  61.7 0.5 collective-permute-start.30
  62.2 0.1 collective-permute-start.32
  62.3 1.5 %collective-permute-done.26.refs_5_ = bf16[1,8,3072]{2,1,0:T(8,128)(2,1)S(1)} collective-permute-done((bf16[1,8,3072]{2,1,0:T(8,128)(2,1)S(1)}, bf16[1,8,3072]{2,1,0:T(8,128)(2,1)S(1)}, u32[]{:S(2)}, u32[]{:S(2)}) %collective-permute-start.26) | collective-permute-done | bytes 49184 | tf_op jit(solution)/shard_map/ppermute | solution.py:382
  63.9 1.4 %collective-permute-done.28.refs_7_ = bf16[1,8,3072]{2,1,0:T(8,128)(2,1)S(1)} collective-permute-done((bf16[1,8,3072]{2,1,0:T(8,128)(2,1)S(1)}, bf16[1,8,3072]{2,1,0:T(8,128)(2,1)S(1)}, u32[]{:S(2)}, u32[]{:S(2)}) %collective-permute-start.28) | collective-permute-done | bytes 49184 | tf_op jit(solution)/shard_map/ppermute | solution.py:382
  65.3 1.2 %collective-permute-done.36.refs_15_ = bf16[1,8,3072]{2,1,0:T(8,128)(2,1)S(1)} collective-permute-done((bf16[1,8,3072]{2,1,0:T(8,128)(2,1)S(1)}, bf16[1,8,3072]{2,1,0:T(8,128)(2,1)S(1)}, u32[]{:S(2)}, u32[]{:S(2)}) %collective-permute-start.36) | collective-permute-done | bytes 49184 | tf_op jit(solution)/shard_map/ppermute | solution.py:382
  66.5 13.2 %experts.1 = (f32[8,8,3072]{2,1,0:T(8,128)S(1)}, bf16[1,8,8,3072]{3,2,1,0:T(8,128)(2,1)S(1)}) custom-call(bf16[1,8,3072]{2,1,0:T(8,128)(2,1)S(1)} %get-tuple-element.61.refs_0_, bf16[1,8,3072]{2,1,0:T(8,128)(2,1)S(1)} %collective-permute-done.22.refs_1_, bf16[1,8,3072]{2,1,0:T(8,128)(2,1)S(1)} %collective-permute-done.23.refs_2_, ...), custom_call_target="tpu_custom_call" | custom-call | tf_op jit(solution)/shard_map/experts/pallas_call | solution.py:304
  79.8 0.2 collective-permute-start.37
  80.0 1.6 %collective-permute-done.37.refs_0_ = bf16[1,8,8,3072]{3,2,1,0:T(8,128)(2,1)S(1)} collective-permute-done((bf16[1,8,8,3072]{3,2,1,0:T(8,128)(2,1)S(1)}, bf16[1,8,8,3072]{3,2,1,0:T(8,128)(2,1)S(1)}, u32[]{:S(2)}, u32[]{:S(2)}) %collective-permute-start.37) | collective-permute-done | bytes 393248 | tf_op jit(solution)/shard_map/ppermute | solution.py:382
  81.6 0.1 terms.1
  81.6 1.2 %collective-permute-start.38 = (bf16[1,8,3072]{2,1,0:T(8,128)(2,1)S(1)}, bf16[1,8,3072]{2,1,0:T(8,128)(2,1)S(1)}, u32[]{:S(2)}, u32[]{:S(2)}) collective-permute-start(bf16[1,8,3072]{2,1,0:T(8,128)(2,1)S(1)} %get-tuple-element.70), channel_id=1, source_target_pairs={{0,1},{1,0},{4,5},{5,4},{8,9},{9,8},{12,13},{13,12},{2,3},{3,2},{6... | collective-permute-start | bytes 147464 | tf_op jit(solution)/shard_map/ppermute | solution.py:382
  82.8 2.4 %collective-permute-start.40 = (bf16[1,8,3072]{2,1,0:T(8,128)(2,1)S(1)}, bf16[1,8,3072]{2,1,0:T(8,128)(2,1)S(1)}, u32[]{:S(2)}, u32[]{:S(2)}) collective-permute-start(bf16[1,8,3072]{2,1,0:T(8,128)(2,1)S(1)} %get-tuple-element.72), channel_id=1, source_target_pairs={{0,5},{1,4},{4,1},{5,0},{8,13},{9,12},{12,9},{13,8},{2,7},{3,6},{6... | collective-permute-start | bytes 147464 | tf_op jit(solution)/shard_map/ppermute | solution.py:382
  85.2 0.3 collective-permute-start.41
  85.5 3.2 %collective-permute-start.42 = (bf16[1,8,3072]{2,1,0:T(8,128)(2,1)S(1)}, bf16[1,8,3072]{2,1,0:T(8,128)(2,1)S(1)}, u32[]{:S(2)}, u32[]{:S(2)}) collective-permute-start(bf16[1,8,3072]{2,1,0:T(8,128)(2,1)S(1)} %get-tuple-element.74), channel_id=1, source_target_pairs={{0,9},{1,8},{4,13},{5,12},{8,1},{9,0},{12,5},{13,4},{2,11},{3,10},... | collective-permute-start | bytes 147464 | tf_op jit(solution)/shard_map/ppermute | solution.py:382
  88.7 1.4 %collective-permute-start.43 = (bf16[1,8,3072]{2,1,0:T(8,128)(2,1)S(1)}, bf16[1,8,3072]{2,1,0:T(8,128)(2,1)S(1)}, u32[]{:S(2)}, u32[]{:S(2)}) collective-permute-start(bf16[1,8,3072]{2,1,0:T(8,128)(2,1)S(1)} %get-tuple-element.75), channel_id=1, source_target_pairs={{0,12},{1,13},{4,8},{5,9},{8,4},{9,5},{12,0},{13,1},{2,14},{3,15},... | collective-permute-start | bytes 147464 | tf_op jit(solution)/shard_map/ppermute | solution.py:382
  90.0 2.8 %collective-permute-start.44 = (bf16[1,8,3072]{2,1,0:T(8,128)(2,1)S(1)}, bf16[1,8,3072]{2,1,0:T(8,128)(2,1)S(1)}, u32[]{:S(2)}, u32[]{:S(2)}) collective-permute-start(bf16[1,8,3072]{2,1,0:T(8,128)(2,1)S(1)} %get-tuple-element.76), channel_id=1, source_target_pairs={{0,13},{1,12},{4,9},{5,8},{8,5},{9,4},{12,1},{13,0},{2,15},{3,14},... | collective-permute-start | bytes 147464 | tf_op jit(solution)/shard_map/ppermute | solution.py:382
  92.8 2.2 %collective-permute-done.42.refs_5_ = bf16[1,8,3072]{2,1,0:T(8,128)(2,1)S(1)} collective-permute-done((bf16[1,8,3072]{2,1,0:T(8,128)(2,1)S(1)}, bf16[1,8,3072]{2,1,0:T(8,128)(2,1)S(1)}, u32[]{:S(2)}, u32[]{:S(2)}) %collective-permute-start.42) | collective-permute-done | bytes 49184 | tf_op jit(solution)/shard_map/ppermute | solution.py:382
  95.1 1.7 %collective-permute-done.44.refs_7_ = bf16[1,8,3072]{2,1,0:T(8,128)(2,1)S(1)} collective-permute-done((bf16[1,8,3072]{2,1,0:T(8,128)(2,1)S(1)}, bf16[1,8,3072]{2,1,0:T(8,128)(2,1)S(1)}, u32[]{:S(2)}, u32[]{:S(2)}) %collective-permute-start.44) | collective-permute-done | bytes 49184 | tf_op jit(solution)/shard_map/ppermute | solution.py:382
  96.8 1.8 %finish.1 = bf16[8,6144]{1,0:T(8,128)(2,1)} custom-call(s32[2,8]{1,0:T(2,128)} %bitcast.7, f32[2,8]{1,0:T(2,128)} %bitcast.8, f32[8,6144]{1,0:T(8,128)S(1)} %get-tuple-element.60.combined_ref, bf16[1,8,3072]{2,1,0:T(8,128)(2,1)S(1)} %get-tuple-element.69.refs_0_, bf16[1,8,3072]{2,1,0:T(8,128)(2,1)S(1)} %collective-permute-done.38.refs_1_, ...), custom_call_target="tpu_custom_call" | custom-call | tf_op jit(solution)/shard_map/finish/pallas_call | solution.py:371
  (34 shorter events, 0.1 us)
Async XLA Ops:
  4.6 7.7 %collective-permute-start.5 = (bf16[16,2048]{1,0:T(8,128)(2,1)S(1)}, bf16[16,2048]{1,0:T(8,128)(2,1)S(1)}, u32[]{:S(2)}, u32[]{:S(2)}) collective-permute-start(bf16[16,2048]{1,0:T(8,128)(2,1)S(1)} %attention.1.refs_2_.refs_0_), channel_id=1, source_target_pairs={{0,12},{4,8},{8,4},{12,0},{1,13},{5,9},{9,5},{13,1},{2,14},{6,10},... | collective-permute-start | bytes 196616 | tf_op jit(solution)/shard_map/ppermute | solution.py:382
  9.7 5.6 %collective-permute-start.3 = (bf16[16,2048]{1,0:T(8,128)(2,1)S(1)}, bf16[16,2048]{1,0:T(8,128)(2,1)S(1)}, u32[]{:S(2)}, u32[]{:S(2)}) collective-permute-start(bf16[16,2048]{1,0:T(8,128)(2,1)S(1)} %attention.1.refs_2_.refs_0_), channel_id=1, source_target_pairs={{0,8},{4,12},{8,0},{12,4},{1,9},{5,13},{9,1},{13,5},{2,10},{6,14},... | collective-permute-start | bytes 196616 | tf_op jit(solution)/shard_map/ppermute | solution.py:382
  9.7 5.6 %collective-permute-start.1 = (bf16[16,2048]{1,0:T(8,128)(2,1)S(1)}, bf16[16,2048]{1,0:T(8,128)(2,1)S(1)}, u32[]{:S(2)}, u32[]{:S(2)}) collective-permute-start(bf16[16,2048]{1,0:T(8,128)(2,1)S(1)} %attention.1.refs_2_.refs_0_), channel_id=1, source_target_pairs={{0,4},{4,0},{8,12},{12,8},{1,5},{5,1},{9,13},{13,9},{2,6},{6,2},{1... | collective-permute-start | bytes 196616 | tf_op jit(solution)/shard_map/ppermute | solution.py:382
  10.3 11.5 %collective-permute-start = (bf16[16,2048]{1,0:T(8,128)(2,1)S(1)}, bf16[16,2048]{1,0:T(8,128)(2,1)S(1)}, u32[]{:S(2)}, u32[]{:S(2)}) collective-permute-start(bf16[16,2048]{1,0:T(8,128)(2,1)S(1)} %attention.1.refs_2_.refs_0_), channel_id=1, source_target_pairs={{0,2},{2,0},{1,3},{3,1},{4,6},{6,4},{5,7},{7,5},{8,10},{10,8},{9,1... | collective-permute-start | bytes 196616 | tf_op jit(solution)/shard_map/ppermute | solution.py:382
  12.3 9.6 %collective-permute-start.6 = (bf16[16,2048]{1,0:T(8,128)(2,1)S(1)}, bf16[16,2048]{1,0:T(8,128)(2,1)S(1)}, u32[]{:S(2)}, u32[]{:S(2)}) collective-permute-start(bf16[16,2048]{1,0:T(8,128)(2,1)S(1)} %collective-permute-done.5.refs_6_), channel_id=1, source_target_pairs={{0,2},{2,0},{1,3},{3,1},{4,6},{6,4},{5,7},{7,5},{8,10},{10,8},{9,1... | collective-permute-start | bytes 196616 | tf_op jit(solution)/shard_map/ppermute | solution.py:382
  15.3 6.5 %collective-permute-start.4 = (bf16[16,2048]{1,0:T(8,128)(2,1)S(1)}, bf16[16,2048]{1,0:T(8,128)(2,1)S(1)}, u32[]{:S(2)}, u32[]{:S(2)}) collective-permute-start(bf16[16,2048]{1,0:T(8,128)(2,1)S(1)} %collective-permute-done.3.refs_4_), channel_id=1, source_target_pairs={{0,2},{2,0},{1,3},{3,1},{4,6},{6,4},{5,7},{7,5},{8,10},{10,8},{9,1... | collective-permute-start | bytes 196616 | tf_op jit(solution)/shard_map/ppermute | solution.py:382
  15.3 6.5 %collective-permute-start.2 = (bf16[16,2048]{1,0:T(8,128)(2,1)S(1)}, bf16[16,2048]{1,0:T(8,128)(2,1)S(1)}, u32[]{:S(2)}, u32[]{:S(2)}) collective-permute-start(bf16[16,2048]{1,0:T(8,128)(2,1)S(1)} %collective-permute-done.1.refs_2_), channel_id=1, source_target_pairs={{0,2},{2,0},{1,3},{3,1},{4,6},{6,4},{5,7},{7,5},{8,10},{10,8},{9,1... | collective-permute-start | bytes 196616 | tf_op jit(solution)/shard_map/ppermute | solution.py:382
  22.5 5.2 %collective-permute-start.7 = (bf16[8,768]{1,0:T(8,128)(2,1)S(1)}, bf16[8,768]{1,0:T(8,128)(2,1)S(1)}, u32[]{:S(2)}, u32[]{:S(2)}) collective-permute-start(bf16[8,768]{1,0:T(8,128)(2,1)S(1)} %get-tuple-element.45), channel_id=1, source_target_pairs={{0,1},{1,0},{2,3},{3,2},{4,5},{5,4},{6,7},{7,6},{8,9},{9,8},{10,11... | collective-permute-start | bytes 36872 | tf_op jit(solution)/shard_map/ppermute | solution.py:382
  24.1 3.6 %collective-permute-start.8 = (bf16[8,768]{1,0:T(8,128)(2,1)S(1)}, bf16[8,768]{1,0:T(8,128)(2,1)S(1)}, u32[]{:S(2)}, u32[]{:S(2)}) collective-permute-start(bf16[8,768]{1,0:T(8,128)(2,1)S(1)} %get-tuple-element.46), channel_id=1, source_target_pairs={{0,2},{1,3},{2,0},{3,1},{4,6},{5,7},{6,4},{7,5},{8,10},{9,11},{10,... | collective-permute-start | bytes 36872 | tf_op jit(solution)/shard_map/ppermute | solution.py:382
  24.1 5.3 %collective-permute-start.9 = (bf16[8,768]{1,0:T(8,128)(2,1)S(1)}, bf16[8,768]{1,0:T(8,128)(2,1)S(1)}, u32[]{:S(2)}, u32[]{:S(2)}) collective-permute-start(bf16[8,768]{1,0:T(8,128)(2,1)S(1)} %get-tuple-element.47), channel_id=1, source_target_pairs={{0,3},{1,2},{2,1},{3,0},{4,7},{5,6},{6,5},{7,4},{8,11},{9,10},{10,... | collective-permute-start | bytes 36872 | tf_op jit(solution)/shard_map/ppermute | solution.py:382
  24.7 6.0 %collective-permute-start.10 = (bf16[8,768]{1,0:T(8,128)(2,1)S(1)}, bf16[8,768]{1,0:T(8,128)(2,1)S(1)}, u32[]{:S(2)}, u32[]{:S(2)}) collective-permute-start(bf16[8,768]{1,0:T(8,128)(2,1)S(1)} %get-tuple-element.48), channel_id=1, source_target_pairs={{0,4},{1,5},{2,6},{3,7},{4,0},{5,1},{6,2},{7,3},{8,12},{9,13},{10,... | collective-permute-start | bytes 36872 | tf_op jit(solution)/shard_map/ppermute | solution.py:382
  25.3 8.0 %collective-permute-start.11 = (bf16[8,768]{1,0:T(8,128)(2,1)S(1)}, bf16[8,768]{1,0:T(8,128)(2,1)S(1)}, u32[]{:S(2)}, u32[]{:S(2)}) collective-permute-start(bf16[8,768]{1,0:T(8,128)(2,1)S(1)} %get-tuple-element.49), channel_id=1, source_target_pairs={{0,5},{1,4},{2,7},{3,6},{4,1},{5,0},{6,3},{7,2},{8,13},{9,12},{10,... | collective-permute-start | bytes 36872 | tf_op jit(solution)/shard_map/ppermute | solution.py:382
  27.7 6.4 %collective-permute-start.12 = (bf16[8,768]{1,0:T(8,128)(2,1)S(1)}, bf16[8,768]{1,0:T(8,128)(2,1)S(1)}, u32[]{:S(2)}, u32[]{:S(2)}) collective-permute-start(bf16[8,768]{1,0:T(8,128)(2,1)S(1)} %get-tuple-element.50), channel_id=1, source_target_pairs={{0,6},{1,7},{2,4},{3,5},{4,2},{5,3},{6,0},{7,1},{8,14},{9,15},{10,... | collective-permute-start | bytes 36872 | tf_op jit(solution)/shard_map/ppermute | solution.py:382
  27.7 8.2 %collective-permute-start.13 = (bf16[8,768]{1,0:T(8,128)(2,1)S(1)}, bf16[8,768]{1,0:T(8,128)(2,1)S(1)}, u32[]{:S(2)}, u32[]{:S(2)}) collective-permute-start(bf16[8,768]{1,0:T(8,128)(2,1)S(1)} %get-tuple-element.51), channel_id=1, source_target_pairs={{0,7},{1,6},{2,5},{3,4},{4,3},{5,2},{6,1},{7,0},{8,15},{9,14},{10,... | collective-permute-start | bytes 36872 | tf_op jit(solution)/shard_map/ppermute | solution.py:382
  29.4 9.2 %collective-permute-start.14 = (bf16[8,768]{1,0:T(8,128)(2,1)S(1)}, bf16[8,768]{1,0:T(8,128)(2,1)S(1)}, u32[]{:S(2)}, u32[]{:S(2)}) collective-permute-start(bf16[8,768]{1,0:T(8,128)(2,1)S(1)} %get-tuple-element.52), channel_id=1, source_target_pairs={{0,8},{1,9},{2,10},{3,11},{4,12},{5,13},{6,14},{7,15},{8,0},{9,1},... | collective-permute-start | bytes 36872 | tf_op jit(solution)/shard_map/ppermute | solution.py:382
  30.7 10.0 %collective-permute-start.15 = (bf16[8,768]{1,0:T(8,128)(2,1)S(1)}, bf16[8,768]{1,0:T(8,128)(2,1)S(1)}, u32[]{:S(2)}, u32[]{:S(2)}) collective-permute-start(bf16[8,768]{1,0:T(8,128)(2,1)S(1)} %get-tuple-element.53), channel_id=1, source_target_pairs={{0,9},{1,8},{2,11},{3,10},{4,13},{5,12},{6,15},{7,14},{8,1},{9,0},... | collective-permute-start | bytes 36872 | tf_op jit(solution)/shard_map/ppermute | solution.py:382
  33.3 8.0 %collective-permute-start.16 = (bf16[8,768]{1,0:T(8,128)(2,1)S(1)}, bf16[8,768]{1,0:T(8,128)(2,1)S(1)}, u32[]{:S(2)}, u32[]{:S(2)}) collective-permute-start(bf16[8,768]{1,0:T(8,128)(2,1)S(1)} %get-tuple-element.54), channel_id=1, source_target_pairs={{0,10},{1,11},{2,8},{3,9},{4,14},{5,15},{6,12},{7,13},{8,2},{9,3},... | collective-permute-start | bytes 36872 | tf_op jit(solution)/shard_map/ppermute | solution.py:382
  34.0 15.2 %collective-permute-start.17 = (bf16[8,768]{1,0:T(8,128)(2,1)S(1)}, bf16[8,768]{1,0:T(8,128)(2,1)S(1)}, u32[]{:S(2)}, u32[]{:S(2)}) collective-permute-start(bf16[8,768]{1,0:T(8,128)(2,1)S(1)} %get-tuple-element.55), channel_id=1, source_target_pairs={{0,11},{1,10},{2,9},{3,8},{4,15},{5,14},{6,13},{7,12},{8,3},{9,2},... | collective-permute-start | bytes 36872 | tf_op jit(solution)/shard_map/ppermute | solution.py:382
  35.9 13.4 %collective-permute-start.18 = (bf16[8,768]{1,0:T(8,128)(2,1)S(1)}, bf16[8,768]{1,0:T(8,128)(2,1)S(1)}, u32[]{:S(2)}, u32[]{:S(2)}) collective-permute-start(bf16[8,768]{1,0:T(8,128)(2,1)S(1)} %get-tuple-element.56), channel_id=1, source_target_pairs={{0,12},{1,13},{2,14},{3,15},{4,8},{5,9},{6,10},{7,11},{8,4},{9,5},... | collective-permute-start | bytes 36872 | tf_op jit(solution)/shard_map/ppermute | solution.py:382
  38.6 10.6 %collective-permute-start.19 = (bf16[8,768]{1,0:T(8,128)(2,1)S(1)}, bf16[8,768]{1,0:T(8,128)(2,1)S(1)}, u32[]{:S(2)}, u32[]{:S(2)}) collective-permute-start(bf16[8,768]{1,0:T(8,128)(2,1)S(1)} %get-tuple-element.57), channel_id=1, source_target_pairs={{0,13},{1,12},{2,15},{3,14},{4,9},{5,8},{6,11},{7,10},{8,5},{9,4},... | collective-permute-start | bytes 36872 | tf_op jit(solution)/shard_map/ppermute | solution.py:382
  40.6 8.6 %collective-permute-start.20 = (bf16[8,768]{1,0:T(8,128)(2,1)S(1)}, bf16[8,768]{1,0:T(8,128)(2,1)S(1)}, u32[]{:S(2)}, u32[]{:S(2)}) collective-permute-start(bf16[8,768]{1,0:T(8,128)(2,1)S(1)} %get-tuple-element.58), channel_id=1, source_target_pairs={{0,14},{1,15},{2,12},{3,13},{4,10},{5,11},{6,8},{7,9},{8,6},{9,7},... | collective-permute-start | bytes 36872 | tf_op jit(solution)/shard_map/ppermute | solution.py:382
  41.3 8.0 %collective-permute-start.21 = (bf16[8,768]{1,0:T(8,128)(2,1)S(1)}, bf16[8,768]{1,0:T(8,128)(2,1)S(1)}, u32[]{:S(2)}, u32[]{:S(2)}) collective-permute-start(bf16[8,768]{1,0:T(8,128)(2,1)S(1)} %get-tuple-element.59), channel_id=1, source_target_pairs={{0,15},{1,14},{2,13},{3,12},{4,11},{5,10},{6,9},{7,8},{8,7},{9,6},... | collective-permute-start | bytes 36872 | tf_op jit(solution)/shard_map/ppermute | solution.py:382
  50.5 6.0 %collective-permute-start.23 = (bf16[1,8,3072]{2,1,0:T(8,128)(2,1)S(1)}, bf16[1,8,3072]{2,1,0:T(8,128)(2,1)S(1)}, u32[]{:S(2)}, u32[]{:S(2)}) collective-permute-start(bf16[1,8,3072]{2,1,0:T(8,128)(2,1)S(1)} %get-tuple-element.62), channel_id=1, source_target_pairs={{0,4},{4,0},{8,12},{12,8},{1,5},{5,1},{9,13},{13,9},{2,6},{6,2},{1... | collective-permute-start | bytes 147464 | tf_op jit(solution)/shard_map/ppermute | solution.py:382
  50.5 6.8 %collective-permute-start.25 = (bf16[1,8,3072]{2,1,0:T(8,128)(2,1)S(1)}, bf16[1,8,3072]{2,1,0:T(8,128)(2,1)S(1)}, u32[]{:S(2)}, u32[]{:S(2)}) collective-permute-start(bf16[1,8,3072]{2,1,0:T(8,128)(2,1)S(1)} %get-tuple-element.63), channel_id=1, source_target_pairs={{0,8},{4,12},{8,0},{12,4},{1,9},{5,13},{9,1},{13,5},{2,10},{6,14},... | collective-permute-start | bytes 147464 | tf_op jit(solution)/shard_map/ppermute | solution.py:382
  53.8 5.9 %collective-permute-start.27 = (bf16[1,8,3072]{2,1,0:T(8,128)(2,1)S(1)}, bf16[1,8,3072]{2,1,0:T(8,128)(2,1)S(1)}, u32[]{:S(2)}, u32[]{:S(2)}) collective-permute-start(bf16[1,8,3072]{2,1,0:T(8,128)(2,1)S(1)} %get-tuple-element.64), channel_id=1, source_target_pairs={{0,12},{4,8},{8,4},{12,0},{1,13},{5,9},{9,5},{13,1},{2,14},{6,10},... | collective-permute-start | bytes 147464 | tf_op jit(solution)/shard_map/ppermute | solution.py:382
  54.9 4.8 %collective-permute-start.29 = (bf16[1,8,3072]{2,1,0:T(8,128)(2,1)S(1)}, bf16[1,8,3072]{2,1,0:T(8,128)(2,1)S(1)}, u32[]{:S(2)}, u32[]{:S(2)}) collective-permute-start(bf16[1,8,3072]{2,1,0:T(8,128)(2,1)S(1)} %get-tuple-element.61.refs_0_), channel_id=1, source_target_pairs={{0,2},{2,0},{1,3},{3,1},{4,6},{6,4},{5,7},{7,5},{8,10},{10,8},{9,1... | collective-permute-start | bytes 147464 | tf_op jit(solution)/shard_map/ppermute | solution.py:382
  54.9 6.3 %collective-permute-start.22 = (bf16[1,8,3072]{2,1,0:T(8,128)(2,1)S(1)}, bf16[1,8,3072]{2,1,0:T(8,128)(2,1)S(1)}, u32[]{:S(2)}, u32[]{:S(2)}) collective-permute-start(bf16[1,8,3072]{2,1,0:T(8,128)(2,1)S(1)} %get-tuple-element.61.refs_0_), channel_id=1, source_target_pairs={{0,1},{1,0},{2,3},{3,2},{4,5},{5,4},{6,7},{7,6},{8,9},{9,8},{10,11... | collective-permute-start | bytes 147464 | tf_op jit(solution)/shard_map/ppermute | solution.py:382
  56.4 5.3 %collective-permute-start.31 = (bf16[1,8,3072]{2,1,0:T(8,128)(2,1)S(1)}, bf16[1,8,3072]{2,1,0:T(8,128)(2,1)S(1)}, u32[]{:S(2)}, u32[]{:S(2)}) collective-permute-start(bf16[1,8,3072]{2,1,0:T(8,128)(2,1)S(1)} %collective-permute-done.23.refs_2_), channel_id=1, source_target_pairs={{0,2},{2,0},{1,3},{3,1},{4,6},{6,4},{5,7},{7,5},{8,10},{10,8},{9,1... | collective-permute-start | bytes 147464 | tf_op jit(solution)/shard_map/ppermute | solution.py:382
  57.3 4.4 %collective-permute-start.24 = (bf16[1,8,3072]{2,1,0:T(8,128)(2,1)S(1)}, bf16[1,8,3072]{2,1,0:T(8,128)(2,1)S(1)}, u32[]{:S(2)}, u32[]{:S(2)}) collective-permute-start(bf16[1,8,3072]{2,1,0:T(8,128)(2,1)S(1)} %collective-permute-done.23.refs_2_), channel_id=1, source_target_pairs={{0,1},{1,0},{2,3},{3,2},{4,5},{5,4},{6,7},{7,6},{8,9},{9,8},{10,11... | collective-permute-start | bytes 147464 | tf_op jit(solution)/shard_map/ppermute | solution.py:382
  59.7 2.6 %collective-permute-start.33 = (bf16[1,8,3072]{2,1,0:T(8,128)(2,1)S(1)}, bf16[1,8,3072]{2,1,0:T(8,128)(2,1)S(1)}, u32[]{:S(2)}, u32[]{:S(2)}) collective-permute-start(bf16[1,8,3072]{2,1,0:T(8,128)(2,1)S(1)} %collective-permute-done.25.refs_4_), channel_id=1, source_target_pairs={{0,2},{2,0},{1,3},{3,1},{4,6},{6,4},{5,7},{7,5},{8,10},{10,8},{9,1... | collective-permute-start | bytes 147464 | tf_op jit(solution)/shard_map/ppermute | solution.py:382
  59.7 4.2 %collective-permute-start.26 = (bf16[1,8,3072]{2,1,0:T(8,128)(2,1)S(1)}, bf16[1,8,3072]{2,1,0:T(8,128)(2,1)S(1)}, u32[]{:S(2)}, u32[]{:S(2)}) collective-permute-start(bf16[1,8,3072]{2,1,0:T(8,128)(2,1)S(1)} %collective-permute-done.25.refs_4_), channel_id=1, source_target_pairs={{0,1},{1,0},{2,3},{3,2},{4,5},{5,4},{6,7},{7,6},{8,9},{9,8},{10,11... | collective-permute-start | bytes 147464 | tf_op jit(solution)/shard_map/ppermute | solution.py:382
  61.2 4.1 %collective-permute-start.28 = (bf16[1,8,3072]{2,1,0:T(8,128)(2,1)S(1)}, bf16[1,8,3072]{2,1,0:T(8,128)(2,1)S(1)}, u32[]{:S(2)}, u32[]{:S(2)}) collective-permute-start(bf16[1,8,3072]{2,1,0:T(8,128)(2,1)S(1)} %collective-permute-done.27.refs_6_), channel_id=1, source_target_pairs={{0,1},{1,0},{2,3},{3,2},{4,5},{5,4},{6,7},{7,6},{8,9},{9,8},{10,11... | collective-permute-start | bytes 147464 | tf_op jit(solution)/shard_map/ppermute | solution.py:382
  61.7 3.6 %collective-permute-start.35 = (bf16[1,8,3072]{2,1,0:T(8,128)(2,1)S(1)}, bf16[1,8,3072]{2,1,0:T(8,128)(2,1)S(1)}, u32[]{:S(2)}, u32[]{:S(2)}) collective-permute-start(bf16[1,8,3072]{2,1,0:T(8,128)(2,1)S(1)} %collective-permute-done.27.refs_6_), channel_id=1, source_target_pairs={{0,2},{2,0},{1,3},{3,1},{4,6},{6,4},{5,7},{7,5},{8,10},{10,8},{9,1... | collective-permute-start | bytes 147464 | tf_op jit(solution)/shard_map/ppermute | solution.py:382
  61.7 3.6 %collective-permute-start.30 = (bf16[1,8,3072]{2,1,0:T(8,128)(2,1)S(1)}, bf16[1,8,3072]{2,1,0:T(8,128)(2,1)S(1)}, u32[]{:S(2)}, u32[]{:S(2)}) collective-permute-start(bf16[1,8,3072]{2,1,0:T(8,128)(2,1)S(1)} %collective-permute-done.22.refs_1_), channel_id=1, source_target_pairs={{0,2},{2,0},{1,3},{3,1},{4,6},{6,4},{5,7},{7,5},{8,10},{10,8},{9,1... | collective-permute-start | bytes 147464 | tf_op jit(solution)/shard_map/ppermute | solution.py:382
  62.2 3.1 %collective-permute-start.32 = (bf16[1,8,3072]{2,1,0:T(8,128)(2,1)S(1)}, bf16[1,8,3072]{2,1,0:T(8,128)(2,1)S(1)}, u32[]{:S(2)}, u32[]{:S(2)}) collective-permute-start(bf16[1,8,3072]{2,1,0:T(8,128)(2,1)S(1)} %collective-permute-done.24.refs_3_), channel_id=1, source_target_pairs={{0,2},{2,0},{1,3},{3,1},{4,6},{6,4},{5,7},{7,5},{8,10},{10,8},{9,1... | collective-permute-start | bytes 147464 | tf_op jit(solution)/shard_map/ppermute | solution.py:382
  63.9 1.5 %collective-permute-start.34 = (bf16[1,8,3072]{2,1,0:T(8,128)(2,1)S(1)}, bf16[1,8,3072]{2,1,0:T(8,128)(2,1)S(1)}, u32[]{:S(2)}, u32[]{:S(2)}) collective-permute-start(bf16[1,8,3072]{2,1,0:T(8,128)(2,1)S(1)} %collective-permute-done.26.refs_5_), channel_id=1, source_target_pairs={{0,2},{2,0},{1,3},{3,1},{4,6},{6,4},{5,7},{7,5},{8,10},{10,8},{9,1... | collective-permute-start | bytes 147464 | tf_op jit(solution)/shard_map/ppermute | solution.py:382
  65.3 1.2 %collective-permute-start.36 = (bf16[1,8,3072]{2,1,0:T(8,128)(2,1)S(1)}, bf16[1,8,3072]{2,1,0:T(8,128)(2,1)S(1)}, u32[]{:S(2)}, u32[]{:S(2)}) collective-permute-start(bf16[1,8,3072]{2,1,0:T(8,128)(2,1)S(1)} %collective-permute-done.28.refs_7_), channel_id=1, source_target_pairs={{0,2},{2,0},{1,3},{3,1},{4,6},{6,4},{5,7},{7,5},{8,10},{10,8},{9,1... | collective-permute-start | bytes 147464 | tf_op jit(solution)/shard_map/ppermute | solution.py:382
  79.8 1.8 %collective-permute-start.37 = (bf16[1,8,8,3072]{3,2,1,0:T(8,128)(2,1)S(1)}, bf16[1,8,8,3072]{3,2,1,0:T(8,128)(2,1)S(1)}, u32[]{:S(2)}, u32[]{:S(2)}) collective-permute-start(bf16[1,8,8,3072]{3,2,1,0:T(8,128)(2,1)S(1)} %get-tuple-element.68), channel_id=1, source_target_pairs={{0,2},{2,0},{1,3},{3,1},{4,6},{6,4},{5,7},{7,5},{8,10},{10,8},{9,1... | collective-permute-start | bytes 1179656 | tf_op jit(solution)/shard_map/ppermute | solution.py:382
  81.6 7.0 %collective-permute-start.38 = (bf16[1,8,3072]{2,1,0:T(8,128)(2,1)S(1)}, bf16[1,8,3072]{2,1,0:T(8,128)(2,1)S(1)}, u32[]{:S(2)}, u32[]{:S(2)}) collective-permute-start(bf16[1,8,3072]{2,1,0:T(8,128)(2,1)S(1)} %get-tuple-element.70), channel_id=1, source_target_pairs={{0,1},{1,0},{4,5},{5,4},{8,9},{9,8},{12,13},{13,12},{2,3},{3,2},{6... | collective-permute-start | bytes 147464 | tf_op jit(solution)/shard_map/ppermute | solution.py:382
  82.8 7.2 %collective-permute-start.39 = (bf16[1,8,3072]{2,1,0:T(8,128)(2,1)S(1)}, bf16[1,8,3072]{2,1,0:T(8,128)(2,1)S(1)}, u32[]{:S(2)}, u32[]{:S(2)}) collective-permute-start(bf16[1,8,3072]{2,1,0:T(8,128)(2,1)S(1)} %get-tuple-element.71), channel_id=1, source_target_pairs={{0,4},{1,5},{4,0},{5,1},{8,12},{9,13},{12,8},{13,9},{2,6},{3,7},{6... | collective-permute-start | bytes 147464 | tf_op jit(solution)/shard_map/ppermute | solution.py:382
  82.8 10.0 %collective-permute-start.40 = (bf16[1,8,3072]{2,1,0:T(8,128)(2,1)S(1)}, bf16[1,8,3072]{2,1,0:T(8,128)(2,1)S(1)}, u32[]{:S(2)}, u32[]{:S(2)}) collective-permute-start(bf16[1,8,3072]{2,1,0:T(8,128)(2,1)S(1)} %get-tuple-element.72), channel_id=1, source_target_pairs={{0,5},{1,4},{4,1},{5,0},{8,13},{9,12},{12,9},{13,8},{2,7},{3,6},{6... | collective-permute-start | bytes 147464 | tf_op jit(solution)/shard_map/ppermute | solution.py:382
  85.2 7.7 %collective-permute-start.41 = (bf16[1,8,3072]{2,1,0:T(8,128)(2,1)S(1)}, bf16[1,8,3072]{2,1,0:T(8,128)(2,1)S(1)}, u32[]{:S(2)}, u32[]{:S(2)}) collective-permute-start(bf16[1,8,3072]{2,1,0:T(8,128)(2,1)S(1)} %get-tuple-element.73), channel_id=1, source_target_pairs={{0,8},{1,9},{4,12},{5,13},{8,0},{9,1},{12,4},{13,5},{2,10},{3,11},... | collective-permute-start | bytes 147464 | tf_op jit(solution)/shard_map/ppermute | solution.py:382
  85.5 9.6 %collective-permute-start.42 = (bf16[1,8,3072]{2,1,0:T(8,128)(2,1)S(1)}, bf16[1,8,3072]{2,1,0:T(8,128)(2,1)S(1)}, u32[]{:S(2)}, u32[]{:S(2)}) collective-permute-start(bf16[1,8,3072]{2,1,0:T(8,128)(2,1)S(1)} %get-tuple-element.74), channel_id=1, source_target_pairs={{0,9},{1,8},{4,13},{5,12},{8,1},{9,0},{12,5},{13,4},{2,11},{3,10},... | collective-permute-start | bytes 147464 | tf_op jit(solution)/shard_map/ppermute | solution.py:382
  88.7 6.4 %collective-permute-start.43 = (bf16[1,8,3072]{2,1,0:T(8,128)(2,1)S(1)}, bf16[1,8,3072]{2,1,0:T(8,128)(2,1)S(1)}, u32[]{:S(2)}, u32[]{:S(2)}) collective-permute-start(bf16[1,8,3072]{2,1,0:T(8,128)(2,1)S(1)} %get-tuple-element.75), channel_id=1, source_target_pairs={{0,12},{1,13},{4,8},{5,9},{8,4},{9,5},{12,0},{13,1},{2,14},{3,15},... | collective-permute-start | bytes 147464 | tf_op jit(solution)/shard_map/ppermute | solution.py:382
  90.0 6.8 %collective-permute-start.44 = (bf16[1,8,3072]{2,1,0:T(8,128)(2,1)S(1)}, bf16[1,8,3072]{2,1,0:T(8,128)(2,1)S(1)}, u32[]{:S(2)}, u32[]{:S(2)}) collective-permute-start(bf16[1,8,3072]{2,1,0:T(8,128)(2,1)S(1)} %get-tuple-element.76), channel_id=1, source_target_pairs={{0,13},{1,12},{4,9},{5,8},{8,5},{9,4},{12,1},{13,0},{2,15},{3,14},... | collective-permute-start | bytes 147464 | tf_op jit(solution)/shard_map/ppermute | solution.py:382

commit v3 on v0

--- a/solution.py
+++ b/solution.py
@@ -1,13 +1,552 @@
+import functools
+
 import jax
 import jax.numpy as jnp
 from jax import lax
+from jax.experimental import pallas as pl
+from jax.experimental.pallas import tpu as pltpu
+from jax.sharding import Mesh
 from jax.sharding import PartitionSpec as P
 
 EPSILON = 1e-06
+F32 = jnp.float32
+BF16 = jnp.bfloat16
+MIB = 1 << 20
+ID_LANES = 128
 HIGHEST = lax.Precision.HIGHEST
-
-
-def attend(queries, key_rows, value_rows, states, decay_rates, head_gain):
+VMEM = pl.BlockSpec(memory_space=pltpu.VMEM)
+SMEM = pl.BlockSpec(memory_space=pltpu.SMEM)
+ANY = pl.BlockSpec(memory_space=pl.ANY)
+
+
+def in_hbm(*arrays):
+    return [pltpu.with_memory_space_constraint(a, pltpu.HBM) for a in arrays]
+
+
+def limits(mib):
+    return pltpu.CompilerParams(vmem_limit_bytes=mib * MIB)
+
+
+def dot(a, b):
+    return jnp.dot(a, b, preferred_element_type=F32)
+
+
+def dot_t(a, b):
+    return lax.dot_general(a, b, (((1,), (1,)), ((), ())), preferred_element_type=F32)
+
+
+def halves_of(x):
+    high = x.astype(BF16)
+    return high, (x - high.astype(F32)).astype(BF16)
+
+
+def attend_kernel(positions, steps, decay_ref, ids_ref, q_ref, k_ref, v_ref, gain_ref, s_ref, residual_ref, *refs):
+    weight_hbm, norm_hbm, gate_hbm = refs[:3]
+    outs, copies_out, sem = refs[3:-4], refs[-4:-1], refs[-1]
+    requests, heads, size, _ = s_ref.shape
+    rows = q_ref.shape[0]
+    step = pl.program_id(0)
+    first = step * heads
+    copies = [
+        pltpu.make_async_copy(source, target, sem.at[i])
+        for i, (source, target) in enumerate(
+            zip((weight_hbm, norm_hbm, gate_hbm.at[: copies_out[2].shape[0]]), copies_out)
+        )
+    ]
+
+    @pl.when(step == 0)
+    def _():
+        copies[0].start()
+        copies[1].start()
+        width = steps * heads * size
+        lanes = ID_LANES
+        row = lax.broadcasted_iota(jnp.int32, (rows, lanes), 0)
+        lane = lax.broadcasted_iota(jnp.int32, (rows, lanes), 1)
+        ids = jnp.zeros((rows, lanes), jnp.int32)
+        for k in range(ids_ref.shape[0]):
+            for t in range(ids_ref.shape[1]):
+                ids = jnp.where((row == t) & (lane == k), ids_ref[k, t], ids)
+        ids = ids.astype(F32).astype(BF16)
+        columns = outs[0].shape[1] - width - lanes
+        expert = lax.axis_index("expert")
+        for d, out in enumerate(outs):
+            out[:, width : width + lanes] = ids
+            base = (expert ^ d) * 2 * columns
+            both = [
+                residual_ref[:, pl.ds(pl.multiple_of(base + h * columns, columns), columns)]
+                for h in range(2)
+            ]
+            both = jnp.concatenate([b.astype(F32) for b in both], axis=0)
+            out[:, width + lanes :] = both.astype(BF16)
+
+    @pl.when(step == min(1, steps - 1))
+    def _():
+        copies[2].start()
+
+    row = lax.broadcasted_iota(jnp.int32, (rows, rows), 0)
+    col = lax.broadcasted_iota(jnp.int32, (rows, rows), 1)
+    seen = (row // positions == col // positions) & (row >= col)
+    distance = jnp.maximum(row - col, 0).astype(F32)
+    owner = lax.broadcasted_iota(jnp.int32, (rows, size), 0)
+    age = (owner % positions + 1).astype(F32)
+    for i in range(heads):
+        rate = decay_ref[first + i]
+        at = slice(i * size, (i + 1) * size)
+        q = q_ref[:, at]
+        spread_q = jnp.concatenate(
+            [jnp.where(owner // positions == r, q, jnp.zeros_like(q)) for r in range(requests)],
+            axis=1,
+        )
+        high, low = halves_of(s_ref[:, i].reshape(requests * size, size))
+        from_state = (dot(spread_q, high) + dot(spread_q, low)) * jnp.exp(-rate * age)
+        scores = jnp.where(seen, dot_t(q, k_ref[:, at]) * jnp.exp(-rate * distance), 0.0)
+        score_high, score_low = halves_of(scores)
+        v = v_ref[:, at]
+        mixed = from_state + dot(score_high, v) + dot(score_low, v)
+        spread = jnp.mean(mixed * mixed, axis=1, keepdims=True)
+        normal = mixed * lax.rsqrt(spread + EPSILON) * gain_ref[:, at]
+        normal = normal.astype(BF16)
+        for out in outs:
+            out[:, pl.ds(pl.multiple_of((first + i) * size, size), size)] = normal
+
+    @pl.when(step == steps - 1)
+    def _():
+        for copy in copies:
+            copy.wait()
+
+
+def attend(
+    queries, key_rows, value_rows, states, decay_rates, head_gain, ids, residual, weight, norm_gain, gate, block, experts
+):
+    requests, heads, size, _ = states.shape
+    rows = queries.shape[0]
+    step = 4 if heads % 4 == 0 else 1
+    wide = pl.BlockSpec((rows, step * size), lambda i: (0, i))
+    message = (rows, queries.shape[1] + ID_LANES + weight.shape[1])
+    kept = [(weight.shape, weight.dtype), (norm_gain.shape, F32), ((block, gate.shape[1]), gate.dtype)]
+    return pl.pallas_call(
+        functools.partial(attend_kernel, rows // requests, heads // step),
+        grid=(heads // step,),
+        in_specs=[
+            SMEM,
+            SMEM,
+            wide,
+            wide,
+            wide,
+            pl.BlockSpec((1, step * size), lambda i: (0, i)),
+            pl.BlockSpec((requests, step, size, size), lambda i: (0, i, 0, 0)),
+            pl.BlockSpec(residual.shape, lambda i: (0, 0)),
+            ANY,
+            ANY,
+            ANY,
+        ],
+        out_specs=[pl.BlockSpec(message, lambda i: (0, 0))] * experts + [VMEM] * 3,
+        out_shape=[jax.ShapeDtypeStruct(message, BF16)] * experts
+        + [pltpu.VMEM(shape, dtype) for shape, dtype in kept],
+        scratch_shapes=[pltpu.SemaphoreType.DMA((3,))],
+        compiler_params=limits(8),
+        name="attention",
+    )(
+        *in_hbm(
+            decay_rates, ids, queries, key_rows, value_rows, head_gain.reshape(1, -1), states, residual,
+            weight, norm_gain, gate,
+        )
+    )
+
+
+def project_kernel(*refs):
+    pieces, weight_ref, keep_ref, send_ref, x_ref, product_ref = refs[:-5], *refs[-5:]
+    depth = weight_ref.shape[0]
+    rows = pieces[0].shape[0]
+    expert, half, pair = lax.axis_index("expert"), lax.axis_index("half"), lax.axis_index("pair")
+    for j, piece in enumerate(pieces):
+        base = (expert ^ (j // 2)) * 2 + (half ^ (j % 2))
+        x_ref[pl.ds(pl.multiple_of(base * rows, rows), rows)] = piece[:, :depth]
+    product_ref[...] = dot(x_ref[...], weight_ref[...])
+    own = rows // 2
+    for b in range(len(pieces)):
+        mine = pl.ds(pl.multiple_of(b * rows + pair * own, own), own)
+        keep_ref[b * own : (b + 1) * own] = product_ref[mine]
+    for b in range(0, len(pieces), 2):
+        theirs = [
+            product_ref[pl.ds(pl.multiple_of(c * rows + (1 - pair) * own, own), own)]
+            for c in (b, b + 1)
+        ]
+        send_ref[b * own : (b + 2) * own] = jnp.concatenate(theirs, axis=0).astype(BF16)
+
+
+def project(pieces, weight):
+    rows = pieces[0].shape[0] * len(pieces)
+    depth, columns = weight.shape
+    return pl.pallas_call(
+        project_kernel,
+        in_specs=[VMEM] * (len(pieces) + 1),
+        out_specs=[VMEM] * 2,
+        out_shape=[
+            jax.ShapeDtypeStruct((rows // 2, columns), F32),
+            jax.ShapeDtypeStruct((rows // 2, columns), BF16),
+        ],
+        scratch_shapes=[pltpu.VMEM((rows, depth), BF16), pltpu.VMEM((rows, columns), F32)],
+        compiler_params=limits(8),
+        name="projection",
+    )(*pieces, weight)
+
+
+def route_kernel(capacity, top, *refs):
+    pieces, choose_ref, residual_ref, ids_ref = refs[:-4], *refs[-3:]
+    columns = residual_ref.shape[1]
+    own = pieces[0].shape[0] // 2
+    rows = ids_ref.shape[0]
+    experts = len(pieces) // 2
+    expert, half = lax.axis_index("expert"), lax.axis_index("half")
+    for j, piece in enumerate(pieces):
+        base = (expert ^ (j // 2)) * 2 + (half ^ (j % 2))
+        at = pl.ds(pl.multiple_of(base * own, own), own)
+        last = piece.shape[1] - columns
+        both = piece[:, last:].astype(F32)
+        residual_ref[at] = jnp.where(half == 0, both[:own], both[own:])
+        ids_ref[at] = piece[:, last - ID_LANES : last].astype(F32)[:own]
+    ids = ids_ref[...].T
+    line = lax.broadcasted_iota(jnp.int32, (8, rows), 0)
+    wanted = jnp.bitwise_xor(line, expert).astype(F32)
+    named = jnp.zeros((8, rows), F32)
+    for k in range(top):
+        named = named + jnp.where(ids[k : k + 1] == wanted, 1.0, 0.0)
+    before = lax.broadcasted_iota(jnp.int32, (rows, rows), 0)
+    after = lax.broadcasted_iota(jnp.int32, (rows, rows), 1)
+    earlier = jnp.where((before // own == after // own) & (before < after), 1.0, 0.0)
+    rank = dot(named.astype(BF16), earlier.astype(BF16))
+    dev = lax.broadcasted_iota(jnp.int32, (8, rows), 1) // own
+    place = (dev % 2 * experts + dev // 2) * capacity
+    place = jnp.where(named > 0.5, place.astype(F32) + rank, -1.0)
+    count = choose_ref.shape[0] // experts
+    slot = lax.broadcasted_iota(jnp.int32, (count, rows), 0).astype(F32)
+    for d in range(experts):
+        choose_ref[d * count : (d + 1) * count] = jnp.where(
+            slot == place[d : d + 1], 1.0, 0.0
+        ).astype(BF16)
+
+
+def route(pieces, after, columns, capacity, top):
+    rows = pieces[0].shape[0] // 2 * len(pieces)
+    experts = len(pieces) // 2
+    return pl.pallas_call(
+        functools.partial(route_kernel, capacity, top),
+        in_specs=[VMEM] * len(pieces) + [ANY],
+        out_specs=[VMEM] * 2,
+        out_shape=[
+            jax.ShapeDtypeStruct((experts * 2 * experts * capacity, rows), BF16),
+            jax.ShapeDtypeStruct((rows, columns), F32),
+        ],
+        scratch_shapes=[pltpu.VMEM((rows, ID_LANES), F32)],
+        compiler_params=limits(4),
+        cost_estimate=pl.CostEstimate(flops=10**6, bytes_accessed=10**6, transcendentals=0),
+        name="route",
+    )(*pieces, after)
+
+
+def pack_kernel(keep_ref, got_ref, residual_ref, choose_ref, *refs):
+    outs, sum_ref = refs[:-1], refs[-1]
+    sum_ref[...] = keep_ref[...] + got_ref[...].astype(F32)
+    combined = (sum_ref[...] + residual_ref[...]).astype(BF16)
+    packed = dot(choose_ref[...], combined).astype(BF16)
+    count = choose_ref.shape[0] // len(outs)
+    own = outs[0].shape[0] - count
+    expert = lax.axis_index("expert")
+    for d, out in enumerate(outs):
+        out[:count] = packed[d * count : (d + 1) * count]
+        at = pl.ds(pl.multiple_of((expert ^ d) * own, own), own)
+        out[count:] = sum_ref[at].astype(BF16)
+
+
+def pack(keep, got, residual, choose, experts):
+    rows, columns = keep.shape
+    count = choose.shape[0] // experts
+    return pl.pallas_call(
+        pack_kernel,
+        in_specs=[VMEM] * 4,
+        out_specs=[VMEM] * experts,
+        out_shape=[jax.ShapeDtypeStruct((count + rows // experts, columns), BF16)] * experts,
+        scratch_shapes=[pltpu.VMEM((rows, columns), F32)],
+        compiler_params=limits(4),
+        name="pack",
+    )(keep, got, residual, choose)
+
+
+def expert_kernel(count, block, wide, *refs):
+    near, far = refs[:8], refs[8:16]
+    gain_ref, first_ref, gate_hbm, up_hbm, down_hbm = refs[16:21]
+    keep_ref, send_ref = refs[21:23]
+    x_ref, turned_ref, hidden_ref, gate_ref, up_ref, down_ref, gate_sem, up_sem, down_sem = refs[23:]
+    units, width = up_hbm.shape
+    columns = width // len(near)
+    rows = x_ref.shape[0]
+    blocks, panels = units // block, width // wide
+
+    def copy_of(hbm, ref, sem, t):
+        at = pl.ds(t * block, block)
+        return pltpu.make_async_copy(hbm.at[at], ref.at[at], sem.at[t])
+
+    def down_copy(n):
+        at = pl.ds(n * wide, wide)
+        return pltpu.make_async_copy(down_hbm.at[:, at], down_ref.at[:, at], down_sem.at[n])
+
+    for t in range(blocks):
+        if t:
+            copy_of(gate_hbm, gate_ref, gate_sem, t).start()
+        copy_of(up_hbm, up_ref, up_sem, t).start()
+    for n in range(panels):
+        down_copy(n).start()
+
+    expert, half = lax.axis_index("expert"), lax.axis_index("half")
+    for p, pieces in enumerate((near, far)):
+        for j, piece in enumerate(pieces):
+            base = ((expert ^ (j // 2)) * 2 + (half ^ (j % 2))) * columns
+            at = pl.ds(pl.multiple_of(base, columns), columns)
+            x_ref[p * count : (p + 1) * count, at] = piece[:count].astype(F32)
+    squares = jnp.zeros((rows, 128), F32)
+    for b in range(width // 128):
+        x = x_ref[:, b * 128 : (b + 1) * 128]
+        squares = squares + x * x
+    scale = lax.rsqrt(jnp.sum(squares, axis=1, keepdims=True) / width + EPSILON)
+    for b in range(len(near)):
+        at = slice(b * columns, (b + 1) * columns)
+        normed = x_ref[:, at] * scale * gain_ref[:, at]
+        turned_ref[at] = normed.T.astype(BF16)
+
+    for t in range(blocks):
+        at = slice(t * block, (t + 1) * block)
+        if t:
+            copy_of(gate_hbm, gate_ref, gate_sem, t).wait()
+            gate_value = dot(gate_ref[at], turned_ref[...])
+        else:
+            gate_value = dot(first_ref[...], turned_ref[...])
+        copy_of(up_hbm, up_ref, up_sem, t).wait()
+        lifted = dot(up_ref[at], turned_ref[...])
+        hidden = gate_value / (1.0 + jnp.exp(-gate_value)) * lifted
+        hidden_ref[:, at] = hidden.T.astype(BF16)
+
+    part = count // 2
+    for n in range(panels):
+        down_copy(n).wait()
+        at = slice(n * wide, (n + 1) * wide)
+        total = dot(hidden_ref[...], down_ref[:, at])
+        for p in range(2):
+            low = total[p * count : p * count + part]
+            high = total[p * count + part : (p + 1) * count]
+            to = slice(p * part, (p + 1) * part)
+            keep_ref[to, at] = jnp.where(half == 0, low, high)
+            send_ref[to, at] = jnp.where(half == 0, high, low).astype(BF16)
+
+
+def expert_apply(near, far, gain, first, gate_part, up_part, down_part, count):
+    units, width = gate_part.shape
+    block = first.shape[0]
+    wide = 512
+    return pl.pallas_call(
+        functools.partial(expert_kernel, count, block, wide),
+        in_specs=[VMEM] * 18 + [ANY] * 3,
+        out_specs=(VMEM, VMEM),
+        out_shape=(
+            jax.ShapeDtypeStruct((count, width), F32),
+            jax.ShapeDtypeStruct((count, width), BF16),
+        ),
+        scratch_shapes=[
+            pltpu.VMEM((2 * count, width), F32),
+            pltpu.VMEM((width, 2 * count), BF16),
+            pltpu.VMEM((2 * count, units), BF16),
+            pltpu.VMEM((units, width), BF16),
+            pltpu.VMEM((units, width), BF16),
+            pltpu.VMEM((units, width), BF16),
+            pltpu.SemaphoreType.DMA((units // block,)),
+            pltpu.SemaphoreType.DMA((units // block,)),
+            pltpu.SemaphoreType.DMA((width // wide,)),
+        ],
+        compiler_params=limits(52),
+        name="experts",
+    )(*near, *far, gain, first, *in_hbm(gate_part, up_part, down_part))
+
+
+def chip_sum_kernel(mine_ref, got_ref, keep_ref, send_ref):
+    rows = keep_ref.shape[0]
+    keep_ref[...] = mine_ref[:rows] + got_ref[:rows].astype(F32)
+    send_ref[...] = (mine_ref[rows:] + got_ref[rows:].astype(F32)).astype(BF16)
+
+
+def chip_sum(mine, got):
+    rows, width = mine.shape
+    return pl.pallas_call(
+        chip_sum_kernel,
+        in_specs=[VMEM] * 2,
+        out_specs=[VMEM] * 2,
+        out_shape=[
+            jax.ShapeDtypeStruct((rows // 2, width), F32),
+            jax.ShapeDtypeStruct((rows // 2, width), BF16),
+        ],
+        compiler_params=limits(4),
+        name="chip_sum",
+    )(mine, got)
+
+
+def pair_sum_kernel(capacity, keep_ref, got_ref, *refs):
+    outs, fold_ref = refs[:-1], refs[-1]
+    experts = len(outs)
+    parts = 8 // capacity
+    part = outs[0].shape[1]
+    total = keep_ref[...] + got_ref[...].astype(F32)
+    for e in range(experts):
+        mine = total[e * capacity : (e + 1) * capacity]
+        fold_ref[e] = jnp.concatenate(
+            [mine[:, h * part : (h + 1) * part] for h in range(parts)], axis=0
+        )
+    expert = lax.axis_index("expert")
+    for d, out in enumerate(outs):
+        out[...] = fold_ref[expert ^ d].astype(BF16)
+
+
+def pair_sum(keep, got, capacity, experts):
+    part = keep.shape[1] * capacity // 8
+    return pl.pallas_call(
+        functools.partial(pair_sum_kernel, capacity),
+        in_specs=[VMEM] * 2,
+        out_specs=[VMEM] * experts,
+        out_shape=[jax.ShapeDtypeStruct((8, part), BF16)] * experts,
+        scratch_shapes=[pltpu.VMEM((experts, 8, part), F32)],
+        compiler_params=limits(4),
+        name="pair_sum",
+    )(keep, got)
+
+
+def own_rows_kernel(capacity, count, ids_ref, weights_ref, residual_ref, *refs):
+    pieces, combined_ref, weighting_ref = refs[:-3], *refs[-2:]
+    rows = combined_ref.shape[0]
+    columns = pieces[0].shape[1]
+    expert, half = lax.axis_index("expert"), lax.axis_index("half")
+    for j, piece in enumerate(pieces):
+        base = ((expert ^ (j // 2)) * 2 + (half ^ (j % 2))) * columns
+        at = pl.ds(pl.multiple_of(base, columns), columns)
+        both = piece[count:].astype(F32)
+        mine = jnp.where(half == 0, both[:rows], both[rows:])
+        combined_ref[:, at] = residual_ref[:, at].astype(F32) + mine
+    places = weighting_ref.shape[1]
+    row = lax.broadcasted_iota(jnp.int32, (rows, places), 0)
+    place = lax.broadcasted_iota(jnp.int32, (rows, places), 1)
+    slot = place // 8 * capacity + place % capacity
+    weighting = jnp.zeros((rows, places), F32)
+    top = ids_ref.shape[0]
+    order = [(t, k) for t in range(rows) for k in range(top)]
+    named = [ids_ref[k, t] for t, k in order]
+    for j, (t, k) in enumerate(order):
+        rank = jnp.int32(0)
+        for i in range(j):
+            rank = rank + jnp.where(named[i] == named[j], 1, 0)
+        at = (named[j] ^ expert) * capacity + rank
+        weighting = jnp.where((slot == at) & (row == t), weights_ref[k, t], weighting)
+    for h in range(8 // capacity):
+        high, low = halves_of(jnp.where(place % 8 // capacity == h, weighting, 0.0))
+        both = jnp.concatenate([high.astype(F32), low.astype(F32)], axis=0)
+        weighting_ref[h * 16 : (h + 1) * 16] = both.astype(BF16)
+
+
+def own_rows(ids, weights, residual, pieces, after, capacity, count):
+    rows, width = residual.shape
+    experts = len(pieces) // 2
+    return pl.pallas_call(
+        functools.partial(own_rows_kernel, capacity, count),
+        in_specs=[SMEM, SMEM, VMEM] + [VMEM] * len(pieces) + [ANY],
+        out_specs=[VMEM] * 2,
+        out_shape=[
+            jax.ShapeDtypeStruct((rows, width), F32),
+            jax.ShapeDtypeStruct((16 * (8 // capacity), experts * 8), BF16),
+        ],
+        compiler_params=limits(4),
+        cost_estimate=pl.CostEstimate(flops=10**6, bytes_accessed=10**6, transcendentals=0),
+        name="own_rows",
+    )(*in_hbm(ids, weights, residual), *pieces, after)
+
+
+def finish_kernel(combined_ref, weighting_ref, *refs):
+    got, out_ref = refs[:-1], refs[-1]
+    part = got[0].shape[1]
+    rows = combined_ref.shape[0]
+    terms = jnp.concatenate([piece[...].astype(F32) for piece in got], axis=0).astype(BF16)
+    for h in range(combined_ref.shape[1] // part):
+        at = slice(h * part, (h + 1) * part)
+        mixture = dot(weighting_ref[h * 16 : (h + 1) * 16], terms)
+        out_ref[:, at] = (combined_ref[:, at] + mixture[:rows] + mixture[rows:]).astype(BF16)
+
+
+def finish(combined, weighting, got):
+    return pl.pallas_call(
+        finish_kernel,
+        in_specs=[VMEM] * (2 + len(got)),
+        out_specs=VMEM,
+        out_shape=jax.ShapeDtypeStruct(combined.shape, BF16),
+        compiler_params=limits(4),
+        name="finish",
+    )(combined, weighting, *got)
+
+
+def swap(x, axis, by):
+    return lax.ppermute(x, axis, [(i, i ^ by) for i in range(lax.axis_size(axis))]) if by else x
+
+
+def on_chips(
+    queries,
+    key_rows,
+    value_rows,
+    states,
+    decay_rates,
+    head_gain,
+    out_weight,
+    residual,
+    norm_gain,
+    expert_ids,
+    gate_weights,
+    expert_gate,
+    expert_up,
+    expert_down,
+):
+    experts = lax.axis_size("expert")
+    local_rows = residual.shape[0]
+    columns = out_weight.shape[1]
+    top = expert_ids.shape[1]
+    capacity = max(2, local_rows * top // experts)
+    count = 2 * experts * capacity
+    block = next(b for b in (384, 256, 128) if expert_gate.shape[0] % b == 0)
+    ids, weights = expert_ids.T, gate_weights.T
+
+    *messages, weight_here, gain_here, gate_first = attend(
+        queries, key_rows, value_rows, states, decay_rates, head_gain, ids, residual,
+        out_weight, norm_gain.reshape(1, -1), expert_gate, block, experts,
+    )
+    pieces = []
+    for d, message in enumerate(messages):
+        message = swap(message, "expert", d)
+        pieces += [message, swap(message, "half", 1)]
+
+    keep, send = project(pieces, weight_here)
+    choose, residual_part = route(pieces, keep, columns, capacity, top)
+    packed = pack(keep, swap(send, "pair", 1), residual_part, choose, experts)
+
+    near, far = [], []
+    for d, rows in enumerate(packed):
+        rows = swap(rows, "expert", d)
+        crossed = swap(rows[:count], "pair", 1)
+        near += [rows, swap(rows, "half", 1)]
+        far += [crossed, swap(crossed, "half", 1)]
+    mine, send = expert_apply(
+        near, far, gain_here, gate_first, expert_gate, expert_up, expert_down, count
+    )
+
+    combined, weighting = own_rows(ids, weights, residual, near, mine, capacity, count)
+    keep, send = chip_sum(mine, swap(send, "half", 1))
+    terms = pair_sum(keep, swap(send, "pair", 1), capacity, experts)
+    back = [swap(term, "expert", d) for d, term in enumerate(terms)]
+    return finish(combined, weighting, back)
+
+
+def plain_attend(queries, key_rows, value_rows, states, decay_rates, head_gain):
     requests = states.shape[0]
     head_count = states.shape[1]
     head_size = states.shape[2]
@@ -39,7 +578,7 @@
     return normal.astype(jnp.bfloat16).reshape(requests * positions, head_count * head_size)
 
 
-def expert_apply(picked, gate_part, up_part, down_part):
+def plain_experts(picked, gate_part, up_part, down_part):
     leading = picked.shape
     flattened = picked.reshape(-1, leading[-1])
     contract = (((1,), (1,)), ((), ()))
@@ -50,7 +589,7 @@
     return output.reshape(leading)
 
 
-def on_device(
+def plain(
     queries,
     key_rows,
     value_rows,
@@ -69,7 +608,7 @@
     outer_count = lax.axis_size("dev")
     pair_count = lax.axis_size("pair")
     core_count = lax.axis_size("sub")
-    attended = attend(queries, key_rows, value_rows, states, decay_rates, head_gain)
+    attended = plain_attend(queries, key_rows, value_rows, states, decay_rates, head_gain)
     partial_value = jnp.dot(
         lax.all_gather(attended, ("dev", "sub"), axis=0, tiled=True),
         out_weight,
@@ -108,7 +647,7 @@
     outgoing = jnp.broadcast_to(slot_rows, (expert_count, 2, capacity, width)).reshape(
         outer_count, capacity, width
     )
-    partials = expert_apply(
+    partials = plain_experts(
         lax.all_gather(
             lax.all_to_all(outgoing, "dev", split_axis=0, concat_axis=0, tiled=True)[None],
             ("pair", "sub"),
@@ -137,25 +676,45 @@
 
 
 def solution(mesh):
-    return jax.shard_map(
-        on_device,
-        mesh=mesh,
-        in_specs=(
-            P(("grp", "dev", "sub"), "pair"),
-            P(("grp", "dev", "sub"), "pair"),
-            P(("grp", "dev", "sub"), "pair"),
-            P(("grp", "dev", "sub"), "pair", None, None),
+    sizes = dict(mesh.shape)
+    plain_axes = (("dev",), ("pair", "sub"), ("sub",))
+    chip_axes = (("expert", "half"), ("pair",), ())
+
+    def specs(dev, inner, sub):
+        requests = P(("grp",) + dev + sub, "pair")
+        tokens = P(("grp",) + dev + inner, None)
+        units = P(dev + inner, None)
+        arguments = (
+            requests,
+            requests,
+            requests,
+            P(("grp",) + dev + sub, "pair", None, None),
             P("pair"),
             P("pair"),
-            P("pair", ("dev", "sub")),
-            P(("grp", "dev", "pair", "sub"), None),
+            P("pair", dev + sub),
+            tokens,
             P(),
-            P(("grp", "dev", "pair", "sub"), None),
-            P(("grp", "dev", "pair", "sub"), None),
-            P(("dev", "pair", "sub"), None),
-            P(("dev", "pair", "sub"), None),
-            P(("dev", "pair", "sub"), None),
-        ),
-        out_specs=P(("grp", "dev", "pair", "sub"), None),
-        check_vma=False,
-    )
+            tokens,
+            tokens,
+            units,
+            units,
+            units,
+        )
+        return dict(in_specs=arguments, out_specs=tokens, check_vma=False)
+
+    experts = sizes["dev"] // 2
+    chips = sizes["pair"] == 2 and sizes["sub"] == 1 and experts in (2, 4, 8)
+
+    def run(*arguments):
+        rows = arguments[7].shape[0] // mesh.size
+        columns = arguments[6].shape[1] // (sizes["dev"] * sizes["sub"])
+        units = arguments[11].shape[0] * sizes["grp"] // mesh.size
+        if chips and rows == 8 and columns % 128 == 0 and units % 128 == 0:
+            cut = Mesh(
+                mesh.devices.reshape(sizes["grp"], experts, 2, 2),
+                ("grp", "expert", "half", "pair"),
+            )
+            return jax.shard_map(on_chips, mesh=cut, **specs(*chip_axes))(*arguments)
+        return jax.shard_map(plain, mesh=mesh, **specs(*plain_axes))(*arguments)
+
+    return run

time: 200 us -> 92.9 us (0.46)
  blocking collectives: 43.1 us -> 0 us
  waiting for transfers between devices: 67 us -> 26.4 us
  matrix products: 38.9 us -> 0 us
  Pallas kernels: 0 us -> 36.5 us
  starting transfers between devices: 9.27 us -> 25.3 us
  local copies, waits for them, and re-layouts: 20.3 us -> 4.43 us
  between operations: 13.5 us -> 0.11 us
  other arithmetic: 7.04 us -> 0 us
    dot_general x8 -> x0, matrix products: 38.9 us -> none  [the longest x1 20.7 us: expert_apply(): output = jnp.dot(hidden, down_part, preferred_element_type=jnp.float32)]
    reduce_scatter x2 -> x0, waiting for transfers between devices: 38.1 us -> none  [the longest x1 24.6 us: on_device(): lax.psum_scatter(partials, ('pair', 'sub'), scatter_dimension=0, tiled=True)]
    pallas_call x0 -> x9, Pallas kernels: none -> 36.5 us  [the longest x1 27.1 us: expert_apply(): pl.pallas_call(functools.partial(expert_kernel, count, block, wide), in_s...]
    all_to_all x2 -> x0, waiting for transfers between devices: 28.9 us -> none  [the longest x1 20.9 us: on_device(): lax.all_to_all(summed_terms[0], 'dev', split_axis=0, concat_axis=0, tiled...]
    all_gather x2 -> x0, blocking collectives: 28.2 us -> none  [the longest x1 16.6 us: on_device(): lax.all_gather(attended, ('dev', 'sub'), axis=0, tiled=True)]
    ppermute x0 -> x28, waiting for transfers between devices: none -> 26.4 us  [swap(): lax.ppermute(x, axis, [(i, i ^ by) for i in range(lax.axis_size(axis))])]
    ppermute x0 -> x28, starting transfers between devices: none -> 25.3 us  [swap(): lax.ppermute(x, axis, [(i, i ^ by) for i in range(lax.axis_size(axis))])]
    all_to_all x1 -> x0, blocking collectives: 14.9 us -> none  [on_device(): lax.all_to_all(outgoing, 'dev', split_axis=0, concat_axis=0, tiled=True)]
  transfers between devices with their start and end apart: 4 -> 28, of which waited for: 4 -> 14; matrix products, arithmetic and copies ran while one was open for 1% -> 0% of each run, Pallas kernels for 0% -> 1%
where the time goes in v3:
time: 92.9 us; the launch traced here: 92.6 us
  Pallas kernels  36.5 us (39%)
  waiting for transfers between devices  26.4 us (28%)
  starting transfers between devices  25.3 us (27%)
  local copies, waits for them, and re-layouts  4.43 us (5%)
    pallas_call x1, Pallas kernels, expert_apply(): pl.pallas_call(functools.partial(expert_kernel, count, block, wide), in_s...  27.1 us
    ppermute x28, waiting for transfers between devices, swap(): lax.ppermute(x, axis, [(i, i ^ by) for i in range(lax.axis_size(axis))])  26.4 us
    ppermute x28, starting transfers between devices, swap(): lax.ppermute(x, axis, [(i, i ^ by) for i in range(lax.axis_size(axis))])  25.3 us
    pallas_call x1, Pallas kernels, attend(): pl.pallas_call(functools.partial(attend_kernel, rows // requests, heads /...  6.17 us
    unnamed x6, local copies, waits for them, and re-layouts  4.41 us
  transfers between devices with their start and end apart: 28, of which 14 were waited for; matrix products, arithmetic and copies ran while one was open for 0% of the time, Pallas kernels for 1%

profile of v3, /device:TPU:0, one launch (start us, length us, event | category | flops | bytes accessed | tf_op | source)
XLA Modules:
  0.0 92.6 jit_solution(2399782731490772625)
XLA Ops:
  0.0 6.2 %attention.1 = (bf16[16,2944]{1,0:T(8,128)(2,1)S(1)}, bf16[16,2944]{1,0:T(8,128)(2,1)S(1)}, bf16[16,2944]{1,0:T(8,128)(2,1)S(1)}, bf16[16,2944]{1,0:T(8,128)(2,1...) custom-call(f32[16]{0:T(128)} %decay_ref.1, s32[2,8]{1,0:T(2,128)} %bitcast.6, ...), custom_call_target="tpu_custom_call" | custom-call | tf_op jit(solution)/shard_map/attention/pallas_call | solution.py:127
  6.2 2.1 %copy-done = bf16[384,6144]{1,0:T(8,128)(2,1)} copy-done((bf16[384,6144]{1,0:T(8,128)(2,1)}, bf16[384,6144]{1,0:T(8,128)(2,1)S(1)}, u32[]{:S(2)}) %copy-start) | copy-done | bytes 4718616
  8.3 3.0 %collective-permute-start.1 = (bf16[16,2944]{1,0:T(8,128)(2,1)S(1)}, bf16[16,2944]{1,0:T(8,128)(2,1)S(1)}, u32[]{:S(2)}, u32[]{:S(2)}) collective-permute-start(bf16[16,2944]{1,0:T(8,128)(2,1)S(1)} %get-tuple-element.31), channel_id=1, source_target_pairs={{0,4},{4,0},{8,12},{12,8},{1,5},{5,1},{9,13},{13,9},{2,6},{6,2},{1... | collective-permute-start | bytes 282632 | tf_op jit(solution)/shard_map/ppermute | solution.py:491
  11.4 2.6 %collective-permute-start.3 = (bf16[16,2944]{1,0:T(8,128)(2,1)S(1)}, bf16[16,2944]{1,0:T(8,128)(2,1)S(1)}, u32[]{:S(2)}, u32[]{:S(2)}) collective-permute-start(bf16[16,2944]{1,0:T(8,128)(2,1)S(1)} %get-tuple-element.32), channel_id=1, source_target_pairs={{0,8},{4,12},{8,0},{12,4},{1,9},{5,13},{9,1},{13,5},{2,10},{6,14},... | collective-permute-start | bytes 282632 | tf_op jit(solution)/shard_map/ppermute | solution.py:491
  13.9 0.0 collective-permute-start.5
  14.0 0.0 collective-permute-start
  14.0 0.1 collective-permute-done.1.refs_2_
  14.1 0.4 collective-permute-start.2
  14.5 7.0 %collective-permute-done.3.refs_4_ = bf16[16,2944]{1,0:T(8,128)(2,1)S(1)} collective-permute-done((bf16[16,2944]{1,0:T(8,128)(2,1)S(1)}, bf16[16,2944]{1,0:T(8,128)(2,1)S(1)}, u32[]{:S(2)}, u32[]{:S(2)}) %collective-permute-start.3) | collective-permute-done | bytes 94240 | tf_op jit(solution)/shard_map/ppermute | solution.py:491
  21.5 0.0 collective-permute-start.4
  21.5 0.0 collective-permute-done.5.refs_6_
  21.5 0.5 collective-permute-start.6
  22.0 0.0 collective-permute-done.refs_1_
  22.0 0.0 collective-permute-done.2.refs_3_
  22.0 0.8 collective-permute-done.4.refs_5_
  22.8 0.2 collective-permute-done.6.refs_7_
  22.9 0.7 projection.1
  23.6 1.6 %collective-permute-start.7 = (bf16[64,768]{1,0:T(8,128)(2,1)S(1)}, bf16[64,768]{1,0:T(8,128)(2,1)S(1)}, u32[]{:S(2)}, u32[]{:S(2)}) collective-permute-start(bf16[64,768]{1,0:T(8,128)(2,1)S(1)} %get-tuple-element.36), channel_id=1, source_target_pairs={{0,1},{1,0},{2,3},{3,2},{4,5},{5,4},{6,7},{7,6},{8,9},{9,8},{10,11... | collective-permute-start | bytes 294920 | tf_op jit(solution)/shard_map/ppermute | solution.py:491
  25.2 0.2 route.1
  25.5 3.3 %collective-permute-done.7.got_ref = bf16[64,768]{1,0:T(8,128)(2,1)S(1)} collective-permute-done((bf16[64,768]{1,0:T(8,128)(2,1)S(1)}, bf16[64,768]{1,0:T(8,128)(2,1)S(1)}, u32[]{:S(2)}, u32[]{:S(2)}) %collective-permute-start.7) | collective-permute-done | bytes 98336 | tf_op jit(solution)/shard_map/ppermute | solution.py:491
  28.8 0.2 pack.1
  29.0 1.3 %collective-permute-start.9 = (bf16[48,768]{1,0:T(8,128)(2,1)S(1)}, bf16[48,768]{1,0:T(8,128)(2,1)S(1)}, u32[]{:S(2)}, u32[]{:S(2)}) collective-permute-start(bf16[48,768]{1,0:T(8,128)(2,1)S(1)} %get-tuple-element.40), channel_id=1, source_target_pairs={{0,4},{4,0},{8,12},{12,8},{1,5},{5,1},{9,13},{13,9},{2,6},{6,2},{1... | collective-permute-start | bytes 221192 | tf_op jit(solution)/shard_map/ppermute | solution.py:491
  30.2 1.8 %collective-permute-start.11 = (bf16[48,768]{1,0:T(8,128)(2,1)S(1)}, bf16[48,768]{1,0:T(8,128)(2,1)S(1)}, u32[]{:S(2)}, u32[]{:S(2)}) collective-permute-start(bf16[48,768]{1,0:T(8,128)(2,1)S(1)} %get-tuple-element.41), channel_id=1, source_target_pairs={{0,8},{4,12},{8,0},{12,4},{1,9},{5,13},{9,1},{13,5},{2,10},{6,14},... | collective-permute-start | bytes 221192 | tf_op jit(solution)/shard_map/ppermute | solution.py:491
  32.1 1.5 %collective-permute-start.15 = (bf16[32,768]{1,0:T(8,128)(2,1)S(1)}, bf16[32,768]{1,0:T(8,128)(2,1)S(1)}, u32[]{:S(2)}, u32[]{:S(2)}) collective-permute-start(bf16[32,768]{1,0:T(8,128)(2,1)S(1)} %slice.12), channel_id=1, source_target_pairs={{0,1},{1,0},{2,3},{3,2},{4,5},{5,4},{6,7},{7,6},{8,9},{9,8},{10,11... | collective-permute-start | bytes 147464 | tf_op jit(solution)/shard_map/ppermute | solution.py:491
  33.6 1.3 %collective-permute-start.13 = (bf16[48,768]{1,0:T(8,128)(2,1)S(1)}, bf16[48,768]{1,0:T(8,128)(2,1)S(1)}, u32[]{:S(2)}, u32[]{:S(2)}) collective-permute-start(bf16[48,768]{1,0:T(8,128)(2,1)S(1)} %get-tuple-element.42), channel_id=1, source_target_pairs={{0,12},{4,8},{8,4},{12,0},{1,13},{5,9},{9,5},{13,1},{2,14},{6,10},... | collective-permute-start | bytes 221192 | tf_op jit(solution)/shard_map/ppermute | solution.py:491
  34.9 0.0 collective-permute-start.8
  34.9 1.2 %collective-permute-done.15.refs_8_ = bf16[32,768]{1,0:T(8,128)(2,1)S(1)} collective-permute-done((bf16[32,768]{1,0:T(8,128)(2,1)S(1)}, bf16[32,768]{1,0:T(8,128)(2,1)S(1)}, u32[]{:S(2)}, u32[]{:S(2)}) %collective-permute-start.15) | collective-permute-done | bytes 49184 | tf_op jit(solution)/shard_map/ppermute | solution.py:491
  36.2 0.0 collective-permute-start.16
  36.2 0.0 collective-permute-done.9.refs_2_
  36.2 1.6 %collective-permute-start.17 = (bf16[32,768]{1,0:T(8,128)(2,1)S(1)}, bf16[32,768]{1,0:T(8,128)(2,1)S(1)}, u32[]{:S(2)}, u32[]{:S(2)}) collective-permute-start(bf16[32,768]{1,0:T(8,128)(2,1)S(1)} %slice.16), channel_id=1, source_target_pairs={{0,1},{1,0},{2,3},{3,2},{4,5},{5,4},{6,7},{7,6},{8,9},{9,8},{10,11... | collective-permute-start | bytes 147464 | tf_op jit(solution)/shard_map/ppermute | solution.py:491
  37.7 0.0 collective-permute-done.11.refs_4_
  37.8 0.2 collective-permute-start.10
  38.0 1.8 %collective-permute-done.13.refs_6_ = bf16[48,768]{1,0:T(8,128)(2,1)S(1)} collective-permute-done((bf16[48,768]{1,0:T(8,128)(2,1)S(1)}, bf16[48,768]{1,0:T(8,128)(2,1)S(1)}, u32[]{:S(2)}, u32[]{:S(2)}) %collective-permute-start.13) | collective-permute-done | bytes 73760 | tf_op jit(solution)/shard_map/ppermute | solution.py:491
  39.7 0.6 collective-permute-start.19
  40.4 1.4 %collective-permute-start.21 = (bf16[32,768]{1,0:T(8,128)(2,1)S(1)}, bf16[32,768]{1,0:T(8,128)(2,1)S(1)}, u32[]{:S(2)}, u32[]{:S(2)}) collective-permute-start(bf16[32,768]{1,0:T(8,128)(2,1)S(1)} %slice.18), channel_id=1, source_target_pairs={{0,1},{1,0},{2,3},{3,2},{4,5},{5,4},{6,7},{7,6},{8,9},{9,8},{10,11... | collective-permute-start | bytes 147464 | tf_op jit(solution)/shard_map/ppermute | solution.py:491
  41.8 0.0 collective-permute-done.16.refs_9_
  41.8 0.0 collective-permute-start.12
  41.8 0.0 collective-permute-done.17.refs_10_
  41.8 0.5 collective-permute-start.14
  42.3 1.5 %collective-permute-done.19.refs_12_ = bf16[32,768]{1,0:T(8,128)(2,1)S(1)} collective-permute-done((bf16[32,768]{1,0:T(8,128)(2,1)S(1)}, bf16[32,768]{1,0:T(8,128)(2,1)S(1)}, u32[]{:S(2)}, u32[]{:S(2)}) %collective-permute-start.19) | collective-permute-done | bytes 49184 | tf_op jit(solution)/shard_map/ppermute | solution.py:491
  43.8 0.0 collective-permute-start.18
  43.8 0.7 collective-permute-done.21.refs_14_
  44.5 0.0 collective-permute-start.20
  44.5 0.0 collective-permute-done.10.refs_3_
  44.5 0.5 collective-permute-start.22
  45.0 0.0 collective-permute-done.12.refs_5_
  45.1 0.7 collective-permute-done.20.refs_13_
  45.8 0.2 collective-permute-done.22.refs_15_
  45.9 27.1 %experts.1 = (f32[32,6144]{1,0:T(8,128)}, bf16[32,6144]{1,0:T(8,128)(2,1)S(1)}) custom-call(bf16[48,768]{1,0:T(8,128)(2,1)S(1)} %get-tuple-element.39.refs_0_, bf16[48,768]{1,0:T(8,128)(2,1)S(1)} %collective-permute-done.8.refs_1_, bf16[48,768]{1,0:T(8,128)(2,1)S(1)} %collective-permute-done.9.refs_2_, bf16[48,768]{1,0:T(8,128)(2,1)S(1)} %collective-permute-done.10.refs_3_, ...), custom_call_target="tpu_custom_call" | custom-call | tf_op jit(solution)/shard_map/experts/pallas_call | solution.py:346
  73.0 0.4 collective-permute-start.23
  73.4 1.4 %collective-permute-done.23.got_ref = bf16[32,6144]{1,0:T(8,128)(2,1)S(1)} collective-permute-done((bf16[32,6144]{1,0:T(8,128)(2,1)S(1)}, bf16[32,6144]{1,0:T(8,128)(2,1)S(1)}, u32[]{:S(2)}, u32[]{:S(2)}) %collective-permute-start.23) | collective-permute-done | bytes 393248 | tf_op jit(solution)/shard_map/ppermute | solution.py:491
  74.8 1.1 %copy-done.1 = f32[32,6144]{1,0:T(8,128)S(1)} copy-done((f32[32,6144]{1,0:T(8,128)S(1)}, f32[32,6144]{1,0:T(8,128)}, u32[]{:S(2)}) %copy-start.1) | copy-done | bytes 786456
  75.9 0.1 chip_sum.1
  76.0 1.5 %collective-permute-start.24 = (bf16[16,6144]{1,0:T(8,128)(2,1)S(1)}, bf16[16,6144]{1,0:T(8,128)(2,1)S(1)}, u32[]{:S(2)}, u32[]{:S(2)}) collective-permute-start(bf16[16,6144]{1,0:T(8,128)(2,1)S(1)} %get-tuple-element.50), channel_id=1, source_target_pairs={{0,1},{1,0},{2,3},{3,2},{4,5},{5,4},{6,7},{7,6},{8,9},{9,8},{10,11... | collective-permute-start | bytes 589832 | tf_op jit(solution)/shard_map/ppermute | solution.py:491
  77.4 5.8 %collective-permute-done.24.got_ref = bf16[16,6144]{1,0:T(8,128)(2,1)S(1)} collective-permute-done((bf16[16,6144]{1,0:T(8,128)(2,1)S(1)}, bf16[16,6144]{1,0:T(8,128)(2,1)S(1)}, u32[]{:S(2)}, u32[]{:S(2)}) %collective-permute-start.24) | collective-permute-done | bytes 196640 | tf_op jit(solution)/shard_map/ppermute | solution.py:491
  83.2 0.1 pair_sum.1
  83.3 0.9 collective-permute-start.25
  84.2 1.8 %collective-permute-start.26 = (bf16[8,3072]{1,0:T(8,128)(2,1)S(1)}, bf16[8,3072]{1,0:T(8,128)(2,1)S(1)}, u32[]{:S(2)}, u32[]{:S(2)}) collective-permute-start(bf16[8,3072]{1,0:T(8,128)(2,1)S(1)} %get-tuple-element.53), channel_id=1, source_target_pairs={{0,8},{4,12},{8,0},{12,4},{1,9},{5,13},{9,1},{13,5},{2,10},{6,14},... | collective-permute-start | bytes 147464 | tf_op jit(solution)/shard_map/ppermute | solution.py:491
  85.9 1.8 %collective-permute-start.27 = (bf16[8,3072]{1,0:T(8,128)(2,1)S(1)}, bf16[8,3072]{1,0:T(8,128)(2,1)S(1)}, u32[]{:S(2)}, u32[]{:S(2)}) collective-permute-start(bf16[8,3072]{1,0:T(8,128)(2,1)S(1)} %get-tuple-element.54), channel_id=1, source_target_pairs={{0,12},{4,8},{8,4},{12,0},{1,13},{5,9},{9,5},{13,1},{2,14},{6,10},... | collective-permute-start | bytes 147464 | tf_op jit(solution)/shard_map/ppermute | solution.py:491
  87.8 1.1 %copy-done.2 = f32[32,6144]{1,0:T(8,128)S(1)} copy-done((f32[32,6144]{1,0:T(8,128)S(1)}, f32[32,6144]{1,0:T(8,128)}, u32[]{:S(2)}) %copy-start.2) | copy-done | bytes 786456
  88.9 1.1 %own_rows.1 = (f32[8,6144]{1,0:T(8,128)S(1)}, bf16[32,32]{1,0:T(8,128)(2,1)S(1)}) custom-call(s32[2,8]{1,0:T(2,128)} %bitcast.7, f32[2,8]{1,0:T(2,128)} %bitcast.8, bf16[8,6144]{1,0:T(8,128)(2,1)} %residual_ref.3, bf16[48,768]{1,0:T(8,128)(2,1)S(1)} %get-tuple-element.39.refs_0_, bf16[48,768]{1,0:T(8,128)(2,1)S(1)} %collective-permute-done.8.refs_1_, ...), custom_call_target="tpu_custom_call" | custom-call | flops 1000000 | bytes 1000000 | tf_op jit(solution)/shard_map/own_rows/pallas_call | solution.py:454
  90.0 0.0 collective-permute-done.25.refs_1_
  90.0 1.8 %collective-permute-done.27.refs_3_ = bf16[8,3072]{1,0:T(8,128)(2,1)S(1)} collective-permute-done((bf16[8,3072]{1,0:T(8,128)(2,1)S(1)}, bf16[8,3072]{1,0:T(8,128)(2,1)S(1)}, u32[]{:S(2)}, u32[]{:S(2)}) %collective-permute-start.27) | collective-permute-done | bytes 49184 | tf_op jit(solution)/shard_map/ppermute | solution.py:491
  91.8 0.8 finish.1
  (11 shorter events, 0.0 us)
Async XLA Ops:
  6.2 2.2 %copy-start = (bf16[384,6144]{1,0:T(8,128)(2,1)}, bf16[384,6144]{1,0:T(8,128)(2,1)S(1)}, u32[]{:S(2)}) copy-start(bf16[384,6144]{1,0:T(8,128)(2,1)S(1)} %get-tuple-element.44.refs_17_) | copy-start | bytes 14155780
  8.3 5.7 %collective-permute-start.1 = (bf16[16,2944]{1,0:T(8,128)(2,1)S(1)}, bf16[16,2944]{1,0:T(8,128)(2,1)S(1)}, u32[]{:S(2)}, u32[]{:S(2)}) collective-permute-start(bf16[16,2944]{1,0:T(8,128)(2,1)S(1)} %get-tuple-element.31), channel_id=1, source_target_pairs={{0,4},{4,0},{8,12},{12,8},{1,5},{5,1},{9,13},{13,9},{2,6},{6,2},{1... | collective-permute-start | bytes 282632 | tf_op jit(solution)/shard_map/ppermute | solution.py:491
  11.4 10.1 %collective-permute-start.3 = (bf16[16,2944]{1,0:T(8,128)(2,1)S(1)}, bf16[16,2944]{1,0:T(8,128)(2,1)S(1)}, u32[]{:S(2)}, u32[]{:S(2)}) collective-permute-start(bf16[16,2944]{1,0:T(8,128)(2,1)S(1)} %get-tuple-element.32), channel_id=1, source_target_pairs={{0,8},{4,12},{8,0},{12,4},{1,9},{5,13},{9,1},{13,5},{2,10},{6,14},... | collective-permute-start | bytes 282632 | tf_op jit(solution)/shard_map/ppermute | solution.py:491
  13.9 7.5 %collective-permute-start.5 = (bf16[16,2944]{1,0:T(8,128)(2,1)S(1)}, bf16[16,2944]{1,0:T(8,128)(2,1)S(1)}, u32[]{:S(2)}, u32[]{:S(2)}) collective-permute-start(bf16[16,2944]{1,0:T(8,128)(2,1)S(1)} %get-tuple-element.33), channel_id=1, source_target_pairs={{0,12},{4,8},{8,4},{12,0},{1,13},{5,9},{9,5},{13,1},{2,14},{6,10},... | collective-permute-start | bytes 282632 | tf_op jit(solution)/shard_map/ppermute | solution.py:491
  14.0 8.0 %collective-permute-start = (bf16[16,2944]{1,0:T(8,128)(2,1)S(1)}, bf16[16,2944]{1,0:T(8,128)(2,1)S(1)}, u32[]{:S(2)}, u32[]{:S(2)}) collective-permute-start(bf16[16,2944]{1,0:T(8,128)(2,1)S(1)} %get-tuple-element.30.refs_0_), channel_id=1, source_target_pairs={{0,2},{2,0},{1,3},{3,1},{4,6},{6,4},{5,7},{7,5},{8,10},{10,8},{9,1... | collective-permute-start | bytes 282632 | tf_op jit(solution)/shard_map/ppermute | solution.py:491
  14.1 7.9 %collective-permute-start.2 = (bf16[16,2944]{1,0:T(8,128)(2,1)S(1)}, bf16[16,2944]{1,0:T(8,128)(2,1)S(1)}, u32[]{:S(2)}, u32[]{:S(2)}) collective-permute-start(bf16[16,2944]{1,0:T(8,128)(2,1)S(1)} %collective-permute-done.1.refs_2_), channel_id=1, source_target_pairs={{0,2},{2,0},{1,3},{3,1},{4,6},{6,4},{5,7},{7,5},{8,10},{10,8},{9,1... | collective-permute-start | bytes 282632 | tf_op jit(solution)/shard_map/ppermute | solution.py:491
  21.5 1.3 %collective-permute-start.4 = (bf16[16,2944]{1,0:T(8,128)(2,1)S(1)}, bf16[16,2944]{1,0:T(8,128)(2,1)S(1)}, u32[]{:S(2)}, u32[]{:S(2)}) collective-permute-start(bf16[16,2944]{1,0:T(8,128)(2,1)S(1)} %collective-permute-done.3.refs_4_), channel_id=1, source_target_pairs={{0,2},{2,0},{1,3},{3,1},{4,6},{6,4},{5,7},{7,5},{8,10},{10,8},{9,1... | collective-permute-start | bytes 282632 | tf_op jit(solution)/shard_map/ppermute | solution.py:491
  21.5 1.4 %collective-permute-start.6 = (bf16[16,2944]{1,0:T(8,128)(2,1)S(1)}, bf16[16,2944]{1,0:T(8,128)(2,1)S(1)}, u32[]{:S(2)}, u32[]{:S(2)}) collective-permute-start(bf16[16,2944]{1,0:T(8,128)(2,1)S(1)} %collective-permute-done.5.refs_6_), channel_id=1, source_target_pairs={{0,2},{2,0},{1,3},{3,1},{4,6},{6,4},{5,7},{7,5},{8,10},{10,8},{9,1... | collective-permute-start | bytes 282632 | tf_op jit(solution)/shard_map/ppermute | solution.py:491
  23.6 5.1 %collective-permute-start.7 = (bf16[64,768]{1,0:T(8,128)(2,1)S(1)}, bf16[64,768]{1,0:T(8,128)(2,1)S(1)}, u32[]{:S(2)}, u32[]{:S(2)}) collective-permute-start(bf16[64,768]{1,0:T(8,128)(2,1)S(1)} %get-tuple-element.36), channel_id=1, source_target_pairs={{0,1},{1,0},{2,3},{3,2},{4,5},{5,4},{6,7},{7,6},{8,9},{9,8},{10,11... | collective-permute-start | bytes 294920 | tf_op jit(solution)/shard_map/ppermute | solution.py:491
  29.0 7.2 %collective-permute-start.9 = (bf16[48,768]{1,0:T(8,128)(2,1)S(1)}, bf16[48,768]{1,0:T(8,128)(2,1)S(1)}, u32[]{:S(2)}, u32[]{:S(2)}) collective-permute-start(bf16[48,768]{1,0:T(8,128)(2,1)S(1)} %get-tuple-element.40), channel_id=1, source_target_pairs={{0,4},{4,0},{8,12},{12,8},{1,5},{5,1},{9,13},{13,9},{2,6},{6,2},{1... | collective-permute-start | bytes 221192 | tf_op jit(solution)/shard_map/ppermute | solution.py:491
  30.2 7.5 %collective-permute-start.11 = (bf16[48,768]{1,0:T(8,128)(2,1)S(1)}, bf16[48,768]{1,0:T(8,128)(2,1)S(1)}, u32[]{:S(2)}, u32[]{:S(2)}) collective-permute-start(bf16[48,768]{1,0:T(8,128)(2,1)S(1)} %get-tuple-element.41), channel_id=1, source_target_pairs={{0,8},{4,12},{8,0},{12,4},{1,9},{5,13},{9,1},{13,5},{2,10},{6,14},... | collective-permute-start | bytes 221192 | tf_op jit(solution)/shard_map/ppermute | solution.py:491
  32.1 4.1 %collective-permute-start.15 = (bf16[32,768]{1,0:T(8,128)(2,1)S(1)}, bf16[32,768]{1,0:T(8,128)(2,1)S(1)}, u32[]{:S(2)}, u32[]{:S(2)}) collective-permute-start(bf16[32,768]{1,0:T(8,128)(2,1)S(1)} %slice.12), channel_id=1, source_target_pairs={{0,1},{1,0},{2,3},{3,2},{4,5},{5,4},{6,7},{7,6},{8,9},{9,8},{10,11... | collective-permute-start | bytes 147464 | tf_op jit(solution)/shard_map/ppermute | solution.py:491
  33.6 6.2 %collective-permute-start.13 = (bf16[48,768]{1,0:T(8,128)(2,1)S(1)}, bf16[48,768]{1,0:T(8,128)(2,1)S(1)}, u32[]{:S(2)}, u32[]{:S(2)}) collective-permute-start(bf16[48,768]{1,0:T(8,128)(2,1)S(1)} %get-tuple-element.42), channel_id=1, source_target_pairs={{0,12},{4,8},{8,4},{12,0},{1,13},{5,9},{9,5},{13,1},{2,14},{6,10},... | collective-permute-start | bytes 221192 | tf_op jit(solution)/shard_map/ppermute | solution.py:491
  34.9 5.4 %collective-permute-start.8 = (bf16[48,768]{1,0:T(8,128)(2,1)S(1)}, bf16[48,768]{1,0:T(8,128)(2,1)S(1)}, u32[]{:S(2)}, u32[]{:S(2)}) collective-permute-start(bf16[48,768]{1,0:T(8,128)(2,1)S(1)} %get-tuple-element.39.refs_0_), channel_id=1, source_target_pairs={{0,2},{2,0},{1,3},{3,1},{4,6},{6,4},{5,7},{7,5},{8,10},{10,8},{9,1... | collective-permute-start | bytes 221192 | tf_op jit(solution)/shard_map/ppermute | solution.py:491
  36.2 5.7 %collective-permute-start.16 = (bf16[32,768]{1,0:T(8,128)(2,1)S(1)}, bf16[32,768]{1,0:T(8,128)(2,1)S(1)}, u32[]{:S(2)}, u32[]{:S(2)}) collective-permute-start(bf16[32,768]{1,0:T(8,128)(2,1)S(1)} %collective-permute-done.15.refs_8_), channel_id=1, source_target_pairs={{0,2},{2,0},{1,3},{3,1},{4,6},{6,4},{5,7},{7,5},{8,10},{10,8},{9,1... | collective-permute-start | bytes 147464 | tf_op jit(solution)/shard_map/ppermute | solution.py:491
  36.2 5.6 %collective-permute-start.17 = (bf16[32,768]{1,0:T(8,128)(2,1)S(1)}, bf16[32,768]{1,0:T(8,128)(2,1)S(1)}, u32[]{:S(2)}, u32[]{:S(2)}) collective-permute-start(bf16[32,768]{1,0:T(8,128)(2,1)S(1)} %slice.16), channel_id=1, source_target_pairs={{0,1},{1,0},{2,3},{3,2},{4,5},{5,4},{6,7},{7,6},{8,9},{9,8},{10,11... | collective-permute-start | bytes 147464 | tf_op jit(solution)/shard_map/ppermute | solution.py:491
  37.8 6.8 %collective-permute-start.10 = (bf16[48,768]{1,0:T(8,128)(2,1)S(1)}, bf16[48,768]{1,0:T(8,128)(2,1)S(1)}, u32[]{:S(2)}, u32[]{:S(2)}) collective-permute-start(bf16[48,768]{1,0:T(8,128)(2,1)S(1)} %collective-permute-done.9.refs_2_), channel_id=1, source_target_pairs={{0,2},{2,0},{1,3},{3,1},{4,6},{6,4},{5,7},{7,5},{8,10},{10,8},{9,1... | collective-permute-start | bytes 221192 | tf_op jit(solution)/shard_map/ppermute | solution.py:491
  39.7 4.1 %collective-permute-start.19 = (bf16[32,768]{1,0:T(8,128)(2,1)S(1)}, bf16[32,768]{1,0:T(8,128)(2,1)S(1)}, u32[]{:S(2)}, u32[]{:S(2)}) collective-permute-start(bf16[32,768]{1,0:T(8,128)(2,1)S(1)} %slice.17), channel_id=1, source_target_pairs={{0,1},{1,0},{2,3},{3,2},{4,5},{5,4},{6,7},{7,6},{8,9},{9,8},{10,11... | collective-permute-start | bytes 147464 | tf_op jit(solution)/shard_map/ppermute | solution.py:491
  40.4 4.2 %collective-permute-start.21 = (bf16[32,768]{1,0:T(8,128)(2,1)S(1)}, bf16[32,768]{1,0:T(8,128)(2,1)S(1)}, u32[]{:S(2)}, u32[]{:S(2)}) collective-permute-start(bf16[32,768]{1,0:T(8,128)(2,1)S(1)} %slice.18), channel_id=1, source_target_pairs={{0,1},{1,0},{2,3},{3,2},{4,5},{5,4},{6,7},{7,6},{8,9},{9,8},{10,11... | collective-permute-start | bytes 147464 | tf_op jit(solution)/shard_map/ppermute | solution.py:491
  41.8 3.2 %collective-permute-start.12 = (bf16[48,768]{1,0:T(8,128)(2,1)S(1)}, bf16[48,768]{1,0:T(8,128)(2,1)S(1)}, u32[]{:S(2)}, u32[]{:S(2)}) collective-permute-start(bf16[48,768]{1,0:T(8,128)(2,1)S(1)} %collective-permute-done.11.refs_4_), channel_id=1, source_target_pairs={{0,2},{2,0},{1,3},{3,1},{4,6},{6,4},{5,7},{7,5},{8,10},{10,8},{9,1... | collective-permute-start | bytes 221192 | tf_op jit(solution)/shard_map/ppermute | solution.py:491
  41.8 3.2 %collective-permute-start.14 = (bf16[48,768]{1,0:T(8,128)(2,1)S(1)}, bf16[48,768]{1,0:T(8,128)(2,1)S(1)}, u32[]{:S(2)}, u32[]{:S(2)}) collective-permute-start(bf16[48,768]{1,0:T(8,128)(2,1)S(1)} %collective-permute-done.13.refs_6_), channel_id=1, source_target_pairs={{0,2},{2,0},{1,3},{3,1},{4,6},{6,4},{5,7},{7,5},{8,10},{10,8},{9,1... | collective-permute-start | bytes 221192 | tf_op jit(solution)/shard_map/ppermute | solution.py:491
  43.8 1.2 %collective-permute-start.18 = (bf16[32,768]{1,0:T(8,128)(2,1)S(1)}, bf16[32,768]{1,0:T(8,128)(2,1)S(1)}, u32[]{:S(2)}, u32[]{:S(2)}) collective-permute-start(bf16[32,768]{1,0:T(8,128)(2,1)S(1)} %collective-permute-done.17.refs_10_), channel_id=1, source_target_pairs={{0,2},{2,0},{1,3},{3,1},{4,6},{6,4},{5,7},{7,5},{8,10},{10,8},{9,1... | collective-permute-start | bytes 147464 | tf_op jit(solution)/shard_map/ppermute | solution.py:491
  44.5 1.2 %collective-permute-start.20 = (bf16[32,768]{1,0:T(8,128)(2,1)S(1)}, bf16[32,768]{1,0:T(8,128)(2,1)S(1)}, u32[]{:S(2)}, u32[]{:S(2)}) collective-permute-start(bf16[32,768]{1,0:T(8,128)(2,1)S(1)} %collective-permute-done.19.refs_12_), channel_id=1, source_target_pairs={{0,2},{2,0},{1,3},{3,1},{4,6},{6,4},{5,7},{7,5},{8,10},{10,8},{9,1... | collective-permute-start | bytes 147464 | tf_op jit(solution)/shard_map/ppermute | solution.py:491
  44.5 1.4 %collective-permute-start.22 = (bf16[32,768]{1,0:T(8,128)(2,1)S(1)}, bf16[32,768]{1,0:T(8,128)(2,1)S(1)}, u32[]{:S(2)}, u32[]{:S(2)}) collective-permute-start(bf16[32,768]{1,0:T(8,128)(2,1)S(1)} %collective-permute-done.21.refs_14_), channel_id=1, source_target_pairs={{0,2},{2,0},{1,3},{3,1},{4,6},{6,4},{5,7},{7,5},{8,10},{10,8},{9,1... | collective-permute-start | bytes 147464 | tf_op jit(solution)/shard_map/ppermute | solution.py:491
  73.0 1.8 %collective-permute-start.23 = (bf16[32,6144]{1,0:T(8,128)(2,1)S(1)}, bf16[32,6144]{1,0:T(8,128)(2,1)S(1)}, u32[]{:S(2)}, u32[]{:S(2)}) collective-permute-start(bf16[32,6144]{1,0:T(8,128)(2,1)S(1)} %get-tuple-element.48), channel_id=1, source_target_pairs={{0,2},{2,0},{1,3},{3,1},{4,6},{6,4},{5,7},{7,5},{8,10},{10,8},{9,1... | collective-permute-start | bytes 1179656 | tf_op jit(solution)/shard_map/ppermute | solution.py:491
  74.8 1.1 %copy-start.1 = (f32[32,6144]{1,0:T(8,128)S(1)}, f32[32,6144]{1,0:T(8,128)}, u32[]{:S(2)}) copy-start(f32[32,6144]{1,0:T(8,128)} %get-tuple-element.45.refs_8_.mine_ref) | copy-start | bytes 2359300
  76.0 7.2 %collective-permute-start.24 = (bf16[16,6144]{1,0:T(8,128)(2,1)S(1)}, bf16[16,6144]{1,0:T(8,128)(2,1)S(1)}, u32[]{:S(2)}, u32[]{:S(2)}) collective-permute-start(bf16[16,6144]{1,0:T(8,128)(2,1)S(1)} %get-tuple-element.50), channel_id=1, source_target_pairs={{0,1},{1,0},{2,3},{3,2},{4,5},{5,4},{6,7},{7,6},{8,9},{9,8},{10,11... | collective-permute-start | bytes 589832 | tf_op jit(solution)/shard_map/ppermute | solution.py:491
  83.3 6.7 %collective-permute-start.25 = (bf16[8,3072]{1,0:T(8,128)(2,1)S(1)}, bf16[8,3072]{1,0:T(8,128)(2,1)S(1)}, u32[]{:S(2)}, u32[]{:S(2)}) collective-permute-start(bf16[8,3072]{1,0:T(8,128)(2,1)S(1)} %get-tuple-element.52), channel_id=1, source_target_pairs={{0,4},{4,0},{8,12},{12,8},{1,5},{5,1},{9,13},{13,9},{2,6},{6,2},{1... | collective-permute-start | bytes 147464 | tf_op jit(solution)/shard_map/ppermute | solution.py:491
  84.2 5.8 %collective-permute-start.26 = (bf16[8,3072]{1,0:T(8,128)(2,1)S(1)}, bf16[8,3072]{1,0:T(8,128)(2,1)S(1)}, u32[]{:S(2)}, u32[]{:S(2)}) collective-permute-start(bf16[8,3072]{1,0:T(8,128)(2,1)S(1)} %get-tuple-element.53), channel_id=1, source_target_pairs={{0,8},{4,12},{8,0},{12,4},{1,9},{5,13},{9,1},{13,5},{2,10},{6,14},... | collective-permute-start | bytes 147464 | tf_op jit(solution)/shard_map/ppermute | solution.py:491
  85.9 5.9 %collective-permute-start.27 = (bf16[8,3072]{1,0:T(8,128)(2,1)S(1)}, bf16[8,3072]{1,0:T(8,128)(2,1)S(1)}, u32[]{:S(2)}, u32[]{:S(2)}) collective-permute-start(bf16[8,3072]{1,0:T(8,128)(2,1)S(1)} %get-tuple-element.54), channel_id=1, source_target_pairs={{0,12},{4,8},{8,4},{12,0},{1,13},{5,9},{9,5},{13,1},{2,14},{6,10},... | collective-permute-start | bytes 147464 | tf_op jit(solution)/shard_map/ppermute | solution.py:491
  87.8 1.1 %copy-start.2 = (f32[32,6144]{1,0:T(8,128)S(1)}, f32[32,6144]{1,0:T(8,128)}, u32[]{:S(2)}) copy-start(f32[32,6144]{1,0:T(8,128)} %get-tuple-element.45.refs_8_.mine_ref) | copy-start | bytes 2359300

commit v4 on v3

--- a/solution.py
+++ b/solution.py
@@ -41,23 +41,20 @@
 
 
 def attend_kernel(positions, steps, decay_ref, ids_ref, q_ref, k_ref, v_ref, gain_ref, s_ref, residual_ref, *refs):
-    weight_hbm, norm_hbm, gate_hbm = refs[:3]
-    outs, copies_out, sem = refs[3:-4], refs[-4:-1], refs[-1]
+    sources, outs, targets, sem = refs[:2], refs[2:-3], refs[-3:-1], refs[-1]
     requests, heads, size, _ = s_ref.shape
     rows = q_ref.shape[0]
     step = pl.program_id(0)
     first = step * heads
     copies = [
         pltpu.make_async_copy(source, target, sem.at[i])
-        for i, (source, target) in enumerate(
-            zip((weight_hbm, norm_hbm, gate_hbm.at[: copies_out[2].shape[0]]), copies_out)
-        )
+        for i, (source, target) in enumerate(zip(sources, targets))
     ]
 
     @pl.when(step == 0)
     def _():
-        copies[0].start()
-        copies[1].start()
+        for copy in copies:
+            copy.start()
         width = steps * heads * size
         lanes = ID_LANES
         row = lax.broadcasted_iota(jnp.int32, (rows, lanes), 0)
@@ -78,10 +75,6 @@
             ]
             both = jnp.concatenate([b.astype(F32) for b in both], axis=0)
             out[:, width + lanes :] = both.astype(BF16)
-
-    @pl.when(step == min(1, steps - 1))
-    def _():
-        copies[2].start()
 
     row = lax.broadcasted_iota(jnp.int32, (rows, rows), 0)
     col = lax.broadcasted_iota(jnp.int32, (rows, rows), 1)
@@ -116,14 +109,13 @@
 
 
 def attend(
-    queries, key_rows, value_rows, states, decay_rates, head_gain, ids, residual, weight, norm_gain, gate, block, experts
+    queries, key_rows, value_rows, states, decay_rates, head_gain, ids, residual, weight, norm_gain, experts
 ):
     requests, heads, size, _ = states.shape
     rows = queries.shape[0]
     step = 4 if heads % 4 == 0 else 1
     wide = pl.BlockSpec((rows, step * size), lambda i: (0, i))
     message = (rows, queries.shape[1] + ID_LANES + weight.shape[1])
-    kept = [(weight.shape, weight.dtype), (norm_gain.shape, F32), ((block, gate.shape[1]), gate.dtype)]
     return pl.pallas_call(
         functools.partial(attend_kernel, rows // requests, heads // step),
         grid=(heads // step,),
@@ -138,20 +130,48 @@
             pl.BlockSpec(residual.shape, lambda i: (0, 0)),
             ANY,
             ANY,
-            ANY,
         ],
-        out_specs=[pl.BlockSpec(message, lambda i: (0, 0))] * experts + [VMEM] * 3,
+        out_specs=[pl.BlockSpec(message, lambda i: (0, 0))] * experts + [VMEM] * 2,
         out_shape=[jax.ShapeDtypeStruct(message, BF16)] * experts
-        + [pltpu.VMEM(shape, dtype) for shape, dtype in kept],
-        scratch_shapes=[pltpu.SemaphoreType.DMA((3,))],
+        + [pltpu.VMEM(a.shape, a.dtype) for a in (weight, norm_gain)],
+        scratch_shapes=[pltpu.SemaphoreType.DMA((2,))],
         compiler_params=limits(8),
         name="attention",
     )(
         *in_hbm(
             decay_rates, ids, queries, key_rows, value_rows, head_gain.reshape(1, -1), states, residual,
-            weight, norm_gain, gate,
+            weight, norm_gain,
         )
     )
+
+
+def load_kernel(rows_hbm, weight_hbm, rows_ref, weight_ref, sem):
+    copies = [
+        pltpu.make_async_copy(weight_hbm, weight_ref, sem.at[0]),
+        pltpu.make_async_copy(rows_hbm, rows_ref, sem.at[1]),
+    ]
+    for copy in copies:
+        copy.start()
+    for copy in copies:
+        copy.wait()
+
+
+def load(rows, weight):
+    return pl.pallas_call(
+        load_kernel,
+        in_specs=[ANY, ANY],
+        out_specs=[VMEM, VMEM],
+        out_shape=[
+            jax.ShapeDtypeStruct(rows.shape, rows.dtype),
+            pltpu.VMEM(weight.shape, weight.dtype),
+        ],
+        scratch_shapes=[pltpu.SemaphoreType.DMA((2,))],
+        compiler_params=limits(1),
+        cost_estimate=pl.CostEstimate(
+            flops=0, bytes_accessed=weight.size * weight.dtype.itemsize, transcendentals=0
+        ),
+        name="load",
+    )(rows, *in_hbm(weight))
 
 
 def project_kernel(*refs):
@@ -193,7 +213,10 @@
 
 
 def route_kernel(capacity, top, *refs):
-    pieces, choose_ref, residual_ref, ids_ref = refs[:-4], *refs[-3:]
+    pieces, weight_hbm = refs[:-7], refs[-6]
+    choose_ref, residual_ref, weight_ref, ids_ref, sem = refs[-5:]
+    copy = pltpu.make_async_copy(weight_hbm.at[: weight_ref.shape[0]], weight_ref, sem)
+    copy.start()
     columns = residual_ref.shape[1]
     own = pieces[0].shape[0] // 2
     rows = ids_ref.shape[0]
@@ -225,38 +248,40 @@
         choose_ref[d * count : (d + 1) * count] = jnp.where(
             slot == place[d : d + 1], 1.0, 0.0
         ).astype(BF16)
-
-
-def route(pieces, after, columns, capacity, top):
+    copy.wait()
+
+
+def route(pieces, after, columns, capacity, top, weight, first):
     rows = pieces[0].shape[0] // 2 * len(pieces)
     experts = len(pieces) // 2
     return pl.pallas_call(
         functools.partial(route_kernel, capacity, top),
-        in_specs=[VMEM] * len(pieces) + [ANY],
-        out_specs=[VMEM] * 2,
+        in_specs=[VMEM] * len(pieces) + [ANY] * 2,
+        out_specs=[VMEM] * 3,
         out_shape=[
             jax.ShapeDtypeStruct((experts * 2 * experts * capacity, rows), BF16),
             jax.ShapeDtypeStruct((rows, columns), F32),
+            pltpu.VMEM((first, weight.shape[1]), weight.dtype),
         ],
-        scratch_shapes=[pltpu.VMEM((rows, ID_LANES), F32)],
+        scratch_shapes=[pltpu.VMEM((rows, ID_LANES), F32), pltpu.SemaphoreType.DMA],
         compiler_params=limits(4),
-        cost_estimate=pl.CostEstimate(flops=10**6, bytes_accessed=10**6, transcendentals=0),
+        cost_estimate=pl.CostEstimate(flops=10**6, bytes_accessed=8 * 10**6, transcendentals=0),
         name="route",
-    )(*pieces, after)
+    )(*pieces, after, *in_hbm(weight))
 
 
 def pack_kernel(keep_ref, got_ref, residual_ref, choose_ref, *refs):
-    outs, sum_ref = refs[:-1], refs[-1]
+    outs, own_ref, sum_ref = refs[:-2], refs[-2], refs[-1]
     sum_ref[...] = keep_ref[...] + got_ref[...].astype(F32)
     combined = (sum_ref[...] + residual_ref[...]).astype(BF16)
     packed = dot(choose_ref[...], combined).astype(BF16)
     count = choose_ref.shape[0] // len(outs)
-    own = outs[0].shape[0] - count
+    own = own_ref.shape[1]
     expert = lax.axis_index("expert")
     for d, out in enumerate(outs):
-        out[:count] = packed[d * count : (d + 1) * count]
+        out[...] = packed[d * count : (d + 1) * count]
         at = pl.ds(pl.multiple_of((expert ^ d) * own, own), own)
-        out[count:] = sum_ref[at].astype(BF16)
+        own_ref[d] = sum_ref[at].astype(BF16)
 
 
 def pack(keep, got, residual, choose, experts):
@@ -265,70 +290,69 @@
     return pl.pallas_call(
         pack_kernel,
         in_specs=[VMEM] * 4,
-        out_specs=[VMEM] * experts,
-        out_shape=[jax.ShapeDtypeStruct((count + rows // experts, columns), BF16)] * experts,
+        out_specs=[VMEM] * (experts + 1),
+        out_shape=[jax.ShapeDtypeStruct((count, columns), BF16)] * experts
+        + [jax.ShapeDtypeStruct((experts, rows // experts, columns), BF16)],
         scratch_shapes=[pltpu.VMEM((rows, columns), F32)],
         compiler_params=limits(4),
         name="pack",
     )(keep, got, residual, choose)
 
 
-def expert_kernel(count, block, wide, *refs):
-    near, far = refs[:8], refs[8:16]
-    gain_ref, first_ref, gate_hbm, up_hbm, down_hbm = refs[16:21]
-    keep_ref, send_ref = refs[21:23]
-    x_ref, turned_ref, hidden_ref, gate_ref, up_ref, down_ref, gate_sem, up_sem, down_sem = refs[23:]
+def expert_kernel(count, wide, each, *refs):
+    groups = 16 // each // 4
+    near, near_cross, far, far_cross = (refs[g * groups : (g + 1) * groups] for g in range(4))
+    refs = refs[4 * groups :]
+    gain_ref, gate_ref, first_ref, up_hbm, down_hbm = refs[:5]
+    keep_ref, send_ref, x_ref, turned_ref, hidden_ref, rest_ref, down_ref, sem, down_sem = refs[5:]
     units, width = up_hbm.shape
-    columns = width // len(near)
+    columns = width // 8
     rows = x_ref.shape[0]
-    blocks, panels = units // block, width // wide
-
-    def copy_of(hbm, ref, sem, t):
-        at = pl.ds(t * block, block)
-        return pltpu.make_async_copy(hbm.at[at], ref.at[at], sem.at[t])
-
-    def down_copy(n):
-        at = pl.ds(n * wide, wide)
-        return pltpu.make_async_copy(down_hbm.at[:, at], down_ref.at[:, at], down_sem.at[n])
-
-    for t in range(blocks):
-        if t:
-            copy_of(gate_hbm, gate_ref, gate_sem, t).start()
-        copy_of(up_hbm, up_ref, up_sem, t).start()
-    for n in range(panels):
-        down_copy(n).start()
+    cut = first_ref.shape[0]
+    rest = pltpu.make_async_copy(up_hbm.at[cut:], rest_ref, sem)
+    rest.start()
+    thirds = down_sem.shape[0]
+    tall = units // thirds
+    downs = [
+        pltpu.make_async_copy(
+            down_hbm.at[t * tall : (t + 1) * tall], down_ref.at[t * tall : (t + 1) * tall], down_sem.at[t]
+        )
+        for t in range(thirds)
+    ]
 
     expert, half = lax.axis_index("expert"), lax.axis_index("half")
-    for p, pieces in enumerate((near, far)):
-        for j, piece in enumerate(pieces):
-            base = ((expert ^ (j // 2)) * 2 + (half ^ (j % 2))) * columns
-            at = pl.ds(pl.multiple_of(base, columns), columns)
-            x_ref[p * count : (p + 1) * count, at] = piece[:count].astype(F32)
+    for p, halves in enumerate(((near, near_cross), (far, far_cross))):
+        for c, pieces in enumerate(halves):
+            for d in range(4):
+                piece = pieces[d // each][d % each * count : (d % each + 1) * count]
+                base = ((expert ^ d) * 2 + (half ^ c)) * columns
+                at = pl.ds(pl.multiple_of(base, columns), columns)
+                x_ref[p * count : (p + 1) * count, at] = piece.astype(F32)
     squares = jnp.zeros((rows, 128), F32)
     for b in range(width // 128):
         x = x_ref[:, b * 128 : (b + 1) * 128]
         squares = squares + x * x
     scale = lax.rsqrt(jnp.sum(squares, axis=1, keepdims=True) / width + EPSILON)
-    for b in range(len(near)):
+    for b in range(8):
         at = slice(b * columns, (b + 1) * columns)
         normed = x_ref[:, at] * scale * gain_ref[:, at]
         turned_ref[at] = normed.T.astype(BF16)
-
-    for t in range(blocks):
-        at = slice(t * block, (t + 1) * block)
-        if t:
-            copy_of(gate_hbm, gate_ref, gate_sem, t).wait()
-            gate_value = dot(gate_ref[at], turned_ref[...])
-        else:
-            gate_value = dot(first_ref[...], turned_ref[...])
-        copy_of(up_hbm, up_ref, up_sem, t).wait()
-        lifted = dot(up_ref[at], turned_ref[...])
+    downs[0].start()
+
+    for at, up_ref in ((slice(0, cut), first_ref), (slice(cut, units), rest_ref)):
+        gate_value = dot(gate_ref[at], turned_ref[...])
+        if up_ref is rest_ref:
+            rest.wait()
+            for down in downs[1:]:
+                down.start()
+        lifted = dot(up_ref[...], turned_ref[...])
         hidden = gate_value / (1.0 + jnp.exp(-gate_value)) * lifted
         hidden_ref[:, at] = hidden.T.astype(BF16)
 
     part = count // 2
-    for n in range(panels):
-        down_copy(n).wait()
+    for down in downs:
+        down.wait()
+    for n in range(width // wide):
         at = slice(n * wide, (n + 1) * wide)
         total = dot(hidden_ref[...], down_ref[:, at])
         for p in range(2):
@@ -339,13 +363,13 @@
             send_ref[to, at] = jnp.where(half == 0, high, low).astype(BF16)
 
 
-def expert_apply(near, far, gain, first, gate_part, up_part, down_part, count):
-    units, width = gate_part.shape
-    block = first.shape[0]
+def expert_apply(pieces, gain, gate, first, up_part, down_part, count):
+    units, width = up_part.shape
     wide = 512
-    return pl.pallas_call(
-        functools.partial(expert_kernel, count, block, wide),
-        in_specs=[VMEM] * 18 + [ANY] * 3,
+    each = pieces[0].shape[0] // count
+    return pl.pallas_call(
+        functools.partial(expert_kernel, count, wide, each),
+        in_specs=[VMEM] * (len(pieces) + 3) + [ANY] * 2,
         out_specs=(VMEM, VMEM),
         out_shape=(
             jax.ShapeDtypeStruct((count, width), F32),
@@ -355,37 +379,38 @@
             pltpu.VMEM((2 * count, width), F32),
             pltpu.VMEM((width, 2 * count), BF16),
             pltpu.VMEM((2 * count, units), BF16),
+            pltpu.VMEM((units - first.shape[0], width), BF16),
             pltpu.VMEM((units, width), BF16),
-            pltpu.VMEM((units, width), BF16),
-            pltpu.VMEM((units, width), BF16),
-            pltpu.SemaphoreType.DMA((units // block,)),
-            pltpu.SemaphoreType.DMA((units // block,)),
-            pltpu.SemaphoreType.DMA((width // wide,)),
+            pltpu.SemaphoreType.DMA,
+            pltpu.SemaphoreType.DMA((3,)),
         ],
-        compiler_params=limits(52),
+        compiler_params=limits(30),
         name="experts",
-    )(*near, *far, gain, first, *in_hbm(gate_part, up_part, down_part))
-
-
-def chip_sum_kernel(mine_ref, got_ref, keep_ref, send_ref):
+    )(*pieces, gain, gate, first, *in_hbm(up_part, down_part))
+
+
+def chip_sum_kernel(mine_ref, got_ref, own_ref, keep_ref, send_ref, *outs):
     rows = keep_ref.shape[0]
     keep_ref[...] = mine_ref[:rows] + got_ref[:rows].astype(F32)
     send_ref[...] = (mine_ref[rows:] + got_ref[rows:].astype(F32)).astype(BF16)
-
-
-def chip_sum(mine, got):
+    for d, out in enumerate(outs):
+        out[...] = own_ref[d]
+
+
+def chip_sum(mine, got, own):
     rows, width = mine.shape
     return pl.pallas_call(
         chip_sum_kernel,
-        in_specs=[VMEM] * 2,
-        out_specs=[VMEM] * 2,
+        in_specs=[VMEM] * 3,
+        out_specs=[VMEM] * (2 + own.shape[0]),
         out_shape=[
             jax.ShapeDtypeStruct((rows // 2, width), F32),
             jax.ShapeDtypeStruct((rows // 2, width), BF16),
-        ],
+        ]
+        + [jax.ShapeDtypeStruct(own.shape[1:], BF16)] * own.shape[0],
         compiler_params=limits(4),
         name="chip_sum",
-    )(mine, got)
+    )(mine, got, own)
 
 
 def pair_sum_kernel(capacity, keep_ref, got_ref, *refs):
@@ -417,17 +442,19 @@
     )(keep, got)
 
 
-def own_rows_kernel(capacity, count, ids_ref, weights_ref, residual_ref, *refs):
-    pieces, combined_ref, weighting_ref = refs[:-3], *refs[-2:]
+def own_rows_kernel(capacity, ids_ref, weights_ref, residual_ref, *refs):
+    pieces, cross_ref, combined_ref, weighting_ref = refs[:-3], *refs[-3:]
     rows = combined_ref.shape[0]
     columns = pieces[0].shape[1]
     expert, half = lax.axis_index("expert"), lax.axis_index("half")
-    for j, piece in enumerate(pieces):
-        base = ((expert ^ (j // 2)) * 2 + (half ^ (j % 2))) * columns
-        at = pl.ds(pl.multiple_of(base, columns), columns)
-        both = piece[count:].astype(F32)
-        mine = jnp.where(half == 0, both[:rows], both[rows:])
-        combined_ref[:, at] = residual_ref[:, at].astype(F32) + mine
+    for d, piece in enumerate(pieces):
+        cross = cross_ref[d * 2 * rows : (d + 1) * 2 * rows]
+        for c, both in enumerate((piece[...], cross)):
+            base = ((expert ^ d) * 2 + (half ^ c)) * columns
+            at = pl.ds(pl.multiple_of(base, columns), columns)
+            both = both.astype(F32)
+            mine = jnp.where(half == 0, both[:rows], both[rows:])
+            combined_ref[:, at] = residual_ref[:, at].astype(F32) + mine
     places = weighting_ref.shape[1]
     row = lax.broadcasted_iota(jnp.int32, (rows, places), 0)
     place = lax.broadcasted_iota(jnp.int32, (rows, places), 1)
@@ -448,12 +475,12 @@
         weighting_ref[h * 16 : (h + 1) * 16] = both.astype(BF16)
 
 
-def own_rows(ids, weights, residual, pieces, after, capacity, count):
+def own_rows(ids, weights, residual, pieces, cross, capacity):
     rows, width = residual.shape
-    experts = len(pieces) // 2
-    return pl.pallas_call(
-        functools.partial(own_rows_kernel, capacity, count),
-        in_specs=[SMEM, SMEM, VMEM] + [VMEM] * len(pieces) + [ANY],
+    experts = len(pieces)
+    return pl.pallas_call(
+        functools.partial(own_rows_kernel, capacity),
+        in_specs=[SMEM, SMEM, VMEM] + [VMEM] * (experts + 1),
         out_specs=[VMEM] * 2,
         out_shape=[
             jax.ShapeDtypeStruct((rows, width), F32),
@@ -462,7 +489,7 @@
         compiler_params=limits(4),
         cost_estimate=pl.CostEstimate(flops=10**6, bytes_accessed=10**6, transcendentals=0),
         name="own_rows",
-    )(*in_hbm(ids, weights, residual), *pieces, after)
+    )(*in_hbm(ids, weights, residual), *pieces, cross)
 
 
 def finish_kernel(combined_ref, weighting_ref, *refs):
@@ -513,35 +540,39 @@
     top = expert_ids.shape[1]
     capacity = max(2, local_rows * top // experts)
     count = 2 * experts * capacity
-    block = next(b for b in (384, 256, 128) if expert_gate.shape[0] % b == 0)
     ids, weights = expert_ids.T, gate_weights.T
 
-    *messages, weight_here, gain_here, gate_first = attend(
+    *messages, weight_here, gain_here = attend(
         queries, key_rows, value_rows, states, decay_rates, head_gain, ids, residual,
-        out_weight, norm_gain.reshape(1, -1), expert_gate, block, experts,
-    )
+        out_weight, norm_gain.reshape(1, -1), experts,
+    )
+    messages[0], gate_here = load(messages[0], expert_gate)
     pieces = []
     for d, message in enumerate(messages):
         message = swap(message, "expert", d)
         pieces += [message, swap(message, "half", 1)]
 
     keep, send = project(pieces, weight_here)
-    choose, residual_part = route(pieces, keep, columns, capacity, top)
-    packed = pack(keep, swap(send, "pair", 1), residual_part, choose, experts)
-
-    near, far = [], []
-    for d, rows in enumerate(packed):
-        rows = swap(rows, "expert", d)
-        crossed = swap(rows[:count], "pair", 1)
-        near += [rows, swap(rows, "half", 1)]
-        far += [crossed, swap(crossed, "half", 1)]
+    first = expert_up.shape[0] // 256 * 128 + 128
+    choose, residual_part, up_first = route(
+        pieces, keep, columns, capacity, top, expert_up, first
+    )
+    *packed, own = pack(keep, swap(send, "pair", 1), residual_part, choose, experts)
+
+    order = [2, 3, 1, 0]
+    arrived = {d: swap(packed[d], "expert", d) for d in order}
+    near = [jnp.concatenate([arrived[d], arrived[d + 1]], axis=0) for d in range(0, experts, 2)]
+    far = [swap(rows, "pair", 1) for rows in near]
+    routed = near + [swap(n, "half", 1) for n in near] + far + [swap(f, "half", 1) for f in far]
     mine, send = expert_apply(
-        near, far, gain_here, gate_first, expert_gate, expert_up, expert_down, count
-    )
-
-    combined, weighting = own_rows(ids, weights, residual, near, mine, capacity, count)
-    keep, send = chip_sum(mine, swap(send, "half", 1))
+        routed, gain_here, gate_here, up_first, expert_up, expert_down, count
+    )
+
+    keep, send, *own = chip_sum(mine, swap(send, "half", 1), own)
     terms = pair_sum(keep, swap(send, "pair", 1), capacity, experts)
+    own = [swap(rows, "expert", d) for d, rows in enumerate(own)]
+    cross = swap(jnp.concatenate(own, axis=0), "half", 1)
+    combined, weighting = own_rows(ids, weights, residual, own, cross, capacity)
     back = [swap(term, "expert", d) for d, term in enumerate(terms)]
     return finish(combined, weighting, back)
 
@@ -703,13 +734,13 @@
         return dict(in_specs=arguments, out_specs=tokens, check_vma=False)
 
     experts = sizes["dev"] // 2
-    chips = sizes["pair"] == 2 and sizes["sub"] == 1 and experts in (2, 4, 8)
+    chips = sizes["pair"] == 2 and sizes["sub"] == 1 and experts == 4
 
     def run(*arguments):
         rows = arguments[7].shape[0] // mesh.size
         columns = arguments[6].shape[1] // (sizes["dev"] * sizes["sub"])
         units = arguments[11].shape[0] * sizes["grp"] // mesh.size
-        if chips and rows == 8 and columns % 128 == 0 and units % 128 == 0:
+        if chips and rows == 8 and columns % 128 == 0 and units % 384 == 0:
             cut = Mesh(
                 mesh.devices.reshape(sizes["grp"], experts, 2, 2),
                 ("grp", "expert", "half", "pair"),

time: 92.9 us -> 77.3 us (0.83)
  Pallas kernels: 36.5 us -> 30.7 us
  waiting for transfers between devices: 26.4 us -> 20.6 us
  local copies, waits for them, and re-layouts: 4.43 us -> 0.02 us
    pallas_call x4 -> x5, Pallas kernels: 28.4 us -> 20.8 us  [the longest x1 14.3 us: expert_apply(): pl.pallas_call(functools.partial(expert_kernel, count, wide, each), in_sp...]
    ppermute x28 -> x26, waiting for transfers between devices: 26.4 us -> 20.6 us  [swap(): lax.ppermute(x, axis, [(i, i ^ by) for i in range(lax.axis_size(axis))])]
    unnamed x6 -> x2, local copies, waits for them, and re-layouts: 4.41 us -> 0.01 us
    pallas_call x1, Pallas kernels: 0.24 us -> 3.28 us  [route(): pl.pallas_call(functools.partial(route_kernel, capacity, top), in_specs=[...]
    pallas_call x1, Pallas kernels: 6.17 us -> 4.99 us  [attend(): pl.pallas_call(functools.partial(attend_kernel, rows // requests, heads /...]
    ppermute x28 -> x26, starting transfers between devices: 25.3 us -> 25.6 us  [swap(): lax.ppermute(x, axis, [(i, i ^ by) for i in range(lax.axis_size(axis))])]
  transfers between devices with their start and end apart: 28 -> 26, of which waited for: 14 -> 13; matrix products, arithmetic and copies ran while one was open for 0% -> 0% of each run, Pallas kernels for 1% -> 12%
where the time goes in v4:
time: 77.3 us; the launch traced here: 77 us
  Pallas kernels  30.7 us (40%)
  starting transfers between devices  25.6 us (33%)
  waiting for transfers between devices  20.6 us (27%)
    ppermute x26, starting transfers between devices, swap(): lax.ppermute(x, axis, [(i, i ^ by) for i in range(lax.axis_size(axis))])  25.6 us
    ppermute x26, waiting for transfers between devices, swap(): lax.ppermute(x, axis, [(i, i ^ by) for i in range(lax.axis_size(axis))])  20.6 us
    pallas_call x1, Pallas kernels, expert_apply(): pl.pallas_call(functools.partial(expert_kernel, count, wide, each), in_sp...  14.3 us
    pallas_call x1, Pallas kernels, load(): pl.pallas_call(load_kernel, in_specs=[ANY, ANY], out_specs=[VMEM, VMEM],...  5.04 us
    pallas_call x1, Pallas kernels, attend(): pl.pallas_call(functools.partial(attend_kernel, rows // requests, heads /...  4.99 us
    pallas_call x1, Pallas kernels, route(): pl.pallas_call(functools.partial(route_kernel, capacity, top), in_specs=[...  3.28 us
  transfers between devices with their start and end apart: 26, of which 13 were waited for; matrix products, arithmetic and copies ran while one was open for 0% of the time, Pallas kernels for 12%

profile of v4, /device:TPU:0, one launch (start us, length us, event | category | flops | bytes accessed | tf_op | source)
XLA Modules:
  0.0 77.0 jit_solution(4106564498692464115)
XLA Ops:
  0.0 5.0 %attention.1 = (bf16[16,2944]{1,0:T(8,128)(2,1)S(1)}, bf16[16,2944]{1,0:T(8,128)(2,1)S(1)}, bf16[16,2944]{1,0:T(8,128)(2,1)S(1)}, bf16[16,2944]{1,0:T(8,128)(2,1...) custom-call(f32[16]{0:T(128)} %decay_ref.1, s32[2,8]{1,0:T(2,128)} %bitcast.6, bf16[16,2048]{1,0:T(8,128)(2,1)} %q_ref.1, ...), custom_call_target="tpu_custom_call" | custom-call | tf_op jit(solution)/shard_map/attention/pallas_call | solution.py:119
  5.0 3.1 %collective-permute-start.1 = (bf16[16,2944]{1,0:T(8,128)(2,1)S(1)}, bf16[16,2944]{1,0:T(8,128)(2,1)S(1)}, u32[]{:S(2)}, u32[]{:S(2)}) collective-permute-start(bf16[16,2944]{1,0:T(8,128)(2,1)S(1)} %get-tuple-element.39), channel_id=1, source_target_pairs={{0,4},{4,0},{8,12},{12,8},{1,5},{5,1},{9,13},{13,9},{2,6},{6,2},{1... | collective-permute-start | bytes 282632 | tf_op jit(solution)/shard_map/ppermute | solution.py:518
  8.1 2.6 %collective-permute-start.3 = (bf16[16,2944]{1,0:T(8,128)(2,1)S(1)}, bf16[16,2944]{1,0:T(8,128)(2,1)S(1)}, u32[]{:S(2)}, u32[]{:S(2)}) collective-permute-start(bf16[16,2944]{1,0:T(8,128)(2,1)S(1)} %get-tuple-element.40), channel_id=1, source_target_pairs={{0,8},{4,12},{8,0},{12,4},{1,9},{5,13},{9,1},{13,5},{2,10},{6,14},... | collective-permute-start | bytes 282632 | tf_op jit(solution)/shard_map/ppermute | solution.py:518
  10.7 0.0 collective-permute-start.5
  10.7 5.0 %load.1 = (bf16[16,2944]{1,0:T(8,128)(2,1)S(1)}, bf16[1152,6144]{1,0:T(8,128)(2,1)S(1)}) custom-call(bf16[16,2944]{1,0:T(8,128)(2,1)S(1)} %get-tuple-element.37.rows_hbm, bf16[1152,6144]{1,0:T(8,128)(2,1)} %weight_hbm.1), custom_call_target="tpu_custom_call" | custom-call | bytes 14155776 | tf_op jit(solution)/shard_map/load/pallas_call | solution.py:160
  15.7 0.1 collective-permute-start
  15.8 0.0 collective-permute-done.1.refs_2_
  15.8 0.5 collective-permute-start.2
  16.3 1.9 %collective-permute-done.3.refs_4_ = bf16[16,2944]{1,0:T(8,128)(2,1)S(1)} collective-permute-done((bf16[16,2944]{1,0:T(8,128)(2,1)S(1)}, bf16[16,2944]{1,0:T(8,128)(2,1)S(1)}, u32[]{:S(2)}, u32[]{:S(2)}) %collective-permute-start.3) | collective-permute-done | bytes 94240 | tf_op jit(solution)/shard_map/ppermute | solution.py:518
  18.2 0.0 collective-permute-start.4
  18.2 0.0 collective-permute-done.5.refs_6_
  18.2 0.5 collective-permute-start.6
  18.7 0.0 collective-permute-done.refs_1_
  18.7 0.0 collective-permute-done.2.refs_3_
  18.7 0.8 %collective-permute-done.4.refs_5_ = bf16[16,2944]{1,0:T(8,128)(2,1)S(1)} collective-permute-done((bf16[16,2944]{1,0:T(8,128)(2,1)S(1)}, bf16[16,2944]{1,0:T(8,128)(2,1)S(1)}, u32[]{:S(2)}, u32[]{:S(2)}) %collective-permute-start.4) | collective-permute-done | bytes 94240 | tf_op jit(solution)/shard_map/ppermute | solution.py:518
  19.5 0.2 collective-permute-done.6.refs_7_
  19.7 0.7 projection.1
  20.4 1.6 %collective-permute-start.7 = (bf16[64,768]{1,0:T(8,128)(2,1)S(1)}, bf16[64,768]{1,0:T(8,128)(2,1)S(1)}, u32[]{:S(2)}, u32[]{:S(2)}) collective-permute-start(bf16[64,768]{1,0:T(8,128)(2,1)S(1)} %get-tuple-element.44), channel_id=1, source_target_pairs={{0,1},{1,0},{2,3},{3,2},{4,5},{5,4},{6,7},{7,6},{8,9},{9,8},{10,11... | collective-permute-start | bytes 294920 | tf_op jit(solution)/shard_map/ppermute | solution.py:518
  21.9 3.3 %route.1 = (bf16[128,64]{1,0:T(8,128)(2,1)S(1)}, f32[64,768]{1,0:T(8,128)S(1)}, bf16[640,6144]{1,0:T(8,128)(2,1)S(1)}) custom-call(bf16[16,2944]{1,0:T(8,128)(2,1)S(1)} %get-tuple-element.38.refs_0_, bf16[16,2944]{1,0:T(8,128)(2,1)S(1)} %collective-permute-done.refs_1_, bf16[16,2944]{1,0:T(8,128)(2,1)S(1)} %collective-permute-done.1.refs_2_, ...), custom_call_target="tpu_custom_call" | custom-call | flops 1000000 | bytes 8000000 | tf_op jit(solution)/shard_map/route/pallas_call | solution.py:257
  25.2 0.3 collective-permute-done.7.got_ref
  25.5 0.2 pack.1
  25.7 2.3 %collective-permute-start.9 = (bf16[32,768]{1,0:T(8,128)(2,1)S(1)}, bf16[32,768]{1,0:T(8,128)(2,1)S(1)}, u32[]{:S(2)}, u32[]{:S(2)}) collective-permute-start(bf16[32,768]{1,0:T(8,128)(2,1)S(1)} %get-tuple-element.49), channel_id=1, source_target_pairs={{0,8},{4,12},{8,0},{12,4},{1,9},{5,13},{9,1},{13,5},{2,10},{6,14},... | collective-permute-start | bytes 147464 | tf_op jit(solution)/shard_map/ppermute | solution.py:518
  28.0 0.8 %collective-permute-start.8 = (bf16[32,768]{1,0:T(8,128)(2,1)S(1)}, bf16[32,768]{1,0:T(8,128)(2,1)S(1)}, u32[]{:S(2)}, u32[]{:S(2)}) collective-permute-start(bf16[32,768]{1,0:T(8,128)(2,1)S(1)} %get-tuple-element.48), channel_id=1, source_target_pairs={{0,4},{4,0},{8,12},{12,8},{1,5},{5,1},{9,13},{13,9},{2,6},{6,2},{1... | collective-permute-start | bytes 147464 | tf_op jit(solution)/shard_map/ppermute | solution.py:518
  28.8 1.3 %collective-permute-start.10 = (bf16[32,768]{1,0:T(8,128)(2,1)S(1)}, bf16[32,768]{1,0:T(8,128)(2,1)S(1)}, u32[]{:S(2)}, u32[]{:S(2)}) collective-permute-start(bf16[32,768]{1,0:T(8,128)(2,1)S(1)} %get-tuple-element.50), channel_id=1, source_target_pairs={{0,12},{4,8},{8,4},{12,0},{1,13},{5,9},{9,5},{13,1},{2,14},{6,10},... | collective-permute-start | bytes 147464 | tf_op jit(solution)/shard_map/ppermute | solution.py:518
  30.1 0.7 collective-permute-done.9
  30.9 3.8 %collective-permute-done.10 = bf16[32,768]{1,0:T(8,128)(2,1)S(1)} collective-permute-done((bf16[32,768]{1,0:T(8,128)(2,1)S(1)}, bf16[32,768]{1,0:T(8,128)(2,1)S(1)}, u32[]{:S(2)}, u32[]{:S(2)}) %collective-permute-start.10) | collective-permute-done | bytes 49184 | tf_op jit(solution)/shard_map/ppermute | solution.py:518
  34.7 1.5 %collective-permute-start.14 = (bf16[64,768]{1,0:T(8,128)(2,1)S(1)}, bf16[64,768]{1,0:T(8,128)(2,1)S(1)}, u32[]{:S(2)}, u32[]{:S(2)}) collective-permute-start(bf16[64,768]{1,0:T(8,128)(2,1)S(1)} %constant_dynamic-update-slice_fusion.2.refs_1_), channel_id=1, source_target_pairs={{0,1},{1,0},{2,3},{3,2},{4,5},{5,4},{6,7},{7,6},{8,9},{9,8},{10,11... | collective-permute-start | bytes 294920 | tf_op jit(solution)/shard_map/ppermute | solution.py:518
  36.2 0.0 collective-permute-done.8
  36.2 0.6 collective-permute-start.13
  36.8 0.0 collective-permute-start.12
  36.8 0.5 collective-permute-start.11
  37.3 2.0 %collective-permute-done.14.refs_5_ = bf16[64,768]{1,0:T(8,128)(2,1)S(1)} collective-permute-done((bf16[64,768]{1,0:T(8,128)(2,1)S(1)}, bf16[64,768]{1,0:T(8,128)(2,1)S(1)}, u32[]{:S(2)}, u32[]{:S(2)}) %collective-permute-start.14) | collective-permute-done | bytes 98336 | tf_op jit(solution)/shard_map/ppermute | solution.py:518
  39.3 0.0 collective-permute-start.16
  39.3 1.6 %collective-permute-done.13.refs_4_ = bf16[64,768]{1,0:T(8,128)(2,1)S(1)} collective-permute-done((bf16[64,768]{1,0:T(8,128)(2,1)S(1)}, bf16[64,768]{1,0:T(8,128)(2,1)S(1)}, u32[]{:S(2)}, u32[]{:S(2)}) %collective-permute-start.13) | collective-permute-done | bytes 98336 | tf_op jit(solution)/shard_map/ppermute | solution.py:518
  40.9 0.0 collective-permute-start.15
  40.9 0.0 collective-permute-done.12.refs_3_
  40.9 0.0 collective-permute-done.11.refs_2_
  40.9 0.0 collective-permute-done.16.refs_7_
  40.9 1.3 %collective-permute-done.15.refs_6_ = bf16[64,768]{1,0:T(8,128)(2,1)S(1)} collective-permute-done((bf16[64,768]{1,0:T(8,128)(2,1)S(1)}, bf16[64,768]{1,0:T(8,128)(2,1)S(1)}, u32[]{:S(2)}, u32[]{:S(2)}) %collective-permute-start.15) | collective-permute-done | bytes 98336 | tf_op jit(solution)/shard_map/ppermute | solution.py:518
  42.2 14.3 %experts.1 = (f32[32,6144]{1,0:T(8,128)S(1)}, bf16[32,6144]{1,0:T(8,128)(2,1)S(1)}) custom-call(bf16[64,768]{1,0:T(8,128)(2,1)S(1)} %constant_dynamic-update-slice_fusion.refs_0_, bf16[64,768]{1,0:T(8,128)(2,1)S(1)} %constant_dynamic-update-slice_fusion.2.refs_1_, bf16[64,768]{1,0:T(8,128)(2,1)S(1)} %collective-permute-done.11.refs_2_, ...), custom_call_target="tpu_custom_call" | custom-call | tf_op jit(solution)/shard_map/experts/pallas_call | solution.py:370
  56.5 0.2 collective-permute-start.17
  56.7 1.6 %collective-permute-done.17.got_ref = bf16[32,6144]{1,0:T(8,128)(2,1)S(1)} collective-permute-done((bf16[32,6144]{1,0:T(8,128)(2,1)S(1)}, bf16[32,6144]{1,0:T(8,128)(2,1)S(1)}, u32[]{:S(2)}, u32[]{:S(2)}) %collective-permute-start.17) | collective-permute-done | bytes 393248 | tf_op jit(solution)/shard_map/ppermute | solution.py:518
  58.3 0.1 chip_sum.1
  58.4 1.1 %collective-permute-start.22 = (bf16[16,6144]{1,0:T(8,128)(2,1)S(1)}, bf16[16,6144]{1,0:T(8,128)(2,1)S(1)}, u32[]{:S(2)}, u32[]{:S(2)}) collective-permute-start(bf16[16,6144]{1,0:T(8,128)(2,1)S(1)} %get-tuple-element.64), channel_id=1, source_target_pairs={{0,1},{1,0},{2,3},{3,2},{4,5},{5,4},{6,7},{7,6},{8,9},{9,8},{10,11... | collective-permute-start | bytes 589832 | tf_op jit(solution)/shard_map/ppermute | solution.py:518
  59.5 0.0 collective-permute-start.18
  59.5 1.9 %collective-permute-start.19 = (bf16[16,768]{1,0:T(8,128)(2,1)S(1)}, bf16[16,768]{1,0:T(8,128)(2,1)S(1)}, u32[]{:S(2)}, u32[]{:S(2)}) collective-permute-start(bf16[16,768]{1,0:T(8,128)(2,1)S(1)} %get-tuple-element.59), channel_id=1, source_target_pairs={{0,8},{4,12},{8,0},{12,4},{1,9},{5,13},{9,1},{13,5},{2,10},{6,14},... | collective-permute-start | bytes 73736 | tf_op jit(solution)/shard_map/ppermute | solution.py:518
  61.4 2.5 %collective-permute-start.20 = (bf16[16,768]{1,0:T(8,128)(2,1)S(1)}, bf16[16,768]{1,0:T(8,128)(2,1)S(1)}, u32[]{:S(2)}, u32[]{:S(2)}) collective-permute-start(bf16[16,768]{1,0:T(8,128)(2,1)S(1)} %get-tuple-element.60), channel_id=1, source_target_pairs={{0,12},{4,8},{8,4},{12,0},{1,13},{5,9},{9,5},{13,1},{2,14},{6,10},... | collective-permute-start | bytes 73736 | tf_op jit(solution)/shard_map/ppermute | solution.py:518
  63.8 0.0 collective-permute-done.18.refs_1_
  63.9 0.6 collective-permute-done.19.refs_2_
  64.5 2.5 %collective-permute-done.20.refs_3_ = bf16[16,768]{1,0:T(8,128)(2,1)S(1)} collective-permute-done((bf16[16,768]{1,0:T(8,128)(2,1)S(1)}, bf16[16,768]{1,0:T(8,128)(2,1)S(1)}, u32[]{:S(2)}, u32[]{:S(2)}) %collective-permute-start.20) | collective-permute-done | bytes 24608 | tf_op jit(solution)/shard_map/ppermute | solution.py:518
  67.0 0.1 collective-permute-start.21
  67.1 0.0 collective-permute-done.22.got_ref
  67.1 0.1 pair_sum.1
  67.2 0.1 collective-permute-start.23
  67.3 3.0 %collective-permute-start.24 = (bf16[8,3072]{1,0:T(8,128)(2,1)S(1)}, bf16[8,3072]{1,0:T(8,128)(2,1)S(1)}, u32[]{:S(2)}, u32[]{:S(2)}) collective-permute-start(bf16[8,3072]{1,0:T(8,128)(2,1)S(1)} %get-tuple-element.67), channel_id=1, source_target_pairs={{0,8},{4,12},{8,0},{12,4},{1,9},{5,13},{9,1},{13,5},{2,10},{6,14},... | collective-permute-start | bytes 147464 | tf_op jit(solution)/shard_map/ppermute | solution.py:518
  70.3 1.3 %collective-permute-start.25 = (bf16[8,3072]{1,0:T(8,128)(2,1)S(1)}, bf16[8,3072]{1,0:T(8,128)(2,1)S(1)}, u32[]{:S(2)}, u32[]{:S(2)}) collective-permute-start(bf16[8,3072]{1,0:T(8,128)(2,1)S(1)} %get-tuple-element.68), channel_id=1, source_target_pairs={{0,12},{4,8},{8,4},{12,0},{1,13},{5,9},{9,5},{13,1},{2,14},{6,10},... | collective-permute-start | bytes 147464 | tf_op jit(solution)/shard_map/ppermute | solution.py:518
  71.7 0.0 collective-permute-done.21.refs_4_
  71.7 1.1 %own_rows.1 = (f32[8,6144]{1,0:T(8,128)S(1)}, bf16[32,32]{1,0:T(8,128)(2,1)S(1)}) custom-call(s32[2,8]{1,0:T(2,128)} %bitcast.7, f32[2,8]{1,0:T(2,128)} %bitcast.8, bf16[8,6144]{1,0:T(8,128)(2,1)} %residual_ref.3, bf16[16,768]{1,0:T(8,128)(2,1)S(1)} %get-tuple-element.57.refs_0_, bf16[16,768]{1,0:T(8,128)(2,1)S(1)} %collective-permute-done.18.refs_1_, ...), custom_call_target="tpu_custom_call" | custom-call | flops 1000000 | bytes 1000000 | tf_op jit(solution)/shard_map/own_rows/pallas_call | solution.py:481
  72.8 0.0 collective-permute-done.23.refs_1_
  72.8 0.0 collective-permute-done.24.refs_2_
  72.8 3.4 %collective-permute-done.25.refs_3_ = bf16[8,3072]{1,0:T(8,128)(2,1)S(1)} collective-permute-done((bf16[8,3072]{1,0:T(8,128)(2,1)S(1)}, bf16[8,3072]{1,0:T(8,128)(2,1)S(1)}, u32[]{:S(2)}, u32[]{:S(2)}) %collective-permute-start.25) | collective-permute-done | bytes 49184 | tf_op jit(solution)/shard_map/ppermute | solution.py:518
  76.2 0.8 %finish.1 = bf16[8,6144]{1,0:T(8,128)(2,1)} custom-call(f32[8,6144]{1,0:T(8,128)S(1)} %get-tuple-element.61.combined_ref, bf16[32,32]{1,0:T(8,128)(2,1)S(1)} %get-tuple-element.62.weighting_ref, bf16[8,3072]{1,0:T(8,128)(2,1)S(1)} %get-tuple-element.65.refs_0_, bf16[8,3072]{1,0:T(8,128)(2,1)S(1)} %collective-permute-done.23.refs_1_, ...), custom_call_target="tpu_custom_call" | custom-call | tf_op jit(solution)/shard_map/finish/pallas_call | solution.py:507
  (5 shorter events, 0.0 us)
Async XLA Ops:
  5.0 10.8 %collective-permute-start.1 = (bf16[16,2944]{1,0:T(8,128)(2,1)S(1)}, bf16[16,2944]{1,0:T(8,128)(2,1)S(1)}, u32[]{:S(2)}, u32[]{:S(2)}) collective-permute-start(bf16[16,2944]{1,0:T(8,128)(2,1)S(1)} %get-tuple-element.39), channel_id=1, source_target_pairs={{0,4},{4,0},{8,12},{12,8},{1,5},{5,1},{9,13},{13,9},{2,6},{6,2},{1... | collective-permute-start | bytes 282632 | tf_op jit(solution)/shard_map/ppermute | solution.py:518
  8.1 10.1 %collective-permute-start.3 = (bf16[16,2944]{1,0:T(8,128)(2,1)S(1)}, bf16[16,2944]{1,0:T(8,128)(2,1)S(1)}, u32[]{:S(2)}, u32[]{:S(2)}) collective-permute-start(bf16[16,2944]{1,0:T(8,128)(2,1)S(1)} %get-tuple-element.40), channel_id=1, source_target_pairs={{0,8},{4,12},{8,0},{12,4},{1,9},{5,13},{9,1},{13,5},{2,10},{6,14},... | collective-permute-start | bytes 282632 | tf_op jit(solution)/shard_map/ppermute | solution.py:518
  10.7 7.5 %collective-permute-start.5 = (bf16[16,2944]{1,0:T(8,128)(2,1)S(1)}, bf16[16,2944]{1,0:T(8,128)(2,1)S(1)}, u32[]{:S(2)}, u32[]{:S(2)}) collective-permute-start(bf16[16,2944]{1,0:T(8,128)(2,1)S(1)} %get-tuple-element.41), channel_id=1, source_target_pairs={{0,12},{4,8},{8,4},{12,0},{1,13},{5,9},{9,5},{13,1},{2,14},{6,10},... | collective-permute-start | bytes 282632 | tf_op jit(solution)/shard_map/ppermute | solution.py:518
  15.7 3.0 %collective-permute-start = (bf16[16,2944]{1,0:T(8,128)(2,1)S(1)}, bf16[16,2944]{1,0:T(8,128)(2,1)S(1)}, u32[]{:S(2)}, u32[]{:S(2)}) collective-permute-start(bf16[16,2944]{1,0:T(8,128)(2,1)S(1)} %get-tuple-element.38.refs_0_), channel_id=1, source_target_pairs={{0,2},{2,0},{1,3},{3,1},{4,6},{6,4},{5,7},{7,5},{8,10},{10,8},{9,1... | collective-permute-start | bytes 282632 | tf_op jit(solution)/shard_map/ppermute | solution.py:518
  15.8 2.9 %collective-permute-start.2 = (bf16[16,2944]{1,0:T(8,128)(2,1)S(1)}, bf16[16,2944]{1,0:T(8,128)(2,1)S(1)}, u32[]{:S(2)}, u32[]{:S(2)}) collective-permute-start(bf16[16,2944]{1,0:T(8,128)(2,1)S(1)} %collective-permute-done.1.refs_2_), channel_id=1, source_target_pairs={{0,2},{2,0},{1,3},{3,1},{4,6},{6,4},{5,7},{7,5},{8,10},{10,8},{9,1... | collective-permute-start | bytes 282632 | tf_op jit(solution)/shard_map/ppermute | solution.py:518
  18.2 1.3 %collective-permute-start.4 = (bf16[16,2944]{1,0:T(8,128)(2,1)S(1)}, bf16[16,2944]{1,0:T(8,128)(2,1)S(1)}, u32[]{:S(2)}, u32[]{:S(2)}) collective-permute-start(bf16[16,2944]{1,0:T(8,128)(2,1)S(1)} %collective-permute-done.3.refs_4_), channel_id=1, source_target_pairs={{0,2},{2,0},{1,3},{3,1},{4,6},{6,4},{5,7},{7,5},{8,10},{10,8},{9,1... | collective-permute-start | bytes 282632 | tf_op jit(solution)/shard_map/ppermute | solution.py:518
  18.2 1.4 %collective-permute-start.6 = (bf16[16,2944]{1,0:T(8,128)(2,1)S(1)}, bf16[16,2944]{1,0:T(8,128)(2,1)S(1)}, u32[]{:S(2)}, u32[]{:S(2)}) collective-permute-start(bf16[16,2944]{1,0:T(8,128)(2,1)S(1)} %collective-permute-done.5.refs_6_), channel_id=1, source_target_pairs={{0,2},{2,0},{1,3},{3,1},{4,6},{6,4},{5,7},{7,5},{8,10},{10,8},{9,1... | collective-permute-start | bytes 282632 | tf_op jit(solution)/shard_map/ppermute | solution.py:518
  20.4 5.1 %collective-permute-start.7 = (bf16[64,768]{1,0:T(8,128)(2,1)S(1)}, bf16[64,768]{1,0:T(8,128)(2,1)S(1)}, u32[]{:S(2)}, u32[]{:S(2)}) collective-permute-start(bf16[64,768]{1,0:T(8,128)(2,1)S(1)} %get-tuple-element.44), channel_id=1, source_target_pairs={{0,1},{1,0},{2,3},{3,2},{4,5},{5,4},{6,7},{7,6},{8,9},{9,8},{10,11... | collective-permute-start | bytes 294920 | tf_op jit(solution)/shard_map/ppermute | solution.py:518
  25.7 5.2 %collective-permute-start.9 = (bf16[32,768]{1,0:T(8,128)(2,1)S(1)}, bf16[32,768]{1,0:T(8,128)(2,1)S(1)}, u32[]{:S(2)}, u32[]{:S(2)}) collective-permute-start(bf16[32,768]{1,0:T(8,128)(2,1)S(1)} %get-tuple-element.49), channel_id=1, source_target_pairs={{0,8},{4,12},{8,0},{12,4},{1,9},{5,13},{9,1},{13,5},{2,10},{6,14},... | collective-permute-start | bytes 147464 | tf_op jit(solution)/shard_map/ppermute | solution.py:518
  28.0 8.2 %collective-permute-start.8 = (bf16[32,768]{1,0:T(8,128)(2,1)S(1)}, bf16[32,768]{1,0:T(8,128)(2,1)S(1)}, u32[]{:S(2)}, u32[]{:S(2)}) collective-permute-start(bf16[32,768]{1,0:T(8,128)(2,1)S(1)} %get-tuple-element.48), channel_id=1, source_target_pairs={{0,4},{4,0},{8,12},{12,8},{1,5},{5,1},{9,13},{13,9},{2,6},{6,2},{1... | collective-permute-start | bytes 147464 | tf_op jit(solution)/shard_map/ppermute | solution.py:518
  28.8 5.9 %collective-permute-start.10 = (bf16[32,768]{1,0:T(8,128)(2,1)S(1)}, bf16[32,768]{1,0:T(8,128)(2,1)S(1)}, u32[]{:S(2)}, u32[]{:S(2)}) collective-permute-start(bf16[32,768]{1,0:T(8,128)(2,1)S(1)} %get-tuple-element.50), channel_id=1, source_target_pairs={{0,12},{4,8},{8,4},{12,0},{1,13},{5,9},{9,5},{13,1},{2,14},{6,10},... | collective-permute-start | bytes 147464 | tf_op jit(solution)/shard_map/ppermute | solution.py:518
  34.7 4.6 %collective-permute-start.14 = (bf16[64,768]{1,0:T(8,128)(2,1)S(1)}, bf16[64,768]{1,0:T(8,128)(2,1)S(1)}, u32[]{:S(2)}, u32[]{:S(2)}) collective-permute-start(bf16[64,768]{1,0:T(8,128)(2,1)S(1)} %constant_dynamic-update-slice_fusion.2.refs_1_), channel_id=1, source_target_pairs={{0,1},{1,0},{2,3},{3,2},{4,5},{5,4},{6,7},{7,6},{8,9},{9,8},{10,11... | collective-permute-start | bytes 294920 | tf_op jit(solution)/shard_map/ppermute | solution.py:518
  36.2 4.7 %collective-permute-start.13 = (bf16[64,768]{1,0:T(8,128)(2,1)S(1)}, bf16[64,768]{1,0:T(8,128)(2,1)S(1)}, u32[]{:S(2)}, u32[]{:S(2)}) collective-permute-start(bf16[64,768]{1,0:T(8,128)(2,1)S(1)} %constant_dynamic-update-slice_fusion.refs_0_), channel_id=1, source_target_pairs={{0,1},{1,0},{2,3},{3,2},{4,5},{5,4},{6,7},{7,6},{8,9},{9,8},{10,11... | collective-permute-start | bytes 294920 | tf_op jit(solution)/shard_map/ppermute | solution.py:518
  36.8 4.1 %collective-permute-start.12 = (bf16[64,768]{1,0:T(8,128)(2,1)S(1)}, bf16[64,768]{1,0:T(8,128)(2,1)S(1)}, u32[]{:S(2)}, u32[]{:S(2)}) collective-permute-start(bf16[64,768]{1,0:T(8,128)(2,1)S(1)} %constant_dynamic-update-slice_fusion.2.refs_1_), channel_id=1, source_target_pairs={{0,2},{2,0},{1,3},{3,1},{4,6},{6,4},{5,7},{7,5},{8,10},{10,8},{9,1... | collective-permute-start | bytes 294920 | tf_op jit(solution)/shard_map/ppermute | solution.py:518
  36.8 4.1 %collective-permute-start.11 = (bf16[64,768]{1,0:T(8,128)(2,1)S(1)}, bf16[64,768]{1,0:T(8,128)(2,1)S(1)}, u32[]{:S(2)}, u32[]{:S(2)}) collective-permute-start(bf16[64,768]{1,0:T(8,128)(2,1)S(1)} %constant_dynamic-update-slice_fusion.refs_0_), channel_id=1, source_target_pairs={{0,2},{2,0},{1,3},{3,1},{4,6},{6,4},{5,7},{7,5},{8,10},{10,8},{9,1... | collective-permute-start | bytes 294920 | tf_op jit(solution)/shard_map/ppermute | solution.py:518
  39.3 1.6 %collective-permute-start.16 = (bf16[64,768]{1,0:T(8,128)(2,1)S(1)}, bf16[64,768]{1,0:T(8,128)(2,1)S(1)}, u32[]{:S(2)}, u32[]{:S(2)}) collective-permute-start(bf16[64,768]{1,0:T(8,128)(2,1)S(1)} %collective-permute-done.14.refs_5_), channel_id=1, source_target_pairs={{0,2},{2,0},{1,3},{3,1},{4,6},{6,4},{5,7},{7,5},{8,10},{10,8},{9,1... | collective-permute-start | bytes 294920 | tf_op jit(solution)/shard_map/ppermute | solution.py:518
  40.9 1.3 %collective-permute-start.15 = (bf16[64,768]{1,0:T(8,128)(2,1)S(1)}, bf16[64,768]{1,0:T(8,128)(2,1)S(1)}, u32[]{:S(2)}, u32[]{:S(2)}) collective-permute-start(bf16[64,768]{1,0:T(8,128)(2,1)S(1)} %collective-permute-done.13.refs_4_), channel_id=1, source_target_pairs={{0,2},{2,0},{1,3},{3,1},{4,6},{6,4},{5,7},{7,5},{8,10},{10,8},{9,1... | collective-permute-start | bytes 294920 | tf_op jit(solution)/shard_map/ppermute | solution.py:518
  56.5 1.8 %collective-permute-start.17 = (bf16[32,6144]{1,0:T(8,128)(2,1)S(1)}, bf16[32,6144]{1,0:T(8,128)(2,1)S(1)}, u32[]{:S(2)}, u32[]{:S(2)}) collective-permute-start(bf16[32,6144]{1,0:T(8,128)(2,1)S(1)} %get-tuple-element.55), channel_id=1, source_target_pairs={{0,2},{2,0},{1,3},{3,1},{4,6},{6,4},{5,7},{7,5},{8,10},{10,8},{9,1... | collective-permute-start | bytes 1179656 | tf_op jit(solution)/shard_map/ppermute | solution.py:518
  58.4 8.7 %collective-permute-start.22 = (bf16[16,6144]{1,0:T(8,128)(2,1)S(1)}, bf16[16,6144]{1,0:T(8,128)(2,1)S(1)}, u32[]{:S(2)}, u32[]{:S(2)}) collective-permute-start(bf16[16,6144]{1,0:T(8,128)(2,1)S(1)} %get-tuple-element.64), channel_id=1, source_target_pairs={{0,1},{1,0},{2,3},{3,2},{4,5},{5,4},{6,7},{7,6},{8,9},{9,8},{10,11... | collective-permute-start | bytes 589832 | tf_op jit(solution)/shard_map/ppermute | solution.py:518
  59.5 4.4 %collective-permute-start.18 = (bf16[16,768]{1,0:T(8,128)(2,1)S(1)}, bf16[16,768]{1,0:T(8,128)(2,1)S(1)}, u32[]{:S(2)}, u32[]{:S(2)}) collective-permute-start(bf16[16,768]{1,0:T(8,128)(2,1)S(1)} %get-tuple-element.58), channel_id=1, source_target_pairs={{0,4},{4,0},{8,12},{12,8},{1,5},{5,1},{9,13},{13,9},{2,6},{6,2},{1... | collective-permute-start | bytes 73736 | tf_op jit(solution)/shard_map/ppermute | solution.py:518
  59.5 5.0 %collective-permute-start.19 = (bf16[16,768]{1,0:T(8,128)(2,1)S(1)}, bf16[16,768]{1,0:T(8,128)(2,1)S(1)}, u32[]{:S(2)}, u32[]{:S(2)}) collective-permute-start(bf16[16,768]{1,0:T(8,128)(2,1)S(1)} %get-tuple-element.59), channel_id=1, source_target_pairs={{0,8},{4,12},{8,0},{12,4},{1,9},{5,13},{9,1},{13,5},{2,10},{6,14},... | collective-permute-start | bytes 73736 | tf_op jit(solution)/shard_map/ppermute | solution.py:518
  61.4 5.6 %collective-permute-start.20 = (bf16[16,768]{1,0:T(8,128)(2,1)S(1)}, bf16[16,768]{1,0:T(8,128)(2,1)S(1)}, u32[]{:S(2)}, u32[]{:S(2)}) collective-permute-start(bf16[16,768]{1,0:T(8,128)(2,1)S(1)} %get-tuple-element.60), channel_id=1, source_target_pairs={{0,12},{4,8},{8,4},{12,0},{1,13},{5,9},{9,5},{13,1},{2,14},{6,10},... | collective-permute-start | bytes 73736 | tf_op jit(solution)/shard_map/ppermute | solution.py:518
  67.0 4.7 %collective-permute-start.21 = (bf16[64,768]{1,0:T(8,128)(2,1)S(1)}, bf16[64,768]{1,0:T(8,128)(2,1)S(1)}, u32[]{:S(2)}, u32[]{:S(2)}) collective-permute-start(bf16[64,768]{1,0:T(8,128)(2,1)S(1)} %pad_maximum_fusion), channel_id=1, source_target_pairs={{0,2},{2,0},{1,3},{3,1},{4,6},{6,4},{5,7},{7,5},{8,10},{10,8},{9,1... | collective-permute-start | bytes 294920 | tf_op jit(solution)/shard_map/ppermute | solution.py:518
  67.2 5.6 %collective-permute-start.23 = (bf16[8,3072]{1,0:T(8,128)(2,1)S(1)}, bf16[8,3072]{1,0:T(8,128)(2,1)S(1)}, u32[]{:S(2)}, u32[]{:S(2)}) collective-permute-start(bf16[8,3072]{1,0:T(8,128)(2,1)S(1)} %get-tuple-element.66), channel_id=1, source_target_pairs={{0,4},{4,0},{8,12},{12,8},{1,5},{5,1},{9,13},{13,9},{2,6},{6,2},{1... | collective-permute-start | bytes 147464 | tf_op jit(solution)/shard_map/ppermute | solution.py:518
  67.3 5.5 %collective-permute-start.24 = (bf16[8,3072]{1,0:T(8,128)(2,1)S(1)}, bf16[8,3072]{1,0:T(8,128)(2,1)S(1)}, u32[]{:S(2)}, u32[]{:S(2)}) collective-permute-start(bf16[8,3072]{1,0:T(8,128)(2,1)S(1)} %get-tuple-element.67), channel_id=1, source_target_pairs={{0,8},{4,12},{8,0},{12,4},{1,9},{5,13},{9,1},{13,5},{2,10},{6,14},... | collective-permute-start | bytes 147464 | tf_op jit(solution)/shard_map/ppermute | solution.py:518
  70.3 5.9 %collective-permute-start.25 = (bf16[8,3072]{1,0:T(8,128)(2,1)S(1)}, bf16[8,3072]{1,0:T(8,128)(2,1)S(1)}, u32[]{:S(2)}, u32[]{:S(2)}) collective-permute-start(bf16[8,3072]{1,0:T(8,128)(2,1)S(1)} %get-tuple-element.68), channel_id=1, source_target_pairs={{0,12},{4,8},{8,4},{12,0},{1,13},{5,9},{9,5},{13,1},{2,14},{6,10},... | collective-permute-start | bytes 147464 | tf_op jit(solution)/shard_map/ppermute | solution.py:518

commit v5 on v4

--- a/solution.py
+++ b/solution.py
@@ -212,9 +212,10 @@
     )(*pieces, weight)
 
 
-def route_kernel(capacity, top, *refs):
-    pieces, weight_hbm = refs[:-7], refs[-6]
-    choose_ref, residual_ref, weight_ref, ids_ref, sem = refs[-5:]
+def route_kernel(capacity, own_ids_ref, weights_ref, *refs):
+    pieces, weight_hbm = refs[:-8], refs[-7]
+    choose_ref, residual_ref, weight_ref, weighting_ref, ids_ref, sem = refs[-6:]
+    top, own_count = own_ids_ref.shape
     copy = pltpu.make_async_copy(weight_hbm.at[: weight_ref.shape[0]], weight_ref, sem)
     copy.start()
     columns = residual_ref.shape[1]
@@ -248,26 +249,45 @@
         choose_ref[d * count : (d + 1) * count] = jnp.where(
             slot == place[d : d + 1], 1.0, 0.0
         ).astype(BF16)
+
+    places = weighting_ref.shape[1]
+    row = lax.broadcasted_iota(jnp.int32, (own_count, places), 0)
+    at_place = lax.broadcasted_iota(jnp.int32, (own_count, places), 1)
+    slot = at_place // 8 * capacity + at_place % capacity
+    weighting = jnp.zeros((own_count, places), F32)
+    order = [(t, k) for t in range(own_count) for k in range(top)]
+    named = [own_ids_ref[k, t] for t, k in order]
+    for j, (t, k) in enumerate(order):
+        rank = jnp.int32(0)
+        for i in range(j):
+            rank = rank + jnp.where(named[i] == named[j], 1, 0)
+        to = (named[j] ^ expert) * capacity + rank
+        weighting = jnp.where((slot == to) & (row == t), weights_ref[k, t], weighting)
+    for h in range(8 // capacity):
+        high, low = halves_of(jnp.where(at_place % 8 // capacity == h, weighting, 0.0))
+        both = jnp.concatenate([high.astype(F32), low.astype(F32)], axis=0)
+        weighting_ref[h * 16 : (h + 1) * 16] = both.astype(BF16)
     copy.wait()
 
 
-def route(pieces, after, columns, capacity, top, weight, first):
+def route(ids, weights, pieces, after, columns, capacity, weight, first):
     rows = pieces[0].shape[0] // 2 * len(pieces)
     experts = len(pieces) // 2
     return pl.pallas_call(
-        functools.partial(route_kernel, capacity, top),
-        in_specs=[VMEM] * len(pieces) + [ANY] * 2,
-        out_specs=[VMEM] * 3,
+        functools.partial(route_kernel, capacity),
+        in_specs=[SMEM] * 2 + [VMEM] * len(pieces) + [ANY] * 2,
+        out_specs=[VMEM] * 4,
         out_shape=[
             jax.ShapeDtypeStruct((experts * 2 * experts * capacity, rows), BF16),
             jax.ShapeDtypeStruct((rows, columns), F32),
             pltpu.VMEM((first, weight.shape[1]), weight.dtype),
+            jax.ShapeDtypeStruct((16 * (8 // capacity), experts * 8), BF16),
         ],
         scratch_shapes=[pltpu.VMEM((rows, ID_LANES), F32), pltpu.SemaphoreType.DMA],
         compiler_params=limits(4),
         cost_estimate=pl.CostEstimate(flops=10**6, bytes_accessed=8 * 10**6, transcendentals=0),
         name="route",
-    )(*pieces, after, *in_hbm(weight))
+    )(*in_hbm(ids, weights), *pieces, after, *in_hbm(weight))
 
 
 def pack_kernel(keep_ref, got_ref, residual_ref, choose_ref, *refs):
@@ -299,118 +319,179 @@
     )(keep, got, residual, choose)
 
 
-def expert_kernel(count, wide, each, *refs):
-    groups = 16 // each // 4
-    near, near_cross, far, far_cross = (refs[g * groups : (g + 1) * groups] for g in range(4))
-    refs = refs[4 * groups :]
-    gain_ref, gate_ref, first_ref, up_hbm, down_hbm = refs[:5]
-    keep_ref, send_ref, x_ref, turned_ref, hidden_ref, rest_ref, down_ref, sem, down_sem = refs[5:]
-    units, width = up_hbm.shape
-    columns = width // 8
-    rows = x_ref.shape[0]
-    cut = first_ref.shape[0]
-    rest = pltpu.make_async_copy(up_hbm.at[cut:], rest_ref, sem)
+def turn(turned_ref, gain_ref, pieces, first, count):
+    near, near_cross, far, far_cross = pieces
+    columns = near.shape[1]
+    expert, half = lax.axis_index("expert"), lax.axis_index("half")
+    squares = jnp.zeros((2 * count, 128), F32)
+    for d in range(2):
+        for c, (mine, theirs) in enumerate(((near, far), (near_cross, far_cross))):
+            rows = slice(d * count, (d + 1) * count)
+            x = jnp.concatenate([mine[rows].astype(F32), theirs[rows].astype(F32)], axis=0)
+            for b in range(columns // 128):
+                part = x[:, b * 128 : (b + 1) * 128]
+                squares = squares + part * part
+            block = (expert ^ (first + d)) * 2 + (half ^ c)
+            at = pl.ds(pl.multiple_of(block * columns, columns), columns)
+            to = pl.ds(pl.multiple_of(block % 4 * columns, columns), columns)
+            turned_ref[to] = (x * gain_ref[:, at]).T.astype(BF16)
+    return squares
+
+
+def half_of(ref, first):
+    width = ref.shape[1] // 2
+    which = (lax.axis_index("expert") ^ first) // 2
+    return pl.ds(pl.multiple_of(which * width, width), width)
+
+
+def expert_first_kernel(count, *refs):
+    pieces, gain_ref, gate_ref, up_ref, up_hbm = refs[:4], *refs[4:8]
+    gate_sum_ref, up_sum_ref, squares_ref, up_rest_ref, turned_ref, sem = refs[8:]
+    cut = up_ref.shape[0]
+    rest = pltpu.make_async_copy(up_hbm.at[cut:], up_rest_ref, sem)
     rest.start()
-    thirds = down_sem.shape[0]
-    tall = units // thirds
-    downs = [
-        pltpu.make_async_copy(
-            down_hbm.at[t * tall : (t + 1) * tall], down_ref.at[t * tall : (t + 1) * tall], down_sem.at[t]
-        )
-        for t in range(thirds)
-    ]
-
-    expert, half = lax.axis_index("expert"), lax.axis_index("half")
-    for p, halves in enumerate(((near, near_cross), (far, far_cross))):
-        for c, pieces in enumerate(halves):
-            for d in range(4):
-                piece = pieces[d // each][d % each * count : (d % each + 1) * count]
-                base = ((expert ^ d) * 2 + (half ^ c)) * columns
-                at = pl.ds(pl.multiple_of(base, columns), columns)
-                x_ref[p * count : (p + 1) * count, at] = piece.astype(F32)
-    squares = jnp.zeros((rows, 128), F32)
-    for b in range(width // 128):
-        x = x_ref[:, b * 128 : (b + 1) * 128]
-        squares = squares + x * x
-    scale = lax.rsqrt(jnp.sum(squares, axis=1, keepdims=True) / width + EPSILON)
-    for b in range(8):
-        at = slice(b * columns, (b + 1) * columns)
-        normed = x_ref[:, at] * scale * gain_ref[:, at]
-        turned_ref[at] = normed.T.astype(BF16)
-    downs[0].start()
-
-    for at, up_ref in ((slice(0, cut), first_ref), (slice(cut, units), rest_ref)):
-        gate_value = dot(gate_ref[at], turned_ref[...])
-        if up_ref is rest_ref:
-            rest.wait()
-            for down in downs[1:]:
-                down.start()
-        lifted = dot(up_ref[...], turned_ref[...])
+    squares_ref[...] = turn(turned_ref, gain_ref, pieces, 0, count)
+    columns = half_of(gate_ref, 0)
+    for at in (slice(0, cut), slice(cut, gate_ref.shape[0])):
+        gate_sum_ref[at] = dot(gate_ref[at, columns], turned_ref[...])
+    up_sum_ref[:cut] = dot(up_ref[:, columns], turned_ref[...])
+    rest.wait()
+    up_sum_ref[cut:] = dot(up_rest_ref[:, columns], turned_ref[...])
+
+
+def expert_second_kernel(count, *refs):
+    pieces, gain_ref, gate_ref, up_ref, up_rest_ref = refs[:4], *refs[4:8]
+    gate_sum_ref, up_sum_ref, squares_ref, down_hbm, hidden_ref, down_ref, turned_ref, sem = refs[8:]
+    units, width = gate_ref.shape
+    cut = up_ref.shape[0]
+    down = pltpu.make_async_copy(down_hbm, down_ref, sem)
+    down.start()
+    squares = squares_ref[...] + turn(turned_ref, gain_ref, pieces, 2, count)
+    spread = jnp.sum(squares.T, axis=0, keepdims=True) / width
+    scale = lax.rsqrt(spread + EPSILON)
+    columns = half_of(gate_ref, 2)
+    for at, weight_ref in ((slice(0, cut), up_ref), (slice(cut, units), up_rest_ref)):
+        gate_value = (gate_sum_ref[at] + dot(gate_ref[at, columns], turned_ref[...])) * scale
+        lifted = (up_sum_ref[at] + dot(weight_ref[:, columns], turned_ref[...])) * scale
         hidden = gate_value / (1.0 + jnp.exp(-gate_value)) * lifted
         hidden_ref[:, at] = hidden.T.astype(BF16)
-
+    down.wait()
+
+
+def down_kernel(start, wide, hidden_ref, weight_ref, keep_ref, send_ref):
+    half = lax.axis_index("half")
+    count = keep_ref.shape[0]
     part = count // 2
-    for down in downs:
-        down.wait()
-    for n in range(width // wide):
-        at = slice(n * wide, (n + 1) * wide)
-        total = dot(hidden_ref[...], down_ref[:, at])
+    for n in range(keep_ref.shape[1] // wide):
+        at = slice(start + n * wide, start + (n + 1) * wide)
+        out = slice(n * wide, (n + 1) * wide)
+        total = dot(hidden_ref[...], weight_ref[:, at])
         for p in range(2):
             low = total[p * count : p * count + part]
             high = total[p * count + part : (p + 1) * count]
             to = slice(p * part, (p + 1) * part)
-            keep_ref[to, at] = jnp.where(half == 0, low, high)
-            send_ref[to, at] = jnp.where(half == 0, high, low).astype(BF16)
-
-
-def expert_apply(pieces, gain, gate, first, up_part, down_part, count):
-    units, width = up_part.shape
-    wide = 512
-    each = pieces[0].shape[0] // count
-    return pl.pallas_call(
-        functools.partial(expert_kernel, count, wide, each),
-        in_specs=[VMEM] * (len(pieces) + 3) + [ANY] * 2,
-        out_specs=(VMEM, VMEM),
-        out_shape=(
+            keep_ref[to, out] = jnp.where(half == 0, low, high)
+            send_ref[to, out] = jnp.where(half == 0, high, low).astype(BF16)
+
+
+def cost(flops, size):
+    return pl.CostEstimate(flops=flops, bytes_accessed=size, transcendentals=0)
+
+
+def expert_first(pieces, gain, gate, up_first, up_part, count):
+    units, width = gate.shape
+    cut = up_first.shape[0]
+    sums = jax.ShapeDtypeStruct((units, 2 * count), F32)
+    return pl.pallas_call(
+        functools.partial(expert_first_kernel, count),
+        in_specs=[VMEM] * 7 + [ANY],
+        out_specs=[VMEM] * 4,
+        out_shape=[
+            sums,
+            sums,
+            jax.ShapeDtypeStruct((2 * count, 128), F32),
+            pltpu.VMEM((units - cut, width), BF16),
+        ],
+        scratch_shapes=[pltpu.VMEM((width // 2, 2 * count), BF16), pltpu.SemaphoreType.DMA],
+        compiler_params=limits(8),
+        cost_estimate=cost(4 * units * width * count, 2 * units * width),
+        name="experts_first",
+    )(*pieces, gain, gate, up_first, *in_hbm(up_part))
+
+
+def relay_kernel(rows_ref, after_ref, out_ref):
+    out_ref[...] = rows_ref[...]
+
+
+def relay(rows, after):
+    return pl.pallas_call(
+        relay_kernel,
+        in_specs=[VMEM] * 2,
+        out_specs=VMEM,
+        out_shape=jax.ShapeDtypeStruct(rows.shape, rows.dtype),
+        compiler_params=limits(2),
+        cost_estimate=cost(0, 10**5),
+        name="relay",
+    )(rows, after)
+
+
+def expert_second(pieces, gain, gate, up_first, up_rest, sums, down_part, count):
+    units, width = gate.shape
+    return pl.pallas_call(
+        functools.partial(expert_second_kernel, count),
+        in_specs=[VMEM] * 11 + [ANY],
+        out_specs=[VMEM] * 2,
+        out_shape=[
+            jax.ShapeDtypeStruct((2 * count, units), BF16),
+            pltpu.VMEM((units, width), BF16),
+        ],
+        scratch_shapes=[pltpu.VMEM((width // 2, 2 * count), BF16), pltpu.SemaphoreType.DMA],
+        compiler_params=limits(8),
+        cost_estimate=cost(4 * units * width * count, 2 * units * width),
+        name="experts_second",
+    )(*pieces, gain, gate, up_first, up_rest, *sums, *in_hbm(down_part))
+
+
+def expert_down(hidden, weight, start, width, count):
+    return pl.pallas_call(
+        functools.partial(down_kernel, start, 512),
+        in_specs=[VMEM] * 2,
+        out_specs=[VMEM] * 2,
+        out_shape=[
             jax.ShapeDtypeStruct((count, width), F32),
             jax.ShapeDtypeStruct((count, width), BF16),
-        ),
-        scratch_shapes=[
-            pltpu.VMEM((2 * count, width), F32),
-            pltpu.VMEM((width, 2 * count), BF16),
-            pltpu.VMEM((2 * count, units), BF16),
-            pltpu.VMEM((units - first.shape[0], width), BF16),
-            pltpu.VMEM((units, width), BF16),
-            pltpu.SemaphoreType.DMA,
-            pltpu.SemaphoreType.DMA((3,)),
         ],
-        compiler_params=limits(30),
-        name="experts",
-    )(*pieces, gain, gate, first, *in_hbm(up_part, down_part))
-
-
-def chip_sum_kernel(mine_ref, got_ref, own_ref, keep_ref, send_ref, *outs):
+        compiler_params=limits(8),
+        cost_estimate=cost(4 * hidden.size * width, 2 * hidden.shape[1] * width),
+        name="experts_down",
+    )(hidden, weight)
+
+
+def chip_sum_kernel(count, *refs):
+    mine, got, own_ref = refs[:count], refs[count : 2 * count], refs[2 * count]
+    keep_ref, send_ref, *outs = refs[2 * count + 1 :]
     rows = keep_ref.shape[0]
-    keep_ref[...] = mine_ref[:rows] + got_ref[:rows].astype(F32)
-    send_ref[...] = (mine_ref[rows:] + got_ref[rows:].astype(F32)).astype(BF16)
+    width = mine[0].shape[1]
+    for g in range(count):
+        at = slice(g * width, (g + 1) * width)
+        keep_ref[:, at] = mine[g][:rows] + got[g][:rows].astype(F32)
+        send_ref[:, at] = (mine[g][rows:] + got[g][rows:].astype(F32)).astype(BF16)
     for d, out in enumerate(outs):
         out[...] = own_ref[d]
 
 
 def chip_sum(mine, got, own):
-    rows, width = mine.shape
-    return pl.pallas_call(
-        chip_sum_kernel,
-        in_specs=[VMEM] * 3,
+    rows, width = mine[0].shape
+    shape = (rows // 2, width * len(mine))
+    return pl.pallas_call(
+        functools.partial(chip_sum_kernel, len(mine)),
+        in_specs=[VMEM] * (2 * len(mine) + 1),
         out_specs=[VMEM] * (2 + own.shape[0]),
-        out_shape=[
-            jax.ShapeDtypeStruct((rows // 2, width), F32),
-            jax.ShapeDtypeStruct((rows // 2, width), BF16),
-        ]
+        out_shape=[jax.ShapeDtypeStruct(shape, F32), jax.ShapeDtypeStruct(shape, BF16)]
         + [jax.ShapeDtypeStruct(own.shape[1:], BF16)] * own.shape[0],
         compiler_params=limits(4),
         name="chip_sum",
-    )(mine, got, own)
+    )(*mine, *got, own)
 
 
 def pair_sum_kernel(capacity, keep_ref, got_ref, *refs):
@@ -442,8 +523,8 @@
     )(keep, got)
 
 
-def own_rows_kernel(capacity, ids_ref, weights_ref, residual_ref, *refs):
-    pieces, cross_ref, combined_ref, weighting_ref = refs[:-3], *refs[-3:]
+def own_rows_kernel(residual_ref, *refs):
+    pieces, cross_ref, combined_ref = refs[:-2], *refs[-2:]
     rows = combined_ref.shape[0]
     columns = pieces[0].shape[1]
     expert, half = lax.axis_index("expert"), lax.axis_index("half")
@@ -455,41 +536,18 @@
             both = both.astype(F32)
             mine = jnp.where(half == 0, both[:rows], both[rows:])
             combined_ref[:, at] = residual_ref[:, at].astype(F32) + mine
-    places = weighting_ref.shape[1]
-    row = lax.broadcasted_iota(jnp.int32, (rows, places), 0)
-    place = lax.broadcasted_iota(jnp.int32, (rows, places), 1)
-    slot = place // 8 * capacity + place % capacity
-    weighting = jnp.zeros((rows, places), F32)
-    top = ids_ref.shape[0]
-    order = [(t, k) for t in range(rows) for k in range(top)]
-    named = [ids_ref[k, t] for t, k in order]
-    for j, (t, k) in enumerate(order):
-        rank = jnp.int32(0)
-        for i in range(j):
-            rank = rank + jnp.where(named[i] == named[j], 1, 0)
-        at = (named[j] ^ expert) * capacity + rank
-        weighting = jnp.where((slot == at) & (row == t), weights_ref[k, t], weighting)
-    for h in range(8 // capacity):
-        high, low = halves_of(jnp.where(place % 8 // capacity == h, weighting, 0.0))
-        both = jnp.concatenate([high.astype(F32), low.astype(F32)], axis=0)
-        weighting_ref[h * 16 : (h + 1) * 16] = both.astype(BF16)
-
-
-def own_rows(ids, weights, residual, pieces, cross, capacity):
-    rows, width = residual.shape
-    experts = len(pieces)
-    return pl.pallas_call(
-        functools.partial(own_rows_kernel, capacity),
-        in_specs=[SMEM, SMEM, VMEM] + [VMEM] * (experts + 1),
-        out_specs=[VMEM] * 2,
-        out_shape=[
-            jax.ShapeDtypeStruct((rows, width), F32),
-            jax.ShapeDtypeStruct((16 * (8 // capacity), experts * 8), BF16),
-        ],
+
+
+def own_rows(residual, pieces, cross):
+    return pl.pallas_call(
+        own_rows_kernel,
+        in_specs=[VMEM] * (len(pieces) + 2),
+        out_specs=VMEM,
+        out_shape=jax.ShapeDtypeStruct(residual.shape, F32),
         compiler_params=limits(4),
-        cost_estimate=pl.CostEstimate(flops=10**6, bytes_accessed=10**6, transcendentals=0),
+        cost_estimate=cost(10**6, 10**6),
         name="own_rows",
-    )(*in_hbm(ids, weights, residual), *pieces, cross)
+    )(*in_hbm(residual), *pieces, cross)
 
 
 def finish_kernel(combined_ref, weighting_ref, *refs):
@@ -532,7 +590,7 @@
     gate_weights,
     expert_gate,
     expert_up,
-    expert_down,
+    expert_down_part,
 ):
     experts = lax.axis_size("expert")
     local_rows = residual.shape[0]
@@ -554,25 +612,36 @@
 
     keep, send = project(pieces, weight_here)
     first = expert_up.shape[0] // 256 * 128 + 128
-    choose, residual_part, up_first = route(
-        pieces, keep, columns, capacity, top, expert_up, first
+    choose, residual_part, up_first, weighting = route(
+        ids, weights, pieces, keep, columns, capacity, expert_up, first
     )
     *packed, own = pack(keep, swap(send, "pair", 1), residual_part, choose, experts)
 
-    order = [2, 3, 1, 0]
-    arrived = {d: swap(packed[d], "expert", d) for d in order}
-    near = [jnp.concatenate([arrived[d], arrived[d + 1]], axis=0) for d in range(0, experts, 2)]
+    arrived = [swap(rows, "expert", d) for d, rows in enumerate(packed)]
+    near = [jnp.concatenate(arrived[d : d + 2], axis=0) for d in range(0, experts, 2)]
     far = [swap(rows, "pair", 1) for rows in near]
-    routed = near + [swap(n, "half", 1) for n in near] + far + [swap(f, "half", 1) for f in far]
-    mine, send = expert_apply(
-        routed, gain_here, gate_here, up_first, expert_up, expert_down, count
-    )
-
-    keep, send, *own = chip_sum(mine, swap(send, "half", 1), own)
+    near_cross = [swap(rows, "half", 1) for rows in near]
+    *sums, up_rest = expert_first(
+        [near[0], near_cross[0], far[0], swap(far[0], "half", 1)],
+        gain_here, gate_here, up_first, expert_up, count,
+    )
+    far[1] = relay(far[1], sums[2])
+    hidden, down_here = expert_second(
+        [near[1], near_cross[1], far[1], swap(far[1], "half", 1)],
+        gain_here, gate_here, up_first, up_rest, sums, expert_down_part, count,
+    )
+
+    width = residual.shape[1] // 2
+    mine, got = [], []
+    for g in range(2):
+        terms, send = expert_down(hidden, down_here, g * width, width, count)
+        mine.append(terms)
+        got.append(swap(send, "half", 1))
+    keep, send, *own = chip_sum(mine, got, own)
     terms = pair_sum(keep, swap(send, "pair", 1), capacity, experts)
     own = [swap(rows, "expert", d) for d, rows in enumerate(own)]
     cross = swap(jnp.concatenate(own, axis=0), "half", 1)
-    combined, weighting = own_rows(ids, weights, residual, own, cross, capacity)
+    combined = own_rows(residual, own, cross)
     back = [swap(term, "expert", d) for d, term in enumerate(terms)]
     return finish(combined, weighting, back)
 

time: 77.3 us -> 76.3 us (0.987)
  starting transfers between devices: 25.6 us -> 24.7 us
    ppermute x26 -> x27, starting transfers between devices: 25.6 us -> 24.7 us  [swap(): lax.ppermute(x, axis, [(i, i ^ by) for i in range(lax.axis_size(axis))])]
    ppermute x26 -> x27, waiting for transfers between devices: 20.6 us -> 20.3 us  [swap(): lax.ppermute(x, axis, [(i, i ^ by) for i in range(lax.axis_size(axis))])]
    pallas_call x4 -> x8, Pallas kernels: 18.8 us -> 19 us  [the longest x1 5.89 us: expert_first(): pl.pallas_call(functools.partial(expert_first_kernel, count), in_specs=[V...]
  transfers between devices with their start and end apart: 26 -> 27, of which waited for: 13 -> 13; matrix products, arithmetic and copies ran while one was open for 0% -> 0% of each run, Pallas kernels for 12% -> 21%
where the time goes in v5:
time: 76.3 us; the launch traced here: 76 us
  Pallas kernels  30.8 us (40%)
  starting transfers between devices  24.7 us (32%)
  waiting for transfers between devices  20.3 us (27%)
    ppermute x27, starting transfers between devices, swap(): lax.ppermute(x, axis, [(i, i ^ by) for i in range(lax.axis_size(axis))])  24.7 us
    ppermute x27, waiting for transfers between devices, swap(): lax.ppermute(x, axis, [(i, i ^ by) for i in range(lax.axis_size(axis))])  20.3 us
    pallas_call x1, Pallas kernels, expert_first(): pl.pallas_call(functools.partial(expert_first_kernel, count), in_specs=[V...  5.89 us
    pallas_call x1, Pallas kernels, expert_second(): pl.pallas_call(functools.partial(expert_second_kernel, count), in_specs=[...  5.23 us
    pallas_call x1, Pallas kernels, load(): pl.pallas_call(load_kernel, in_specs=[ANY, ANY], out_specs=[VMEM, VMEM],...  5.04 us
    pallas_call x1, Pallas kernels, attend(): pl.pallas_call(functools.partial(attend_kernel, rows // requests, heads /...  4.99 us
    pallas_call x1, Pallas kernels, route(): pl.pallas_call(functools.partial(route_kernel, capacity), in_specs=[SMEM]...  4.14 us
    pallas_call x2, Pallas kernels, expert_down(): pl.pallas_call(functools.partial(down_kernel, start, 512), in_specs=[VMEM...  2.71 us
  transfers between devices with their start and end apart: 27, of which 13 were waited for; matrix products, arithmetic and copies ran while one was open for 0% of the time, Pallas kernels for 21%

profile of v5, /device:TPU:0, one launch (start us, length us, event | category | flops | bytes accessed | tf_op | source)
XLA Modules:
  0.0 76.0 jit_solution(16721642046417224399)
XLA Ops:
  0.0 5.0 %attention.1 = (bf16[16,2944]{1,0:T(8,128)(2,1)S(1)}, bf16[16,2944]{1,0:T(8,128)(2,1)S(1)}, bf16[16,2944]{1,0:T(8,128)(2,1)S(1)}, bf16[16,2944]{1,0:T(8,128)(2,1...) custom-call(f32[16]{0:T(128)} %decay_ref.1, s32[2,8]{1,0:T(2,128)} %bitcast.6, bf16[16,2048]{1,0:T(8,128)(2,1)} %q_ref.1, ...), custom_call_target="tpu_custom_call" | custom-call | tf_op jit(solution)/shard_map/attention/pallas_call | solution.py:119
  5.0 3.1 %collective-permute-start.1 = (bf16[16,2944]{1,0:T(8,128)(2,1)S(1)}, bf16[16,2944]{1,0:T(8,128)(2,1)S(1)}, u32[]{:S(2)}, u32[]{:S(2)}) collective-permute-start(bf16[16,2944]{1,0:T(8,128)(2,1)S(1)} %get-tuple-element.46), channel_id=1, source_target_pairs={{0,4},{4,0},{8,12},{12,8},{1,5},{5,1},{9,13},{13,9},{2,6},{6,2},{1... | collective-permute-start | bytes 282632 | tf_op jit(solution)/shard_map/ppermute | solution.py:576
  8.1 2.6 %collective-permute-start.3 = (bf16[16,2944]{1,0:T(8,128)(2,1)S(1)}, bf16[16,2944]{1,0:T(8,128)(2,1)S(1)}, u32[]{:S(2)}, u32[]{:S(2)}) collective-permute-start(bf16[16,2944]{1,0:T(8,128)(2,1)S(1)} %get-tuple-element.47), channel_id=1, source_target_pairs={{0,8},{4,12},{8,0},{12,4},{1,9},{5,13},{9,1},{13,5},{2,10},{6,14},... | collective-permute-start | bytes 282632 | tf_op jit(solution)/shard_map/ppermute | solution.py:576
  10.7 0.0 collective-permute-start.5
  10.7 5.0 %load.1 = (bf16[16,2944]{1,0:T(8,128)(2,1)S(1)}, bf16[1152,6144]{1,0:T(8,128)(2,1)S(1)}) custom-call(bf16[16,2944]{1,0:T(8,128)(2,1)S(1)} %get-tuple-element.44.rows_hbm, bf16[1152,6144]{1,0:T(8,128)(2,1)} %weight_hbm.1), custom_call_target="tpu_custom_call" | custom-call | bytes 14155776 | tf_op jit(solution)/shard_map/load/pallas_call | solution.py:160
  15.7 0.1 collective-permute-start
  15.8 0.0 collective-permute-done.1.refs_2_
  15.8 0.5 collective-permute-start.2
  16.3 1.9 %collective-permute-done.3.refs_4_ = bf16[16,2944]{1,0:T(8,128)(2,1)S(1)} collective-permute-done((bf16[16,2944]{1,0:T(8,128)(2,1)S(1)}, bf16[16,2944]{1,0:T(8,128)(2,1)S(1)}, u32[]{:S(2)}, u32[]{:S(2)}) %collective-permute-start.3) | collective-permute-done | bytes 94240 | tf_op jit(solution)/shard_map/ppermute | solution.py:576
  18.2 0.0 collective-permute-start.4
  18.2 0.0 collective-permute-done.5.refs_6_
  18.2 0.5 collective-permute-start.6
  18.7 0.0 collective-permute-done.refs_1_
  18.7 0.0 collective-permute-done.2.refs_3_
  18.7 0.8 %collective-permute-done.4.refs_5_ = bf16[16,2944]{1,0:T(8,128)(2,1)S(1)} collective-permute-done((bf16[16,2944]{1,0:T(8,128)(2,1)S(1)}, bf16[16,2944]{1,0:T(8,128)(2,1)S(1)}, u32[]{:S(2)}, u32[]{:S(2)}) %collective-permute-start.4) | collective-permute-done | bytes 94240 | tf_op jit(solution)/shard_map/ppermute | solution.py:576
  19.5 0.2 collective-permute-done.6.refs_7_
  19.7 0.7 projection.1
  20.4 1.6 %collective-permute-start.7 = (bf16[64,768]{1,0:T(8,128)(2,1)S(1)}, bf16[64,768]{1,0:T(8,128)(2,1)S(1)}, u32[]{:S(2)}, u32[]{:S(2)}) collective-permute-start(bf16[64,768]{1,0:T(8,128)(2,1)S(1)} %get-tuple-element.51), channel_id=1, source_target_pairs={{0,1},{1,0},{2,3},{3,2},{4,5},{5,4},{6,7},{7,6},{8,9},{9,8},{10,11... | collective-permute-start | bytes 294920 | tf_op jit(solution)/shard_map/ppermute | solution.py:576
  21.9 4.1 %route.1 = (bf16[128,64]{1,0:T(8,128)(2,1)S(1)}, f32[64,768]{1,0:T(8,128)S(1)}, bf16[640,6144]{1,0:T(8,128)(2,1)S(1)}, bf16[32,32]{1,0:T(8,128)(2,1)S(1)}) custom-call(s32[2,8]{1,0:T(2,128)} %bitcast.7, f32[2,8]{1,0:T(2,128)} %bitcast.8, bf16[16,2944]{1,0:T(8,128)(2,1)S(1)} %get-tuple-element.45.refs_0_, bf16[16,2944]{1,0:T(8,128)(2,1)S(1)} %collective-permute-done.refs_1_, ...), custom_call_target="tpu_custom_call" | custom-call | flops 1000000 | bytes 8000000 | tf_op jit(solution)/shard_map/route/pallas_call | solution.py:276
  26.1 0.0 collective-permute-done.7.got_ref
  26.1 0.2 pack.1
  26.3 2.5 %collective-permute-start.8 = (bf16[32,768]{1,0:T(8,128)(2,1)S(1)}, bf16[32,768]{1,0:T(8,128)(2,1)S(1)}, u32[]{:S(2)}, u32[]{:S(2)}) collective-permute-start(bf16[32,768]{1,0:T(8,128)(2,1)S(1)} %get-tuple-element.54), channel_id=1, source_target_pairs={{0,8},{4,12},{8,0},{12,4},{1,9},{5,13},{9,1},{13,5},{2,10},{6,14},... | collective-permute-start | bytes 147464 | tf_op jit(solution)/shard_map/ppermute | solution.py:576
  28.8 1.3 %collective-permute-start.9 = (bf16[32,768]{1,0:T(8,128)(2,1)S(1)}, bf16[32,768]{1,0:T(8,128)(2,1)S(1)}, u32[]{:S(2)}, u32[]{:S(2)}) collective-permute-start(bf16[32,768]{1,0:T(8,128)(2,1)S(1)} %get-tuple-element.55), channel_id=1, source_target_pairs={{0,12},{4,8},{8,4},{12,0},{1,13},{5,9},{9,5},{13,1},{2,14},{6,10},... | collective-permute-start | bytes 147464 | tf_op jit(solution)/shard_map/ppermute | solution.py:576
  30.1 0.0 collective-permute-start.12
  30.1 4.1 %collective-permute-done.12 = bf16[32,768]{1,0:T(8,128)(2,1)S(1)} collective-permute-done((bf16[32,768]{1,0:T(8,128)(2,1)S(1)}, bf16[32,768]{1,0:T(8,128)(2,1)S(1)}, u32[]{:S(2)}, u32[]{:S(2)}) %collective-permute-start.12) | collective-permute-done | bytes 49184 | tf_op jit(solution)/shard_map/ppermute | solution.py:576
  34.2 0.7 collective-permute-start.14
  34.9 0.0 collective-permute-start.13
  34.9 0.0 collective-permute-done.8
  34.9 3.9 %collective-permute-done.14.refs_2_ = bf16[64,768]{1,0:T(8,128)(2,1)S(1)} collective-permute-done((bf16[64,768]{1,0:T(8,128)(2,1)S(1)}, bf16[64,768]{1,0:T(8,128)(2,1)S(1)}, u32[]{:S(2)}, u32[]{:S(2)}) %collective-permute-start.14) | collective-permute-done | bytes 98336 | tf_op jit(solution)/shard_map/ppermute | solution.py:576
  38.8 0.0 collective-permute-start.15
  38.8 0.0 collective-permute-done.9
  38.9 0.8 %collective-permute-start.11 = (bf16[64,768]{1,0:T(8,128)(2,1)S(1)}, bf16[64,768]{1,0:T(8,128)(2,1)S(1)}, u32[]{:S(2)}, u32[]{:S(2)}) collective-permute-start(bf16[64,768]{1,0:T(8,128)(2,1)S(1)} %constant_dynamic-update-slice_fusion.refs_0_), channel_id=1, source_target_pairs={{0,1},{1,0},{2,3},{3,2},{4,5},{5,4},{6,7},{7,6},{8,9},{9,8},{10,11... | collective-permute-start | bytes 294920 | tf_op jit(solution)/shard_map/ppermute | solution.py:576
  39.6 0.2 collective-permute-start.10
  39.8 0.0 collective-permute-done.13.refs_1_
  39.8 0.3 collective-permute-done.15.refs_3_
  40.1 5.9 %experts_first.1 = (f32[1152,64]{1,0:T(8,128)S(1)}, f32[1152,64]{1,0:T(8,128)S(1)}, f32[64,128]{1,0:T(8,128)S(1)}, bf16[512,6144]{1,0:T(8,128)(2,1)S(1)}) custom-call(bf16[64,768]{1,0:T(8,128)(2,1)S(1)} %constant_dynamic-update-slice_fusion.2.refs_0_, bf16[64,768]{1,0:T(8,128)(2,1)S(1)} %collective-permute-done.13.refs_1_, ...), custom_call_target="tpu_custom_call" | custom-call | flops 905969664 | bytes 14155776 | tf_op jit(solution)/shard_map/experts_first/pallas_call | solution.py:405
  46.0 0.0 collective-permute-done.11.rows_ref
  46.1 0.2 collective-permute-start.16
  46.3 1.1 %collective-permute-done.16.refs_3_ = bf16[64,768]{1,0:T(8,128)(2,1)S(1)} collective-permute-done((bf16[64,768]{1,0:T(8,128)(2,1)S(1)}, bf16[64,768]{1,0:T(8,128)(2,1)S(1)}, u32[]{:S(2)}, u32[]{:S(2)}) %collective-permute-start.16) | collective-permute-done | bytes 98336 | tf_op jit(solution)/shard_map/ppermute | solution.py:576
  47.4 5.2 %experts_second.1 = (bf16[64,1152]{1,0:T(8,128)(2,1)S(1)}, bf16[1152,6144]{1,0:T(8,128)(2,1)S(1)}) custom-call(bf16[64,768]{1,0:T(8,128)(2,1)S(1)} %constant_dynamic-update-slice_fusion.refs_0_, bf16[64,768]{1,0:T(8,128)(2,1)S(1)} %collective-permute-done.10.refs_1_, bf16[64,768]{1,0:T(8,128)(2,1)S(1)} %relay.1.refs_2_, ...), custom_call_target="tpu_custom_call" | custom-call | flops 905969664 | bytes 14155776 | tf_op jit(solution)/shard_map/experts_second/pallas_call | solution.py:440
  52.7 1.4 %experts_down.3 = (f32[32,3072]{1,0:T(8,128)S(1)}, bf16[32,3072]{1,0:T(8,128)(2,1)S(1)}) custom-call(bf16[64,1152]{1,0:T(8,128)(2,1)S(1)} %get-tuple-element.65.hidden_ref, bf16[1152,6144]{1,0:T(8,128)(2,1)S(1)} %get-tuple-element.66.weight_ref), custom_call_target="tpu_custom_call" | custom-call | flops 905969664 | bytes 7077888 | tf_op jit(solution)/shard_map/experts_down/pallas_call | solution.py:456
  54.0 1.4 %experts_down.2 = (f32[32,3072]{1,0:T(8,128)S(1)}, bf16[32,3072]{1,0:T(8,128)(2,1)S(1)}) custom-call(bf16[64,1152]{1,0:T(8,128)(2,1)S(1)} %get-tuple-element.65.hidden_ref, bf16[1152,6144]{1,0:T(8,128)(2,1)S(1)} %get-tuple-element.66.weight_ref), custom_call_target="tpu_custom_call" | custom-call | flops 905969664 | bytes 7077888 | tf_op jit(solution)/shard_map/experts_down/pallas_call | solution.py:456
  55.4 0.2 collective-permute-start.18
  55.6 0.4 collective-permute-start.17
  56.0 0.9 %collective-permute-done.18.refs_3_ = bf16[32,3072]{1,0:T(8,128)(2,1)S(1)} collective-permute-done((bf16[32,3072]{1,0:T(8,128)(2,1)S(1)}, bf16[32,3072]{1,0:T(8,128)(2,1)S(1)}, u32[]{:S(2)}, u32[]{:S(2)}) %collective-permute-start.18) | collective-permute-done | bytes 196640 | tf_op jit(solution)/shard_map/ppermute | solution.py:576
  56.9 0.3 collective-permute-done.17.refs_2_
  57.2 0.1 chip_sum.1
  57.3 1.1 %collective-permute-start.23 = (bf16[16,6144]{1,0:T(8,128)(2,1)S(1)}, bf16[16,6144]{1,0:T(8,128)(2,1)S(1)}, u32[]{:S(2)}, u32[]{:S(2)}) collective-permute-start(bf16[16,6144]{1,0:T(8,128)(2,1)S(1)} %get-tuple-element.78), channel_id=1, source_target_pairs={{0,1},{1,0},{2,3},{3,2},{4,5},{5,4},{6,7},{7,6},{8,9},{9,8},{10,11... | collective-permute-start | bytes 589832 | tf_op jit(solution)/shard_map/ppermute | solution.py:576
  58.4 0.7 collective-permute-start.19
  59.1 2.4 %collective-permute-start.20 = (bf16[16,768]{1,0:T(8,128)(2,1)S(1)}, bf16[16,768]{1,0:T(8,128)(2,1)S(1)}, u32[]{:S(2)}, u32[]{:S(2)}) collective-permute-start(bf16[16,768]{1,0:T(8,128)(2,1)S(1)} %get-tuple-element.74), channel_id=1, source_target_pairs={{0,8},{4,12},{8,0},{12,4},{1,9},{5,13},{9,1},{13,5},{2,10},{6,14},... | collective-permute-start | bytes 73736 | tf_op jit(solution)/shard_map/ppermute | solution.py:576
  61.5 1.3 %collective-permute-start.21 = (bf16[16,768]{1,0:T(8,128)(2,1)S(1)}, bf16[16,768]{1,0:T(8,128)(2,1)S(1)}, u32[]{:S(2)}, u32[]{:S(2)}) collective-permute-start(bf16[16,768]{1,0:T(8,128)(2,1)S(1)} %get-tuple-element.75), channel_id=1, source_target_pairs={{0,12},{4,8},{8,4},{12,0},{1,13},{5,9},{9,5},{13,1},{2,14},{6,10},... | collective-permute-start | bytes 73736 | tf_op jit(solution)/shard_map/ppermute | solution.py:576
  62.8 0.0 collective-permute-done.19.refs_1_
  62.8 1.2 %collective-permute-done.20.refs_2_ = bf16[16,768]{1,0:T(8,128)(2,1)S(1)} collective-permute-done((bf16[16,768]{1,0:T(8,128)(2,1)S(1)}, bf16[16,768]{1,0:T(8,128)(2,1)S(1)}, u32[]{:S(2)}, u32[]{:S(2)}) %collective-permute-start.20) | collective-permute-done | bytes 24608 | tf_op jit(solution)/shard_map/ppermute | solution.py:576
  64.0 3.2 %collective-permute-done.21.refs_3_ = bf16[16,768]{1,0:T(8,128)(2,1)S(1)} collective-permute-done((bf16[16,768]{1,0:T(8,128)(2,1)S(1)}, bf16[16,768]{1,0:T(8,128)(2,1)S(1)}, u32[]{:S(2)}, u32[]{:S(2)}) %collective-permute-start.21) | collective-permute-done | bytes 24608 | tf_op jit(solution)/shard_map/ppermute | solution.py:576
  67.1 0.1 collective-permute-start.22
  67.2 0.0 collective-permute-done.23.got_ref
  67.2 0.1 pair_sum.1
  67.3 0.1 collective-permute-start.24
  67.4 1.8 %collective-permute-start.25 = (bf16[8,3072]{1,0:T(8,128)(2,1)S(1)}, bf16[8,3072]{1,0:T(8,128)(2,1)S(1)}, u32[]{:S(2)}, u32[]{:S(2)}) collective-permute-start(bf16[8,3072]{1,0:T(8,128)(2,1)S(1)} %get-tuple-element.81), channel_id=1, source_target_pairs={{0,8},{4,12},{8,0},{12,4},{1,9},{5,13},{9,1},{13,5},{2,10},{6,14},... | collective-permute-start | bytes 147464 | tf_op jit(solution)/shard_map/ppermute | solution.py:576
  69.2 2.6 %collective-permute-start.26 = (bf16[8,3072]{1,0:T(8,128)(2,1)S(1)}, bf16[8,3072]{1,0:T(8,128)(2,1)S(1)}, u32[]{:S(2)}, u32[]{:S(2)}) collective-permute-start(bf16[8,3072]{1,0:T(8,128)(2,1)S(1)} %get-tuple-element.82), channel_id=1, source_target_pairs={{0,12},{4,8},{8,4},{12,0},{1,13},{5,9},{9,5},{13,1},{2,14},{6,10},... | collective-permute-start | bytes 147464 | tf_op jit(solution)/shard_map/ppermute | solution.py:576
  71.8 0.9 %own_rows.1.combined_ref = f32[8,6144]{1,0:T(8,128)S(1)} custom-call(bf16[8,6144]{1,0:T(8,128)(2,1)} %residual_ref.3, bf16[16,768]{1,0:T(8,128)(2,1)S(1)} %get-tuple-element.72.refs_0_, bf16[16,768]{1,0:T(8,128)(2,1)S(1)} %collective-permute-done.19.refs_1_, bf16[16,768]{1,0:T(8,128)(2,1)S(1)} %collective-permute-done.20.refs_2_, ...), custom_call_target="tpu_custom_call" | custom-call | flops 1000000 | bytes 1000000 | tf_op jit(solution)/shard_map/own_rows/pallas_call | solution.py:542
  72.8 1.7 %collective-permute-done.25.refs_2_ = bf16[8,3072]{1,0:T(8,128)(2,1)S(1)} collective-permute-done((bf16[8,3072]{1,0:T(8,128)(2,1)S(1)}, bf16[8,3072]{1,0:T(8,128)(2,1)S(1)}, u32[]{:S(2)}, u32[]{:S(2)}) %collective-permute-start.25) | collective-permute-done | bytes 49184 | tf_op jit(solution)/shard_map/ppermute | solution.py:576
  74.5 0.7 collective-permute-done.26.refs_3_
  75.2 0.8 %finish.1 = bf16[8,6144]{1,0:T(8,128)(2,1)} custom-call(f32[8,6144]{1,0:T(8,128)S(1)} %own_rows.1.combined_ref, bf16[32,32]{1,0:T(8,128)(2,1)S(1)} %get-tuple-element.76.weighting_ref, bf16[8,3072]{1,0:T(8,128)(2,1)S(1)} %get-tuple-element.79.refs_0_, bf16[8,3072]{1,0:T(8,128)(2,1)S(1)} %collective-permute-done.24.refs_1_, ...), custom_call_target="tpu_custom_call" | custom-call | tf_op jit(solution)/shard_map/finish/pallas_call | solution.py:565
  (9 shorter events, 0.0 us)
Async XLA Ops:
  5.0 10.8 %collective-permute-start.1 = (bf16[16,2944]{1,0:T(8,128)(2,1)S(1)}, bf16[16,2944]{1,0:T(8,128)(2,1)S(1)}, u32[]{:S(2)}, u32[]{:S(2)}) collective-permute-start(bf16[16,2944]{1,0:T(8,128)(2,1)S(1)} %get-tuple-element.46), channel_id=1, source_target_pairs={{0,4},{4,0},{8,12},{12,8},{1,5},{5,1},{9,13},{13,9},{2,6},{6,2},{1... | collective-permute-start | bytes 282632 | tf_op jit(solution)/shard_map/ppermute | solution.py:576
  8.1 10.1 %collective-permute-start.3 = (bf16[16,2944]{1,0:T(8,128)(2,1)S(1)}, bf16[16,2944]{1,0:T(8,128)(2,1)S(1)}, u32[]{:S(2)}, u32[]{:S(2)}) collective-permute-start(bf16[16,2944]{1,0:T(8,128)(2,1)S(1)} %get-tuple-element.47), channel_id=1, source_target_pairs={{0,8},{4,12},{8,0},{12,4},{1,9},{5,13},{9,1},{13,5},{2,10},{6,14},... | collective-permute-start | bytes 282632 | tf_op jit(solution)/shard_map/ppermute | solution.py:576
  10.7 7.5 %collective-permute-start.5 = (bf16[16,2944]{1,0:T(8,128)(2,1)S(1)}, bf16[16,2944]{1,0:T(8,128)(2,1)S(1)}, u32[]{:S(2)}, u32[]{:S(2)}) collective-permute-start(bf16[16,2944]{1,0:T(8,128)(2,1)S(1)} %get-tuple-element.48), channel_id=1, source_target_pairs={{0,12},{4,8},{8,4},{12,0},{1,13},{5,9},{9,5},{13,1},{2,14},{6,10},... | collective-permute-start | bytes 282632 | tf_op jit(solution)/shard_map/ppermute | solution.py:576
  15.7 3.0 %collective-permute-start = (bf16[16,2944]{1,0:T(8,128)(2,1)S(1)}, bf16[16,2944]{1,0:T(8,128)(2,1)S(1)}, u32[]{:S(2)}, u32[]{:S(2)}) collective-permute-start(bf16[16,2944]{1,0:T(8,128)(2,1)S(1)} %get-tuple-element.45.refs_0_), channel_id=1, source_target_pairs={{0,2},{2,0},{1,3},{3,1},{4,6},{6,4},{5,7},{7,5},{8,10},{10,8},{9,1... | collective-permute-start | bytes 282632 | tf_op jit(solution)/shard_map/ppermute | solution.py:576
  15.8 2.9 %collective-permute-start.2 = (bf16[16,2944]{1,0:T(8,128)(2,1)S(1)}, bf16[16,2944]{1,0:T(8,128)(2,1)S(1)}, u32[]{:S(2)}, u32[]{:S(2)}) collective-permute-start(bf16[16,2944]{1,0:T(8,128)(2,1)S(1)} %collective-permute-done.1.refs_2_), channel_id=1, source_target_pairs={{0,2},{2,0},{1,3},{3,1},{4,6},{6,4},{5,7},{7,5},{8,10},{10,8},{9,1... | collective-permute-start | bytes 282632 | tf_op jit(solution)/shard_map/ppermute | solution.py:576
  18.2 1.3 %collective-permute-start.4 = (bf16[16,2944]{1,0:T(8,128)(2,1)S(1)}, bf16[16,2944]{1,0:T(8,128)(2,1)S(1)}, u32[]{:S(2)}, u32[]{:S(2)}) collective-permute-start(bf16[16,2944]{1,0:T(8,128)(2,1)S(1)} %collective-permute-done.3.refs_4_), channel_id=1, source_target_pairs={{0,2},{2,0},{1,3},{3,1},{4,6},{6,4},{5,7},{7,5},{8,10},{10,8},{9,1... | collective-permute-start | bytes 282632 | tf_op jit(solution)/shard_map/ppermute | solution.py:576
  18.2 1.4 %collective-permute-start.6 = (bf16[16,2944]{1,0:T(8,128)(2,1)S(1)}, bf16[16,2944]{1,0:T(8,128)(2,1)S(1)}, u32[]{:S(2)}, u32[]{:S(2)}) collective-permute-start(bf16[16,2944]{1,0:T(8,128)(2,1)S(1)} %collective-permute-done.5.refs_6_), channel_id=1, source_target_pairs={{0,2},{2,0},{1,3},{3,1},{4,6},{6,4},{5,7},{7,5},{8,10},{10,8},{9,1... | collective-permute-start | bytes 282632 | tf_op jit(solution)/shard_map/ppermute | solution.py:576
  20.4 5.7 %collective-permute-start.7 = (bf16[64,768]{1,0:T(8,128)(2,1)S(1)}, bf16[64,768]{1,0:T(8,128)(2,1)S(1)}, u32[]{:S(2)}, u32[]{:S(2)}) collective-permute-start(bf16[64,768]{1,0:T(8,128)(2,1)S(1)} %get-tuple-element.51), channel_id=1, source_target_pairs={{0,1},{1,0},{2,3},{3,2},{4,5},{5,4},{6,7},{7,6},{8,9},{9,8},{10,11... | collective-permute-start | bytes 294920 | tf_op jit(solution)/shard_map/ppermute | solution.py:576
  26.3 8.7 %collective-permute-start.8 = (bf16[32,768]{1,0:T(8,128)(2,1)S(1)}, bf16[32,768]{1,0:T(8,128)(2,1)S(1)}, u32[]{:S(2)}, u32[]{:S(2)}) collective-permute-start(bf16[32,768]{1,0:T(8,128)(2,1)S(1)} %get-tuple-element.54), channel_id=1, source_target_pairs={{0,8},{4,12},{8,0},{12,4},{1,9},{5,13},{9,1},{13,5},{2,10},{6,14},... | collective-permute-start | bytes 147464 | tf_op jit(solution)/shard_map/ppermute | solution.py:576
  28.8 10.1 %collective-permute-start.9 = (bf16[32,768]{1,0:T(8,128)(2,1)S(1)}, bf16[32,768]{1,0:T(8,128)(2,1)S(1)}, u32[]{:S(2)}, u32[]{:S(2)}) collective-permute-start(bf16[32,768]{1,0:T(8,128)(2,1)S(1)} %get-tuple-element.55), channel_id=1, source_target_pairs={{0,12},{4,8},{8,4},{12,0},{1,13},{5,9},{9,5},{13,1},{2,14},{6,10},... | collective-permute-start | bytes 147464 | tf_op jit(solution)/shard_map/ppermute | solution.py:576
  30.1 4.1 %collective-permute-start.12 = (bf16[32,768]{1,0:T(8,128)(2,1)S(1)}, bf16[32,768]{1,0:T(8,128)(2,1)S(1)}, u32[]{:S(2)}, u32[]{:S(2)}) collective-permute-start(bf16[32,768]{1,0:T(8,128)(2,1)S(1)} %get-tuple-element.57), channel_id=1, source_target_pairs={{0,4},{4,0},{8,12},{12,8},{1,5},{5,1},{9,13},{13,9},{2,6},{6,2},{1... | collective-permute-start | bytes 147464 | tf_op jit(solution)/shard_map/ppermute | solution.py:576
  34.2 4.6 %collective-permute-start.14 = (bf16[64,768]{1,0:T(8,128)(2,1)S(1)}, bf16[64,768]{1,0:T(8,128)(2,1)S(1)}, u32[]{:S(2)}, u32[]{:S(2)}) collective-permute-start(bf16[64,768]{1,0:T(8,128)(2,1)S(1)} %constant_dynamic-update-slice_fusion.2.refs_0_), channel_id=1, source_target_pairs={{0,1},{1,0},{2,3},{3,2},{4,5},{5,4},{6,7},{7,6},{8,9},{9,8},{10,11... | collective-permute-start | bytes 294920 | tf_op jit(solution)/shard_map/ppermute | solution.py:576
  34.9 4.9 %collective-permute-start.13 = (bf16[64,768]{1,0:T(8,128)(2,1)S(1)}, bf16[64,768]{1,0:T(8,128)(2,1)S(1)}, u32[]{:S(2)}, u32[]{:S(2)}) collective-permute-start(bf16[64,768]{1,0:T(8,128)(2,1)S(1)} %constant_dynamic-update-slice_fusion.2.refs_0_), channel_id=1, source_target_pairs={{0,2},{2,0},{1,3},{3,1},{4,6},{6,4},{5,7},{7,5},{8,10},{10,8},{9,1... | collective-permute-start | bytes 294920 | tf_op jit(solution)/shard_map/ppermute | solution.py:576
  38.8 1.3 %collective-permute-start.15 = (bf16[64,768]{1,0:T(8,128)(2,1)S(1)}, bf16[64,768]{1,0:T(8,128)(2,1)S(1)}, u32[]{:S(2)}, u32[]{:S(2)}) collective-permute-start(bf16[64,768]{1,0:T(8,128)(2,1)S(1)} %collective-permute-done.14.refs_2_), channel_id=1, source_target_pairs={{0,2},{2,0},{1,3},{3,1},{4,6},{6,4},{5,7},{7,5},{8,10},{10,8},{9,1... | collective-permute-start | bytes 294920 | tf_op jit(solution)/shard_map/ppermute | solution.py:576
  38.9 7.2 %collective-permute-start.11 = (bf16[64,768]{1,0:T(8,128)(2,1)S(1)}, bf16[64,768]{1,0:T(8,128)(2,1)S(1)}, u32[]{:S(2)}, u32[]{:S(2)}) collective-permute-start(bf16[64,768]{1,0:T(8,128)(2,1)S(1)} %constant_dynamic-update-slice_fusion.refs_0_), channel_id=1, source_target_pairs={{0,1},{1,0},{2,3},{3,2},{4,5},{5,4},{6,7},{7,6},{8,9},{9,8},{10,11... | collective-permute-start | bytes 294920 | tf_op jit(solution)/shard_map/ppermute | solution.py:576
  39.6 6.7 %collective-permute-start.10 = (bf16[64,768]{1,0:T(8,128)(2,1)S(1)}, bf16[64,768]{1,0:T(8,128)(2,1)S(1)}, u32[]{:S(2)}, u32[]{:S(2)}) collective-permute-start(bf16[64,768]{1,0:T(8,128)(2,1)S(1)} %constant_dynamic-update-slice_fusion.refs_0_), channel_id=1, source_target_pairs={{0,2},{2,0},{1,3},{3,1},{4,6},{6,4},{5,7},{7,5},{8,10},{10,8},{9,1... | collective-permute-start | bytes 294920 | tf_op jit(solution)/shard_map/ppermute | solution.py:576
  46.1 1.4 %collective-permute-start.16 = (bf16[64,768]{1,0:T(8,128)(2,1)S(1)}, bf16[64,768]{1,0:T(8,128)(2,1)S(1)}, u32[]{:S(2)}, u32[]{:S(2)}) collective-permute-start(bf16[64,768]{1,0:T(8,128)(2,1)S(1)} %relay.1.refs_2_), channel_id=1, source_target_pairs={{0,2},{2,0},{1,3},{3,1},{4,6},{6,4},{5,7},{7,5},{8,10},{10,8},{9,1... | collective-permute-start | bytes 294920 | tf_op jit(solution)/shard_map/ppermute | solution.py:576
  55.4 1.5 %collective-permute-start.18 = (bf16[32,3072]{1,0:T(8,128)(2,1)S(1)}, bf16[32,3072]{1,0:T(8,128)(2,1)S(1)}, u32[]{:S(2)}, u32[]{:S(2)}) collective-permute-start(bf16[32,3072]{1,0:T(8,128)(2,1)S(1)} %get-tuple-element.70), channel_id=1, source_target_pairs={{0,2},{2,0},{1,3},{3,1},{4,6},{6,4},{5,7},{7,5},{8,10},{10,8},{9,1... | collective-permute-start | bytes 589832 | tf_op jit(solution)/shard_map/ppermute | solution.py:576
  55.6 1.6 %collective-permute-start.17 = (bf16[32,3072]{1,0:T(8,128)(2,1)S(1)}, bf16[32,3072]{1,0:T(8,128)(2,1)S(1)}, u32[]{:S(2)}, u32[]{:S(2)}) collective-permute-start(bf16[32,3072]{1,0:T(8,128)(2,1)S(1)} %get-tuple-element.69), channel_id=1, source_target_pairs={{0,2},{2,0},{1,3},{3,1},{4,6},{6,4},{5,7},{7,5},{8,10},{10,8},{9,1... | collective-permute-start | bytes 589832 | tf_op jit(solution)/shard_map/ppermute | solution.py:576
  57.3 10.0 %collective-permute-start.23 = (bf16[16,6144]{1,0:T(8,128)(2,1)S(1)}, bf16[16,6144]{1,0:T(8,128)(2,1)S(1)}, u32[]{:S(2)}, u32[]{:S(2)}) collective-permute-start(bf16[16,6144]{1,0:T(8,128)(2,1)S(1)} %get-tuple-element.78), channel_id=1, source_target_pairs={{0,1},{1,0},{2,3},{3,2},{4,5},{5,4},{6,7},{7,6},{8,9},{9,8},{10,11... | collective-permute-start | bytes 589832 | tf_op jit(solution)/shard_map/ppermute | solution.py:576
  58.4 4.4 %collective-permute-start.19 = (bf16[16,768]{1,0:T(8,128)(2,1)S(1)}, bf16[16,768]{1,0:T(8,128)(2,1)S(1)}, u32[]{:S(2)}, u32[]{:S(2)}) collective-permute-start(bf16[16,768]{1,0:T(8,128)(2,1)S(1)} %get-tuple-element.73), channel_id=1, source_target_pairs={{0,4},{4,0},{8,12},{12,8},{1,5},{5,1},{9,13},{13,9},{2,6},{6,2},{1... | collective-permute-start | bytes 73736 | tf_op jit(solution)/shard_map/ppermute | solution.py:576
  59.1 4.8 %collective-permute-start.20 = (bf16[16,768]{1,0:T(8,128)(2,1)S(1)}, bf16[16,768]{1,0:T(8,128)(2,1)S(1)}, u32[]{:S(2)}, u32[]{:S(2)}) collective-permute-start(bf16[16,768]{1,0:T(8,128)(2,1)S(1)} %get-tuple-element.74), channel_id=1, source_target_pairs={{0,8},{4,12},{8,0},{12,4},{1,9},{5,13},{9,1},{13,5},{2,10},{6,14},... | collective-permute-start | bytes 73736 | tf_op jit(solution)/shard_map/ppermute | solution.py:576
  61.5 5.6 %collective-permute-start.21 = (bf16[16,768]{1,0:T(8,128)(2,1)S(1)}, bf16[16,768]{1,0:T(8,128)(2,1)S(1)}, u32[]{:S(2)}, u32[]{:S(2)}) collective-permute-start(bf16[16,768]{1,0:T(8,128)(2,1)S(1)} %get-tuple-element.75), channel_id=1, source_target_pairs={{0,12},{4,8},{8,4},{12,0},{1,13},{5,9},{9,5},{13,1},{2,14},{6,10},... | collective-permute-start | bytes 73736 | tf_op jit(solution)/shard_map/ppermute | solution.py:576
  67.1 4.7 %collective-permute-start.22 = (bf16[64,768]{1,0:T(8,128)(2,1)S(1)}, bf16[64,768]{1,0:T(8,128)(2,1)S(1)}, u32[]{:S(2)}, u32[]{:S(2)}) collective-permute-start(bf16[64,768]{1,0:T(8,128)(2,1)S(1)} %pad_maximum_fusion), channel_id=1, source_target_pairs={{0,2},{2,0},{1,3},{3,1},{4,6},{6,4},{5,7},{7,5},{8,10},{10,8},{9,1... | collective-permute-start | bytes 294920 | tf_op jit(solution)/shard_map/ppermute | solution.py:576
  67.3 5.4 %collective-permute-start.24 = (bf16[8,3072]{1,0:T(8,128)(2,1)S(1)}, bf16[8,3072]{1,0:T(8,128)(2,1)S(1)}, u32[]{:S(2)}, u32[]{:S(2)}) collective-permute-start(bf16[8,3072]{1,0:T(8,128)(2,1)S(1)} %get-tuple-element.80), channel_id=1, source_target_pairs={{0,4},{4,0},{8,12},{12,8},{1,5},{5,1},{9,13},{13,9},{2,6},{6,2},{1... | collective-permute-start | bytes 147464 | tf_op jit(solution)/shard_map/ppermute | solution.py:576
  67.4 7.1 %collective-permute-start.25 = (bf16[8,3072]{1,0:T(8,128)(2,1)S(1)}, bf16[8,3072]{1,0:T(8,128)(2,1)S(1)}, u32[]{:S(2)}, u32[]{:S(2)}) collective-permute-start(bf16[8,3072]{1,0:T(8,128)(2,1)S(1)} %get-tuple-element.81), channel_id=1, source_target_pairs={{0,8},{4,12},{8,0},{12,4},{1,9},{5,13},{9,1},{13,5},{2,10},{6,14},... | collective-permute-start | bytes 147464 | tf_op jit(solution)/shard_map/ppermute | solution.py:576
  69.2 5.9 %collective-permute-start.26 = (bf16[8,3072]{1,0:T(8,128)(2,1)S(1)}, bf16[8,3072]{1,0:T(8,128)(2,1)S(1)}, u32[]{:S(2)}, u32[]{:S(2)}) collective-permute-start(bf16[8,3072]{1,0:T(8,128)(2,1)S(1)} %get-tuple-element.82), channel_id=1, source_target_pairs={{0,12},{4,8},{8,4},{12,0},{1,13},{5,9},{9,5},{13,1},{2,14},{6,10},... | collective-permute-start | bytes 147464 | tf_op jit(solution)/shard_map/ppermute | solution.py:576

commit v6 on v5

--- a/solution.py
+++ b/solution.py
@@ -41,20 +41,13 @@
 
 
 def attend_kernel(positions, steps, decay_ref, ids_ref, q_ref, k_ref, v_ref, gain_ref, s_ref, residual_ref, *refs):
-    sources, outs, targets, sem = refs[:2], refs[2:-3], refs[-3:-1], refs[-1]
+    outs = refs
     requests, heads, size, _ = s_ref.shape
     rows = q_ref.shape[0]
     step = pl.program_id(0)
     first = step * heads
-    copies = [
-        pltpu.make_async_copy(source, target, sem.at[i])
-        for i, (source, target) in enumerate(zip(sources, targets))
-    ]
-
     @pl.when(step == 0)
     def _():
-        for copy in copies:
-            copy.start()
         width = steps * heads * size
         lanes = ID_LANES
         row = lax.broadcasted_iota(jnp.int32, (rows, lanes), 0)
@@ -102,20 +95,15 @@
         for out in outs:
             out[:, pl.ds(pl.multiple_of((first + i) * size, size), size)] = normal
 
-    @pl.when(step == steps - 1)
-    def _():
-        for copy in copies:
-            copy.wait()
-
 
 def attend(
-    queries, key_rows, value_rows, states, decay_rates, head_gain, ids, residual, weight, norm_gain, experts
+    queries, key_rows, value_rows, states, decay_rates, head_gain, ids, residual, columns, experts
 ):
     requests, heads, size, _ = states.shape
     rows = queries.shape[0]
     step = 4 if heads % 4 == 0 else 1
     wide = pl.BlockSpec((rows, step * size), lambda i: (0, i))
-    message = (rows, queries.shape[1] + ID_LANES + weight.shape[1])
+    message = (rows, queries.shape[1] + ID_LANES + columns)
     return pl.pallas_call(
         functools.partial(attend_kernel, rows // requests, heads // step),
         grid=(heads // step,),
@@ -128,50 +116,44 @@
             pl.BlockSpec((1, step * size), lambda i: (0, i)),
             pl.BlockSpec((requests, step, size, size), lambda i: (0, i, 0, 0)),
             pl.BlockSpec(residual.shape, lambda i: (0, 0)),
-            ANY,
-            ANY,
         ],
-        out_specs=[pl.BlockSpec(message, lambda i: (0, 0))] * experts + [VMEM] * 2,
-        out_shape=[jax.ShapeDtypeStruct(message, BF16)] * experts
-        + [pltpu.VMEM(a.shape, a.dtype) for a in (weight, norm_gain)],
-        scratch_shapes=[pltpu.SemaphoreType.DMA((2,))],
+        out_specs=[pl.BlockSpec(message, lambda i: (0, 0))] * experts,
+        out_shape=[jax.ShapeDtypeStruct(message, BF16)] * experts,
         compiler_params=limits(8),
         name="attention",
     )(
         *in_hbm(
             decay_rates, ids, queries, key_rows, value_rows, head_gain.reshape(1, -1), states, residual,
-            weight, norm_gain,
         )
     )
 
 
-def load_kernel(rows_hbm, weight_hbm, rows_ref, weight_ref, sem):
+def load_kernel(count, rows_hbm, *refs):
+    sources, rows_ref, targets, sem = refs[:count], refs[count], refs[count + 1 : -1], refs[-1]
     copies = [
-        pltpu.make_async_copy(weight_hbm, weight_ref, sem.at[0]),
-        pltpu.make_async_copy(rows_hbm, rows_ref, sem.at[1]),
+        pltpu.make_async_copy(source, target, sem.at[i])
+        for i, (source, target) in enumerate(zip(sources, targets))
     ]
+    copies.append(pltpu.make_async_copy(rows_hbm, rows_ref, sem.at[count]))
     for copy in copies:
         copy.start()
     for copy in copies:
         copy.wait()
 
 
-def load(rows, weight):
-    return pl.pallas_call(
-        load_kernel,
-        in_specs=[ANY, ANY],
-        out_specs=[VMEM, VMEM],
-        out_shape=[
-            jax.ShapeDtypeStruct(rows.shape, rows.dtype),
-            pltpu.VMEM(weight.shape, weight.dtype),
-        ],
-        scratch_shapes=[pltpu.SemaphoreType.DMA((2,))],
+def load(rows, weights):
+    size = sum(w.size * w.dtype.itemsize for w in weights)
+    return pl.pallas_call(
+        functools.partial(load_kernel, len(weights)),
+        in_specs=[ANY] * (1 + len(weights)),
+        out_specs=[VMEM] * (1 + len(weights)),
+        out_shape=[jax.ShapeDtypeStruct(rows.shape, rows.dtype)]
+        + [pltpu.VMEM(w.shape, w.dtype) for w in weights],
+        scratch_shapes=[pltpu.SemaphoreType.DMA((1 + len(weights),))],
         compiler_params=limits(1),
-        cost_estimate=pl.CostEstimate(
-            flops=0, bytes_accessed=weight.size * weight.dtype.itemsize, transcendentals=0
-        ),
+        cost_estimate=pl.CostEstimate(flops=0, bytes_accessed=size, transcendentals=0),
         name="load",
-    )(rows, *in_hbm(weight))
+    )(rows, *in_hbm(*weights))
 
 
 def project_kernel(*refs):
@@ -419,20 +401,20 @@
     )(*pieces, gain, gate, up_first, *in_hbm(up_part))
 
 
-def relay_kernel(rows_ref, after_ref, out_ref):
-    out_ref[...] = rows_ref[...]
-
-
-def relay(rows, after):
+def relay_kernel(rows_ref, *refs):
+    refs[-1][...] = rows_ref[...]
+
+
+def relay(rows, *after):
     return pl.pallas_call(
         relay_kernel,
-        in_specs=[VMEM] * 2,
+        in_specs=[VMEM] * (1 + len(after)),
         out_specs=VMEM,
         out_shape=jax.ShapeDtypeStruct(rows.shape, rows.dtype),
         compiler_params=limits(2),
         cost_estimate=cost(0, 10**5),
         name="relay",
-    )(rows, after)
+    )(rows, *after)
 
 
 def expert_second(pieces, gain, gate, up_first, up_rest, sums, down_part, count):
@@ -468,30 +450,64 @@
 
 
 def chip_sum_kernel(count, *refs):
-    mine, got, own_ref = refs[:count], refs[count : 2 * count], refs[2 * count]
-    keep_ref, send_ref, *outs = refs[2 * count + 1 :]
+    mine, got = refs[:count], refs[count : 2 * count]
+    keep_ref, send_ref = refs[2 * count :]
     rows = keep_ref.shape[0]
     width = mine[0].shape[1]
     for g in range(count):
         at = slice(g * width, (g + 1) * width)
         keep_ref[:, at] = mine[g][:rows] + got[g][:rows].astype(F32)
         send_ref[:, at] = (mine[g][rows:] + got[g][rows:].astype(F32)).astype(BF16)
+
+
+def chip_sum(mine, got):
+    rows, width = mine[0].shape
+    shape = (rows // 2, width * len(mine))
+    return pl.pallas_call(
+        functools.partial(chip_sum_kernel, len(mine)),
+        in_specs=[VMEM] * (2 * len(mine)),
+        out_specs=[VMEM] * 2,
+        out_shape=[jax.ShapeDtypeStruct(shape, F32), jax.ShapeDtypeStruct(shape, BF16)],
+        compiler_params=limits(4),
+        name="chip_sum",
+    )(*mine, *got)
+
+
+def cut_kernel(own_ref, after_ref, *outs):
     for d, out in enumerate(outs):
         out[...] = own_ref[d]
 
 
-def chip_sum(mine, got, own):
-    rows, width = mine[0].shape
-    shape = (rows // 2, width * len(mine))
-    return pl.pallas_call(
-        functools.partial(chip_sum_kernel, len(mine)),
-        in_specs=[VMEM] * (2 * len(mine) + 1),
-        out_specs=[VMEM] * (2 + own.shape[0]),
-        out_shape=[jax.ShapeDtypeStruct(shape, F32), jax.ShapeDtypeStruct(shape, BF16)]
-        + [jax.ShapeDtypeStruct(own.shape[1:], BF16)] * own.shape[0],
-        compiler_params=limits(4),
-        name="chip_sum",
-    )(*mine, *got, own)
+def cut(own, after):
+    return pl.pallas_call(
+        cut_kernel,
+        in_specs=[VMEM] * 2,
+        out_specs=[VMEM] * own.shape[0],
+        out_shape=[jax.ShapeDtypeStruct(own.shape[1:], own.dtype)] * own.shape[0],
+        compiler_params=limits(2),
+        cost_estimate=cost(0, 10**5),
+        name="cut",
+    )(own, after)
+
+
+def join_kernel(*refs):
+    pieces, out_ref = refs[:-2], refs[-1]
+    rows = pieces[0].shape[0]
+    for d, piece in enumerate(pieces):
+        out_ref[d * rows : (d + 1) * rows] = piece[...]
+
+
+def join(pieces, after):
+    rows, columns = pieces[0].shape
+    return pl.pallas_call(
+        join_kernel,
+        in_specs=[VMEM] * (len(pieces) + 1),
+        out_specs=VMEM,
+        out_shape=jax.ShapeDtypeStruct((rows * len(pieces), columns), pieces[0].dtype),
+        compiler_params=limits(2),
+        cost_estimate=cost(0, 10**5),
+        name="join",
+    )(*pieces, after)
 
 
 def pair_sum_kernel(capacity, keep_ref, got_ref, *refs):
@@ -600,23 +616,26 @@
     count = 2 * experts * capacity
     ids, weights = expert_ids.T, gate_weights.T
 
-    *messages, weight_here, gain_here = attend(
-        queries, key_rows, value_rows, states, decay_rates, head_gain, ids, residual,
-        out_weight, norm_gain.reshape(1, -1), experts,
-    )
-    messages[0], gate_here = load(messages[0], expert_gate)
+    messages = attend(
+        queries, key_rows, value_rows, states, decay_rates, head_gain, ids, residual, columns, experts
+    )
+    messages = list(messages)
+    messages[0], weight_here, gain_here, gate_here = load(
+        messages[0], [out_weight, norm_gain.reshape(1, -1), expert_gate]
+    )
     pieces = []
     for d, message in enumerate(messages):
         message = swap(message, "expert", d)
         pieces += [message, swap(message, "half", 1)]
 
     keep, send = project(pieces, weight_here)
-    first = expert_up.shape[0] // 256 * 128 + 128
+    first = expert_up.shape[0] // 256 * 128
     choose, residual_part, up_first, weighting = route(
         ids, weights, pieces, keep, columns, capacity, expert_up, first
     )
     *packed, own = pack(keep, swap(send, "pair", 1), residual_part, choose, experts)
 
+    packed[2:] = [relay(rows, packed[1]) for rows in packed[2:]]
     arrived = [swap(rows, "expert", d) for d, rows in enumerate(packed)]
     near = [jnp.concatenate(arrived[d : d + 2], axis=0) for d in range(0, experts, 2)]
     far = [swap(rows, "pair", 1) for rows in near]
@@ -637,10 +656,10 @@
         terms, send = expert_down(hidden, down_here, g * width, width, count)
         mine.append(terms)
         got.append(swap(send, "half", 1))
-    keep, send, *own = chip_sum(mine, got, own)
+    keep, send = chip_sum(mine, got)
+    own = [swap(rows, "expert", d) for d, rows in enumerate(cut(own, keep))]
     terms = pair_sum(keep, swap(send, "pair", 1), capacity, experts)
-    own = [swap(rows, "expert", d) for d, rows in enumerate(own)]
-    cross = swap(jnp.concatenate(own, axis=0), "half", 1)
+    cross = swap(join(own, terms[0]), "half", 1)
     combined = own_rows(residual, own, cross)
     back = [swap(term, "expert", d) for d, term in enumerate(terms)]
     return finish(combined, weighting, back)

time: 76.3 us -> 77.1 us (1.010)
  waiting for transfers between devices: 20.3 us -> 14.7 us
  Pallas kernels: 30.8 us -> 35.8 us
  starting transfers between devices: 24.7 us -> 26.2 us
    ppermute x27, waiting for transfers between devices: 20.3 us -> 14.7 us  [swap(): lax.ppermute(x, axis, [(i, i ^ by) for i in range(lax.axis_size(axis))])]
    pallas_call x1, Pallas kernels: 5.23 us -> 8.06 us  [expert_second(): pl.pallas_call(functools.partial(expert_second_kernel, count), in_specs=[...]
    pallas_call x1, Pallas kernels: 5.89 us -> 7.79 us  [expert_first(): pl.pallas_call(functools.partial(expert_first_kernel, count), in_specs=[V...]
    ppermute x27, starting transfers between devices: 24.7 us -> 26.2 us  [swap(): lax.ppermute(x, axis, [(i, i ^ by) for i in range(lax.axis_size(axis))])]
    pallas_call x2 -> x6, Pallas kernels: 5.05 us -> 6.07 us  [the longest x1 6.03 us: load(): pl.pallas_call(functools.partial(load_kernel, len(weights)), in_specs=[AN...]
  transfers between devices with their start and end apart: 27 -> 27, of which waited for: 13 -> 13; matrix products, arithmetic and copies ran while one was open for 0% -> 0% of each run, Pallas kernels for 21% -> 24%
where the time goes in v6:
time: 77.1 us; the launch traced here: 76.8 us
  Pallas kernels  35.8 us (46%)
  starting transfers between devices  26.2 us (34%)
  waiting for transfers between devices  14.7 us (19%)
    ppermute x27, starting transfers between devices, swap(): lax.ppermute(x, axis, [(i, i ^ by) for i in range(lax.axis_size(axis))])  26.2 us
    ppermute x27, waiting for transfers between devices, swap(): lax.ppermute(x, axis, [(i, i ^ by) for i in range(lax.axis_size(axis))])  14.7 us
    pallas_call x1, Pallas kernels, expert_second(): pl.pallas_call(functools.partial(expert_second_kernel, count), in_specs=[...  8.06 us
    pallas_call x1, Pallas kernels, expert_first(): pl.pallas_call(functools.partial(expert_first_kernel, count), in_specs=[V...  7.79 us
    pallas_call x1, Pallas kernels, load(): pl.pallas_call(functools.partial(load_kernel, len(weights)), in_specs=[AN...  6.03 us
    pallas_call x1, Pallas kernels, attend(): pl.pallas_call(functools.partial(attend_kernel, rows // requests, heads /...  4.6 us
    pallas_call x1, Pallas kernels, route(): pl.pallas_call(functools.partial(route_kernel, capacity), in_specs=[SMEM]...  3.69 us
    pallas_call x2, Pallas kernels, expert_down(): pl.pallas_call(functools.partial(down_kernel, start, 512), in_specs=[VMEM...  2.71 us
  transfers between devices with their start and end apart: 27, of which 13 were waited for; matrix products, arithmetic and copies ran while one was open for 0% of the time, Pallas kernels for 24%

profile of v6, /device:TPU:0, one launch (start us, length us, event | category | flops | bytes accessed | tf_op | source)
XLA Modules:
  0.0 76.8 jit_solution(1965014463573950093)
XLA Ops:
  0.0 4.6 %attention.1 = (bf16[16,2944]{1,0:T(8,128)(2,1)S(1)}, bf16[16,2944]{1,0:T(8,128)(2,1)S(1)}, bf16[16,2944]{1,0:T(8,128)(2,1)S(1)}, bf16[16,2944]{1,0:T(8,128)(2,1)S(1)}) custom-call(f32[16]{0:T(128)} %decay_ref.1, s32[2,8]{1,0:T(2,128)} %bitcast.6, bf16[16,2048]{1,0:T(8,128)(2,1)} %q_ref.1, bf16[16,2048]{1,0:T(8,128)(2,1)} %k_ref.1, bf16[16,2048]{1,0:T(8,128)(2,1)} %v_ref.1, ...), custom_call_target="tpu_custom_call" | custom-call | tf_op jit(solution)/shard_map/attention/pallas_call | solution.py:107
  4.6 3.1 %collective-permute-start.1 = (bf16[16,2944]{1,0:T(8,128)(2,1)S(1)}, bf16[16,2944]{1,0:T(8,128)(2,1)S(1)}, u32[]{:S(2)}, u32[]{:S(2)}) collective-permute-start(bf16[16,2944]{1,0:T(8,128)(2,1)S(1)} %get-tuple-element.46), channel_id=1, source_target_pairs={{0,4},{4,0},{8,12},{12,8},{1,5},{5,1},{9,13},{13,9},{2,6},{6,2},{1... | collective-permute-start | bytes 282632 | tf_op jit(solution)/shard_map/ppermute | solution.py:592
  7.7 2.6 %collective-permute-start.3 = (bf16[16,2944]{1,0:T(8,128)(2,1)S(1)}, bf16[16,2944]{1,0:T(8,128)(2,1)S(1)}, u32[]{:S(2)}, u32[]{:S(2)}) collective-permute-start(bf16[16,2944]{1,0:T(8,128)(2,1)S(1)} %get-tuple-element.47), channel_id=1, source_target_pairs={{0,8},{4,12},{8,0},{12,4},{1,9},{5,13},{9,1},{13,5},{2,10},{6,14},... | collective-permute-start | bytes 282632 | tf_op jit(solution)/shard_map/ppermute | solution.py:592
  10.3 0.0 collective-permute-start.5
  10.3 6.0 %load.1 = (bf16[16,2944]{1,0:T(8,128)(2,1)S(1)}, bf16[2048,768]{1,0:T(8,128)(2,1)S(1)}, f32[1,6144]{1,0:T(1,128)S(1)}, bf16[1152,6144]{1,0:T(8,128)(2,1)S(1)}) custom-call(bf16[16,2944]{1,0:T(8,128)(2,1)S(1)} %get-tuple-element.44.rows_hbm, bf16[2048,768]{1,0:T(8,128)(2,1)} %refs_0_.1, f32[1,6144]{1,0:T(1,128)} %bitcast.4, bf16[1152,6144]{1,0:T(8,128)(2,1)} %refs_2_.1), custom_call_target="tpu_custom_call" | custom-call | bytes 17326080 | tf_op jit(solution)/shard_map/load/pallas_call | solution.py:146
  16.3 0.1 collective-permute-start
  16.4 0.0 collective-permute-done.1.refs_2_
  16.4 0.5 collective-permute-start.2
  16.9 0.9 %collective-permute-done.3.refs_4_ = bf16[16,2944]{1,0:T(8,128)(2,1)S(1)} collective-permute-done((bf16[16,2944]{1,0:T(8,128)(2,1)S(1)}, bf16[16,2944]{1,0:T(8,128)(2,1)S(1)}, u32[]{:S(2)}, u32[]{:S(2)}) %collective-permute-start.3) | collective-permute-done | bytes 94240 | tf_op jit(solution)/shard_map/ppermute | solution.py:592
  17.8 0.0 collective-permute-start.4
  17.8 0.0 collective-permute-done.5.refs_6_
  17.8 0.5 collective-permute-start.6
  18.3 0.0 collective-permute-done.refs_1_
  18.3 0.0 collective-permute-done.2.refs_3_
  18.3 0.8 %collective-permute-done.4.refs_5_ = bf16[16,2944]{1,0:T(8,128)(2,1)S(1)} collective-permute-done((bf16[16,2944]{1,0:T(8,128)(2,1)S(1)}, bf16[16,2944]{1,0:T(8,128)(2,1)S(1)}, u32[]{:S(2)}, u32[]{:S(2)}) %collective-permute-start.4) | collective-permute-done | bytes 94240 | tf_op jit(solution)/shard_map/ppermute | solution.py:592
  19.1 0.2 collective-permute-done.6.refs_7_
  19.3 0.7 projection.1
  20.0 1.6 %collective-permute-start.7 = (bf16[64,768]{1,0:T(8,128)(2,1)S(1)}, bf16[64,768]{1,0:T(8,128)(2,1)S(1)}, u32[]{:S(2)}, u32[]{:S(2)}) collective-permute-start(bf16[64,768]{1,0:T(8,128)(2,1)S(1)} %get-tuple-element.51), channel_id=1, source_target_pairs={{0,1},{1,0},{2,3},{3,2},{4,5},{5,4},{6,7},{7,6},{8,9},{9,8},{10,11... | collective-permute-start | bytes 294920 | tf_op jit(solution)/shard_map/ppermute | solution.py:592
  21.5 3.7 %route.1 = (bf16[128,64]{1,0:T(8,128)(2,1)S(1)}, f32[64,768]{1,0:T(8,128)S(1)}, bf16[512,6144]{1,0:T(8,128)(2,1)S(1)}, bf16[32,32]{1,0:T(8,128)(2,1)S(1)}) custom-call(s32[2,8]{1,0:T(2,128)} %bitcast.7, f32[2,8]{1,0:T(2,128)} %bitcast.8, bf16[16,2944]{1,0:T(8,128)(2,1)S(1)} %get-tuple-element.45.refs_0_, bf16[16,2944]{1,0:T(8,128)(2,1)S(1)} %collective-permute-done.refs_1_, ...), custom_call_target="tpu_custom_call" | custom-call | flops 1000000 | bytes 8000000 | tf_op jit(solution)/shard_map/route/pallas_call | solution.py:258
  25.2 0.0 collective-permute-done.7.got_ref
  25.2 0.2 pack.1
  25.4 1.5 %collective-permute-start.12 = (bf16[32,768]{1,0:T(8,128)(2,1)S(1)}, bf16[32,768]{1,0:T(8,128)(2,1)S(1)}, u32[]{:S(2)}, u32[]{:S(2)}) collective-permute-start(bf16[32,768]{1,0:T(8,128)(2,1)S(1)} %get-tuple-element.56.refs_0_), channel_id=1, source_target_pairs={{0,4},{4,0},{8,12},{12,8},{1,5},{5,1},{9,13},{13,9},{2,6},{6,2},{1... | collective-permute-start | bytes 147464 | tf_op jit(solution)/shard_map/ppermute | solution.py:592
  26.9 2.5 %collective-permute-start.9 = (bf16[32,768]{1,0:T(8,128)(2,1)S(1)}, bf16[32,768]{1,0:T(8,128)(2,1)S(1)}, u32[]{:S(2)}, u32[]{:S(2)}) collective-permute-start(bf16[32,768]{1,0:T(8,128)(2,1)S(1)} %relay.4), channel_id=1, source_target_pairs={{0,12},{4,8},{8,4},{12,0},{1,13},{5,9},{9,5},{13,1},{2,14},{6,10},... | collective-permute-start | bytes 147464 | tf_op jit(solution)/shard_map/ppermute | solution.py:592
  29.5 0.0 collective-permute-start.8
  29.5 0.1 collective-permute-done.12
  29.6 1.3 %collective-permute-start.14 = (bf16[64,768]{1,0:T(8,128)(2,1)S(1)}, bf16[64,768]{1,0:T(8,128)(2,1)S(1)}, u32[]{:S(2)}, u32[]{:S(2)}) collective-permute-start(bf16[64,768]{1,0:T(8,128)(2,1)S(1)} %constant_dynamic-update-slice_fusion.2.refs_0_), channel_id=1, source_target_pairs={{0,1},{1,0},{2,3},{3,2},{4,5},{5,4},{6,7},{7,6},{8,9},{9,8},{10,11... | collective-permute-start | bytes 294920 | tf_op jit(solution)/shard_map/ppermute | solution.py:592
  31.0 0.0 collective-permute-start.13
  31.0 3.8 %collective-permute-done.8 = bf16[32,768]{1,0:T(8,128)(2,1)S(1)} collective-permute-done((bf16[32,768]{1,0:T(8,128)(2,1)S(1)}, bf16[32,768]{1,0:T(8,128)(2,1)S(1)}, u32[]{:S(2)}, u32[]{:S(2)}) %collective-permute-start.8) | collective-permute-done | bytes 49184 | tf_op jit(solution)/shard_map/ppermute | solution.py:592
  34.7 0.0 collective-permute-done.14.refs_2_
  34.7 0.1 collective-permute-start.15
  34.8 0.0 collective-permute-done.9
  34.8 1.3 %collective-permute-start.11 = (bf16[64,768]{1,0:T(8,128)(2,1)S(1)}, bf16[64,768]{1,0:T(8,128)(2,1)S(1)}, u32[]{:S(2)}, u32[]{:S(2)}) collective-permute-start(bf16[64,768]{1,0:T(8,128)(2,1)S(1)} %constant_dynamic-update-slice_fusion.refs_0_), channel_id=1, source_target_pairs={{0,1},{1,0},{2,3},{3,2},{4,5},{5,4},{6,7},{7,6},{8,9},{9,8},{10,11... | collective-permute-start | bytes 294920 | tf_op jit(solution)/shard_map/ppermute | solution.py:592
  36.1 0.2 collective-permute-start.10
  36.3 0.0 collective-permute-done.13.refs_1_
  36.3 0.0 collective-permute-done.15.refs_3_
  36.3 7.8 %experts_first.1 = (f32[1152,64]{1,0:T(8,128)S(1)}, f32[1152,64]{1,0:T(8,128)S(1)}, f32[64,128]{1,0:T(8,128)S(1)}, bf16[640,6144]{1,0:T(8,128)(2,1)S(1)}) custom-call(bf16[64,768]{1,0:T(8,128)(2,1)S(1)} %constant_dynamic-update-slice_fusion.2.refs_0_, bf16[64,768]{1,0:T(8,128)(2,1)S(1)} %collective-permute-done.13.refs_1_, ...), custom_call_target="tpu_custom_call" | custom-call | flops 905969664 | bytes 14155776 | tf_op jit(solution)/shard_map/experts_first/pallas_call | solution.py:387
  44.2 0.4 collective-permute-start.16
  44.5 1.0 %collective-permute-done.16.refs_3_ = bf16[64,768]{1,0:T(8,128)(2,1)S(1)} collective-permute-done((bf16[64,768]{1,0:T(8,128)(2,1)S(1)}, bf16[64,768]{1,0:T(8,128)(2,1)S(1)}, u32[]{:S(2)}, u32[]{:S(2)}) %collective-permute-start.16) | collective-permute-done | bytes 98336 | tf_op jit(solution)/shard_map/ppermute | solution.py:592
  45.5 8.1 %experts_second.1 = (bf16[64,1152]{1,0:T(8,128)(2,1)S(1)}, bf16[1152,6144]{1,0:T(8,128)(2,1)S(1)}) custom-call(bf16[64,768]{1,0:T(8,128)(2,1)S(1)} %constant_dynamic-update-slice_fusion.refs_0_, bf16[64,768]{1,0:T(8,128)(2,1)S(1)} %collective-permute-done.10.refs_1_, bf16[64,768]{1,0:T(8,128)(2,1)S(1)} %relay.5.refs_2_, ...), custom_call_target="tpu_custom_call" | custom-call | flops 905969664 | bytes 14155776 | tf_op jit(solution)/shard_map/experts_second/pallas_call | solution.py:422
  53.6 1.4 %experts_down.3 = (f32[32,3072]{1,0:T(8,128)S(1)}, bf16[32,3072]{1,0:T(8,128)(2,1)S(1)}) custom-call(bf16[64,1152]{1,0:T(8,128)(2,1)S(1)} %get-tuple-element.66.hidden_ref, bf16[1152,6144]{1,0:T(8,128)(2,1)S(1)} %get-tuple-element.67.weight_ref), custom_call_target="tpu_custom_call" | custom-call | flops 905969664 | bytes 7077888 | tf_op jit(solution)/shard_map/experts_down/pallas_call | solution.py:438
  55.0 1.4 %experts_down.2 = (f32[32,3072]{1,0:T(8,128)S(1)}, bf16[32,3072]{1,0:T(8,128)(2,1)S(1)}) custom-call(bf16[64,1152]{1,0:T(8,128)(2,1)S(1)} %get-tuple-element.66.hidden_ref, bf16[1152,6144]{1,0:T(8,128)(2,1)S(1)} %get-tuple-element.67.weight_ref), custom_call_target="tpu_custom_call" | custom-call | flops 905969664 | bytes 7077888 | tf_op jit(solution)/shard_map/experts_down/pallas_call | solution.py:438
  56.3 0.4 collective-permute-start.18
  56.7 0.2 collective-permute-start.17
  56.9 0.9 %collective-permute-done.18.refs_3_ = bf16[32,3072]{1,0:T(8,128)(2,1)S(1)} collective-permute-done((bf16[32,3072]{1,0:T(8,128)(2,1)S(1)}, bf16[32,3072]{1,0:T(8,128)(2,1)S(1)}, u32[]{:S(2)}, u32[]{:S(2)}) %collective-permute-start.18) | collective-permute-done | bytes 196640 | tf_op jit(solution)/shard_map/ppermute | solution.py:592
  57.8 0.3 collective-permute-done.17.refs_2_
  58.1 0.1 chip_sum.1
  58.2 1.0 %collective-permute-start.22 = (bf16[16,6144]{1,0:T(8,128)(2,1)S(1)}, bf16[16,6144]{1,0:T(8,128)(2,1)S(1)}, u32[]{:S(2)}, u32[]{:S(2)}) collective-permute-start(bf16[16,6144]{1,0:T(8,128)(2,1)S(1)} %get-tuple-element.77), channel_id=1, source_target_pairs={{0,1},{1,0},{2,3},{3,2},{4,5},{5,4},{6,7},{7,6},{8,9},{9,8},{10,11... | collective-permute-start | bytes 589832 | tf_op jit(solution)/shard_map/ppermute | solution.py:592
  59.3 1.3 %collective-permute-start.19 = (bf16[16,768]{1,0:T(8,128)(2,1)S(1)}, bf16[16,768]{1,0:T(8,128)(2,1)S(1)}, u32[]{:S(2)}, u32[]{:S(2)}) collective-permute-start(bf16[16,768]{1,0:T(8,128)(2,1)S(1)} %get-tuple-element.74), channel_id=1, source_target_pairs={{0,4},{4,0},{8,12},{12,8},{1,5},{5,1},{9,13},{13,9},{2,6},{6,2},{1... | collective-permute-start | bytes 73736 | tf_op jit(solution)/shard_map/ppermute | solution.py:592
  60.5 1.8 %collective-permute-start.20 = (bf16[16,768]{1,0:T(8,128)(2,1)S(1)}, bf16[16,768]{1,0:T(8,128)(2,1)S(1)}, u32[]{:S(2)}, u32[]{:S(2)}) collective-permute-start(bf16[16,768]{1,0:T(8,128)(2,1)S(1)} %get-tuple-element.75), channel_id=1, source_target_pairs={{0,8},{4,12},{8,0},{12,4},{1,9},{5,13},{9,1},{13,5},{2,10},{6,14},... | collective-permute-start | bytes 73736 | tf_op jit(solution)/shard_map/ppermute | solution.py:592
  62.4 1.3 %collective-permute-start.21 = (bf16[16,768]{1,0:T(8,128)(2,1)S(1)}, bf16[16,768]{1,0:T(8,128)(2,1)S(1)}, u32[]{:S(2)}, u32[]{:S(2)}) collective-permute-start(bf16[16,768]{1,0:T(8,128)(2,1)S(1)} %get-tuple-element.76), channel_id=1, source_target_pairs={{0,12},{4,8},{8,4},{12,0},{1,13},{5,9},{9,5},{13,1},{2,14},{6,10},... | collective-permute-start | bytes 73736 | tf_op jit(solution)/shard_map/ppermute | solution.py:592
  63.7 1.7 %collective-permute-done.22.got_ref = bf16[16,6144]{1,0:T(8,128)(2,1)S(1)} collective-permute-done((bf16[16,6144]{1,0:T(8,128)(2,1)S(1)}, bf16[16,6144]{1,0:T(8,128)(2,1)S(1)}, u32[]{:S(2)}, u32[]{:S(2)}) %collective-permute-start.22) | collective-permute-done | bytes 196640 | tf_op jit(solution)/shard_map/ppermute | solution.py:592
  65.4 0.1 pair_sum.1
  65.5 0.3 collective-permute-done.20.refs_2_
  65.8 2.2 %collective-permute-done.21.refs_3_ = bf16[16,768]{1,0:T(8,128)(2,1)S(1)} collective-permute-done((bf16[16,768]{1,0:T(8,128)(2,1)S(1)}, bf16[16,768]{1,0:T(8,128)(2,1)S(1)}, u32[]{:S(2)}, u32[]{:S(2)}) %collective-permute-start.21) | collective-permute-done | bytes 24608 | tf_op jit(solution)/shard_map/ppermute | solution.py:592
  68.0 0.1 collective-permute-start.23
  68.1 0.1 collective-permute-start.24
  68.1 1.9 %collective-permute-start.25 = (bf16[8,3072]{1,0:T(8,128)(2,1)S(1)}, bf16[8,3072]{1,0:T(8,128)(2,1)S(1)}, u32[]{:S(2)}, u32[]{:S(2)}) collective-permute-start(bf16[8,3072]{1,0:T(8,128)(2,1)S(1)} %get-tuple-element.81), channel_id=1, source_target_pairs={{0,8},{4,12},{8,0},{12,4},{1,9},{5,13},{9,1},{13,5},{2,10},{6,14},... | collective-permute-start | bytes 147464 | tf_op jit(solution)/shard_map/ppermute | solution.py:592
  70.0 2.5 %collective-permute-start.26 = (bf16[8,3072]{1,0:T(8,128)(2,1)S(1)}, bf16[8,3072]{1,0:T(8,128)(2,1)S(1)}, u32[]{:S(2)}, u32[]{:S(2)}) collective-permute-start(bf16[8,3072]{1,0:T(8,128)(2,1)S(1)} %get-tuple-element.82), channel_id=1, source_target_pairs={{0,12},{4,8},{8,4},{12,0},{1,13},{5,9},{9,5},{13,1},{2,14},{6,10},... | collective-permute-start | bytes 147464 | tf_op jit(solution)/shard_map/ppermute | solution.py:592
  72.5 0.0 collective-permute-done.23.refs_4_
  72.5 0.9 %own_rows.1.combined_ref = f32[8,6144]{1,0:T(8,128)S(1)} custom-call(bf16[8,6144]{1,0:T(8,128)(2,1)} %residual_ref.3, bf16[16,768]{1,0:T(8,128)(2,1)S(1)} %get-tuple-element.73.refs_0_, bf16[16,768]{1,0:T(8,128)(2,1)S(1)} %collective-permute-done.19.refs_1_, bf16[16,768]{1,0:T(8,128)(2,1)S(1)} %collective-permute-done.20.refs_2_, ...), custom_call_target="tpu_custom_call" | custom-call | flops 1000000 | bytes 1000000 | tf_op jit(solution)/shard_map/own_rows/pallas_call | solution.py:558
  73.5 0.0 collective-permute-done.24.refs_1_
  73.5 1.7 %collective-permute-done.25.refs_2_ = bf16[8,3072]{1,0:T(8,128)(2,1)S(1)} collective-permute-done((bf16[8,3072]{1,0:T(8,128)(2,1)S(1)}, bf16[8,3072]{1,0:T(8,128)(2,1)S(1)}, u32[]{:S(2)}, u32[]{:S(2)}) %collective-permute-start.25) | collective-permute-done | bytes 49184 | tf_op jit(solution)/shard_map/ppermute | solution.py:592
  75.2 0.8 collective-permute-done.26.refs_3_
  76.0 0.8 %finish.1 = bf16[8,6144]{1,0:T(8,128)(2,1)} custom-call(f32[8,6144]{1,0:T(8,128)S(1)} %own_rows.1.combined_ref, bf16[32,32]{1,0:T(8,128)(2,1)S(1)} %get-tuple-element.79.weighting_ref, bf16[8,3072]{1,0:T(8,128)(2,1)S(1)} %get-tuple-element.78.refs_4_.refs_0_, bf16[8,3072]{1,0:T(8,128)(2,1)S(1)} %collective-permute-done.24.refs_1_, ...), custom_call_target="tpu_custom_call" | custom-call | tf_op jit(solution)/shard_map/finish/pallas_call | solution.py:581
  (12 shorter events, 0.1 us)
Async XLA Ops:
  4.6 11.8 %collective-permute-start.1 = (bf16[16,2944]{1,0:T(8,128)(2,1)S(1)}, bf16[16,2944]{1,0:T(8,128)(2,1)S(1)}, u32[]{:S(2)}, u32[]{:S(2)}) collective-permute-start(bf16[16,2944]{1,0:T(8,128)(2,1)S(1)} %get-tuple-element.46), channel_id=1, source_target_pairs={{0,4},{4,0},{8,12},{12,8},{1,5},{5,1},{9,13},{13,9},{2,6},{6,2},{1... | collective-permute-start | bytes 282632 | tf_op jit(solution)/shard_map/ppermute | solution.py:592
  7.7 10.1 %collective-permute-start.3 = (bf16[16,2944]{1,0:T(8,128)(2,1)S(1)}, bf16[16,2944]{1,0:T(8,128)(2,1)S(1)}, u32[]{:S(2)}, u32[]{:S(2)}) collective-permute-start(bf16[16,2944]{1,0:T(8,128)(2,1)S(1)} %get-tuple-element.47), channel_id=1, source_target_pairs={{0,8},{4,12},{8,0},{12,4},{1,9},{5,13},{9,1},{13,5},{2,10},{6,14},... | collective-permute-start | bytes 282632 | tf_op jit(solution)/shard_map/ppermute | solution.py:592
  10.3 7.5 %collective-permute-start.5 = (bf16[16,2944]{1,0:T(8,128)(2,1)S(1)}, bf16[16,2944]{1,0:T(8,128)(2,1)S(1)}, u32[]{:S(2)}, u32[]{:S(2)}) collective-permute-start(bf16[16,2944]{1,0:T(8,128)(2,1)S(1)} %get-tuple-element.48), channel_id=1, source_target_pairs={{0,12},{4,8},{8,4},{12,0},{1,13},{5,9},{9,5},{13,1},{2,14},{6,10},... | collective-permute-start | bytes 282632 | tf_op jit(solution)/shard_map/ppermute | solution.py:592
  16.3 2.0 %collective-permute-start = (bf16[16,2944]{1,0:T(8,128)(2,1)S(1)}, bf16[16,2944]{1,0:T(8,128)(2,1)S(1)}, u32[]{:S(2)}, u32[]{:S(2)}) collective-permute-start(bf16[16,2944]{1,0:T(8,128)(2,1)S(1)} %get-tuple-element.45.refs_0_), channel_id=1, source_target_pairs={{0,2},{2,0},{1,3},{3,1},{4,6},{6,4},{5,7},{7,5},{8,10},{10,8},{9,1... | collective-permute-start | bytes 282632 | tf_op jit(solution)/shard_map/ppermute | solution.py:592
  16.4 1.9 %collective-permute-start.2 = (bf16[16,2944]{1,0:T(8,128)(2,1)S(1)}, bf16[16,2944]{1,0:T(8,128)(2,1)S(1)}, u32[]{:S(2)}, u32[]{:S(2)}) collective-permute-start(bf16[16,2944]{1,0:T(8,128)(2,1)S(1)} %collective-permute-done.1.refs_2_), channel_id=1, source_target_pairs={{0,2},{2,0},{1,3},{3,1},{4,6},{6,4},{5,7},{7,5},{8,10},{10,8},{9,1... | collective-permute-start | bytes 282632 | tf_op jit(solution)/shard_map/ppermute | solution.py:592
  17.8 1.3 %collective-permute-start.4 = (bf16[16,2944]{1,0:T(8,128)(2,1)S(1)}, bf16[16,2944]{1,0:T(8,128)(2,1)S(1)}, u32[]{:S(2)}, u32[]{:S(2)}) collective-permute-start(bf16[16,2944]{1,0:T(8,128)(2,1)S(1)} %collective-permute-done.3.refs_4_), channel_id=1, source_target_pairs={{0,2},{2,0},{1,3},{3,1},{4,6},{6,4},{5,7},{7,5},{8,10},{10,8},{9,1... | collective-permute-start | bytes 282632 | tf_op jit(solution)/shard_map/ppermute | solution.py:592
  17.8 1.4 %collective-permute-start.6 = (bf16[16,2944]{1,0:T(8,128)(2,1)S(1)}, bf16[16,2944]{1,0:T(8,128)(2,1)S(1)}, u32[]{:S(2)}, u32[]{:S(2)}) collective-permute-start(bf16[16,2944]{1,0:T(8,128)(2,1)S(1)} %collective-permute-done.5.refs_6_), channel_id=1, source_target_pairs={{0,2},{2,0},{1,3},{3,1},{4,6},{6,4},{5,7},{7,5},{8,10},{10,8},{9,1... | collective-permute-start | bytes 282632 | tf_op jit(solution)/shard_map/ppermute | solution.py:592
  20.0 5.3 %collective-permute-start.7 = (bf16[64,768]{1,0:T(8,128)(2,1)S(1)}, bf16[64,768]{1,0:T(8,128)(2,1)S(1)}, u32[]{:S(2)}, u32[]{:S(2)}) collective-permute-start(bf16[64,768]{1,0:T(8,128)(2,1)S(1)} %get-tuple-element.51), channel_id=1, source_target_pairs={{0,1},{1,0},{2,3},{3,2},{4,5},{5,4},{6,7},{7,6},{8,9},{9,8},{10,11... | collective-permute-start | bytes 294920 | tf_op jit(solution)/shard_map/ppermute | solution.py:592
  25.4 4.2 %collective-permute-start.12 = (bf16[32,768]{1,0:T(8,128)(2,1)S(1)}, bf16[32,768]{1,0:T(8,128)(2,1)S(1)}, u32[]{:S(2)}, u32[]{:S(2)}) collective-permute-start(bf16[32,768]{1,0:T(8,128)(2,1)S(1)} %get-tuple-element.56.refs_0_), channel_id=1, source_target_pairs={{0,4},{4,0},{8,12},{12,8},{1,5},{5,1},{9,13},{13,9},{2,6},{6,2},{1... | collective-permute-start | bytes 147464 | tf_op jit(solution)/shard_map/ppermute | solution.py:592
  26.9 7.9 %collective-permute-start.9 = (bf16[32,768]{1,0:T(8,128)(2,1)S(1)}, bf16[32,768]{1,0:T(8,128)(2,1)S(1)}, u32[]{:S(2)}, u32[]{:S(2)}) collective-permute-start(bf16[32,768]{1,0:T(8,128)(2,1)S(1)} %relay.4), channel_id=1, source_target_pairs={{0,12},{4,8},{8,4},{12,0},{1,13},{5,9},{9,5},{13,1},{2,14},{6,10},... | collective-permute-start | bytes 147464 | tf_op jit(solution)/shard_map/ppermute | solution.py:592
  29.5 5.2 %collective-permute-start.8 = (bf16[32,768]{1,0:T(8,128)(2,1)S(1)}, bf16[32,768]{1,0:T(8,128)(2,1)S(1)}, u32[]{:S(2)}, u32[]{:S(2)}) collective-permute-start(bf16[32,768]{1,0:T(8,128)(2,1)S(1)} %relay.3), channel_id=1, source_target_pairs={{0,8},{4,12},{8,0},{12,4},{1,9},{5,13},{9,1},{13,5},{2,10},{6,14},... | collective-permute-start | bytes 147464 | tf_op jit(solution)/shard_map/ppermute | solution.py:592
  29.6 5.1 %collective-permute-start.14 = (bf16[64,768]{1,0:T(8,128)(2,1)S(1)}, bf16[64,768]{1,0:T(8,128)(2,1)S(1)}, u32[]{:S(2)}, u32[]{:S(2)}) collective-permute-start(bf16[64,768]{1,0:T(8,128)(2,1)S(1)} %constant_dynamic-update-slice_fusion.2.refs_0_), channel_id=1, source_target_pairs={{0,1},{1,0},{2,3},{3,2},{4,5},{5,4},{6,7},{7,6},{8,9},{9,8},{10,11... | collective-permute-start | bytes 294920 | tf_op jit(solution)/shard_map/ppermute | solution.py:592
  31.0 5.4 %collective-permute-start.13 = (bf16[64,768]{1,0:T(8,128)(2,1)S(1)}, bf16[64,768]{1,0:T(8,128)(2,1)S(1)}, u32[]{:S(2)}, u32[]{:S(2)}) collective-permute-start(bf16[64,768]{1,0:T(8,128)(2,1)S(1)} %constant_dynamic-update-slice_fusion.2.refs_0_), channel_id=1, source_target_pairs={{0,2},{2,0},{1,3},{3,1},{4,6},{6,4},{5,7},{7,5},{8,10},{10,8},{9,1... | collective-permute-start | bytes 294920 | tf_op jit(solution)/shard_map/ppermute | solution.py:592
  34.7 1.6 %collective-permute-start.15 = (bf16[64,768]{1,0:T(8,128)(2,1)S(1)}, bf16[64,768]{1,0:T(8,128)(2,1)S(1)}, u32[]{:S(2)}, u32[]{:S(2)}) collective-permute-start(bf16[64,768]{1,0:T(8,128)(2,1)S(1)} %collective-permute-done.14.refs_2_), channel_id=1, source_target_pairs={{0,2},{2,0},{1,3},{3,1},{4,6},{6,4},{5,7},{7,5},{8,10},{10,8},{9,1... | collective-permute-start | bytes 294920 | tf_op jit(solution)/shard_map/ppermute | solution.py:592
  34.8 9.3 %collective-permute-start.11 = (bf16[64,768]{1,0:T(8,128)(2,1)S(1)}, bf16[64,768]{1,0:T(8,128)(2,1)S(1)}, u32[]{:S(2)}, u32[]{:S(2)}) collective-permute-start(bf16[64,768]{1,0:T(8,128)(2,1)S(1)} %constant_dynamic-update-slice_fusion.refs_0_), channel_id=1, source_target_pairs={{0,1},{1,0},{2,3},{3,2},{4,5},{5,4},{6,7},{7,6},{8,9},{9,8},{10,11... | collective-permute-start | bytes 294920 | tf_op jit(solution)/shard_map/ppermute | solution.py:592
  36.1 8.4 %collective-permute-start.10 = (bf16[64,768]{1,0:T(8,128)(2,1)S(1)}, bf16[64,768]{1,0:T(8,128)(2,1)S(1)}, u32[]{:S(2)}, u32[]{:S(2)}) collective-permute-start(bf16[64,768]{1,0:T(8,128)(2,1)S(1)} %constant_dynamic-update-slice_fusion.refs_0_), channel_id=1, source_target_pairs={{0,2},{2,0},{1,3},{3,1},{4,6},{6,4},{5,7},{7,5},{8,10},{10,8},{9,1... | collective-permute-start | bytes 294920 | tf_op jit(solution)/shard_map/ppermute | solution.py:592
  44.2 1.4 %collective-permute-start.16 = (bf16[64,768]{1,0:T(8,128)(2,1)S(1)}, bf16[64,768]{1,0:T(8,128)(2,1)S(1)}, u32[]{:S(2)}, u32[]{:S(2)}) collective-permute-start(bf16[64,768]{1,0:T(8,128)(2,1)S(1)} %relay.5.refs_2_), channel_id=1, source_target_pairs={{0,2},{2,0},{1,3},{3,1},{4,6},{6,4},{5,7},{7,5},{8,10},{10,8},{9,1... | collective-permute-start | bytes 294920 | tf_op jit(solution)/shard_map/ppermute | solution.py:592
  56.3 1.5 %collective-permute-start.18 = (bf16[32,3072]{1,0:T(8,128)(2,1)S(1)}, bf16[32,3072]{1,0:T(8,128)(2,1)S(1)}, u32[]{:S(2)}, u32[]{:S(2)}) collective-permute-start(bf16[32,3072]{1,0:T(8,128)(2,1)S(1)} %get-tuple-element.71), channel_id=1, source_target_pairs={{0,2},{2,0},{1,3},{3,1},{4,6},{6,4},{5,7},{7,5},{8,10},{10,8},{9,1... | collective-permute-start | bytes 589832 | tf_op jit(solution)/shard_map/ppermute | solution.py:592
  56.7 1.4 %collective-permute-start.17 = (bf16[32,3072]{1,0:T(8,128)(2,1)S(1)}, bf16[32,3072]{1,0:T(8,128)(2,1)S(1)}, u32[]{:S(2)}, u32[]{:S(2)}) collective-permute-start(bf16[32,3072]{1,0:T(8,128)(2,1)S(1)} %get-tuple-element.70), channel_id=1, source_target_pairs={{0,2},{2,0},{1,3},{3,1},{4,6},{6,4},{5,7},{7,5},{8,10},{10,8},{9,1... | collective-permute-start | bytes 589832 | tf_op jit(solution)/shard_map/ppermute | solution.py:592
  58.2 7.2 %collective-permute-start.22 = (bf16[16,6144]{1,0:T(8,128)(2,1)S(1)}, bf16[16,6144]{1,0:T(8,128)(2,1)S(1)}, u32[]{:S(2)}, u32[]{:S(2)}) collective-permute-start(bf16[16,6144]{1,0:T(8,128)(2,1)S(1)} %get-tuple-element.77), channel_id=1, source_target_pairs={{0,1},{1,0},{2,3},{3,2},{4,5},{5,4},{6,7},{7,6},{8,9},{9,8},{10,11... | collective-permute-start | bytes 589832 | tf_op jit(solution)/shard_map/ppermute | solution.py:592
  59.3 6.2 %collective-permute-start.19 = (bf16[16,768]{1,0:T(8,128)(2,1)S(1)}, bf16[16,768]{1,0:T(8,128)(2,1)S(1)}, u32[]{:S(2)}, u32[]{:S(2)}) collective-permute-start(bf16[16,768]{1,0:T(8,128)(2,1)S(1)} %get-tuple-element.74), channel_id=1, source_target_pairs={{0,4},{4,0},{8,12},{12,8},{1,5},{5,1},{9,13},{13,9},{2,6},{6,2},{1... | collective-permute-start | bytes 73736 | tf_op jit(solution)/shard_map/ppermute | solution.py:592
  60.5 5.2 %collective-permute-start.20 = (bf16[16,768]{1,0:T(8,128)(2,1)S(1)}, bf16[16,768]{1,0:T(8,128)(2,1)S(1)}, u32[]{:S(2)}, u32[]{:S(2)}) collective-permute-start(bf16[16,768]{1,0:T(8,128)(2,1)S(1)} %get-tuple-element.75), channel_id=1, source_target_pairs={{0,8},{4,12},{8,0},{12,4},{1,9},{5,13},{9,1},{13,5},{2,10},{6,14},... | collective-permute-start | bytes 73736 | tf_op jit(solution)/shard_map/ppermute | solution.py:592
  62.4 5.6 %collective-permute-start.21 = (bf16[16,768]{1,0:T(8,128)(2,1)S(1)}, bf16[16,768]{1,0:T(8,128)(2,1)S(1)}, u32[]{:S(2)}, u32[]{:S(2)}) collective-permute-start(bf16[16,768]{1,0:T(8,128)(2,1)S(1)} %get-tuple-element.76), channel_id=1, source_target_pairs={{0,12},{4,8},{8,4},{12,0},{1,13},{5,9},{9,5},{13,1},{2,14},{6,10},... | collective-permute-start | bytes 73736 | tf_op jit(solution)/shard_map/ppermute | solution.py:592
  68.0 4.5 %collective-permute-start.23 = (bf16[64,768]{1,0:T(8,128)(2,1)S(1)}, bf16[64,768]{1,0:T(8,128)(2,1)S(1)}, u32[]{:S(2)}, u32[]{:S(2)}) collective-permute-start(bf16[64,768]{1,0:T(8,128)(2,1)S(1)} %join.1), channel_id=1, source_target_pairs={{0,2},{2,0},{1,3},{3,1},{4,6},{6,4},{5,7},{7,5},{8,10},{10,8},{9,1... | collective-permute-start | bytes 294920 | tf_op jit(solution)/shard_map/ppermute | solution.py:592
  68.1 5.4 %collective-permute-start.24 = (bf16[8,3072]{1,0:T(8,128)(2,1)S(1)}, bf16[8,3072]{1,0:T(8,128)(2,1)S(1)}, u32[]{:S(2)}, u32[]{:S(2)}) collective-permute-start(bf16[8,3072]{1,0:T(8,128)(2,1)S(1)} %get-tuple-element.80), channel_id=1, source_target_pairs={{0,4},{4,0},{8,12},{12,8},{1,5},{5,1},{9,13},{13,9},{2,6},{6,2},{1... | collective-permute-start | bytes 147464 | tf_op jit(solution)/shard_map/ppermute | solution.py:592
  68.1 7.1 %collective-permute-start.25 = (bf16[8,3072]{1,0:T(8,128)(2,1)S(1)}, bf16[8,3072]{1,0:T(8,128)(2,1)S(1)}, u32[]{:S(2)}, u32[]{:S(2)}) collective-permute-start(bf16[8,3072]{1,0:T(8,128)(2,1)S(1)} %get-tuple-element.81), channel_id=1, source_target_pairs={{0,8},{4,12},{8,0},{12,4},{1,9},{5,13},{9,1},{13,5},{2,10},{6,14},... | collective-permute-start | bytes 147464 | tf_op jit(solution)/shard_map/ppermute | solution.py:592
  70.0 5.9 %collective-permute-start.26 = (bf16[8,3072]{1,0:T(8,128)(2,1)S(1)}, bf16[8,3072]{1,0:T(8,128)(2,1)S(1)}, u32[]{:S(2)}, u32[]{:S(2)}) collective-permute-start(bf16[8,3072]{1,0:T(8,128)(2,1)S(1)} %get-tuple-element.82), channel_id=1, source_target_pairs={{0,12},{4,8},{8,4},{12,0},{1,13},{5,9},{9,5},{13,1},{2,14},{6,10},... | collective-permute-start | bytes 147464 | tf_op jit(solution)/shard_map/ppermute | solution.py:592

commit v7 on v6

--- a/solution.py
+++ b/solution.py
@@ -273,17 +273,22 @@
 
 
 def pack_kernel(keep_ref, got_ref, residual_ref, choose_ref, *refs):
-    outs, own_ref, sum_ref = refs[:-2], refs[-2], refs[-1]
+    outs, own_ref, cross_ref, sum_ref = refs[:-3], *refs[-3:]
     sum_ref[...] = keep_ref[...] + got_ref[...].astype(F32)
     combined = (sum_ref[...] + residual_ref[...]).astype(BF16)
     packed = dot(choose_ref[...], combined).astype(BF16)
     count = choose_ref.shape[0] // len(outs)
-    own = own_ref.shape[1]
-    expert = lax.axis_index("expert")
+    own = sum_ref.shape[0] // len(outs) // 2
+    expert, half = lax.axis_index("expert"), lax.axis_index("half")
     for d, out in enumerate(outs):
         out[...] = packed[d * count : (d + 1) * count]
-        at = pl.ds(pl.multiple_of((expert ^ d) * own, own), own)
-        own_ref[d] = sum_ref[at].astype(BF16)
+    for d in range(0, len(outs), 2):
+        for ref, which in ((own_ref, half), (cross_ref, 1 - half)):
+            rows = [
+                sum_ref[pl.ds(pl.multiple_of(((expert ^ c) * 2 + which) * own, own), own)]
+                for c in (d, d + 1)
+            ]
+            ref[d * own : (d + 2) * own] = jnp.concatenate(rows, axis=0).astype(BF16)
 
 
 def pack(keep, got, residual, choose, experts):
@@ -292,9 +297,9 @@
     return pl.pallas_call(
         pack_kernel,
         in_specs=[VMEM] * 4,
-        out_specs=[VMEM] * (experts + 1),
+        out_specs=[VMEM] * (experts + 2),
         out_shape=[jax.ShapeDtypeStruct((count, columns), BF16)] * experts
-        + [jax.ShapeDtypeStruct((experts, rows // experts, columns), BF16)],
+        + [jax.ShapeDtypeStruct((rows // 2, columns), BF16)] * 2,
         scratch_shapes=[pltpu.VMEM((rows, columns), F32)],
         compiler_params=limits(4),
         name="pack",
@@ -473,45 +478,29 @@
     )(*mine, *got)
 
 
-def cut_kernel(own_ref, after_ref, *outs):
+def cut_kernel(own_ref, cross_ref, after_ref, *outs):
+    rows = own_ref.shape[0] // len(outs)
+    own, cross = own_ref[...].astype(F32), cross_ref[...].astype(F32)
     for d, out in enumerate(outs):
-        out[...] = own_ref[d]
-
-
-def cut(own, after):
+        at = slice(d * rows, (d + 1) * rows)
+        out[...] = jnp.concatenate([own[at], cross[at]], axis=0).astype(BF16)
+
+
+def cut(own, cross, after, experts):
+    rows, columns = own.shape
     return pl.pallas_call(
         cut_kernel,
-        in_specs=[VMEM] * 2,
-        out_specs=[VMEM] * own.shape[0],
-        out_shape=[jax.ShapeDtypeStruct(own.shape[1:], own.dtype)] * own.shape[0],
+        in_specs=[VMEM] * 3,
+        out_specs=[VMEM] * experts,
+        out_shape=[jax.ShapeDtypeStruct((2 * rows // experts, columns), BF16)] * experts,
         compiler_params=limits(2),
         cost_estimate=cost(0, 10**5),
         name="cut",
-    )(own, after)
-
-
-def join_kernel(*refs):
-    pieces, out_ref = refs[:-2], refs[-1]
-    rows = pieces[0].shape[0]
-    for d, piece in enumerate(pieces):
-        out_ref[d * rows : (d + 1) * rows] = piece[...]
-
-
-def join(pieces, after):
-    rows, columns = pieces[0].shape
-    return pl.pallas_call(
-        join_kernel,
-        in_specs=[VMEM] * (len(pieces) + 1),
-        out_specs=VMEM,
-        out_shape=jax.ShapeDtypeStruct((rows * len(pieces), columns), pieces[0].dtype),
-        compiler_params=limits(2),
-        cost_estimate=cost(0, 10**5),
-        name="join",
-    )(*pieces, after)
-
-
-def pair_sum_kernel(capacity, keep_ref, got_ref, *refs):
-    outs, fold_ref = refs[:-1], refs[-1]
+    )(own, cross, after)
+
+
+def pair_sum_kernel(capacity, extra, keep_ref, got_ref, *refs):
+    outs, fold_ref = refs[extra:-1], refs[-1]
     experts = len(outs)
     parts = 8 // capacity
     part = outs[0].shape[1]
@@ -526,44 +515,42 @@
         out[...] = fold_ref[expert ^ d].astype(BF16)
 
 
-def pair_sum(keep, got, capacity, experts):
+def pair_sum(keep, got, capacity, experts, after):
     part = keep.shape[1] * capacity // 8
     return pl.pallas_call(
-        functools.partial(pair_sum_kernel, capacity),
-        in_specs=[VMEM] * 2,
+        functools.partial(pair_sum_kernel, capacity, len(after)),
+        in_specs=[VMEM] * (2 + len(after)),
         out_specs=[VMEM] * experts,
         out_shape=[jax.ShapeDtypeStruct((8, part), BF16)] * experts,
         scratch_shapes=[pltpu.VMEM((experts, 8, part), F32)],
         compiler_params=limits(4),
         name="pair_sum",
-    )(keep, got)
+    )(keep, got, *after)
 
 
 def own_rows_kernel(residual_ref, *refs):
-    pieces, cross_ref, combined_ref = refs[:-2], *refs[-2:]
+    pieces, combined_ref = refs[:-1], refs[-1]
     rows = combined_ref.shape[0]
     columns = pieces[0].shape[1]
     expert, half = lax.axis_index("expert"), lax.axis_index("half")
     for d, piece in enumerate(pieces):
-        cross = cross_ref[d * 2 * rows : (d + 1) * 2 * rows]
-        for c, both in enumerate((piece[...], cross)):
+        both = piece[...].astype(F32)
+        for c in range(2):
             base = ((expert ^ d) * 2 + (half ^ c)) * columns
             at = pl.ds(pl.multiple_of(base, columns), columns)
-            both = both.astype(F32)
-            mine = jnp.where(half == 0, both[:rows], both[rows:])
-            combined_ref[:, at] = residual_ref[:, at].astype(F32) + mine
-
-
-def own_rows(residual, pieces, cross):
+            combined_ref[:, at] = residual_ref[:, at].astype(F32) + both[c * rows : (c + 1) * rows]
+
+
+def own_rows(residual, pieces):
     return pl.pallas_call(
         own_rows_kernel,
-        in_specs=[VMEM] * (len(pieces) + 2),
+        in_specs=[VMEM] * (len(pieces) + 1),
         out_specs=VMEM,
         out_shape=jax.ShapeDtypeStruct(residual.shape, F32),
         compiler_params=limits(4),
         cost_estimate=cost(10**6, 10**6),
         name="own_rows",
-    )(*in_hbm(residual), *pieces, cross)
+    )(*in_hbm(residual), *pieces)
 
 
 def finish_kernel(combined_ref, weighting_ref, *refs):
@@ -629,11 +616,11 @@
         pieces += [message, swap(message, "half", 1)]
 
     keep, send = project(pieces, weight_here)
-    first = expert_up.shape[0] // 256 * 128
+    first = expert_up.shape[0] // 256 * 128 + 128
     choose, residual_part, up_first, weighting = route(
         ids, weights, pieces, keep, columns, capacity, expert_up, first
     )
-    *packed, own = pack(keep, swap(send, "pair", 1), residual_part, choose, experts)
+    *packed, own, cross = pack(keep, swap(send, "pair", 1), residual_part, choose, experts)
 
     packed[2:] = [relay(rows, packed[1]) for rows in packed[2:]]
     arrived = [swap(rows, "expert", d) for d, rows in enumerate(packed)]
@@ -644,7 +631,8 @@
         [near[0], near_cross[0], far[0], swap(far[0], "half", 1)],
         gain_here, gate_here, up_first, expert_up, count,
     )
-    far[1] = relay(far[1], sums[2])
+    cross = swap(cross, "half", 1)
+    far[1] = relay(far[1], sums[2], cross)
     hidden, down_here = expert_second(
         [near[1], near_cross[1], far[1], swap(far[1], "half", 1)],
         gain_here, gate_here, up_first, up_rest, sums, expert_down_part, count,
@@ -657,10 +645,10 @@
         mine.append(terms)
         got.append(swap(send, "half", 1))
     keep, send = chip_sum(mine, got)
-    own = [swap(rows, "expert", d) for d, rows in enumerate(cut(own, keep))]
-    terms = pair_sum(keep, swap(send, "pair", 1), capacity, experts)
-    cross = swap(join(own, terms[0]), "half", 1)
-    combined = own_rows(residual, own, cross)
+    own = cut(own, cross, keep, experts)
+    own = [swap(rows, "expert", d) for d, rows in enumerate(own)]
+    terms = pair_sum(keep, swap(send, "pair", 1), capacity, experts, own)
+    combined = own_rows(residual, own)
     back = [swap(term, "expert", d) for d, term in enumerate(terms)]
     return finish(combined, weighting, back)
 

time: 77.1 us -> 72.9 us (0.946)
  Pallas kernels: 35.8 us -> 31.4 us
    pallas_call x1, Pallas kernels: 8.06 us -> 5.23 us  [expert_second(): pl.pallas_call(functools.partial(expert_second_kernel, count), in_specs=[...]
    pallas_call x1, Pallas kernels: 7.79 us -> 5.9 us  [expert_first(): pl.pallas_call(functools.partial(expert_first_kernel, count), in_specs=[V...]
  transfers between devices with their start and end apart: 27 -> 27, of which waited for: 13 -> 11; matrix products, arithmetic and copies ran while one was open for 0% -> 0% of each run, Pallas kernels for 24% -> 23%
where the time goes in v7:
time: 72.9 us; the launch traced here: 72.6 us
  Pallas kernels  31.4 us (43%)
  starting transfers between devices  25.7 us (35%)
  waiting for transfers between devices  15.3 us (21%)
    ppermute x27, starting transfers between devices, swap(): lax.ppermute(x, axis, [(i, i ^ by) for i in range(lax.axis_size(axis))])  25.7 us
    ppermute x27, waiting for transfers between devices, swap(): lax.ppermute(x, axis, [(i, i ^ by) for i in range(lax.axis_size(axis))])  15.3 us
    pallas_call x1, Pallas kernels, load(): pl.pallas_call(functools.partial(load_kernel, len(weights)), in_specs=[AN...  6.03 us
    pallas_call x1, Pallas kernels, expert_first(): pl.pallas_call(functools.partial(expert_first_kernel, count), in_specs=[V...  5.9 us
    pallas_call x1, Pallas kernels, expert_second(): pl.pallas_call(functools.partial(expert_second_kernel, count), in_specs=[...  5.23 us
    pallas_call x1, Pallas kernels, attend(): pl.pallas_call(functools.partial(attend_kernel, rows // requests, heads /...  4.6 us
    pallas_call x1, Pallas kernels, route(): pl.pallas_call(functools.partial(route_kernel, capacity), in_specs=[SMEM]...  4.14 us
    pallas_call x2, Pallas kernels, expert_down(): pl.pallas_call(functools.partial(down_kernel, start, 512), in_specs=[VMEM...  2.71 us
  transfers between devices with their start and end apart: 27, of which 11 were waited for; matrix products, arithmetic and copies ran while one was open for 0% of the time, Pallas kernels for 23%

profile of v7, /device:TPU:0, one launch (start us, length us, event | category | flops | bytes accessed | tf_op | source)
XLA Modules:
  0.0 72.6 jit_solution(11359987210790407193)
XLA Ops:
  0.0 4.6 %attention.1 = (bf16[16,2944]{1,0:T(8,128)(2,1)S(1)}, bf16[16,2944]{1,0:T(8,128)(2,1)S(1)}, bf16[16,2944]{1,0:T(8,128)(2,1)S(1)}, bf16[16,2944]{1,0:T(8,128)(2,1)S(1)}) custom-call(f32[16]{0:T(128)} %decay_ref.1, s32[2,8]{1,0:T(2,128)} %bitcast.6, bf16[16,2048]{1,0:T(8,128)(2,1)} %q_ref.1, bf16[16,2048]{1,0:T(8,128)(2,1)} %k_ref.1, bf16[16,2048]{1,0:T(8,128)(2,1)} %v_ref.1, ...), custom_call_target="tpu_custom_call" | custom-call | tf_op jit(solution)/shard_map/attention/pallas_call | solution.py:107
  4.6 3.1 %collective-permute-start.1 = (bf16[16,2944]{1,0:T(8,128)(2,1)S(1)}, bf16[16,2944]{1,0:T(8,128)(2,1)S(1)}, u32[]{:S(2)}, u32[]{:S(2)}) collective-permute-start(bf16[16,2944]{1,0:T(8,128)(2,1)S(1)} %get-tuple-element.47), channel_id=1, source_target_pairs={{0,4},{4,0},{8,12},{12,8},{1,5},{5,1},{9,13},{13,9},{2,6},{6,2},{1... | collective-permute-start | bytes 282632 | tf_op jit(solution)/shard_map/ppermute | solution.py:579
  7.7 2.6 %collective-permute-start.3 = (bf16[16,2944]{1,0:T(8,128)(2,1)S(1)}, bf16[16,2944]{1,0:T(8,128)(2,1)S(1)}, u32[]{:S(2)}, u32[]{:S(2)}) collective-permute-start(bf16[16,2944]{1,0:T(8,128)(2,1)S(1)} %get-tuple-element.48), channel_id=1, source_target_pairs={{0,8},{4,12},{8,0},{12,4},{1,9},{5,13},{9,1},{13,5},{2,10},{6,14},... | collective-permute-start | bytes 282632 | tf_op jit(solution)/shard_map/ppermute | solution.py:579
  10.3 0.0 collective-permute-start.5
  10.3 6.0 %load.1 = (bf16[16,2944]{1,0:T(8,128)(2,1)S(1)}, bf16[2048,768]{1,0:T(8,128)(2,1)S(1)}, f32[1,6144]{1,0:T(1,128)S(1)}, bf16[1152,6144]{1,0:T(8,128)(2,1)S(1)}) custom-call(bf16[16,2944]{1,0:T(8,128)(2,1)S(1)} %get-tuple-element.45.rows_hbm, bf16[2048,768]{1,0:T(8,128)(2,1)} %refs_0_.1, f32[1,6144]{1,0:T(1,128)} %bitcast.4, bf16[1152,6144]{1,0:T(8,128)(2,1)} %refs_2_.1), custom_call_target="tpu_custom_call" | custom-call | bytes 17326080 | tf_op jit(solution)/shard_map/load/pallas_call | solution.py:146
  16.3 0.1 collective-permute-start
  16.4 0.0 collective-permute-done.1.refs_2_
  16.4 0.5 collective-permute-start.2
  16.9 0.9 %collective-permute-done.3.refs_4_ = bf16[16,2944]{1,0:T(8,128)(2,1)S(1)} collective-permute-done((bf16[16,2944]{1,0:T(8,128)(2,1)S(1)}, bf16[16,2944]{1,0:T(8,128)(2,1)S(1)}, u32[]{:S(2)}, u32[]{:S(2)}) %collective-permute-start.3) | collective-permute-done | bytes 94240 | tf_op jit(solution)/shard_map/ppermute | solution.py:579
  17.8 0.0 collective-permute-start.4
  17.8 0.0 collective-permute-done.5.refs_6_
  17.8 0.5 collective-permute-start.6
  18.3 0.0 collective-permute-done.refs_1_
  18.3 0.0 collective-permute-done.2.refs_3_
  18.3 0.8 %collective-permute-done.4.refs_5_ = bf16[16,2944]{1,0:T(8,128)(2,1)S(1)} collective-permute-done((bf16[16,2944]{1,0:T(8,128)(2,1)S(1)}, bf16[16,2944]{1,0:T(8,128)(2,1)S(1)}, u32[]{:S(2)}, u32[]{:S(2)}) %collective-permute-start.4) | collective-permute-done | bytes 94240 | tf_op jit(solution)/shard_map/ppermute | solution.py:579
  19.1 0.2 collective-permute-done.6.refs_7_
  19.3 0.7 projection.1
  20.0 1.6 %collective-permute-start.7 = (bf16[64,768]{1,0:T(8,128)(2,1)S(1)}, bf16[64,768]{1,0:T(8,128)(2,1)S(1)}, u32[]{:S(2)}, u32[]{:S(2)}) collective-permute-start(bf16[64,768]{1,0:T(8,128)(2,1)S(1)} %get-tuple-element.52), channel_id=1, source_target_pairs={{0,1},{1,0},{2,3},{3,2},{4,5},{5,4},{6,7},{7,6},{8,9},{9,8},{10,11... | collective-permute-start | bytes 294920 | tf_op jit(solution)/shard_map/ppermute | solution.py:579
  21.5 4.1 %route.1 = (bf16[128,64]{1,0:T(8,128)(2,1)S(1)}, f32[64,768]{1,0:T(8,128)S(1)}, bf16[640,6144]{1,0:T(8,128)(2,1)S(1)}, bf16[32,32]{1,0:T(8,128)(2,1)S(1)}) custom-call(s32[2,8]{1,0:T(2,128)} %bitcast.7, f32[2,8]{1,0:T(2,128)} %bitcast.8, bf16[16,2944]{1,0:T(8,128)(2,1)S(1)} %get-tuple-element.46.refs_0_, bf16[16,2944]{1,0:T(8,128)(2,1)S(1)} %collective-permute-done.refs_1_, ...), custom_call_target="tpu_custom_call" | custom-call | flops 1000000 | bytes 8000000 | tf_op jit(solution)/shard_map/route/pallas_call | solution.py:258
  25.7 0.0 collective-permute-done.7.got_ref
  25.7 0.2 pack.1
  25.9 1.5 %collective-permute-start.13 = (bf16[32,768]{1,0:T(8,128)(2,1)S(1)}, bf16[32,768]{1,0:T(8,128)(2,1)S(1)}, u32[]{:S(2)}, u32[]{:S(2)}) collective-permute-start(bf16[32,768]{1,0:T(8,128)(2,1)S(1)} %get-tuple-element.58.refs_0_), channel_id=1, source_target_pairs={{0,4},{4,0},{8,12},{12,8},{1,5},{5,1},{9,13},{13,9},{2,6},{6,2},{1... | collective-permute-start | bytes 147464 | tf_op jit(solution)/shard_map/ppermute | solution.py:579
  27.4 2.5 %collective-permute-start.10 = (bf16[32,768]{1,0:T(8,128)(2,1)S(1)}, bf16[32,768]{1,0:T(8,128)(2,1)S(1)}, u32[]{:S(2)}, u32[]{:S(2)}) collective-permute-start(bf16[32,768]{1,0:T(8,128)(2,1)S(1)} %relay.4), channel_id=1, source_target_pairs={{0,12},{4,8},{8,4},{12,0},{1,13},{5,9},{9,5},{13,1},{2,14},{6,10},... | collective-permute-start | bytes 147464 | tf_op jit(solution)/shard_map/ppermute | solution.py:579
  29.9 0.0 collective-permute-start.9
  29.9 0.1 collective-permute-done.13
  30.1 0.9 %collective-permute-start.15 = (bf16[64,768]{1,0:T(8,128)(2,1)S(1)}, bf16[64,768]{1,0:T(8,128)(2,1)S(1)}, u32[]{:S(2)}, u32[]{:S(2)}) collective-permute-start(bf16[64,768]{1,0:T(8,128)(2,1)S(1)} %constant_dynamic-update-slice_fusion.2.refs_0_), channel_id=1, source_target_pairs={{0,1},{1,0},{2,3},{3,2},{4,5},{5,4},{6,7},{7,6},{8,9},{9,8},{10,11... | collective-permute-start | bytes 294920 | tf_op jit(solution)/shard_map/ppermute | solution.py:579
  30.9 0.0 collective-permute-start.14
  31.0 4.2 %collective-permute-done.9 = bf16[32,768]{1,0:T(8,128)(2,1)S(1)} collective-permute-done((bf16[32,768]{1,0:T(8,128)(2,1)S(1)}, bf16[32,768]{1,0:T(8,128)(2,1)S(1)}, u32[]{:S(2)}, u32[]{:S(2)}) %collective-permute-start.9) | collective-permute-done | bytes 49184 | tf_op jit(solution)/shard_map/ppermute | solution.py:579
  35.2 0.0 collective-permute-done.15.refs_2_
  35.2 0.1 collective-permute-start.16
  35.3 0.0 collective-permute-done.10
  35.3 0.8 %collective-permute-start.12 = (bf16[64,768]{1,0:T(8,128)(2,1)S(1)}, bf16[64,768]{1,0:T(8,128)(2,1)S(1)}, u32[]{:S(2)}, u32[]{:S(2)}) collective-permute-start(bf16[64,768]{1,0:T(8,128)(2,1)S(1)} %constant_dynamic-update-slice_fusion.refs_0_), channel_id=1, source_target_pairs={{0,1},{1,0},{2,3},{3,2},{4,5},{5,4},{6,7},{7,6},{8,9},{9,8},{10,11... | collective-permute-start | bytes 294920 | tf_op jit(solution)/shard_map/ppermute | solution.py:579
  36.1 0.2 collective-permute-start.8
  36.3 0.3 collective-permute-start.11
  36.6 0.0 collective-permute-done.14.refs_1_
  36.6 0.0 collective-permute-done.16.refs_3_
  36.6 5.9 %experts_first.1 = (f32[1152,64]{1,0:T(8,128)S(1)}, f32[1152,64]{1,0:T(8,128)S(1)}, f32[64,128]{1,0:T(8,128)S(1)}, bf16[512,6144]{1,0:T(8,128)(2,1)S(1)}) custom-call(bf16[64,768]{1,0:T(8,128)(2,1)S(1)} %constant_dynamic-update-slice_fusion.2.refs_0_, bf16[64,768]{1,0:T(8,128)(2,1)S(1)} %collective-permute-done.14.refs_1_, ...), custom_call_target="tpu_custom_call" | custom-call | flops 905969664 | bytes 14155776 | tf_op jit(solution)/shard_map/experts_first/pallas_call | solution.py:392
  42.5 0.0 collective-permute-done.8.refs_1_.cross_ref
  42.6 0.0 collective-permute-done.12.rows_ref
  42.6 0.3 collective-permute-start.17
  42.8 0.0 collective-permute-done.11.refs_1_
  42.8 1.1 %collective-permute-done.17.refs_3_ = bf16[64,768]{1,0:T(8,128)(2,1)S(1)} collective-permute-done((bf16[64,768]{1,0:T(8,128)(2,1)S(1)}, bf16[64,768]{1,0:T(8,128)(2,1)S(1)}, u32[]{:S(2)}, u32[]{:S(2)}) %collective-permute-start.17) | collective-permute-done | bytes 98336 | tf_op jit(solution)/shard_map/ppermute | solution.py:579
  43.9 5.2 %experts_second.1 = (bf16[64,1152]{1,0:T(8,128)(2,1)S(1)}, bf16[1152,6144]{1,0:T(8,128)(2,1)S(1)}) custom-call(bf16[64,768]{1,0:T(8,128)(2,1)S(1)} %constant_dynamic-update-slice_fusion.refs_0_, bf16[64,768]{1,0:T(8,128)(2,1)S(1)} %collective-permute-done.11.refs_1_, bf16[64,768]{1,0:T(8,128)(2,1)S(1)} %relay.5.refs_2_, ...), custom_call_target="tpu_custom_call" | custom-call | flops 905969664 | bytes 14155776 | tf_op jit(solution)/shard_map/experts_second/pallas_call | solution.py:427
  49.2 1.4 %experts_down.3 = (f32[32,3072]{1,0:T(8,128)S(1)}, bf16[32,3072]{1,0:T(8,128)(2,1)S(1)}) custom-call(bf16[64,1152]{1,0:T(8,128)(2,1)S(1)} %get-tuple-element.68.hidden_ref, bf16[1152,6144]{1,0:T(8,128)(2,1)S(1)} %get-tuple-element.69.weight_ref), custom_call_target="tpu_custom_call" | custom-call | flops 905969664 | bytes 7077888 | tf_op jit(solution)/shard_map/experts_down/pallas_call | solution.py:443
  50.6 1.4 %experts_down.2 = (f32[32,3072]{1,0:T(8,128)S(1)}, bf16[32,3072]{1,0:T(8,128)(2,1)S(1)}) custom-call(bf16[64,1152]{1,0:T(8,128)(2,1)S(1)} %get-tuple-element.68.hidden_ref, bf16[1152,6144]{1,0:T(8,128)(2,1)S(1)} %get-tuple-element.69.weight_ref), custom_call_target="tpu_custom_call" | custom-call | flops 905969664 | bytes 7077888 | tf_op jit(solution)/shard_map/experts_down/pallas_call | solution.py:443
  51.9 0.3 collective-permute-start.19
  52.2 0.3 collective-permute-start.18
  52.5 0.9 %collective-permute-done.19.refs_3_ = bf16[32,3072]{1,0:T(8,128)(2,1)S(1)} collective-permute-done((bf16[32,3072]{1,0:T(8,128)(2,1)S(1)}, bf16[32,3072]{1,0:T(8,128)(2,1)S(1)}, u32[]{:S(2)}, u32[]{:S(2)}) %collective-permute-start.19) | collective-permute-done | bytes 196640 | tf_op jit(solution)/shard_map/ppermute | solution.py:579
  53.4 0.3 collective-permute-done.18.refs_2_
  53.7 0.1 chip_sum.1
  53.8 1.3 %collective-permute-start.23 = (bf16[16,6144]{1,0:T(8,128)(2,1)S(1)}, bf16[16,6144]{1,0:T(8,128)(2,1)S(1)}, u32[]{:S(2)}, u32[]{:S(2)}) collective-permute-start(bf16[16,6144]{1,0:T(8,128)(2,1)S(1)} %get-tuple-element.80), channel_id=1, source_target_pairs={{0,1},{1,0},{2,3},{3,2},{4,5},{5,4},{6,7},{7,6},{8,9},{9,8},{10,11... | collective-permute-start | bytes 589832 | tf_op jit(solution)/shard_map/ppermute | solution.py:579
  55.1 1.3 %collective-permute-start.20 = (bf16[16,768]{1,0:T(8,128)(2,1)S(1)}, bf16[16,768]{1,0:T(8,128)(2,1)S(1)}, u32[]{:S(2)}, u32[]{:S(2)}) collective-permute-start(bf16[16,768]{1,0:T(8,128)(2,1)S(1)} %get-tuple-element.76), channel_id=1, source_target_pairs={{0,4},{4,0},{8,12},{12,8},{1,5},{5,1},{9,13},{13,9},{2,6},{6,2},{1... | collective-permute-start | bytes 73736 | tf_op jit(solution)/shard_map/ppermute | solution.py:579
  56.4 1.7 %collective-permute-start.21 = (bf16[16,768]{1,0:T(8,128)(2,1)S(1)}, bf16[16,768]{1,0:T(8,128)(2,1)S(1)}, u32[]{:S(2)}, u32[]{:S(2)}) collective-permute-start(bf16[16,768]{1,0:T(8,128)(2,1)S(1)} %get-tuple-element.77), channel_id=1, source_target_pairs={{0,8},{4,12},{8,0},{12,4},{1,9},{5,13},{9,1},{13,5},{2,10},{6,14},... | collective-permute-start | bytes 73736 | tf_op jit(solution)/shard_map/ppermute | solution.py:579
  58.1 1.4 %collective-permute-start.22 = (bf16[16,768]{1,0:T(8,128)(2,1)S(1)}, bf16[16,768]{1,0:T(8,128)(2,1)S(1)}, u32[]{:S(2)}, u32[]{:S(2)}) collective-permute-start(bf16[16,768]{1,0:T(8,128)(2,1)S(1)} %get-tuple-element.78), channel_id=1, source_target_pairs={{0,12},{4,8},{8,4},{12,0},{1,13},{5,9},{9,5},{13,1},{2,14},{6,10},... | collective-permute-start | bytes 73736 | tf_op jit(solution)/shard_map/ppermute | solution.py:579
  59.6 2.1 %collective-permute-done.21.refs_2_ = bf16[16,768]{1,0:T(8,128)(2,1)S(1)} collective-permute-done((bf16[16,768]{1,0:T(8,128)(2,1)S(1)}, bf16[16,768]{1,0:T(8,128)(2,1)S(1)}, u32[]{:S(2)}, u32[]{:S(2)}) %collective-permute-start.21) | collective-permute-done | bytes 24608 | tf_op jit(solution)/shard_map/ppermute | solution.py:579
  61.7 2.1 %collective-permute-done.22.refs_3_ = bf16[16,768]{1,0:T(8,128)(2,1)S(1)} collective-permute-done((bf16[16,768]{1,0:T(8,128)(2,1)S(1)}, bf16[16,768]{1,0:T(8,128)(2,1)S(1)}, u32[]{:S(2)}, u32[]{:S(2)}) %collective-permute-start.22) | collective-permute-done | bytes 24608 | tf_op jit(solution)/shard_map/ppermute | solution.py:579
  63.8 0.1 pair_sum.1
  63.9 0.1 collective-permute-start.24
  64.0 2.0 %collective-permute-start.25 = (bf16[8,3072]{1,0:T(8,128)(2,1)S(1)}, bf16[8,3072]{1,0:T(8,128)(2,1)S(1)}, u32[]{:S(2)}, u32[]{:S(2)}) collective-permute-start(bf16[8,3072]{1,0:T(8,128)(2,1)S(1)} %get-tuple-element.83), channel_id=1, source_target_pairs={{0,8},{4,12},{8,0},{12,4},{1,9},{5,13},{9,1},{13,5},{2,10},{6,14},... | collective-permute-start | bytes 147464 | tf_op jit(solution)/shard_map/ppermute | solution.py:579
  65.9 2.4 %collective-permute-start.26 = (bf16[8,3072]{1,0:T(8,128)(2,1)S(1)}, bf16[8,3072]{1,0:T(8,128)(2,1)S(1)}, u32[]{:S(2)}, u32[]{:S(2)}) collective-permute-start(bf16[8,3072]{1,0:T(8,128)(2,1)S(1)} %get-tuple-element.84), channel_id=1, source_target_pairs={{0,12},{4,8},{8,4},{12,0},{1,13},{5,9},{9,5},{13,1},{2,14},{6,10},... | collective-permute-start | bytes 147464 | tf_op jit(solution)/shard_map/ppermute | solution.py:579
  68.3 0.9 %own_rows.1.combined_ref = f32[8,6144]{1,0:T(8,128)S(1)} custom-call(bf16[8,6144]{1,0:T(8,128)(2,1)} %residual_ref.3, bf16[16,768]{1,0:T(8,128)(2,1)S(1)} %get-tuple-element.75.refs_0_, bf16[16,768]{1,0:T(8,128)(2,1)S(1)} %collective-permute-done.20.refs_1_, bf16[16,768]{1,0:T(8,128)(2,1)S(1)} %collective-permute-done.21.refs_2_, ...), custom_call_target="tpu_custom_call" | custom-call | flops 1000000 | bytes 1000000 | tf_op jit(solution)/shard_map/own_rows/pallas_call | solution.py:545
  69.3 0.0 collective-permute-done.25.refs_2_
  69.3 2.5 %collective-permute-done.26.refs_3_ = bf16[8,3072]{1,0:T(8,128)(2,1)S(1)} collective-permute-done((bf16[8,3072]{1,0:T(8,128)(2,1)S(1)}, bf16[8,3072]{1,0:T(8,128)(2,1)S(1)}, u32[]{:S(2)}, u32[]{:S(2)}) %collective-permute-start.26) | collective-permute-done | bytes 49184 | tf_op jit(solution)/shard_map/ppermute | solution.py:579
  71.8 0.8 %finish.1 = bf16[8,6144]{1,0:T(8,128)(2,1)} custom-call(f32[8,6144]{1,0:T(8,128)S(1)} %own_rows.1.combined_ref, bf16[32,32]{1,0:T(8,128)(2,1)S(1)} %get-tuple-element.79.weighting_ref, bf16[8,3072]{1,0:T(8,128)(2,1)S(1)} %get-tuple-element.81.refs_0_, bf16[8,3072]{1,0:T(8,128)(2,1)S(1)} %collective-permute-done.24.refs_1_, ...), custom_call_target="tpu_custom_call" | custom-call | tf_op jit(solution)/shard_map/finish/pallas_call | solution.py:568
  (11 shorter events, 0.1 us)
Async XLA Ops:
  4.6 11.8 %collective-permute-start.1 = (bf16[16,2944]{1,0:T(8,128)(2,1)S(1)}, bf16[16,2944]{1,0:T(8,128)(2,1)S(1)}, u32[]{:S(2)}, u32[]{:S(2)}) collective-permute-start(bf16[16,2944]{1,0:T(8,128)(2,1)S(1)} %get-tuple-element.47), channel_id=1, source_target_pairs={{0,4},{4,0},{8,12},{12,8},{1,5},{5,1},{9,13},{13,9},{2,6},{6,2},{1... | collective-permute-start | bytes 282632 | tf_op jit(solution)/shard_map/ppermute | solution.py:579
  7.7 10.1 %collective-permute-start.3 = (bf16[16,2944]{1,0:T(8,128)(2,1)S(1)}, bf16[16,2944]{1,0:T(8,128)(2,1)S(1)}, u32[]{:S(2)}, u32[]{:S(2)}) collective-permute-start(bf16[16,2944]{1,0:T(8,128)(2,1)S(1)} %get-tuple-element.48), channel_id=1, source_target_pairs={{0,8},{4,12},{8,0},{12,4},{1,9},{5,13},{9,1},{13,5},{2,10},{6,14},... | collective-permute-start | bytes 282632 | tf_op jit(solution)/shard_map/ppermute | solution.py:579
  10.3 7.5 %collective-permute-start.5 = (bf16[16,2944]{1,0:T(8,128)(2,1)S(1)}, bf16[16,2944]{1,0:T(8,128)(2,1)S(1)}, u32[]{:S(2)}, u32[]{:S(2)}) collective-permute-start(bf16[16,2944]{1,0:T(8,128)(2,1)S(1)} %get-tuple-element.49), channel_id=1, source_target_pairs={{0,12},{4,8},{8,4},{12,0},{1,13},{5,9},{9,5},{13,1},{2,14},{6,10},... | collective-permute-start | bytes 282632 | tf_op jit(solution)/shard_map/ppermute | solution.py:579
  16.3 2.0 %collective-permute-start = (bf16[16,2944]{1,0:T(8,128)(2,1)S(1)}, bf16[16,2944]{1,0:T(8,128)(2,1)S(1)}, u32[]{:S(2)}, u32[]{:S(2)}) collective-permute-start(bf16[16,2944]{1,0:T(8,128)(2,1)S(1)} %get-tuple-element.46.refs_0_), channel_id=1, source_target_pairs={{0,2},{2,0},{1,3},{3,1},{4,6},{6,4},{5,7},{7,5},{8,10},{10,8},{9,1... | collective-permute-start | bytes 282632 | tf_op jit(solution)/shard_map/ppermute | solution.py:579
  16.4 1.9 %collective-permute-start.2 = (bf16[16,2944]{1,0:T(8,128)(2,1)S(1)}, bf16[16,2944]{1,0:T(8,128)(2,1)S(1)}, u32[]{:S(2)}, u32[]{:S(2)}) collective-permute-start(bf16[16,2944]{1,0:T(8,128)(2,1)S(1)} %collective-permute-done.1.refs_2_), channel_id=1, source_target_pairs={{0,2},{2,0},{1,3},{3,1},{4,6},{6,4},{5,7},{7,5},{8,10},{10,8},{9,1... | collective-permute-start | bytes 282632 | tf_op jit(solution)/shard_map/ppermute | solution.py:579
  17.8 1.3 %collective-permute-start.4 = (bf16[16,2944]{1,0:T(8,128)(2,1)S(1)}, bf16[16,2944]{1,0:T(8,128)(2,1)S(1)}, u32[]{:S(2)}, u32[]{:S(2)}) collective-permute-start(bf16[16,2944]{1,0:T(8,128)(2,1)S(1)} %collective-permute-done.3.refs_4_), channel_id=1, source_target_pairs={{0,2},{2,0},{1,3},{3,1},{4,6},{6,4},{5,7},{7,5},{8,10},{10,8},{9,1... | collective-permute-start | bytes 282632 | tf_op jit(solution)/shard_map/ppermute | solution.py:579
  17.8 1.4 %collective-permute-start.6 = (bf16[16,2944]{1,0:T(8,128)(2,1)S(1)}, bf16[16,2944]{1,0:T(8,128)(2,1)S(1)}, u32[]{:S(2)}, u32[]{:S(2)}) collective-permute-start(bf16[16,2944]{1,0:T(8,128)(2,1)S(1)} %collective-permute-done.5.refs_6_), channel_id=1, source_target_pairs={{0,2},{2,0},{1,3},{3,1},{4,6},{6,4},{5,7},{7,5},{8,10},{10,8},{9,1... | collective-permute-start | bytes 282632 | tf_op jit(solution)/shard_map/ppermute | solution.py:579
  20.0 5.7 %collective-permute-start.7 = (bf16[64,768]{1,0:T(8,128)(2,1)S(1)}, bf16[64,768]{1,0:T(8,128)(2,1)S(1)}, u32[]{:S(2)}, u32[]{:S(2)}) collective-permute-start(bf16[64,768]{1,0:T(8,128)(2,1)S(1)} %get-tuple-element.52), channel_id=1, source_target_pairs={{0,1},{1,0},{2,3},{3,2},{4,5},{5,4},{6,7},{7,6},{8,9},{9,8},{10,11... | collective-permute-start | bytes 294920 | tf_op jit(solution)/shard_map/ppermute | solution.py:579
  25.9 4.2 %collective-permute-start.13 = (bf16[32,768]{1,0:T(8,128)(2,1)S(1)}, bf16[32,768]{1,0:T(8,128)(2,1)S(1)}, u32[]{:S(2)}, u32[]{:S(2)}) collective-permute-start(bf16[32,768]{1,0:T(8,128)(2,1)S(1)} %get-tuple-element.58.refs_0_), channel_id=1, source_target_pairs={{0,4},{4,0},{8,12},{12,8},{1,5},{5,1},{9,13},{13,9},{2,6},{6,2},{1... | collective-permute-start | bytes 147464 | tf_op jit(solution)/shard_map/ppermute | solution.py:579
  27.4 7.9 %collective-permute-start.10 = (bf16[32,768]{1,0:T(8,128)(2,1)S(1)}, bf16[32,768]{1,0:T(8,128)(2,1)S(1)}, u32[]{:S(2)}, u32[]{:S(2)}) collective-permute-start(bf16[32,768]{1,0:T(8,128)(2,1)S(1)} %relay.4), channel_id=1, source_target_pairs={{0,12},{4,8},{8,4},{12,0},{1,13},{5,9},{9,5},{13,1},{2,14},{6,10},... | collective-permute-start | bytes 147464 | tf_op jit(solution)/shard_map/ppermute | solution.py:579
  29.9 5.2 %collective-permute-start.9 = (bf16[32,768]{1,0:T(8,128)(2,1)S(1)}, bf16[32,768]{1,0:T(8,128)(2,1)S(1)}, u32[]{:S(2)}, u32[]{:S(2)}) collective-permute-start(bf16[32,768]{1,0:T(8,128)(2,1)S(1)} %relay.3), channel_id=1, source_target_pairs={{0,8},{4,12},{8,0},{12,4},{1,9},{5,13},{9,1},{13,5},{2,10},{6,14},... | collective-permute-start | bytes 147464 | tf_op jit(solution)/shard_map/ppermute | solution.py:579
  30.1 5.1 %collective-permute-start.15 = (bf16[64,768]{1,0:T(8,128)(2,1)S(1)}, bf16[64,768]{1,0:T(8,128)(2,1)S(1)}, u32[]{:S(2)}, u32[]{:S(2)}) collective-permute-start(bf16[64,768]{1,0:T(8,128)(2,1)S(1)} %constant_dynamic-update-slice_fusion.2.refs_0_), channel_id=1, source_target_pairs={{0,1},{1,0},{2,3},{3,2},{4,5},{5,4},{6,7},{7,6},{8,9},{9,8},{10,11... | collective-permute-start | bytes 294920 | tf_op jit(solution)/shard_map/ppermute | solution.py:579
  30.9 5.7 %collective-permute-start.14 = (bf16[64,768]{1,0:T(8,128)(2,1)S(1)}, bf16[64,768]{1,0:T(8,128)(2,1)S(1)}, u32[]{:S(2)}, u32[]{:S(2)}) collective-permute-start(bf16[64,768]{1,0:T(8,128)(2,1)S(1)} %constant_dynamic-update-slice_fusion.2.refs_0_), channel_id=1, source_target_pairs={{0,2},{2,0},{1,3},{3,1},{4,6},{6,4},{5,7},{7,5},{8,10},{10,8},{9,1... | collective-permute-start | bytes 294920 | tf_op jit(solution)/shard_map/ppermute | solution.py:579
  35.2 1.5 %collective-permute-start.16 = (bf16[64,768]{1,0:T(8,128)(2,1)S(1)}, bf16[64,768]{1,0:T(8,128)(2,1)S(1)}, u32[]{:S(2)}, u32[]{:S(2)}) collective-permute-start(bf16[64,768]{1,0:T(8,128)(2,1)S(1)} %collective-permute-done.15.refs_2_), channel_id=1, source_target_pairs={{0,2},{2,0},{1,3},{3,1},{4,6},{6,4},{5,7},{7,5},{8,10},{10,8},{9,1... | collective-permute-start | bytes 294920 | tf_op jit(solution)/shard_map/ppermute | solution.py:579
  35.3 7.3 %collective-permute-start.12 = (bf16[64,768]{1,0:T(8,128)(2,1)S(1)}, bf16[64,768]{1,0:T(8,128)(2,1)S(1)}, u32[]{:S(2)}, u32[]{:S(2)}) collective-permute-start(bf16[64,768]{1,0:T(8,128)(2,1)S(1)} %constant_dynamic-update-slice_fusion.refs_0_), channel_id=1, source_target_pairs={{0,1},{1,0},{2,3},{3,2},{4,5},{5,4},{6,7},{7,6},{8,9},{9,8},{10,11... | collective-permute-start | bytes 294920 | tf_op jit(solution)/shard_map/ppermute | solution.py:579
  36.1 6.4 %collective-permute-start.8 = (bf16[32,768]{1,0:T(8,128)(2,1)S(1)}, bf16[32,768]{1,0:T(8,128)(2,1)S(1)}, u32[]{:S(2)}, u32[]{:S(2)}) collective-permute-start(bf16[32,768]{1,0:T(8,128)(2,1)S(1)} %get-tuple-element.56), channel_id=1, source_target_pairs={{0,2},{2,0},{1,3},{3,1},{4,6},{6,4},{5,7},{7,5},{8,10},{10,8},{9,1... | collective-permute-start | bytes 147464 | tf_op jit(solution)/shard_map/ppermute | solution.py:579
  36.3 6.5 %collective-permute-start.11 = (bf16[64,768]{1,0:T(8,128)(2,1)S(1)}, bf16[64,768]{1,0:T(8,128)(2,1)S(1)}, u32[]{:S(2)}, u32[]{:S(2)}) collective-permute-start(bf16[64,768]{1,0:T(8,128)(2,1)S(1)} %constant_dynamic-update-slice_fusion.refs_0_), channel_id=1, source_target_pairs={{0,2},{2,0},{1,3},{3,1},{4,6},{6,4},{5,7},{7,5},{8,10},{10,8},{9,1... | collective-permute-start | bytes 294920 | tf_op jit(solution)/shard_map/ppermute | solution.py:579
  42.6 1.4 %collective-permute-start.17 = (bf16[64,768]{1,0:T(8,128)(2,1)S(1)}, bf16[64,768]{1,0:T(8,128)(2,1)S(1)}, u32[]{:S(2)}, u32[]{:S(2)}) collective-permute-start(bf16[64,768]{1,0:T(8,128)(2,1)S(1)} %relay.5.refs_2_), channel_id=1, source_target_pairs={{0,2},{2,0},{1,3},{3,1},{4,6},{6,4},{5,7},{7,5},{8,10},{10,8},{9,1... | collective-permute-start | bytes 294920 | tf_op jit(solution)/shard_map/ppermute | solution.py:579
  51.9 1.5 %collective-permute-start.19 = (bf16[32,3072]{1,0:T(8,128)(2,1)S(1)}, bf16[32,3072]{1,0:T(8,128)(2,1)S(1)}, u32[]{:S(2)}, u32[]{:S(2)}) collective-permute-start(bf16[32,3072]{1,0:T(8,128)(2,1)S(1)} %get-tuple-element.73), channel_id=1, source_target_pairs={{0,2},{2,0},{1,3},{3,1},{4,6},{6,4},{5,7},{7,5},{8,10},{10,8},{9,1... | collective-permute-start | bytes 589832 | tf_op jit(solution)/shard_map/ppermute | solution.py:579
  52.2 1.5 %collective-permute-start.18 = (bf16[32,3072]{1,0:T(8,128)(2,1)S(1)}, bf16[32,3072]{1,0:T(8,128)(2,1)S(1)}, u32[]{:S(2)}, u32[]{:S(2)}) collective-permute-start(bf16[32,3072]{1,0:T(8,128)(2,1)S(1)} %get-tuple-element.72), channel_id=1, source_target_pairs={{0,2},{2,0},{1,3},{3,1},{4,6},{6,4},{5,7},{7,5},{8,10},{10,8},{9,1... | collective-permute-start | bytes 589832 | tf_op jit(solution)/shard_map/ppermute | solution.py:579
  53.8 10.0 %collective-permute-start.23 = (bf16[16,6144]{1,0:T(8,128)(2,1)S(1)}, bf16[16,6144]{1,0:T(8,128)(2,1)S(1)}, u32[]{:S(2)}, u32[]{:S(2)}) collective-permute-start(bf16[16,6144]{1,0:T(8,128)(2,1)S(1)} %get-tuple-element.80), channel_id=1, source_target_pairs={{0,1},{1,0},{2,3},{3,2},{4,5},{5,4},{6,7},{7,6},{8,9},{9,8},{10,11... | collective-permute-start | bytes 589832 | tf_op jit(solution)/shard_map/ppermute | solution.py:579
  55.1 4.5 %collective-permute-start.20 = (bf16[16,768]{1,0:T(8,128)(2,1)S(1)}, bf16[16,768]{1,0:T(8,128)(2,1)S(1)}, u32[]{:S(2)}, u32[]{:S(2)}) collective-permute-start(bf16[16,768]{1,0:T(8,128)(2,1)S(1)} %get-tuple-element.76), channel_id=1, source_target_pairs={{0,4},{4,0},{8,12},{12,8},{1,5},{5,1},{9,13},{13,9},{2,6},{6,2},{1... | collective-permute-start | bytes 73736 | tf_op jit(solution)/shard_map/ppermute | solution.py:579
  56.4 5.2 %collective-permute-start.21 = (bf16[16,768]{1,0:T(8,128)(2,1)S(1)}, bf16[16,768]{1,0:T(8,128)(2,1)S(1)}, u32[]{:S(2)}, u32[]{:S(2)}) collective-permute-start(bf16[16,768]{1,0:T(8,128)(2,1)S(1)} %get-tuple-element.77), channel_id=1, source_target_pairs={{0,8},{4,12},{8,0},{12,4},{1,9},{5,13},{9,1},{13,5},{2,10},{6,14},... | collective-permute-start | bytes 73736 | tf_op jit(solution)/shard_map/ppermute | solution.py:579
  58.1 5.6 %collective-permute-start.22 = (bf16[16,768]{1,0:T(8,128)(2,1)S(1)}, bf16[16,768]{1,0:T(8,128)(2,1)S(1)}, u32[]{:S(2)}, u32[]{:S(2)}) collective-permute-start(bf16[16,768]{1,0:T(8,128)(2,1)S(1)} %get-tuple-element.78), channel_id=1, source_target_pairs={{0,12},{4,8},{8,4},{12,0},{1,13},{5,9},{9,5},{13,1},{2,14},{6,10},... | collective-permute-start | bytes 73736 | tf_op jit(solution)/shard_map/ppermute | solution.py:579
  63.9 5.4 %collective-permute-start.24 = (bf16[8,3072]{1,0:T(8,128)(2,1)S(1)}, bf16[8,3072]{1,0:T(8,128)(2,1)S(1)}, u32[]{:S(2)}, u32[]{:S(2)}) collective-permute-start(bf16[8,3072]{1,0:T(8,128)(2,1)S(1)} %get-tuple-element.82), channel_id=1, source_target_pairs={{0,4},{4,0},{8,12},{12,8},{1,5},{5,1},{9,13},{13,9},{2,6},{6,2},{1... | collective-permute-start | bytes 147464 | tf_op jit(solution)/shard_map/ppermute | solution.py:579
  64.0 5.3 %collective-permute-start.25 = (bf16[8,3072]{1,0:T(8,128)(2,1)S(1)}, bf16[8,3072]{1,0:T(8,128)(2,1)S(1)}, u32[]{:S(2)}, u32[]{:S(2)}) collective-permute-start(bf16[8,3072]{1,0:T(8,128)(2,1)S(1)} %get-tuple-element.83), channel_id=1, source_target_pairs={{0,8},{4,12},{8,0},{12,4},{1,9},{5,13},{9,1},{13,5},{2,10},{6,14},... | collective-permute-start | bytes 147464 | tf_op jit(solution)/shard_map/ppermute | solution.py:579
  65.9 5.9 %collective-permute-start.26 = (bf16[8,3072]{1,0:T(8,128)(2,1)S(1)}, bf16[8,3072]{1,0:T(8,128)(2,1)S(1)}, u32[]{:S(2)}, u32[]{:S(2)}) collective-permute-start(bf16[8,3072]{1,0:T(8,128)(2,1)S(1)} %get-tuple-element.84), channel_id=1, source_target_pairs={{0,12},{4,8},{8,4},{12,0},{1,13},{5,9},{9,5},{13,1},{2,14},{6,10},... | collective-permute-start | bytes 147464 | tf_op jit(solution)/shard_map/ppermute | solution.py:579

commit v8 on v7

--- a/solution.py
+++ b/solution.py
@@ -75,14 +75,14 @@
     distance = jnp.maximum(row - col, 0).astype(F32)
     owner = lax.broadcasted_iota(jnp.int32, (rows, size), 0)
     age = (owner % positions + 1).astype(F32)
+    of_request = [
+        jnp.where(owner // positions == r, 1.0, 0.0).astype(BF16) for r in range(requests)
+    ]
     for i in range(heads):
         rate = decay_ref[first + i]
         at = slice(i * size, (i + 1) * size)
         q = q_ref[:, at]
-        spread_q = jnp.concatenate(
-            [jnp.where(owner // positions == r, q, jnp.zeros_like(q)) for r in range(requests)],
-            axis=1,
-        )
+        spread_q = jnp.concatenate([q * mask for mask in of_request], axis=1)
         high, low = halves_of(s_ref[:, i].reshape(requests * size, size))
         from_state = (dot(spread_q, high) + dot(spread_q, low)) * jnp.exp(-rate * age)
         scores = jnp.where(seen, dot_t(q, k_ref[:, at]) * jnp.exp(-rate * distance), 0.0)
@@ -101,7 +101,7 @@
 ):
     requests, heads, size, _ = states.shape
     rows = queries.shape[0]
-    step = 4 if heads % 4 == 0 else 1
+    step = 8 if heads % 8 == 0 else 1
     wide = pl.BlockSpec((rows, step * size), lambda i: (0, i))
     message = (rows, queries.shape[1] + ID_LANES + columns)
     return pl.pallas_call(
@@ -119,7 +119,7 @@
         ],
         out_specs=[pl.BlockSpec(message, lambda i: (0, 0))] * experts,
         out_shape=[jax.ShapeDtypeStruct(message, BF16)] * experts,
-        compiler_params=limits(8),
+        compiler_params=limits(16),
         name="attention",
     )(
         *in_hbm(
@@ -194,10 +194,9 @@
     )(*pieces, weight)
 
 
-def route_kernel(capacity, own_ids_ref, weights_ref, *refs):
-    pieces, weight_hbm = refs[:-8], refs[-7]
-    choose_ref, residual_ref, weight_ref, weighting_ref, ids_ref, sem = refs[-6:]
-    top, own_count = own_ids_ref.shape
+def route_kernel(capacity, top, *refs):
+    pieces, weight_hbm = refs[:-7], refs[-6]
+    choose_ref, residual_ref, weight_ref, ids_ref, sem = refs[-5:]
     copy = pltpu.make_async_copy(weight_hbm.at[: weight_ref.shape[0]], weight_ref, sem)
     copy.start()
     columns = residual_ref.shape[1]
@@ -231,6 +230,296 @@
         choose_ref[d * count : (d + 1) * count] = jnp.where(
             slot == place[d : d + 1], 1.0, 0.0
         ).astype(BF16)
+    copy.wait()
+
+
+def route(pieces, after, columns, capacity, top, weight, first):
+    rows = pieces[0].shape[0] // 2 * len(pieces)
+    experts = len(pieces) // 2
+    return pl.pallas_call(
+        functools.partial(route_kernel, capacity, top),
+        in_specs=[VMEM] * len(pieces) + [ANY] * 2,
+        out_specs=[VMEM] * 3,
+        out_shape=[
+            jax.ShapeDtypeStruct((experts * 2 * experts * capacity, rows), BF16),
+            jax.ShapeDtypeStruct((rows, columns), F32),
+            pltpu.VMEM((first, weight.shape[1]), weight.dtype),
+        ],
+        scratch_shapes=[pltpu.VMEM((rows, ID_LANES), F32), pltpu.SemaphoreType.DMA],
+        compiler_params=limits(4),
+        cost_estimate=pl.CostEstimate(flops=10**6, bytes_accessed=8 * 10**6, transcendentals=0),
+        name="route",
+    )(*pieces, after, *in_hbm(weight))
+
+
+def pack_kernel(keep_ref, got_ref, residual_ref, choose_ref, *refs):
+    outs, own_ref, cross_ref, sum_ref = refs[:-3], *refs[-3:]
+    sum_ref[...] = keep_ref[...] + got_ref[...].astype(F32)
+    combined = (sum_ref[...] + residual_ref[...]).astype(BF16)
+    packed = dot(choose_ref[...], combined).astype(BF16)
+    count = choose_ref.shape[0] // len(outs)
+    own = sum_ref.shape[0] // len(outs) // 2
+    expert, half = lax.axis_index("expert"), lax.axis_index("half")
+    for d, out in enumerate(outs):
+        out[...] = packed[d * count : (d + 1) * count]
+    for d in range(0, len(outs), 2):
+        for ref, which in ((own_ref, half), (cross_ref, 1 - half)):
+            rows = [
+                sum_ref[pl.ds(pl.multiple_of(((expert ^ c) * 2 + which) * own, own), own)]
+                for c in (d, d + 1)
+            ]
+            ref[d * own : (d + 2) * own] = jnp.concatenate(rows, axis=0).astype(BF16)
+
+
+def pack(keep, got, residual, choose, experts):
+    rows, columns = keep.shape
+    count = choose.shape[0] // experts
+    return pl.pallas_call(
+        pack_kernel,
+        in_specs=[VMEM] * 4,
+        out_specs=[VMEM] * (experts + 2),
+        out_shape=[jax.ShapeDtypeStruct((count, columns), BF16)] * experts
+        + [jax.ShapeDtypeStruct((rows // 2, columns), BF16)] * 2,
+        scratch_shapes=[pltpu.VMEM((rows, columns), F32)],
+        compiler_params=limits(4),
+        name="pack",
+    )(keep, got, residual, choose)
+
+
+def turn(turned_ref, gain_ref, pieces, first, count):
+    near, near_cross, far, far_cross = pieces
+    columns = near.shape[1]
+    expert, half = lax.axis_index("expert"), lax.axis_index("half")
+    squares = jnp.zeros((2 * count, 128), F32)
+    for d in range(2):
+        for c, (mine, theirs) in enumerate(((near, far), (near_cross, far_cross))):
+            rows = slice(d * count, (d + 1) * count)
+            x = jnp.concatenate([mine[rows].astype(F32), theirs[rows].astype(F32)], axis=0)
+            for b in range(columns // 128):
+                part = x[:, b * 128 : (b + 1) * 128]
+                squares = squares + part * part
+            block = (expert ^ (first + d)) * 2 + (half ^ c)
+            at = pl.ds(pl.multiple_of(block * columns, columns), columns)
+            to = pl.ds(pl.multiple_of(block % 4 * columns, columns), columns)
+            turned_ref[to] = (x * gain_ref[:, at]).T.astype(BF16)
+    return squares
+
+
+def half_of(ref, first):
+    width = ref.shape[1] // 2
+    which = (lax.axis_index("expert") ^ first) // 2
+    return pl.ds(pl.multiple_of(which * width, width), width)
+
+
+def expert_first_kernel(count, *refs):
+    pieces, gain_ref, gate_ref, up_ref, up_hbm = refs[:4], *refs[4:8]
+    gate_sum_ref, up_sum_ref, squares_ref, up_rest_ref, turned_ref, sem = refs[8:]
+    cut = up_ref.shape[0]
+    rest = pltpu.make_async_copy(up_hbm.at[cut:], up_rest_ref, sem)
+    rest.start()
+    squares_ref[...] = turn(turned_ref, gain_ref, pieces, 0, count)
+    columns = half_of(gate_ref, 0)
+    for at in (slice(0, cut), slice(cut, gate_ref.shape[0])):
+        gate_sum_ref[at] = dot(gate_ref[at, columns], turned_ref[...])
+    up_sum_ref[:cut] = dot(up_ref[:, columns], turned_ref[...])
+    rest.wait()
+    up_sum_ref[cut:] = dot(up_rest_ref[:, columns], turned_ref[...])
+
+
+def expert_second_kernel(count, *refs):
+    pieces, gain_ref, gate_ref, up_ref, up_rest_ref = refs[:4], *refs[4:8]
+    gate_sum_ref, up_sum_ref, squares_ref, down_hbm, hidden_ref, down_ref, turned_ref, sem = refs[8:]
+    units, width = gate_ref.shape
+    cut = up_ref.shape[0]
+    down = pltpu.make_async_copy(down_hbm, down_ref, sem)
+    down.start()
+    squares = squares_ref[...] + turn(turned_ref, gain_ref, pieces, 2, count)
+    spread = jnp.sum(squares.T, axis=0, keepdims=True) / width
+    scale = lax.rsqrt(spread + EPSILON)
+    columns = half_of(gate_ref, 2)
+    for at, weight_ref in ((slice(0, cut), up_ref), (slice(cut, units), up_rest_ref)):
+        gate_value = (gate_sum_ref[at] + dot(gate_ref[at, columns], turned_ref[...])) * scale
+        lifted = (up_sum_ref[at] + dot(weight_ref[:, columns], turned_ref[...])) * scale
+        hidden = gate_value / (1.0 + jnp.exp(-gate_value)) * lifted
+        hidden_ref[:, at] = hidden.T.astype(BF16)
+    down.wait()
+
+
+def down_kernel(start, wide, hidden_ref, weight_ref, keep_ref, send_ref):
+    half = lax.axis_index("half")
+    count = keep_ref.shape[0]
+    part = count // 2
+    for n in range(keep_ref.shape[1] // wide):
+        at = slice(start + n * wide, start + (n + 1) * wide)
+        out = slice(n * wide, (n + 1) * wide)
+        total = dot(hidden_ref[...], weight_ref[:, at])
+        for p in range(2):
+            low = total[p * count : p * count + part]
+            high = total[p * count + part : (p + 1) * count]
+            to = slice(p * part, (p + 1) * part)
+            keep_ref[to, out] = jnp.where(half == 0, low, high)
+            send_ref[to, out] = jnp.where(half == 0, high, low).astype(BF16)
+
+
+def cost(flops, size):
+    return pl.CostEstimate(flops=flops, bytes_accessed=size, transcendentals=0)
+
+
+def expert_first(pieces, gain, gate, up_first, up_part, count):
+    units, width = gate.shape
+    cut = up_first.shape[0]
+    sums = jax.ShapeDtypeStruct((units, 2 * count), F32)
+    return pl.pallas_call(
+        functools.partial(expert_first_kernel, count),
+        in_specs=[VMEM] * 7 + [ANY],
+        out_specs=[VMEM] * 4,
+        out_shape=[
+            sums,
+            sums,
+            jax.ShapeDtypeStruct((2 * count, 128), F32),
+            pltpu.VMEM((units - cut, width), BF16),
+        ],
+        scratch_shapes=[pltpu.VMEM((width // 2, 2 * count), BF16), pltpu.SemaphoreType.DMA],
+        compiler_params=limits(8),
+        cost_estimate=cost(4 * units * width * count, 2 * units * width),
+        name="experts_first",
+    )(*pieces, gain, gate, up_first, *in_hbm(up_part))
+
+
+def relay_kernel(rows_ref, *refs):
+    refs[-1][...] = rows_ref[...]
+
+
+def relay(rows, *after):
+    return pl.pallas_call(
+        relay_kernel,
+        in_specs=[VMEM] * (1 + len(after)),
+        out_specs=VMEM,
+        out_shape=jax.ShapeDtypeStruct(rows.shape, rows.dtype),
+        compiler_params=limits(2),
+        cost_estimate=cost(0, 10**5),
+        name="relay",
+    )(rows, *after)
+
+
+def expert_second(pieces, gain, gate, up_first, up_rest, sums, down_part, count):
+    units, width = gate.shape
+    return pl.pallas_call(
+        functools.partial(expert_second_kernel, count),
+        in_specs=[VMEM] * 11 + [ANY],
+        out_specs=[VMEM] * 2,
+        out_shape=[
+            jax.ShapeDtypeStruct((2 * count, units), BF16),
+            pltpu.VMEM((units, width), BF16),
+        ],
+        scratch_shapes=[pltpu.VMEM((width // 2, 2 * count), BF16), pltpu.SemaphoreType.DMA],
+        compiler_params=limits(8),
+        cost_estimate=cost(4 * units * width * count, 2 * units * width),
+        name="experts_second",
+    )(*pieces, gain, gate, up_first, up_rest, *sums, *in_hbm(down_part))
+
+
+def expert_down(hidden, weight, start, width, count):
+    return pl.pallas_call(
+        functools.partial(down_kernel, start, 512),
+        in_specs=[VMEM] * 2,
+        out_specs=[VMEM] * 2,
+        out_shape=[
+            jax.ShapeDtypeStruct((count, width), F32),
+            jax.ShapeDtypeStruct((count, width), BF16),
+        ],
+        compiler_params=limits(8),
+        cost_estimate=cost(4 * hidden.size * width, 2 * hidden.shape[1] * width),
+        name="experts_down",
+    )(hidden, weight)
+
+
+def chip_sum_kernel(count, *refs):
+    mine, got = refs[:count], refs[count : 2 * count]
+    keep_ref, send_ref = refs[2 * count :]
+    rows = keep_ref.shape[0]
+    width = mine[0].shape[1]
+    for g in range(count):
+        at = slice(g * width, (g + 1) * width)
+        keep_ref[:, at] = mine[g][:rows] + got[g][:rows].astype(F32)
+        send_ref[:, at] = (mine[g][rows:] + got[g][rows:].astype(F32)).astype(BF16)
+
+
+def chip_sum(mine, got):
+    rows, width = mine[0].shape
+    shape = (rows // 2, width * len(mine))
+    return pl.pallas_call(
+        functools.partial(chip_sum_kernel, len(mine)),
+        in_specs=[VMEM] * (2 * len(mine)),
+        out_specs=[VMEM] * 2,
+        out_shape=[jax.ShapeDtypeStruct(shape, F32), jax.ShapeDtypeStruct(shape, BF16)],
+        compiler_params=limits(4),
+        name="chip_sum",
+    )(*mine, *got)
+
+
+def cut_kernel(own_ref, cross_ref, after_ref, *outs):
+    rows = own_ref.shape[0] // len(outs)
+    own, cross = own_ref[...].astype(F32), cross_ref[...].astype(F32)
+    for d, out in enumerate(outs):
+        at = slice(d * rows, (d + 1) * rows)
+        out[...] = jnp.concatenate([own[at], cross[at]], axis=0).astype(BF16)
+
+
+def cut(own, cross, after, experts):
+    rows, columns = own.shape
+    return pl.pallas_call(
+        cut_kernel,
+        in_specs=[VMEM] * 3,
+        out_specs=[VMEM] * experts,
+        out_shape=[jax.ShapeDtypeStruct((2 * rows // experts, columns), BF16)] * experts,
+        compiler_params=limits(2),
+        cost_estimate=cost(0, 10**5),
+        name="cut",
+    )(own, cross, after)
+
+
+def pair_sum_kernel(capacity, extra, keep_ref, got_ref, *refs):
+    outs, fold_ref = refs[extra:-1], refs[-1]
+    experts = len(outs)
+    parts = 8 // capacity
+    part = outs[0].shape[1]
+    total = keep_ref[...] + got_ref[...].astype(F32)
+    for e in range(experts):
+        mine = total[e * capacity : (e + 1) * capacity]
+        fold_ref[e] = jnp.concatenate(
+            [mine[:, h * part : (h + 1) * part] for h in range(parts)], axis=0
+        )
+    expert = lax.axis_index("expert")
+    for d, out in enumerate(outs):
+        out[...] = fold_ref[expert ^ d].astype(BF16)
+
+
+def pair_sum(keep, got, capacity, experts, after):
+    part = keep.shape[1] * capacity // 8
+    return pl.pallas_call(
+        functools.partial(pair_sum_kernel, capacity, len(after)),
+        in_specs=[VMEM] * (2 + len(after)),
+        out_specs=[VMEM] * experts,
+        out_shape=[jax.ShapeDtypeStruct((8, part), BF16)] * experts,
+        scratch_shapes=[pltpu.VMEM((experts, 8, part), F32)],
+        compiler_params=limits(4),
+        name="pair_sum",
+    )(keep, got, *after)
+
+
+def own_rows_kernel(capacity, own_ids_ref, weights_ref, residual_ref, *refs):
+    pieces, combined_ref, weighting_ref = refs[:-2], *refs[-2:]
+    rows = combined_ref.shape[0]
+    top, own_count = own_ids_ref.shape
+    columns = pieces[0].shape[1]
+    expert, half = lax.axis_index("expert"), lax.axis_index("half")
+    for d, piece in enumerate(pieces):
+        both = piece[...].astype(F32)
+        for c in range(2):
+            base = ((expert ^ d) * 2 + (half ^ c)) * columns
+            at = pl.ds(pl.multiple_of(base, columns), columns)
+            combined_ref[:, at] = residual_ref[:, at].astype(F32) + both[c * rows : (c + 1) * rows]
 
     places = weighting_ref.shape[1]
     row = lax.broadcasted_iota(jnp.int32, (own_count, places), 0)
@@ -249,308 +538,22 @@
         high, low = halves_of(jnp.where(at_place % 8 // capacity == h, weighting, 0.0))
         both = jnp.concatenate([high.astype(F32), low.astype(F32)], axis=0)
         weighting_ref[h * 16 : (h + 1) * 16] = both.astype(BF16)
-    copy.wait()
-
-
-def route(ids, weights, pieces, after, columns, capacity, weight, first):
-    rows = pieces[0].shape[0] // 2 * len(pieces)
-    experts = len(pieces) // 2
-    return pl.pallas_call(
-        functools.partial(route_kernel, capacity),
-        in_specs=[SMEM] * 2 + [VMEM] * len(pieces) + [ANY] * 2,
-        out_specs=[VMEM] * 4,
+
+
+def own_rows(ids, weights, residual, pieces, capacity):
+    experts = len(pieces)
+    return pl.pallas_call(
+        functools.partial(own_rows_kernel, capacity),
+        in_specs=[SMEM] * 2 + [VMEM] * (len(pieces) + 1),
+        out_specs=[VMEM] * 2,
         out_shape=[
-            jax.ShapeDtypeStruct((experts * 2 * experts * capacity, rows), BF16),
-            jax.ShapeDtypeStruct((rows, columns), F32),
-            pltpu.VMEM((first, weight.shape[1]), weight.dtype),
+            jax.ShapeDtypeStruct(residual.shape, F32),
             jax.ShapeDtypeStruct((16 * (8 // capacity), experts * 8), BF16),
         ],
-        scratch_shapes=[pltpu.VMEM((rows, ID_LANES), F32), pltpu.SemaphoreType.DMA],
-        compiler_params=limits(4),
-        cost_estimate=pl.CostEstimate(flops=10**6, bytes_accessed=8 * 10**6, transcendentals=0),
-        name="route",
-    )(*in_hbm(ids, weights), *pieces, after, *in_hbm(weight))
-
-
-def pack_kernel(keep_ref, got_ref, residual_ref, choose_ref, *refs):
-    outs, own_ref, cross_ref, sum_ref = refs[:-3], *refs[-3:]
-    sum_ref[...] = keep_ref[...] + got_ref[...].astype(F32)
-    combined = (sum_ref[...] + residual_ref[...]).astype(BF16)
-    packed = dot(choose_ref[...], combined).astype(BF16)
-    count = choose_ref.shape[0] // len(outs)
-    own = sum_ref.shape[0] // len(outs) // 2
-    expert, half = lax.axis_index("expert"), lax.axis_index("half")
-    for d, out in enumerate(outs):
-        out[...] = packed[d * count : (d + 1) * count]
-    for d in range(0, len(outs), 2):
-        for ref, which in ((own_ref, half), (cross_ref, 1 - half)):
-            rows = [
-                sum_ref[pl.ds(pl.multiple_of(((expert ^ c) * 2 + which) * own, own), own)]
-                for c in (d, d + 1)
-            ]
-            ref[d * own : (d + 2) * own] = jnp.concatenate(rows, axis=0).astype(BF16)
-
-
-def pack(keep, got, residual, choose, experts):
-    rows, columns = keep.shape
-    count = choose.shape[0] // experts
-    return pl.pallas_call(
-        pack_kernel,
-        in_specs=[VMEM] * 4,
-        out_specs=[VMEM] * (experts + 2),
-        out_shape=[jax.ShapeDtypeStruct((count, columns), BF16)] * experts
-        + [jax.ShapeDtypeStruct((rows // 2, columns), BF16)] * 2,
-        scratch_shapes=[pltpu.VMEM((rows, columns), F32)],
-        compiler_params=limits(4),
-        name="pack",
-    )(keep, got, residual, choose)
-
-
-def turn(turned_ref, gain_ref, pieces, first, count):
-    near, near_cross, far, far_cross = pieces
-    columns = near.shape[1]
-    expert, half = lax.axis_index("expert"), lax.axis_index("half")
-    squares = jnp.zeros((2 * count, 128), F32)
-    for d in range(2):
-        for c, (mine, theirs) in enumerate(((near, far), (near_cross, far_cross))):
-            rows = slice(d * count, (d + 1) * count)
-            x = jnp.concatenate([mine[rows].astype(F32), theirs[rows].astype(F32)], axis=0)
-            for b in range(columns // 128):
-                part = x[:, b * 128 : (b + 1) * 128]
-                squares = squares + part * part
-            block = (expert ^ (first + d)) * 2 + (half ^ c)
-            at = pl.ds(pl.multiple_of(block * columns, columns), columns)
-            to = pl.ds(pl.multiple_of(block % 4 * columns, columns), columns)
-            turned_ref[to] = (x * gain_ref[:, at]).T.astype(BF16)
-    return squares
-
-
-def half_of(ref, first):
-    width = ref.shape[1] // 2
-    which = (lax.axis_index("expert") ^ first) // 2
-    return pl.ds(pl.multiple_of(which * width, width), width)
-
-
-def expert_first_kernel(count, *refs):
-    pieces, gain_ref, gate_ref, up_ref, up_hbm = refs[:4], *refs[4:8]
-    gate_sum_ref, up_sum_ref, squares_ref, up_rest_ref, turned_ref, sem = refs[8:]
-    cut = up_ref.shape[0]
-    rest = pltpu.make_async_copy(up_hbm.at[cut:], up_rest_ref, sem)
-    rest.start()
-    squares_ref[...] = turn(turned_ref, gain_ref, pieces, 0, count)
-    columns = half_of(gate_ref, 0)
-    for at in (slice(0, cut), slice(cut, gate_ref.shape[0])):
-        gate_sum_ref[at] = dot(gate_ref[at, columns], turned_ref[...])
-    up_sum_ref[:cut] = dot(up_ref[:, columns], turned_ref[...])
-    rest.wait()
-    up_sum_ref[cut:] = dot(up_rest_ref[:, columns], turned_ref[...])
-
-
-def expert_second_kernel(count, *refs):
-    pieces, gain_ref, gate_ref, up_ref, up_rest_ref = refs[:4], *refs[4:8]
-    gate_sum_ref, up_sum_ref, squares_ref, down_hbm, hidden_ref, down_ref, turned_ref, sem = refs[8:]
-    units, width = gate_ref.shape
-    cut = up_ref.shape[0]
-    down = pltpu.make_async_copy(down_hbm, down_ref, sem)
-    down.start()
-    squares = squares_ref[...] + turn(turned_ref, gain_ref, pieces, 2, count)
-    spread = jnp.sum(squares.T, axis=0, keepdims=True) / width
-    scale = lax.rsqrt(spread + EPSILON)
-    columns = half_of(gate_ref, 2)
-    for at, weight_ref in ((slice(0, cut), up_ref), (slice(cut, units), up_rest_ref)):
-        gate_value = (gate_sum_ref[at] + dot(gate_ref[at, columns], turned_ref[...])) * scale
-        lifted = (up_sum_ref[at] + dot(weight_ref[:, columns], turned_ref[...])) * scale
-        hidden = gate_value / (1.0 + jnp.exp(-gate_value)) * lifted
-        hidden_ref[:, at] = hidden.T.astype(BF16)
-    down.wait()
-
-
-def down_kernel(start, wide, hidden_ref, weight_ref, keep_ref, send_ref):
-    half = lax.axis_index("half")
-    count = keep_ref.shape[0]
-    part = count // 2
-    for n in range(keep_ref.shape[1] // wide):
-        at = slice(start + n * wide, start + (n + 1) * wide)
-        out = slice(n * wide, (n + 1) * wide)
-        total = dot(hidden_ref[...], weight_ref[:, at])
-        for p in range(2):
-            low = total[p * count : p * count + part]
-            high = total[p * count + part : (p + 1) * count]
-            to = slice(p * part, (p + 1) * part)
-            keep_ref[to, out] = jnp.where(half == 0, low, high)
-            send_ref[to, out] = jnp.where(half == 0, high, low).astype(BF16)
-
-
-def cost(flops, size):
-    return pl.CostEstimate(flops=flops, bytes_accessed=size, transcendentals=0)
-
-
-def expert_first(pieces, gain, gate, up_first, up_part, count):
-    units, width = gate.shape
-    cut = up_first.shape[0]
-    sums = jax.ShapeDtypeStruct((units, 2 * count), F32)
-    return pl.pallas_call(
-        functools.partial(expert_first_kernel, count),
-        in_specs=[VMEM] * 7 + [ANY],
-        out_specs=[VMEM] * 4,
-        out_shape=[
-            sums,
-            sums,
-            jax.ShapeDtypeStruct((2 * count, 128), F32),
-            pltpu.VMEM((units - cut, width), BF16),
-        ],
-        scratch_shapes=[pltpu.VMEM((width // 2, 2 * count), BF16), pltpu.SemaphoreType.DMA],
-        compiler_params=limits(8),
-        cost_estimate=cost(4 * units * width * count, 2 * units * width),
-        name="experts_first",
-    )(*pieces, gain, gate, up_first, *in_hbm(up_part))
-
-
-def relay_kernel(rows_ref, *refs):
-    refs[-1][...] = rows_ref[...]
-
-
-def relay(rows, *after):
-    return pl.pallas_call(
-        relay_kernel,
-        in_specs=[VMEM] * (1 + len(after)),
-        out_specs=VMEM,
-        out_shape=jax.ShapeDtypeStruct(rows.shape, rows.dtype),
-        compiler_params=limits(2),
-        cost_estimate=cost(0, 10**5),
-        name="relay",
-    )(rows, *after)
-
-
-def expert_second(pieces, gain, gate, up_first, up_rest, sums, down_part, count):
-    units, width = gate.shape
-    return pl.pallas_call(
-        functools.partial(expert_second_kernel, count),
-        in_specs=[VMEM] * 11 + [ANY],
-        out_specs=[VMEM] * 2,
-        out_shape=[
-            jax.ShapeDtypeStruct((2 * count, units), BF16),
-            pltpu.VMEM((units, width), BF16),
-        ],
-        scratch_shapes=[pltpu.VMEM((width // 2, 2 * count), BF16), pltpu.SemaphoreType.DMA],
-        compiler_params=limits(8),
-        cost_estimate=cost(4 * units * width * count, 2 * units * width),
-        name="experts_second",
-    )(*pieces, gain, gate, up_first, up_rest, *sums, *in_hbm(down_part))
-
-
-def expert_down(hidden, weight, start, width, count):
-    return pl.pallas_call(
-        functools.partial(down_kernel, start, 512),
-        in_specs=[VMEM] * 2,
-        out_specs=[VMEM] * 2,
-        out_shape=[
-            jax.ShapeDtypeStruct((count, width), F32),
-            jax.ShapeDtypeStruct((count, width), BF16),
-        ],
-        compiler_params=limits(8),
-        cost_estimate=cost(4 * hidden.size * width, 2 * hidden.shape[1] * width),
-        name="experts_down",
-    )(hidden, weight)
-
-
-def chip_sum_kernel(count, *refs):
-    mine, got = refs[:count], refs[count : 2 * count]
-    keep_ref, send_ref = refs[2 * count :]
-    rows = keep_ref.shape[0]
-    width = mine[0].shape[1]
-    for g in range(count):
-        at = slice(g * width, (g + 1) * width)
-        keep_ref[:, at] = mine[g][:rows] + got[g][:rows].astype(F32)
-        send_ref[:, at] = (mine[g][rows:] + got[g][rows:].astype(F32)).astype(BF16)
-
-
-def chip_sum(mine, got):
-    rows, width = mine[0].shape
-    shape = (rows // 2, width * len(mine))
-    return pl.pallas_call(
-        functools.partial(chip_sum_kernel, len(mine)),
-        in_specs=[VMEM] * (2 * len(mine)),
-        out_specs=[VMEM] * 2,
-        out_shape=[jax.ShapeDtypeStruct(shape, F32), jax.ShapeDtypeStruct(shape, BF16)],
-        compiler_params=limits(4),
-        name="chip_sum",
-    )(*mine, *got)
-
-
-def cut_kernel(own_ref, cross_ref, after_ref, *outs):
-    rows = own_ref.shape[0] // len(outs)
-    own, cross = own_ref[...].astype(F32), cross_ref[...].astype(F32)
-    for d, out in enumerate(outs):
-        at = slice(d * rows, (d + 1) * rows)
-        out[...] = jnp.concatenate([own[at], cross[at]], axis=0).astype(BF16)
-
-
-def cut(own, cross, after, experts):
-    rows, columns = own.shape
-    return pl.pallas_call(
-        cut_kernel,
-        in_specs=[VMEM] * 3,
-        out_specs=[VMEM] * experts,
-        out_shape=[jax.ShapeDtypeStruct((2 * rows // experts, columns), BF16)] * experts,
-        compiler_params=limits(2),
-        cost_estimate=cost(0, 10**5),
-        name="cut",
-    )(own, cross, after)
-
-
-def pair_sum_kernel(capacity, extra, keep_ref, got_ref, *refs):
-    outs, fold_ref = refs[extra:-1], refs[-1]
-    experts = len(outs)
-    parts = 8 // capacity
-    part = outs[0].shape[1]
-    total = keep_ref[...] + got_ref[...].astype(F32)
-    for e in range(experts):
-        mine = total[e * capacity : (e + 1) * capacity]
-        fold_ref[e] = jnp.concatenate(
-            [mine[:, h * part : (h + 1) * part] for h in range(parts)], axis=0
-        )
-    expert = lax.axis_index("expert")
-    for d, out in enumerate(outs):
-        out[...] = fold_ref[expert ^ d].astype(BF16)
-
-
-def pair_sum(keep, got, capacity, experts, after):
-    part = keep.shape[1] * capacity // 8
-    return pl.pallas_call(
-        functools.partial(pair_sum_kernel, capacity, len(after)),
-        in_specs=[VMEM] * (2 + len(after)),
-        out_specs=[VMEM] * experts,
-        out_shape=[jax.ShapeDtypeStruct((8, part), BF16)] * experts,
-        scratch_shapes=[pltpu.VMEM((experts, 8, part), F32)],
-        compiler_params=limits(4),
-        name="pair_sum",
-    )(keep, got, *after)
-
-
-def own_rows_kernel(residual_ref, *refs):
-    pieces, combined_ref = refs[:-1], refs[-1]
-    rows = combined_ref.shape[0]
-    columns = pieces[0].shape[1]
-    expert, half = lax.axis_index("expert"), lax.axis_index("half")
-    for d, piece in enumerate(pieces):
-        both = piece[...].astype(F32)
-        for c in range(2):
-            base = ((expert ^ d) * 2 + (half ^ c)) * columns
-            at = pl.ds(pl.multiple_of(base, columns), columns)
-            combined_ref[:, at] = residual_ref[:, at].astype(F32) + both[c * rows : (c + 1) * rows]
-
-
-def own_rows(residual, pieces):
-    return pl.pallas_call(
-        own_rows_kernel,
-        in_specs=[VMEM] * (len(pieces) + 1),
-        out_specs=VMEM,
-        out_shape=jax.ShapeDtypeStruct(residual.shape, F32),
         compiler_params=limits(4),
         cost_estimate=cost(10**6, 10**6),
         name="own_rows",
-    )(*in_hbm(residual), *pieces)
+    )(*in_hbm(ids, weights, residual), *pieces)
 
 
 def finish_kernel(combined_ref, weighting_ref, *refs):
@@ -617,8 +620,8 @@
 
     keep, send = project(pieces, weight_here)
     first = expert_up.shape[0] // 256 * 128 + 128
-    choose, residual_part, up_first, weighting = route(
-        ids, weights, pieces, keep, columns, capacity, expert_up, first
+    choose, residual_part, up_first = route(
+        pieces, keep, columns, capacity, expert_ids.shape[1], expert_up, first
     )
     *packed, own, cross = pack(keep, swap(send, "pair", 1), residual_part, choose, experts)
 
@@ -648,7 +651,7 @@
     own = cut(own, cross, keep, experts)
     own = [swap(rows, "expert", d) for d, rows in enumerate(own)]
     terms = pair_sum(keep, swap(send, "pair", 1), capacity, experts, own)
-    combined = own_rows(residual, own)
+    combined, weighting = own_rows(ids, weights, residual, own, capacity)
     back = [swap(term, "expert", d) for d, term in enumerate(terms)]
     return finish(combined, weighting, back)
 

time: 72.9 us -> 71.5 us (0.981)
  Pallas kernels: 31.4 us -> 29.9 us
    pallas_call x1, Pallas kernels: 4.6 us -> 3.76 us  [attend(): pl.pallas_call(functools.partial(attend_kernel, rows // requests, heads /...]
  transfers between devices with their start and end apart: 27 -> 27, of which waited for: 11 -> 12; matrix products, arithmetic and copies ran while one was open for 0% -> 0% of each run, Pallas kernels for 23% -> 23%
where the time goes in v8:
time: 71.5 us; the launch traced here: 71.2 us
  Pallas kernels  29.9 us (42%)
  starting transfers between devices  26.2 us (37%)
  waiting for transfers between devices  14.8 us (21%)
    ppermute x27, starting transfers between devices, swap(): lax.ppermute(x, axis, [(i, i ^ by) for i in range(lax.axis_size(axis))])  26.2 us
    ppermute x27, waiting for transfers between devices, swap(): lax.ppermute(x, axis, [(i, i ^ by) for i in range(lax.axis_size(axis))])  14.8 us
    pallas_call x1, Pallas kernels, load(): pl.pallas_call(functools.partial(load_kernel, len(weights)), in_specs=[AN...  6.03 us
    pallas_call x1, Pallas kernels, expert_first(): pl.pallas_call(functools.partial(expert_first_kernel, count), in_specs=[V...  5.9 us
    pallas_call x1, Pallas kernels, expert_second(): pl.pallas_call(functools.partial(expert_second_kernel, count), in_specs=[...  5.23 us
    pallas_call x1, Pallas kernels, attend(): pl.pallas_call(functools.partial(attend_kernel, rows // requests, heads /...  3.76 us
    pallas_call x1, Pallas kernels, route(): pl.pallas_call(functools.partial(route_kernel, capacity, top), in_specs=[...  3.28 us
    pallas_call x2, Pallas kernels, expert_down(): pl.pallas_call(functools.partial(down_kernel, start, 512), in_specs=[VMEM...  2.73 us
  transfers between devices with their start and end apart: 27, of which 12 were waited for; matrix products, arithmetic and copies ran while one was open for 0% of the time, Pallas kernels for 23%

profile of v8, /device:TPU:0, one launch (start us, length us, event | category | flops | bytes accessed | tf_op | source)
XLA Modules:
  0.0 71.2 jit_solution(15281633791795222581)
XLA Ops:
  0.0 3.8 %attention.1 = (bf16[16,2944]{1,0:T(8,128)(2,1)S(1)}, bf16[16,2944]{1,0:T(8,128)(2,1)S(1)}, bf16[16,2944]{1,0:T(8,128)(2,1)S(1)}, bf16[16,2944]{1,0:T(8,128)(2,1)S(1)}) custom-call(f32[16]{0:T(128)} %decay_ref.1, s32[2,8]{1,0:T(2,128)} %bitcast.6, bf16[16,2048]{1,0:T(8,128)(2,1)} %q_ref.1, bf16[16,2048]{1,0:T(8,128)(2,1)} %k_ref.1, bf16[16,2048]{1,0:T(8,128)(2,1)} %v_ref.1, ...), custom_call_target="tpu_custom_call" | custom-call | tf_op jit(solution)/shard_map/attention/pallas_call | solution.py:107
  3.8 3.1 %collective-permute-start.1 = (bf16[16,2944]{1,0:T(8,128)(2,1)S(1)}, bf16[16,2944]{1,0:T(8,128)(2,1)S(1)}, u32[]{:S(2)}, u32[]{:S(2)}) collective-permute-start(bf16[16,2944]{1,0:T(8,128)(2,1)S(1)} %get-tuple-element.48), channel_id=1, source_target_pairs={{0,4},{4,0},{8,12},{12,8},{1,5},{5,1},{9,13},{13,9},{2,6},{6,2},{1... | collective-permute-start | bytes 282632 | tf_op jit(solution)/shard_map/ppermute | solution.py:582
  6.9 2.6 %collective-permute-start.3 = (bf16[16,2944]{1,0:T(8,128)(2,1)S(1)}, bf16[16,2944]{1,0:T(8,128)(2,1)S(1)}, u32[]{:S(2)}, u32[]{:S(2)}) collective-permute-start(bf16[16,2944]{1,0:T(8,128)(2,1)S(1)} %get-tuple-element.49), channel_id=1, source_target_pairs={{0,8},{4,12},{8,0},{12,4},{1,9},{5,13},{9,1},{13,5},{2,10},{6,14},... | collective-permute-start | bytes 282632 | tf_op jit(solution)/shard_map/ppermute | solution.py:582
  9.4 0.0 collective-permute-start.5
  9.5 6.0 %load.1 = (bf16[16,2944]{1,0:T(8,128)(2,1)S(1)}, bf16[2048,768]{1,0:T(8,128)(2,1)S(1)}, f32[1,6144]{1,0:T(1,128)S(1)}, bf16[1152,6144]{1,0:T(8,128)(2,1)S(1)}) custom-call(bf16[16,2944]{1,0:T(8,128)(2,1)S(1)} %get-tuple-element.46.rows_hbm, bf16[2048,768]{1,0:T(8,128)(2,1)} %refs_0_.1, f32[1,6144]{1,0:T(1,128)} %bitcast.4, bf16[1152,6144]{1,0:T(8,128)(2,1)} %refs_2_.1), custom_call_target="tpu_custom_call" | custom-call | bytes 17326080 | tf_op jit(solution)/shard_map/load/pallas_call | solution.py:146
  15.5 0.1 collective-permute-start
  15.6 0.0 collective-permute-done.1.refs_2_
  15.6 0.5 collective-permute-start.2
  16.1 0.9 %collective-permute-done.3.refs_4_ = bf16[16,2944]{1,0:T(8,128)(2,1)S(1)} collective-permute-done((bf16[16,2944]{1,0:T(8,128)(2,1)S(1)}, bf16[16,2944]{1,0:T(8,128)(2,1)S(1)}, u32[]{:S(2)}, u32[]{:S(2)}) %collective-permute-start.3) | collective-permute-done | bytes 94240 | tf_op jit(solution)/shard_map/ppermute | solution.py:582
  17.0 0.0 collective-permute-start.4
  17.0 0.0 collective-permute-done.5.refs_6_
  17.0 0.5 collective-permute-start.6
  17.5 0.0 collective-permute-done.refs_1_
  17.5 0.0 collective-permute-done.2.refs_3_
  17.5 0.8 %collective-permute-done.4.refs_5_ = bf16[16,2944]{1,0:T(8,128)(2,1)S(1)} collective-permute-done((bf16[16,2944]{1,0:T(8,128)(2,1)S(1)}, bf16[16,2944]{1,0:T(8,128)(2,1)S(1)}, u32[]{:S(2)}, u32[]{:S(2)}) %collective-permute-start.4) | collective-permute-done | bytes 94240 | tf_op jit(solution)/shard_map/ppermute | solution.py:582
  18.3 0.2 collective-permute-done.6.refs_7_
  18.4 0.7 projection.1
  19.1 1.6 %collective-permute-start.7 = (bf16[64,768]{1,0:T(8,128)(2,1)S(1)}, bf16[64,768]{1,0:T(8,128)(2,1)S(1)}, u32[]{:S(2)}, u32[]{:S(2)}) collective-permute-start(bf16[64,768]{1,0:T(8,128)(2,1)S(1)} %get-tuple-element.53), channel_id=1, source_target_pairs={{0,1},{1,0},{2,3},{3,2},{4,5},{5,4},{6,7},{7,6},{8,9},{9,8},{10,11... | collective-permute-start | bytes 294920 | tf_op jit(solution)/shard_map/ppermute | solution.py:582
  20.7 3.3 %route.1 = (bf16[128,64]{1,0:T(8,128)(2,1)S(1)}, f32[64,768]{1,0:T(8,128)S(1)}, bf16[640,6144]{1,0:T(8,128)(2,1)S(1)}) custom-call(bf16[16,2944]{1,0:T(8,128)(2,1)S(1)} %get-tuple-element.47.refs_0_, bf16[16,2944]{1,0:T(8,128)(2,1)S(1)} %collective-permute-done.refs_1_, bf16[16,2944]{1,0:T(8,128)(2,1)S(1)} %collective-permute-done.1.refs_2_, ...), custom_call_target="tpu_custom_call" | custom-call | flops 1000000 | bytes 8000000 | tf_op jit(solution)/shard_map/route/pallas_call | solution.py:239
  24.0 0.3 collective-permute-done.7.got_ref
  24.3 0.2 pack.1
  24.5 1.3 %collective-permute-start.13 = (bf16[32,768]{1,0:T(8,128)(2,1)S(1)}, bf16[32,768]{1,0:T(8,128)(2,1)S(1)}, u32[]{:S(2)}, u32[]{:S(2)}) collective-permute-start(bf16[32,768]{1,0:T(8,128)(2,1)S(1)} %get-tuple-element.59.refs_0_), channel_id=1, source_target_pairs={{0,4},{4,0},{8,12},{12,8},{1,5},{5,1},{9,13},{13,9},{2,6},{6,2},{1... | collective-permute-start | bytes 147464 | tf_op jit(solution)/shard_map/ppermute | solution.py:582
  25.8 2.5 %collective-permute-start.10 = (bf16[32,768]{1,0:T(8,128)(2,1)S(1)}, bf16[32,768]{1,0:T(8,128)(2,1)S(1)}, u32[]{:S(2)}, u32[]{:S(2)}) collective-permute-start(bf16[32,768]{1,0:T(8,128)(2,1)S(1)} %relay.4), channel_id=1, source_target_pairs={{0,12},{4,8},{8,4},{12,0},{1,13},{5,9},{9,5},{13,1},{2,14},{6,10},... | collective-permute-start | bytes 147464 | tf_op jit(solution)/shard_map/ppermute | solution.py:582
  28.3 0.0 collective-permute-start.9
  28.3 0.3 collective-permute-done.13
  28.6 1.5 %collective-permute-start.15 = (bf16[64,768]{1,0:T(8,128)(2,1)S(1)}, bf16[64,768]{1,0:T(8,128)(2,1)S(1)}, u32[]{:S(2)}, u32[]{:S(2)}) collective-permute-start(bf16[64,768]{1,0:T(8,128)(2,1)S(1)} %constant_dynamic-update-slice_fusion.2.refs_0_), channel_id=1, source_target_pairs={{0,1},{1,0},{2,3},{3,2},{4,5},{5,4},{6,7},{7,6},{8,9},{9,8},{10,11... | collective-permute-start | bytes 294920 | tf_op jit(solution)/shard_map/ppermute | solution.py:582
  30.1 0.0 collective-permute-start.14
  30.1 3.5 %collective-permute-done.9 = bf16[32,768]{1,0:T(8,128)(2,1)S(1)} collective-permute-done((bf16[32,768]{1,0:T(8,128)(2,1)S(1)}, bf16[32,768]{1,0:T(8,128)(2,1)S(1)}, u32[]{:S(2)}, u32[]{:S(2)}) %collective-permute-start.9) | collective-permute-done | bytes 49184 | tf_op jit(solution)/shard_map/ppermute | solution.py:582
  33.6 0.0 collective-permute-done.15.refs_2_
  33.6 0.1 collective-permute-start.16
  33.7 0.0 collective-permute-done.10
  33.7 1.6 %collective-permute-start.12 = (bf16[64,768]{1,0:T(8,128)(2,1)S(1)}, bf16[64,768]{1,0:T(8,128)(2,1)S(1)}, u32[]{:S(2)}, u32[]{:S(2)}) collective-permute-start(bf16[64,768]{1,0:T(8,128)(2,1)S(1)} %constant_dynamic-update-slice_fusion.refs_0_), channel_id=1, source_target_pairs={{0,1},{1,0},{2,3},{3,2},{4,5},{5,4},{6,7},{7,6},{8,9},{9,8},{10,11... | collective-permute-start | bytes 294920 | tf_op jit(solution)/shard_map/ppermute | solution.py:582
  35.3 0.2 collective-permute-start.8
  35.5 0.3 collective-permute-start.11
  35.8 0.0 collective-permute-done.14.refs_1_
  35.8 0.0 collective-permute-done.16.refs_3_
  35.8 5.9 %experts_first.1 = (f32[1152,64]{1,0:T(8,128)S(1)}, f32[1152,64]{1,0:T(8,128)S(1)}, f32[64,128]{1,0:T(8,128)S(1)}, bf16[512,6144]{1,0:T(8,128)(2,1)S(1)}) custom-call(bf16[64,768]{1,0:T(8,128)(2,1)S(1)} %constant_dynamic-update-slice_fusion.2.refs_0_, bf16[64,768]{1,0:T(8,128)(2,1)S(1)} %collective-permute-done.14.refs_1_, ...), custom_call_target="tpu_custom_call" | custom-call | flops 905969664 | bytes 14155776 | tf_op jit(solution)/shard_map/experts_first/pallas_call | solution.py:372
  41.7 0.0 collective-permute-done.8.refs_1_.cross_ref
  41.7 0.0 collective-permute-done.12.rows_ref
  41.8 0.3 collective-permute-start.17
  42.0 0.0 collective-permute-done.11.refs_1_
  42.0 1.1 %collective-permute-done.17.refs_3_ = bf16[64,768]{1,0:T(8,128)(2,1)S(1)} collective-permute-done((bf16[64,768]{1,0:T(8,128)(2,1)S(1)}, bf16[64,768]{1,0:T(8,128)(2,1)S(1)}, u32[]{:S(2)}, u32[]{:S(2)}) %collective-permute-start.17) | collective-permute-done | bytes 98336 | tf_op jit(solution)/shard_map/ppermute | solution.py:582
  43.1 5.2 %experts_second.1 = (bf16[64,1152]{1,0:T(8,128)(2,1)S(1)}, bf16[1152,6144]{1,0:T(8,128)(2,1)S(1)}) custom-call(bf16[64,768]{1,0:T(8,128)(2,1)S(1)} %constant_dynamic-update-slice_fusion.refs_0_, bf16[64,768]{1,0:T(8,128)(2,1)S(1)} %collective-permute-done.11.refs_1_, bf16[64,768]{1,0:T(8,128)(2,1)S(1)} %relay.5.refs_2_, ...), custom_call_target="tpu_custom_call" | custom-call | flops 905969664 | bytes 14155776 | tf_op jit(solution)/shard_map/experts_second/pallas_call | solution.py:407
  48.4 1.4 %experts_down.3 = (f32[32,3072]{1,0:T(8,128)S(1)}, bf16[32,3072]{1,0:T(8,128)(2,1)S(1)}) custom-call(bf16[64,1152]{1,0:T(8,128)(2,1)S(1)} %get-tuple-element.69.hidden_ref, bf16[1152,6144]{1,0:T(8,128)(2,1)S(1)} %get-tuple-element.70.weight_ref), custom_call_target="tpu_custom_call" | custom-call | flops 905969664 | bytes 7077888 | tf_op jit(solution)/shard_map/experts_down/pallas_call | solution.py:423
  49.7 1.4 %experts_down.2 = (f32[32,3072]{1,0:T(8,128)S(1)}, bf16[32,3072]{1,0:T(8,128)(2,1)S(1)}) custom-call(bf16[64,1152]{1,0:T(8,128)(2,1)S(1)} %get-tuple-element.69.hidden_ref, bf16[1152,6144]{1,0:T(8,128)(2,1)S(1)} %get-tuple-element.70.weight_ref), custom_call_target="tpu_custom_call" | custom-call | flops 905969664 | bytes 7077888 | tf_op jit(solution)/shard_map/experts_down/pallas_call | solution.py:423
  51.1 0.2 collective-permute-start.19
  51.3 0.3 collective-permute-start.18
  51.7 0.9 %collective-permute-done.19.refs_3_ = bf16[32,3072]{1,0:T(8,128)(2,1)S(1)} collective-permute-done((bf16[32,3072]{1,0:T(8,128)(2,1)S(1)}, bf16[32,3072]{1,0:T(8,128)(2,1)S(1)}, u32[]{:S(2)}, u32[]{:S(2)}) %collective-permute-start.19) | collective-permute-done | bytes 196640 | tf_op jit(solution)/shard_map/ppermute | solution.py:582
  52.6 0.3 collective-permute-done.18.refs_2_
  52.9 0.1 chip_sum.1
  53.0 0.7 %collective-permute-start.23 = (bf16[16,6144]{1,0:T(8,128)(2,1)S(1)}, bf16[16,6144]{1,0:T(8,128)(2,1)S(1)}, u32[]{:S(2)}, u32[]{:S(2)}) collective-permute-start(bf16[16,6144]{1,0:T(8,128)(2,1)S(1)} %get-tuple-element.82), channel_id=1, source_target_pairs={{0,1},{1,0},{2,3},{3,2},{4,5},{5,4},{6,7},{7,6},{8,9},{9,8},{10,11... | collective-permute-start | bytes 589832 | tf_op jit(solution)/shard_map/ppermute | solution.py:582
  53.7 1.3 %collective-permute-start.20 = (bf16[16,768]{1,0:T(8,128)(2,1)S(1)}, bf16[16,768]{1,0:T(8,128)(2,1)S(1)}, u32[]{:S(2)}, u32[]{:S(2)}) collective-permute-start(bf16[16,768]{1,0:T(8,128)(2,1)S(1)} %get-tuple-element.77), channel_id=1, source_target_pairs={{0,4},{4,0},{8,12},{12,8},{1,5},{5,1},{9,13},{13,9},{2,6},{6,2},{1... | collective-permute-start | bytes 73736 | tf_op jit(solution)/shard_map/ppermute | solution.py:582
  55.0 1.8 %collective-permute-start.21 = (bf16[16,768]{1,0:T(8,128)(2,1)S(1)}, bf16[16,768]{1,0:T(8,128)(2,1)S(1)}, u32[]{:S(2)}, u32[]{:S(2)}) collective-permute-start(bf16[16,768]{1,0:T(8,128)(2,1)S(1)} %get-tuple-element.78), channel_id=1, source_target_pairs={{0,8},{4,12},{8,0},{12,4},{1,9},{5,13},{9,1},{13,5},{2,10},{6,14},... | collective-permute-start | bytes 73736 | tf_op jit(solution)/shard_map/ppermute | solution.py:582
  56.8 1.4 %collective-permute-start.22 = (bf16[16,768]{1,0:T(8,128)(2,1)S(1)}, bf16[16,768]{1,0:T(8,128)(2,1)S(1)}, u32[]{:S(2)}, u32[]{:S(2)}) collective-permute-start(bf16[16,768]{1,0:T(8,128)(2,1)S(1)} %get-tuple-element.79), channel_id=1, source_target_pairs={{0,12},{4,8},{8,4},{12,0},{1,13},{5,9},{9,5},{13,1},{2,14},{6,10},... | collective-permute-start | bytes 73736 | tf_op jit(solution)/shard_map/ppermute | solution.py:582
  58.2 0.0 collective-permute-done.20.refs_1_
  58.2 2.1 %collective-permute-done.21.refs_2_ = bf16[16,768]{1,0:T(8,128)(2,1)S(1)} collective-permute-done((bf16[16,768]{1,0:T(8,128)(2,1)S(1)}, bf16[16,768]{1,0:T(8,128)(2,1)S(1)}, u32[]{:S(2)}, u32[]{:S(2)}) %collective-permute-start.21) | collective-permute-done | bytes 24608 | tf_op jit(solution)/shard_map/ppermute | solution.py:582
  60.2 2.2 %collective-permute-done.22.refs_3_ = bf16[16,768]{1,0:T(8,128)(2,1)S(1)} collective-permute-done((bf16[16,768]{1,0:T(8,128)(2,1)S(1)}, bf16[16,768]{1,0:T(8,128)(2,1)S(1)}, u32[]{:S(2)}, u32[]{:S(2)}) %collective-permute-start.22) | collective-permute-done | bytes 24608 | tf_op jit(solution)/shard_map/ppermute | solution.py:582
  62.4 0.1 pair_sum.1
  62.5 0.1 collective-permute-start.24
  62.6 1.9 %collective-permute-start.25 = (bf16[8,3072]{1,0:T(8,128)(2,1)S(1)}, bf16[8,3072]{1,0:T(8,128)(2,1)S(1)}, u32[]{:S(2)}, u32[]{:S(2)}) collective-permute-start(bf16[8,3072]{1,0:T(8,128)(2,1)S(1)} %get-tuple-element.85), channel_id=1, source_target_pairs={{0,8},{4,12},{8,0},{12,4},{1,9},{5,13},{9,1},{13,5},{2,10},{6,14},... | collective-permute-start | bytes 147464 | tf_op jit(solution)/shard_map/ppermute | solution.py:582
  64.5 2.5 %collective-permute-start.26 = (bf16[8,3072]{1,0:T(8,128)(2,1)S(1)}, bf16[8,3072]{1,0:T(8,128)(2,1)S(1)}, u32[]{:S(2)}, u32[]{:S(2)}) collective-permute-start(bf16[8,3072]{1,0:T(8,128)(2,1)S(1)} %get-tuple-element.86), channel_id=1, source_target_pairs={{0,12},{4,8},{8,4},{12,0},{1,13},{5,9},{9,5},{13,1},{2,14},{6,10},... | collective-permute-start | bytes 147464 | tf_op jit(solution)/shard_map/ppermute | solution.py:582
  67.0 1.1 %own_rows.1 = (f32[8,6144]{1,0:T(8,128)S(1)}, bf16[32,32]{1,0:T(8,128)(2,1)S(1)}) custom-call(s32[2,8]{1,0:T(2,128)} %bitcast.7, f32[2,8]{1,0:T(2,128)} %bitcast.8, bf16[8,6144]{1,0:T(8,128)(2,1)} %residual_ref.3, bf16[16,768]{1,0:T(8,128)(2,1)S(1)} %get-tuple-element.76.refs_0_, bf16[16,768]{1,0:T(8,128)(2,1)S(1)} %collective-permute-done.20.refs_1_, ...), custom_call_target="tpu_custom_call" | custom-call | flops 1000000 | bytes 1000000 | tf_op jit(solution)/shard_map/own_rows/pallas_call | solution.py:545
  68.1 2.3 %collective-permute-done.26.refs_3_ = bf16[8,3072]{1,0:T(8,128)(2,1)S(1)} collective-permute-done((bf16[8,3072]{1,0:T(8,128)(2,1)S(1)}, bf16[8,3072]{1,0:T(8,128)(2,1)S(1)}, u32[]{:S(2)}, u32[]{:S(2)}) %collective-permute-start.26) | collective-permute-done | bytes 49184 | tf_op jit(solution)/shard_map/ppermute | solution.py:582
  70.4 0.8 %finish.1 = bf16[8,6144]{1,0:T(8,128)(2,1)} custom-call(f32[8,6144]{1,0:T(8,128)S(1)} %get-tuple-element.80.combined_ref, bf16[32,32]{1,0:T(8,128)(2,1)S(1)} %get-tuple-element.81.weighting_ref, bf16[8,3072]{1,0:T(8,128)(2,1)S(1)} %get-tuple-element.83.refs_0_, bf16[8,3072]{1,0:T(8,128)(2,1)S(1)} %collective-permute-done.24.refs_1_, ...), custom_call_target="tpu_custom_call" | custom-call | tf_op jit(solution)/shard_map/finish/pallas_call | solution.py:571
  (11 shorter events, 0.1 us)
Async XLA Ops:
  3.8 11.8 %collective-permute-start.1 = (bf16[16,2944]{1,0:T(8,128)(2,1)S(1)}, bf16[16,2944]{1,0:T(8,128)(2,1)S(1)}, u32[]{:S(2)}, u32[]{:S(2)}) collective-permute-start(bf16[16,2944]{1,0:T(8,128)(2,1)S(1)} %get-tuple-element.48), channel_id=1, source_target_pairs={{0,4},{4,0},{8,12},{12,8},{1,5},{5,1},{9,13},{13,9},{2,6},{6,2},{1... | collective-permute-start | bytes 282632 | tf_op jit(solution)/shard_map/ppermute | solution.py:582
  6.9 10.1 %collective-permute-start.3 = (bf16[16,2944]{1,0:T(8,128)(2,1)S(1)}, bf16[16,2944]{1,0:T(8,128)(2,1)S(1)}, u32[]{:S(2)}, u32[]{:S(2)}) collective-permute-start(bf16[16,2944]{1,0:T(8,128)(2,1)S(1)} %get-tuple-element.49), channel_id=1, source_target_pairs={{0,8},{4,12},{8,0},{12,4},{1,9},{5,13},{9,1},{13,5},{2,10},{6,14},... | collective-permute-start | bytes 282632 | tf_op jit(solution)/shard_map/ppermute | solution.py:582
  9.4 7.5 %collective-permute-start.5 = (bf16[16,2944]{1,0:T(8,128)(2,1)S(1)}, bf16[16,2944]{1,0:T(8,128)(2,1)S(1)}, u32[]{:S(2)}, u32[]{:S(2)}) collective-permute-start(bf16[16,2944]{1,0:T(8,128)(2,1)S(1)} %get-tuple-element.50), channel_id=1, source_target_pairs={{0,12},{4,8},{8,4},{12,0},{1,13},{5,9},{9,5},{13,1},{2,14},{6,10},... | collective-permute-start | bytes 282632 | tf_op jit(solution)/shard_map/ppermute | solution.py:582
  15.5 2.0 %collective-permute-start = (bf16[16,2944]{1,0:T(8,128)(2,1)S(1)}, bf16[16,2944]{1,0:T(8,128)(2,1)S(1)}, u32[]{:S(2)}, u32[]{:S(2)}) collective-permute-start(bf16[16,2944]{1,0:T(8,128)(2,1)S(1)} %get-tuple-element.47.refs_0_), channel_id=1, source_target_pairs={{0,2},{2,0},{1,3},{3,1},{4,6},{6,4},{5,7},{7,5},{8,10},{10,8},{9,1... | collective-permute-start | bytes 282632 | tf_op jit(solution)/shard_map/ppermute | solution.py:582
  15.6 1.9 %collective-permute-start.2 = (bf16[16,2944]{1,0:T(8,128)(2,1)S(1)}, bf16[16,2944]{1,0:T(8,128)(2,1)S(1)}, u32[]{:S(2)}, u32[]{:S(2)}) collective-permute-start(bf16[16,2944]{1,0:T(8,128)(2,1)S(1)} %collective-permute-done.1.refs_2_), channel_id=1, source_target_pairs={{0,2},{2,0},{1,3},{3,1},{4,6},{6,4},{5,7},{7,5},{8,10},{10,8},{9,1... | collective-permute-start | bytes 282632 | tf_op jit(solution)/shard_map/ppermute | solution.py:582
  17.0 1.3 %collective-permute-start.4 = (bf16[16,2944]{1,0:T(8,128)(2,1)S(1)}, bf16[16,2944]{1,0:T(8,128)(2,1)S(1)}, u32[]{:S(2)}, u32[]{:S(2)}) collective-permute-start(bf16[16,2944]{1,0:T(8,128)(2,1)S(1)} %collective-permute-done.3.refs_4_), channel_id=1, source_target_pairs={{0,2},{2,0},{1,3},{3,1},{4,6},{6,4},{5,7},{7,5},{8,10},{10,8},{9,1... | collective-permute-start | bytes 282632 | tf_op jit(solution)/shard_map/ppermute | solution.py:582
  17.0 1.4 %collective-permute-start.6 = (bf16[16,2944]{1,0:T(8,128)(2,1)S(1)}, bf16[16,2944]{1,0:T(8,128)(2,1)S(1)}, u32[]{:S(2)}, u32[]{:S(2)}) collective-permute-start(bf16[16,2944]{1,0:T(8,128)(2,1)S(1)} %collective-permute-done.5.refs_6_), channel_id=1, source_target_pairs={{0,2},{2,0},{1,3},{3,1},{4,6},{6,4},{5,7},{7,5},{8,10},{10,8},{9,1... | collective-permute-start | bytes 282632 | tf_op jit(solution)/shard_map/ppermute | solution.py:582
  19.1 5.1 %collective-permute-start.7 = (bf16[64,768]{1,0:T(8,128)(2,1)S(1)}, bf16[64,768]{1,0:T(8,128)(2,1)S(1)}, u32[]{:S(2)}, u32[]{:S(2)}) collective-permute-start(bf16[64,768]{1,0:T(8,128)(2,1)S(1)} %get-tuple-element.53), channel_id=1, source_target_pairs={{0,1},{1,0},{2,3},{3,2},{4,5},{5,4},{6,7},{7,6},{8,9},{9,8},{10,11... | collective-permute-start | bytes 294920 | tf_op jit(solution)/shard_map/ppermute | solution.py:582
  24.5 4.2 %collective-permute-start.13 = (bf16[32,768]{1,0:T(8,128)(2,1)S(1)}, bf16[32,768]{1,0:T(8,128)(2,1)S(1)}, u32[]{:S(2)}, u32[]{:S(2)}) collective-permute-start(bf16[32,768]{1,0:T(8,128)(2,1)S(1)} %get-tuple-element.59.refs_0_), channel_id=1, source_target_pairs={{0,4},{4,0},{8,12},{12,8},{1,5},{5,1},{9,13},{13,9},{2,6},{6,2},{1... | collective-permute-start | bytes 147464 | tf_op jit(solution)/shard_map/ppermute | solution.py:582
  25.8 7.9 %collective-permute-start.10 = (bf16[32,768]{1,0:T(8,128)(2,1)S(1)}, bf16[32,768]{1,0:T(8,128)(2,1)S(1)}, u32[]{:S(2)}, u32[]{:S(2)}) collective-permute-start(bf16[32,768]{1,0:T(8,128)(2,1)S(1)} %relay.4), channel_id=1, source_target_pairs={{0,12},{4,8},{8,4},{12,0},{1,13},{5,9},{9,5},{13,1},{2,14},{6,10},... | collective-permute-start | bytes 147464 | tf_op jit(solution)/shard_map/ppermute | solution.py:582
  28.3 5.3 %collective-permute-start.9 = (bf16[32,768]{1,0:T(8,128)(2,1)S(1)}, bf16[32,768]{1,0:T(8,128)(2,1)S(1)}, u32[]{:S(2)}, u32[]{:S(2)}) collective-permute-start(bf16[32,768]{1,0:T(8,128)(2,1)S(1)} %relay.3), channel_id=1, source_target_pairs={{0,8},{4,12},{8,0},{12,4},{1,9},{5,13},{9,1},{13,5},{2,10},{6,14},... | collective-permute-start | bytes 147464 | tf_op jit(solution)/shard_map/ppermute | solution.py:582
  28.6 5.0 %collective-permute-start.15 = (bf16[64,768]{1,0:T(8,128)(2,1)S(1)}, bf16[64,768]{1,0:T(8,128)(2,1)S(1)}, u32[]{:S(2)}, u32[]{:S(2)}) collective-permute-start(bf16[64,768]{1,0:T(8,128)(2,1)S(1)} %constant_dynamic-update-slice_fusion.2.refs_0_), channel_id=1, source_target_pairs={{0,1},{1,0},{2,3},{3,2},{4,5},{5,4},{6,7},{7,6},{8,9},{9,8},{10,11... | collective-permute-start | bytes 294920 | tf_op jit(solution)/shard_map/ppermute | solution.py:582
  30.1 5.7 %collective-permute-start.14 = (bf16[64,768]{1,0:T(8,128)(2,1)S(1)}, bf16[64,768]{1,0:T(8,128)(2,1)S(1)}, u32[]{:S(2)}, u32[]{:S(2)}) collective-permute-start(bf16[64,768]{1,0:T(8,128)(2,1)S(1)} %constant_dynamic-update-slice_fusion.2.refs_0_), channel_id=1, source_target_pairs={{0,2},{2,0},{1,3},{3,1},{4,6},{6,4},{5,7},{7,5},{8,10},{10,8},{9,1... | collective-permute-start | bytes 294920 | tf_op jit(solution)/shard_map/ppermute | solution.py:582
  33.6 2.2 %collective-permute-start.16 = (bf16[64,768]{1,0:T(8,128)(2,1)S(1)}, bf16[64,768]{1,0:T(8,128)(2,1)S(1)}, u32[]{:S(2)}, u32[]{:S(2)}) collective-permute-start(bf16[64,768]{1,0:T(8,128)(2,1)S(1)} %collective-permute-done.15.refs_2_), channel_id=1, source_target_pairs={{0,2},{2,0},{1,3},{3,1},{4,6},{6,4},{5,7},{7,5},{8,10},{10,8},{9,1... | collective-permute-start | bytes 294920 | tf_op jit(solution)/shard_map/ppermute | solution.py:582
  33.7 8.0 %collective-permute-start.12 = (bf16[64,768]{1,0:T(8,128)(2,1)S(1)}, bf16[64,768]{1,0:T(8,128)(2,1)S(1)}, u32[]{:S(2)}, u32[]{:S(2)}) collective-permute-start(bf16[64,768]{1,0:T(8,128)(2,1)S(1)} %constant_dynamic-update-slice_fusion.refs_0_), channel_id=1, source_target_pairs={{0,1},{1,0},{2,3},{3,2},{4,5},{5,4},{6,7},{7,6},{8,9},{9,8},{10,11... | collective-permute-start | bytes 294920 | tf_op jit(solution)/shard_map/ppermute | solution.py:582
  35.3 6.4 %collective-permute-start.8 = (bf16[32,768]{1,0:T(8,128)(2,1)S(1)}, bf16[32,768]{1,0:T(8,128)(2,1)S(1)}, u32[]{:S(2)}, u32[]{:S(2)}) collective-permute-start(bf16[32,768]{1,0:T(8,128)(2,1)S(1)} %get-tuple-element.57), channel_id=1, source_target_pairs={{0,2},{2,0},{1,3},{3,1},{4,6},{6,4},{5,7},{7,5},{8,10},{10,8},{9,1... | collective-permute-start | bytes 147464 | tf_op jit(solution)/shard_map/ppermute | solution.py:582
  35.5 6.5 %collective-permute-start.11 = (bf16[64,768]{1,0:T(8,128)(2,1)S(1)}, bf16[64,768]{1,0:T(8,128)(2,1)S(1)}, u32[]{:S(2)}, u32[]{:S(2)}) collective-permute-start(bf16[64,768]{1,0:T(8,128)(2,1)S(1)} %constant_dynamic-update-slice_fusion.refs_0_), channel_id=1, source_target_pairs={{0,2},{2,0},{1,3},{3,1},{4,6},{6,4},{5,7},{7,5},{8,10},{10,8},{9,1... | collective-permute-start | bytes 294920 | tf_op jit(solution)/shard_map/ppermute | solution.py:582
  41.8 1.4 %collective-permute-start.17 = (bf16[64,768]{1,0:T(8,128)(2,1)S(1)}, bf16[64,768]{1,0:T(8,128)(2,1)S(1)}, u32[]{:S(2)}, u32[]{:S(2)}) collective-permute-start(bf16[64,768]{1,0:T(8,128)(2,1)S(1)} %relay.5.refs_2_), channel_id=1, source_target_pairs={{0,2},{2,0},{1,3},{3,1},{4,6},{6,4},{5,7},{7,5},{8,10},{10,8},{9,1... | collective-permute-start | bytes 294920 | tf_op jit(solution)/shard_map/ppermute | solution.py:582
  51.1 1.5 %collective-permute-start.19 = (bf16[32,3072]{1,0:T(8,128)(2,1)S(1)}, bf16[32,3072]{1,0:T(8,128)(2,1)S(1)}, u32[]{:S(2)}, u32[]{:S(2)}) collective-permute-start(bf16[32,3072]{1,0:T(8,128)(2,1)S(1)} %get-tuple-element.74), channel_id=1, source_target_pairs={{0,2},{2,0},{1,3},{3,1},{4,6},{6,4},{5,7},{7,5},{8,10},{10,8},{9,1... | collective-permute-start | bytes 589832 | tf_op jit(solution)/shard_map/ppermute | solution.py:582
  51.3 1.5 %collective-permute-start.18 = (bf16[32,3072]{1,0:T(8,128)(2,1)S(1)}, bf16[32,3072]{1,0:T(8,128)(2,1)S(1)}, u32[]{:S(2)}, u32[]{:S(2)}) collective-permute-start(bf16[32,3072]{1,0:T(8,128)(2,1)S(1)} %get-tuple-element.73), channel_id=1, source_target_pairs={{0,2},{2,0},{1,3},{3,1},{4,6},{6,4},{5,7},{7,5},{8,10},{10,8},{9,1... | collective-permute-start | bytes 589832 | tf_op jit(solution)/shard_map/ppermute | solution.py:582
  53.0 9.5 %collective-permute-start.23 = (bf16[16,6144]{1,0:T(8,128)(2,1)S(1)}, bf16[16,6144]{1,0:T(8,128)(2,1)S(1)}, u32[]{:S(2)}, u32[]{:S(2)}) collective-permute-start(bf16[16,6144]{1,0:T(8,128)(2,1)S(1)} %get-tuple-element.82), channel_id=1, source_target_pairs={{0,1},{1,0},{2,3},{3,2},{4,5},{5,4},{6,7},{7,6},{8,9},{9,8},{10,11... | collective-permute-start | bytes 589832 | tf_op jit(solution)/shard_map/ppermute | solution.py:582
  53.7 4.5 %collective-permute-start.20 = (bf16[16,768]{1,0:T(8,128)(2,1)S(1)}, bf16[16,768]{1,0:T(8,128)(2,1)S(1)}, u32[]{:S(2)}, u32[]{:S(2)}) collective-permute-start(bf16[16,768]{1,0:T(8,128)(2,1)S(1)} %get-tuple-element.77), channel_id=1, source_target_pairs={{0,4},{4,0},{8,12},{12,8},{1,5},{5,1},{9,13},{13,9},{2,6},{6,2},{1... | collective-permute-start | bytes 73736 | tf_op jit(solution)/shard_map/ppermute | solution.py:582
  55.0 5.2 %collective-permute-start.21 = (bf16[16,768]{1,0:T(8,128)(2,1)S(1)}, bf16[16,768]{1,0:T(8,128)(2,1)S(1)}, u32[]{:S(2)}, u32[]{:S(2)}) collective-permute-start(bf16[16,768]{1,0:T(8,128)(2,1)S(1)} %get-tuple-element.78), channel_id=1, source_target_pairs={{0,8},{4,12},{8,0},{12,4},{1,9},{5,13},{9,1},{13,5},{2,10},{6,14},... | collective-permute-start | bytes 73736 | tf_op jit(solution)/shard_map/ppermute | solution.py:582
  56.8 5.6 %collective-permute-start.22 = (bf16[16,768]{1,0:T(8,128)(2,1)S(1)}, bf16[16,768]{1,0:T(8,128)(2,1)S(1)}, u32[]{:S(2)}, u32[]{:S(2)}) collective-permute-start(bf16[16,768]{1,0:T(8,128)(2,1)S(1)} %get-tuple-element.79), channel_id=1, source_target_pairs={{0,12},{4,8},{8,4},{12,0},{1,13},{5,9},{9,5},{13,1},{2,14},{6,10},... | collective-permute-start | bytes 73736 | tf_op jit(solution)/shard_map/ppermute | solution.py:582
  62.5 5.6 %collective-permute-start.24 = (bf16[8,3072]{1,0:T(8,128)(2,1)S(1)}, bf16[8,3072]{1,0:T(8,128)(2,1)S(1)}, u32[]{:S(2)}, u32[]{:S(2)}) collective-permute-start(bf16[8,3072]{1,0:T(8,128)(2,1)S(1)} %get-tuple-element.84), channel_id=1, source_target_pairs={{0,4},{4,0},{8,12},{12,8},{1,5},{5,1},{9,13},{13,9},{2,6},{6,2},{1... | collective-permute-start | bytes 147464 | tf_op jit(solution)/shard_map/ppermute | solution.py:582
  62.6 5.5 %collective-permute-start.25 = (bf16[8,3072]{1,0:T(8,128)(2,1)S(1)}, bf16[8,3072]{1,0:T(8,128)(2,1)S(1)}, u32[]{:S(2)}, u32[]{:S(2)}) collective-permute-start(bf16[8,3072]{1,0:T(8,128)(2,1)S(1)} %get-tuple-element.85), channel_id=1, source_target_pairs={{0,8},{4,12},{8,0},{12,4},{1,9},{5,13},{9,1},{13,5},{2,10},{6,14},... | collective-permute-start | bytes 147464 | tf_op jit(solution)/shard_map/ppermute | solution.py:582
  64.5 5.9 %collective-permute-start.26 = (bf16[8,3072]{1,0:T(8,128)(2,1)S(1)}, bf16[8,3072]{1,0:T(8,128)(2,1)S(1)}, u32[]{:S(2)}, u32[]{:S(2)}) collective-permute-start(bf16[8,3072]{1,0:T(8,128)(2,1)S(1)} %get-tuple-element.86), channel_id=1, source_target_pairs={{0,12},{4,8},{8,4},{12,0},{1,13},{5,9},{9,5},{13,1},{2,14},{6,10},... | collective-permute-start | bytes 147464 | tf_op jit(solution)/shard_map/ppermute | solution.py:582

commit v9 on v8

--- a/solution.py
+++ b/solution.py
@@ -25,6 +25,10 @@
 
 def limits(mib):
     return pltpu.CompilerParams(vmem_limit_bytes=mib * MIB)
+
+
+def far_first(count):
+    return [-d % count for d in range(count)]
 
 
 def dot(a, b):
@@ -162,7 +166,7 @@
     rows = pieces[0].shape[0]
     expert, half, pair = lax.axis_index("expert"), lax.axis_index("half"), lax.axis_index("pair")
     for j, piece in enumerate(pieces):
-        base = (expert ^ (j // 2)) * 2 + (half ^ (j % 2))
+        base = (expert ^ far_first(len(pieces) // 2)[j // 2]) * 2 + (half ^ (j % 2))
         x_ref[pl.ds(pl.multiple_of(base * rows, rows), rows)] = piece[:, :depth]
     product_ref[...] = dot(x_ref[...], weight_ref[...])
     own = rows // 2
@@ -205,7 +209,7 @@
     experts = len(pieces) // 2
     expert, half = lax.axis_index("expert"), lax.axis_index("half")
     for j, piece in enumerate(pieces):
-        base = (expert ^ (j // 2)) * 2 + (half ^ (j % 2))
+        base = (expert ^ far_first(len(pieces) // 2)[j // 2]) * 2 + (half ^ (j % 2))
         at = pl.ds(pl.multiple_of(base * own, own), own)
         last = piece.shape[1] - columns
         both = piece[:, last:].astype(F32)
@@ -514,7 +518,7 @@
     top, own_count = own_ids_ref.shape
     columns = pieces[0].shape[1]
     expert, half = lax.axis_index("expert"), lax.axis_index("half")
-    for d, piece in enumerate(pieces):
+    for d, piece in zip(far_first(len(pieces)), pieces):
         both = piece[...].astype(F32)
         for c in range(2):
             base = ((expert ^ d) * 2 + (half ^ c)) * columns
@@ -560,7 +564,8 @@
     got, out_ref = refs[:-1], refs[-1]
     part = got[0].shape[1]
     rows = combined_ref.shape[0]
-    terms = jnp.concatenate([piece[...].astype(F32) for piece in got], axis=0).astype(BF16)
+    terms = [got[d][...].astype(F32) for d in far_first(len(got))]
+    terms = jnp.concatenate(terms, axis=0).astype(BF16)
     for h in range(combined_ref.shape[1] // part):
         at = slice(h * part, (h + 1) * part)
         mixture = dot(weighting_ref[h * 16 : (h + 1) * 16], terms)
@@ -614,8 +619,8 @@
         messages[0], [out_weight, norm_gain.reshape(1, -1), expert_gate]
     )
     pieces = []
-    for d, message in enumerate(messages):
-        message = swap(message, "expert", d)
+    for d in far_first(experts):
+        message = swap(messages[d], "expert", d)
         pieces += [message, swap(message, "half", 1)]
 
     keep, send = project(pieces, weight_here)
@@ -649,10 +654,10 @@
         got.append(swap(send, "half", 1))
     keep, send = chip_sum(mine, got)
     own = cut(own, cross, keep, experts)
-    own = [swap(rows, "expert", d) for d, rows in enumerate(own)]
+    own = [swap(own[d], "expert", d) for d in far_first(experts)]
     terms = pair_sum(keep, swap(send, "pair", 1), capacity, experts, own)
     combined, weighting = own_rows(ids, weights, residual, own, capacity)
-    back = [swap(term, "expert", d) for d, term in enumerate(terms)]
+    back = [swap(terms[d], "expert", d) for d in far_first(experts)]
     return finish(combined, weighting, back)
 
 

time: 71.5 us -> 69.4 us (0.971)
  waiting for transfers between devices: 14.8 us -> 12.7 us
    ppermute x27, waiting for transfers between devices: 14.8 us -> 12.7 us  [swap(): lax.ppermute(x, axis, [(i, i ^ by) for i in range(lax.axis_size(axis))])]
  transfers between devices with their start and end apart: 27 -> 27, of which waited for: 12 -> 14; matrix products, arithmetic and copies ran while one was open for 0% -> 0% of each run, Pallas kernels for 23% -> 24%
where the time goes in v9:
time: 69.4 us; the launch traced here: 69.2 us
  Pallas kernels  29.9 us (43%)
  starting transfers between devices  26.4 us (38%)
  waiting for transfers between devices  12.7 us (18%)
    ppermute x27, starting transfers between devices, swap(): lax.ppermute(x, axis, [(i, i ^ by) for i in range(lax.axis_size(axis))])  26.4 us
    ppermute x27, waiting for transfers between devices, swap(): lax.ppermute(x, axis, [(i, i ^ by) for i in range(lax.axis_size(axis))])  12.7 us
    pallas_call x1, Pallas kernels, load(): pl.pallas_call(functools.partial(load_kernel, len(weights)), in_specs=[AN...  6.03 us
    pallas_call x1, Pallas kernels, expert_first(): pl.pallas_call(functools.partial(expert_first_kernel, count), in_specs=[V...  5.9 us
    pallas_call x1, Pallas kernels, expert_second(): pl.pallas_call(functools.partial(expert_second_kernel, count), in_specs=[...  5.23 us
    pallas_call x1, Pallas kernels, attend(): pl.pallas_call(functools.partial(attend_kernel, rows // requests, heads /...  3.76 us
    pallas_call x1, Pallas kernels, route(): pl.pallas_call(functools.partial(route_kernel, capacity, top), in_specs=[...  3.28 us
    pallas_call x2, Pallas kernels, expert_down(): pl.pallas_call(functools.partial(down_kernel, start, 512), in_specs=[VMEM...  2.71 us
  transfers between devices with their start and end apart: 27, of which 14 were waited for; matrix products, arithmetic and copies ran while one was open for 0% of the time, Pallas kernels for 24%

profile of v9, /device:TPU:0, one launch (start us, length us, event | category | flops | bytes accessed | tf_op | source)
XLA Modules:
  0.0 69.2 jit_solution(10827787157721678481)
XLA Ops:
  0.0 3.8 %attention.1 = (bf16[16,2944]{1,0:T(8,128)(2,1)S(1)}, bf16[16,2944]{1,0:T(8,128)(2,1)S(1)}, bf16[16,2944]{1,0:T(8,128)(2,1)S(1)}, bf16[16,2944]{1,0:T(8,128)(2,1)S(1)}) custom-call(f32[16]{0:T(128)} %decay_ref.1, s32[2,8]{1,0:T(2,128)} %bitcast.6, bf16[16,2048]{1,0:T(8,128)(2,1)} %q_ref.1, bf16[16,2048]{1,0:T(8,128)(2,1)} %k_ref.1, bf16[16,2048]{1,0:T(8,128)(2,1)} %v_ref.1, ...), custom_call_target="tpu_custom_call" | custom-call | tf_op jit(solution)/shard_map/attention/pallas_call | solution.py:111
  3.8 5.1 %collective-permute-start.1 = (bf16[16,2944]{1,0:T(8,128)(2,1)S(1)}, bf16[16,2944]{1,0:T(8,128)(2,1)S(1)}, u32[]{:S(2)}, u32[]{:S(2)}) collective-permute-start(bf16[16,2944]{1,0:T(8,128)(2,1)S(1)} %get-tuple-element.48), channel_id=1, source_target_pairs={{0,12},{4,8},{8,4},{12,0},{1,13},{5,9},{9,5},{13,1},{2,14},{6,10},... | collective-permute-start | bytes 282632 | tf_op jit(solution)/shard_map/ppermute | solution.py:587
  8.9 0.0 collective-permute-start.3
  8.9 0.6 collective-permute-start.5
  9.5 6.0 %load.1 = (bf16[16,2944]{1,0:T(8,128)(2,1)S(1)}, bf16[2048,768]{1,0:T(8,128)(2,1)S(1)}, f32[1,6144]{1,0:T(1,128)S(1)}, bf16[1152,6144]{1,0:T(8,128)(2,1)S(1)}) custom-call(bf16[16,2944]{1,0:T(8,128)(2,1)S(1)} %get-tuple-element.46.rows_hbm, bf16[2048,768]{1,0:T(8,128)(2,1)} %refs_0_.1, f32[1,6144]{1,0:T(1,128)} %bitcast.4, bf16[1152,6144]{1,0:T(8,128)(2,1)} %refs_2_.1), custom_call_target="tpu_custom_call" | custom-call | bytes 17326080 | tf_op jit(solution)/shard_map/load/pallas_call | solution.py:150
  15.6 0.1 collective-permute-start
  15.6 0.0 collective-permute-done.1.refs_2_
  15.7 0.5 collective-permute-start.2
  16.1 0.6 collective-permute-done.3.refs_4_
  16.8 0.0 collective-permute-start.4
  16.8 0.0 collective-permute-done.5.refs_6_
  16.8 0.5 collective-permute-start.6
  17.3 0.0 collective-permute-done.refs_1_
  17.3 0.0 collective-permute-done.2.refs_3_
  17.3 0.8 %collective-permute-done.4.refs_5_ = bf16[16,2944]{1,0:T(8,128)(2,1)S(1)} collective-permute-done((bf16[16,2944]{1,0:T(8,128)(2,1)S(1)}, bf16[16,2944]{1,0:T(8,128)(2,1)S(1)}, u32[]{:S(2)}, u32[]{:S(2)}) %collective-permute-start.4) | collective-permute-done | bytes 94240 | tf_op jit(solution)/shard_map/ppermute | solution.py:587
  18.1 0.2 collective-permute-done.6.refs_7_
  18.3 0.7 %projection.1 = (f32[64,768]{1,0:T(8,128)S(1)}, bf16[64,768]{1,0:T(8,128)(2,1)S(1)}) custom-call(bf16[16,2944]{1,0:T(8,128)(2,1)S(1)} %get-tuple-element.47.refs_0_, bf16[16,2944]{1,0:T(8,128)(2,1)S(1)} %collective-permute-done.refs_1_, bf16[16,2944]{1,0:T(8,128)(2,1)S(1)} %collective-permute-done.1.refs_2_, ...), custom_call_target="tpu_custom_call" | custom-call | tf_op jit(solution)/shard_map/projection/pallas_call | solution.py:187
  19.0 1.6 %collective-permute-start.7 = (bf16[64,768]{1,0:T(8,128)(2,1)S(1)}, bf16[64,768]{1,0:T(8,128)(2,1)S(1)}, u32[]{:S(2)}, u32[]{:S(2)}) collective-permute-start(bf16[64,768]{1,0:T(8,128)(2,1)S(1)} %get-tuple-element.53), channel_id=1, source_target_pairs={{0,1},{1,0},{2,3},{3,2},{4,5},{5,4},{6,7},{7,6},{8,9},{9,8},{10,11... | collective-permute-start | bytes 294920 | tf_op jit(solution)/shard_map/ppermute | solution.py:587
  20.5 3.3 %route.1 = (bf16[128,64]{1,0:T(8,128)(2,1)S(1)}, f32[64,768]{1,0:T(8,128)S(1)}, bf16[640,6144]{1,0:T(8,128)(2,1)S(1)}) custom-call(bf16[16,2944]{1,0:T(8,128)(2,1)S(1)} %get-tuple-element.47.refs_0_, bf16[16,2944]{1,0:T(8,128)(2,1)S(1)} %collective-permute-done.refs_1_, bf16[16,2944]{1,0:T(8,128)(2,1)S(1)} %collective-permute-done.1.refs_2_, ...), custom_call_target="tpu_custom_call" | custom-call | flops 1000000 | bytes 8000000 | tf_op jit(solution)/shard_map/route/pallas_call | solution.py:243
  23.8 0.3 collective-permute-done.7.got_ref
  24.1 0.2 pack.1
  24.3 0.8 %collective-permute-start.13 = (bf16[32,768]{1,0:T(8,128)(2,1)S(1)}, bf16[32,768]{1,0:T(8,128)(2,1)S(1)}, u32[]{:S(2)}, u32[]{:S(2)}) collective-permute-start(bf16[32,768]{1,0:T(8,128)(2,1)S(1)} %get-tuple-element.59.refs_0_), channel_id=1, source_target_pairs={{0,4},{4,0},{8,12},{12,8},{1,5},{5,1},{9,13},{13,9},{2,6},{6,2},{1... | collective-permute-start | bytes 147464 | tf_op jit(solution)/shard_map/ppermute | solution.py:587
  25.1 2.4 %collective-permute-start.10 = (bf16[32,768]{1,0:T(8,128)(2,1)S(1)}, bf16[32,768]{1,0:T(8,128)(2,1)S(1)}, u32[]{:S(2)}, u32[]{:S(2)}) collective-permute-start(bf16[32,768]{1,0:T(8,128)(2,1)S(1)} %relay.4), channel_id=1, source_target_pairs={{0,12},{4,8},{8,4},{12,0},{1,13},{5,9},{9,5},{13,1},{2,14},{6,10},... | collective-permute-start | bytes 147464 | tf_op jit(solution)/shard_map/ppermute | solution.py:587
  27.6 0.6 collective-permute-start.9
  28.2 0.3 collective-permute-done.13
  28.5 1.5 %collective-permute-start.15 = (bf16[64,768]{1,0:T(8,128)(2,1)S(1)}, bf16[64,768]{1,0:T(8,128)(2,1)S(1)}, u32[]{:S(2)}, u32[]{:S(2)}) collective-permute-start(bf16[64,768]{1,0:T(8,128)(2,1)S(1)} %constant_dynamic-update-slice_fusion.2.refs_0_), channel_id=1, source_target_pairs={{0,1},{1,0},{2,3},{3,2},{4,5},{5,4},{6,7},{7,6},{8,9},{9,8},{10,11... | collective-permute-start | bytes 294920 | tf_op jit(solution)/shard_map/ppermute | solution.py:587
  30.0 0.0 collective-permute-start.14
  30.0 2.7 %collective-permute-done.9 = bf16[32,768]{1,0:T(8,128)(2,1)S(1)} collective-permute-done((bf16[32,768]{1,0:T(8,128)(2,1)S(1)}, bf16[32,768]{1,0:T(8,128)(2,1)S(1)}, u32[]{:S(2)}, u32[]{:S(2)}) %collective-permute-start.9) | collective-permute-done | bytes 49184 | tf_op jit(solution)/shard_map/ppermute | solution.py:587
  32.7 0.4 collective-permute-done.15.refs_2_
  33.1 0.0 collective-permute-start.16
  33.1 0.0 collective-permute-done.10
  33.1 1.6 %collective-permute-start.12 = (bf16[64,768]{1,0:T(8,128)(2,1)S(1)}, bf16[64,768]{1,0:T(8,128)(2,1)S(1)}, u32[]{:S(2)}, u32[]{:S(2)}) collective-permute-start(bf16[64,768]{1,0:T(8,128)(2,1)S(1)} %constant_dynamic-update-slice_fusion.refs_0_), channel_id=1, source_target_pairs={{0,1},{1,0},{2,3},{3,2},{4,5},{5,4},{6,7},{7,6},{8,9},{9,8},{10,11... | collective-permute-start | bytes 294920 | tf_op jit(solution)/shard_map/ppermute | solution.py:587
  34.6 0.2 collective-permute-start.8
  34.9 0.3 collective-permute-start.11
  35.2 0.0 collective-permute-done.14.refs_1_
  35.2 0.0 collective-permute-done.16.refs_3_
  35.2 5.9 %experts_first.1 = (f32[1152,64]{1,0:T(8,128)S(1)}, f32[1152,64]{1,0:T(8,128)S(1)}, f32[64,128]{1,0:T(8,128)S(1)}, bf16[512,6144]{1,0:T(8,128)(2,1)S(1)}) custom-call(bf16[64,768]{1,0:T(8,128)(2,1)S(1)} %constant_dynamic-update-slice_fusion.2.refs_0_, bf16[64,768]{1,0:T(8,128)(2,1)S(1)} %collective-permute-done.14.refs_1_, ...), custom_call_target="tpu_custom_call" | custom-call | flops 905969664 | bytes 14155776 | tf_op jit(solution)/shard_map/experts_first/pallas_call | solution.py:376
  41.1 0.0 collective-permute-done.8.refs_1_.cross_ref
  41.1 0.3 collective-permute-start.17
  41.4 0.0 collective-permute-done.11.refs_1_
  41.4 1.1 %collective-permute-done.17.refs_3_ = bf16[64,768]{1,0:T(8,128)(2,1)S(1)} collective-permute-done((bf16[64,768]{1,0:T(8,128)(2,1)S(1)}, bf16[64,768]{1,0:T(8,128)(2,1)S(1)}, u32[]{:S(2)}, u32[]{:S(2)}) %collective-permute-start.17) | collective-permute-done | bytes 98336 | tf_op jit(solution)/shard_map/ppermute | solution.py:587
  42.5 5.2 %experts_second.1 = (bf16[64,1152]{1,0:T(8,128)(2,1)S(1)}, bf16[1152,6144]{1,0:T(8,128)(2,1)S(1)}) custom-call(bf16[64,768]{1,0:T(8,128)(2,1)S(1)} %constant_dynamic-update-slice_fusion.refs_0_, bf16[64,768]{1,0:T(8,128)(2,1)S(1)} %collective-permute-done.11.refs_1_, bf16[64,768]{1,0:T(8,128)(2,1)S(1)} %relay.5.refs_2_, ...), custom_call_target="tpu_custom_call" | custom-call | flops 905969664 | bytes 14155776 | tf_op jit(solution)/shard_map/experts_second/pallas_call | solution.py:411
  47.7 1.4 %experts_down.3 = (f32[32,3072]{1,0:T(8,128)S(1)}, bf16[32,3072]{1,0:T(8,128)(2,1)S(1)}) custom-call(bf16[64,1152]{1,0:T(8,128)(2,1)S(1)} %get-tuple-element.69.hidden_ref, bf16[1152,6144]{1,0:T(8,128)(2,1)S(1)} %get-tuple-element.70.weight_ref), custom_call_target="tpu_custom_call" | custom-call | flops 905969664 | bytes 7077888 | tf_op jit(solution)/shard_map/experts_down/pallas_call | solution.py:427
  49.1 1.4 %experts_down.2 = (f32[32,3072]{1,0:T(8,128)S(1)}, bf16[32,3072]{1,0:T(8,128)(2,1)S(1)}) custom-call(bf16[64,1152]{1,0:T(8,128)(2,1)S(1)} %get-tuple-element.69.hidden_ref, bf16[1152,6144]{1,0:T(8,128)(2,1)S(1)} %get-tuple-element.70.weight_ref), custom_call_target="tpu_custom_call" | custom-call | flops 905969664 | bytes 7077888 | tf_op jit(solution)/shard_map/experts_down/pallas_call | solution.py:427
  50.4 0.3 collective-permute-start.19
  50.7 0.3 collective-permute-start.18
  51.0 0.9 %collective-permute-done.19.refs_3_ = bf16[32,3072]{1,0:T(8,128)(2,1)S(1)} collective-permute-done((bf16[32,3072]{1,0:T(8,128)(2,1)S(1)}, bf16[32,3072]{1,0:T(8,128)(2,1)S(1)}, u32[]{:S(2)}, u32[]{:S(2)}) %collective-permute-start.19) | collective-permute-done | bytes 196640 | tf_op jit(solution)/shard_map/ppermute | solution.py:587
  51.9 0.3 collective-permute-done.18.refs_2_
  52.2 0.1 chip_sum.1
  52.3 0.8 %collective-permute-start.23 = (bf16[16,6144]{1,0:T(8,128)(2,1)S(1)}, bf16[16,6144]{1,0:T(8,128)(2,1)S(1)}, u32[]{:S(2)}, u32[]{:S(2)}) collective-permute-start(bf16[16,6144]{1,0:T(8,128)(2,1)S(1)} %get-tuple-element.82), channel_id=1, source_target_pairs={{0,1},{1,0},{2,3},{3,2},{4,5},{5,4},{6,7},{7,6},{8,9},{9,8},{10,11... | collective-permute-start | bytes 589832 | tf_op jit(solution)/shard_map/ppermute | solution.py:587
  53.1 3.2 %collective-permute-start.20 = (bf16[16,768]{1,0:T(8,128)(2,1)S(1)}, bf16[16,768]{1,0:T(8,128)(2,1)S(1)}, u32[]{:S(2)}, u32[]{:S(2)}) collective-permute-start(bf16[16,768]{1,0:T(8,128)(2,1)S(1)} %get-tuple-element.77), channel_id=1, source_target_pairs={{0,12},{4,8},{8,4},{12,0},{1,13},{5,9},{9,5},{13,1},{2,14},{6,10},... | collective-permute-start | bytes 73736 | tf_op jit(solution)/shard_map/ppermute | solution.py:587
  56.2 0.0 collective-permute-start.21
  56.2 1.3 %collective-permute-start.22 = (bf16[16,768]{1,0:T(8,128)(2,1)S(1)}, bf16[16,768]{1,0:T(8,128)(2,1)S(1)}, u32[]{:S(2)}, u32[]{:S(2)}) collective-permute-start(bf16[16,768]{1,0:T(8,128)(2,1)S(1)} %get-tuple-element.79), channel_id=1, source_target_pairs={{0,4},{4,0},{8,12},{12,8},{1,5},{5,1},{9,13},{13,9},{2,6},{6,2},{1... | collective-permute-start | bytes 73736 | tf_op jit(solution)/shard_map/ppermute | solution.py:587
  57.5 1.5 %collective-permute-done.20.refs_1_ = bf16[16,768]{1,0:T(8,128)(2,1)S(1)} collective-permute-done((bf16[16,768]{1,0:T(8,128)(2,1)S(1)}, bf16[16,768]{1,0:T(8,128)(2,1)S(1)}, u32[]{:S(2)}, u32[]{:S(2)}) %collective-permute-start.20) | collective-permute-done | bytes 24608 | tf_op jit(solution)/shard_map/ppermute | solution.py:587
  59.0 1.9 %collective-permute-done.21.refs_2_ = bf16[16,768]{1,0:T(8,128)(2,1)S(1)} collective-permute-done((bf16[16,768]{1,0:T(8,128)(2,1)S(1)}, bf16[16,768]{1,0:T(8,128)(2,1)S(1)}, u32[]{:S(2)}, u32[]{:S(2)}) %collective-permute-start.21) | collective-permute-done | bytes 24608 | tf_op jit(solution)/shard_map/ppermute | solution.py:587
  61.0 0.1 pair_sum.1
  61.1 1.6 %collective-permute-start.24 = (bf16[8,3072]{1,0:T(8,128)(2,1)S(1)}, bf16[8,3072]{1,0:T(8,128)(2,1)S(1)}, u32[]{:S(2)}, u32[]{:S(2)}) collective-permute-start(bf16[8,3072]{1,0:T(8,128)(2,1)S(1)} %get-tuple-element.84), channel_id=1, source_target_pairs={{0,12},{4,8},{8,4},{12,0},{1,13},{5,9},{9,5},{13,1},{2,14},{6,10},... | collective-permute-start | bytes 147464 | tf_op jit(solution)/shard_map/ppermute | solution.py:587
  62.7 0.6 collective-permute-start.25
  63.2 2.3 %collective-permute-start.26 = (bf16[8,3072]{1,0:T(8,128)(2,1)S(1)}, bf16[8,3072]{1,0:T(8,128)(2,1)S(1)}, u32[]{:S(2)}, u32[]{:S(2)}) collective-permute-start(bf16[8,3072]{1,0:T(8,128)(2,1)S(1)} %get-tuple-element.86), channel_id=1, source_target_pairs={{0,4},{4,0},{8,12},{12,8},{1,5},{5,1},{9,13},{13,9},{2,6},{6,2},{1... | collective-permute-start | bytes 147464 | tf_op jit(solution)/shard_map/ppermute | solution.py:587
  65.5 1.1 %own_rows.1 = (f32[8,6144]{1,0:T(8,128)S(1)}, bf16[32,32]{1,0:T(8,128)(2,1)S(1)}) custom-call(s32[2,8]{1,0:T(2,128)} %bitcast.7, f32[2,8]{1,0:T(2,128)} %bitcast.8, bf16[8,6144]{1,0:T(8,128)(2,1)} %residual_ref.3, bf16[16,768]{1,0:T(8,128)(2,1)S(1)} %get-tuple-element.76.refs_0_, bf16[16,768]{1,0:T(8,128)(2,1)S(1)} %collective-permute-done.20.refs_1_, ...), custom_call_target="tpu_custom_call" | custom-call | flops 1000000 | bytes 1000000 | tf_op jit(solution)/shard_map/own_rows/pallas_call | solution.py:549
  66.6 1.1 %collective-permute-done.24.refs_1_ = bf16[8,3072]{1,0:T(8,128)(2,1)S(1)} collective-permute-done((bf16[8,3072]{1,0:T(8,128)(2,1)S(1)}, bf16[8,3072]{1,0:T(8,128)(2,1)S(1)}, u32[]{:S(2)}, u32[]{:S(2)}) %collective-permute-start.24) | collective-permute-done | bytes 49184 | tf_op jit(solution)/shard_map/ppermute | solution.py:587
  67.7 0.7 collective-permute-done.25.refs_2_
  68.4 0.0 collective-permute-done.26.refs_3_
  68.4 0.8 %finish.1 = bf16[8,6144]{1,0:T(8,128)(2,1)} custom-call(f32[8,6144]{1,0:T(8,128)S(1)} %get-tuple-element.80.combined_ref, bf16[32,32]{1,0:T(8,128)(2,1)S(1)} %get-tuple-element.81.weighting_ref, bf16[8,3072]{1,0:T(8,128)(2,1)S(1)} %get-tuple-element.83.refs_0_, bf16[8,3072]{1,0:T(8,128)(2,1)S(1)} %collective-permute-done.24.refs_1_, ...), custom_call_target="tpu_custom_call" | custom-call | tf_op jit(solution)/shard_map/finish/pallas_call | solution.py:576
  (11 shorter events, 0.1 us)
Async XLA Ops:
  3.8 11.9 %collective-permute-start.1 = (bf16[16,2944]{1,0:T(8,128)(2,1)S(1)}, bf16[16,2944]{1,0:T(8,128)(2,1)S(1)}, u32[]{:S(2)}, u32[]{:S(2)}) collective-permute-start(bf16[16,2944]{1,0:T(8,128)(2,1)S(1)} %get-tuple-element.48), channel_id=1, source_target_pairs={{0,12},{4,8},{8,4},{12,0},{1,13},{5,9},{9,5},{13,1},{2,14},{6,10},... | collective-permute-start | bytes 282632 | tf_op jit(solution)/shard_map/ppermute | solution.py:587
  8.9 7.9 %collective-permute-start.3 = (bf16[16,2944]{1,0:T(8,128)(2,1)S(1)}, bf16[16,2944]{1,0:T(8,128)(2,1)S(1)}, u32[]{:S(2)}, u32[]{:S(2)}) collective-permute-start(bf16[16,2944]{1,0:T(8,128)(2,1)S(1)} %get-tuple-element.49), channel_id=1, source_target_pairs={{0,8},{4,12},{8,0},{12,4},{1,9},{5,13},{9,1},{13,5},{2,10},{6,14},... | collective-permute-start | bytes 282632 | tf_op jit(solution)/shard_map/ppermute | solution.py:587
  8.9 7.9 %collective-permute-start.5 = (bf16[16,2944]{1,0:T(8,128)(2,1)S(1)}, bf16[16,2944]{1,0:T(8,128)(2,1)S(1)}, u32[]{:S(2)}, u32[]{:S(2)}) collective-permute-start(bf16[16,2944]{1,0:T(8,128)(2,1)S(1)} %get-tuple-element.50), channel_id=1, source_target_pairs={{0,4},{4,0},{8,12},{12,8},{1,5},{5,1},{9,13},{13,9},{2,6},{6,2},{1... | collective-permute-start | bytes 282632 | tf_op jit(solution)/shard_map/ppermute | solution.py:587
  15.6 1.7 %collective-permute-start = (bf16[16,2944]{1,0:T(8,128)(2,1)S(1)}, bf16[16,2944]{1,0:T(8,128)(2,1)S(1)}, u32[]{:S(2)}, u32[]{:S(2)}) collective-permute-start(bf16[16,2944]{1,0:T(8,128)(2,1)S(1)} %get-tuple-element.47.refs_0_), channel_id=1, source_target_pairs={{0,2},{2,0},{1,3},{3,1},{4,6},{6,4},{5,7},{7,5},{8,10},{10,8},{9,1... | collective-permute-start | bytes 282632 | tf_op jit(solution)/shard_map/ppermute | solution.py:587
  15.7 1.7 %collective-permute-start.2 = (bf16[16,2944]{1,0:T(8,128)(2,1)S(1)}, bf16[16,2944]{1,0:T(8,128)(2,1)S(1)}, u32[]{:S(2)}, u32[]{:S(2)}) collective-permute-start(bf16[16,2944]{1,0:T(8,128)(2,1)S(1)} %collective-permute-done.1.refs_2_), channel_id=1, source_target_pairs={{0,2},{2,0},{1,3},{3,1},{4,6},{6,4},{5,7},{7,5},{8,10},{10,8},{9,1... | collective-permute-start | bytes 282632 | tf_op jit(solution)/shard_map/ppermute | solution.py:587
  16.8 1.3 %collective-permute-start.4 = (bf16[16,2944]{1,0:T(8,128)(2,1)S(1)}, bf16[16,2944]{1,0:T(8,128)(2,1)S(1)}, u32[]{:S(2)}, u32[]{:S(2)}) collective-permute-start(bf16[16,2944]{1,0:T(8,128)(2,1)S(1)} %collective-permute-done.3.refs_4_), channel_id=1, source_target_pairs={{0,2},{2,0},{1,3},{3,1},{4,6},{6,4},{5,7},{7,5},{8,10},{10,8},{9,1... | collective-permute-start | bytes 282632 | tf_op jit(solution)/shard_map/ppermute | solution.py:587
  16.8 1.4 %collective-permute-start.6 = (bf16[16,2944]{1,0:T(8,128)(2,1)S(1)}, bf16[16,2944]{1,0:T(8,128)(2,1)S(1)}, u32[]{:S(2)}, u32[]{:S(2)}) collective-permute-start(bf16[16,2944]{1,0:T(8,128)(2,1)S(1)} %collective-permute-done.5.refs_6_), channel_id=1, source_target_pairs={{0,2},{2,0},{1,3},{3,1},{4,6},{6,4},{5,7},{7,5},{8,10},{10,8},{9,1... | collective-permute-start | bytes 282632 | tf_op jit(solution)/shard_map/ppermute | solution.py:587
  19.0 5.1 %collective-permute-start.7 = (bf16[64,768]{1,0:T(8,128)(2,1)S(1)}, bf16[64,768]{1,0:T(8,128)(2,1)S(1)}, u32[]{:S(2)}, u32[]{:S(2)}) collective-permute-start(bf16[64,768]{1,0:T(8,128)(2,1)S(1)} %get-tuple-element.53), channel_id=1, source_target_pairs={{0,1},{1,0},{2,3},{3,2},{4,5},{5,4},{6,7},{7,6},{8,9},{9,8},{10,11... | collective-permute-start | bytes 294920 | tf_op jit(solution)/shard_map/ppermute | solution.py:587
  24.3 4.2 %collective-permute-start.13 = (bf16[32,768]{1,0:T(8,128)(2,1)S(1)}, bf16[32,768]{1,0:T(8,128)(2,1)S(1)}, u32[]{:S(2)}, u32[]{:S(2)}) collective-permute-start(bf16[32,768]{1,0:T(8,128)(2,1)S(1)} %get-tuple-element.59.refs_0_), channel_id=1, source_target_pairs={{0,4},{4,0},{8,12},{12,8},{1,5},{5,1},{9,13},{13,9},{2,6},{6,2},{1... | collective-permute-start | bytes 147464 | tf_op jit(solution)/shard_map/ppermute | solution.py:587
  25.1 8.0 %collective-permute-start.10 = (bf16[32,768]{1,0:T(8,128)(2,1)S(1)}, bf16[32,768]{1,0:T(8,128)(2,1)S(1)}, u32[]{:S(2)}, u32[]{:S(2)}) collective-permute-start(bf16[32,768]{1,0:T(8,128)(2,1)S(1)} %relay.4), channel_id=1, source_target_pairs={{0,12},{4,8},{8,4},{12,0},{1,13},{5,9},{9,5},{13,1},{2,14},{6,10},... | collective-permute-start | bytes 147464 | tf_op jit(solution)/shard_map/ppermute | solution.py:587
  27.6 5.1 %collective-permute-start.9 = (bf16[32,768]{1,0:T(8,128)(2,1)S(1)}, bf16[32,768]{1,0:T(8,128)(2,1)S(1)}, u32[]{:S(2)}, u32[]{:S(2)}) collective-permute-start(bf16[32,768]{1,0:T(8,128)(2,1)S(1)} %relay.3), channel_id=1, source_target_pairs={{0,8},{4,12},{8,0},{12,4},{1,9},{5,13},{9,1},{13,5},{2,10},{6,14},... | collective-permute-start | bytes 147464 | tf_op jit(solution)/shard_map/ppermute | solution.py:587
  28.5 4.6 %collective-permute-start.15 = (bf16[64,768]{1,0:T(8,128)(2,1)S(1)}, bf16[64,768]{1,0:T(8,128)(2,1)S(1)}, u32[]{:S(2)}, u32[]{:S(2)}) collective-permute-start(bf16[64,768]{1,0:T(8,128)(2,1)S(1)} %constant_dynamic-update-slice_fusion.2.refs_0_), channel_id=1, source_target_pairs={{0,1},{1,0},{2,3},{3,2},{4,5},{5,4},{6,7},{7,6},{8,9},{9,8},{10,11... | collective-permute-start | bytes 294920 | tf_op jit(solution)/shard_map/ppermute | solution.py:587
  30.0 5.2 %collective-permute-start.14 = (bf16[64,768]{1,0:T(8,128)(2,1)S(1)}, bf16[64,768]{1,0:T(8,128)(2,1)S(1)}, u32[]{:S(2)}, u32[]{:S(2)}) collective-permute-start(bf16[64,768]{1,0:T(8,128)(2,1)S(1)} %constant_dynamic-update-slice_fusion.2.refs_0_), channel_id=1, source_target_pairs={{0,2},{2,0},{1,3},{3,1},{4,6},{6,4},{5,7},{7,5},{8,10},{10,8},{9,1... | collective-permute-start | bytes 294920 | tf_op jit(solution)/shard_map/ppermute | solution.py:587
  33.1 2.1 %collective-permute-start.16 = (bf16[64,768]{1,0:T(8,128)(2,1)S(1)}, bf16[64,768]{1,0:T(8,128)(2,1)S(1)}, u32[]{:S(2)}, u32[]{:S(2)}) collective-permute-start(bf16[64,768]{1,0:T(8,128)(2,1)S(1)} %collective-permute-done.15.refs_2_), channel_id=1, source_target_pairs={{0,2},{2,0},{1,3},{3,1},{4,6},{6,4},{5,7},{7,5},{8,10},{10,8},{9,1... | collective-permute-start | bytes 294920 | tf_op jit(solution)/shard_map/ppermute | solution.py:587
  33.1 8.0 %collective-permute-start.12 = (bf16[64,768]{1,0:T(8,128)(2,1)S(1)}, bf16[64,768]{1,0:T(8,128)(2,1)S(1)}, u32[]{:S(2)}, u32[]{:S(2)}) collective-permute-start(bf16[64,768]{1,0:T(8,128)(2,1)S(1)} %constant_dynamic-update-slice_fusion.refs_0_), channel_id=1, source_target_pairs={{0,1},{1,0},{2,3},{3,2},{4,5},{5,4},{6,7},{7,6},{8,9},{9,8},{10,11... | collective-permute-start | bytes 294920 | tf_op jit(solution)/shard_map/ppermute | solution.py:587
  34.6 6.4 %collective-permute-start.8 = (bf16[32,768]{1,0:T(8,128)(2,1)S(1)}, bf16[32,768]{1,0:T(8,128)(2,1)S(1)}, u32[]{:S(2)}, u32[]{:S(2)}) collective-permute-start(bf16[32,768]{1,0:T(8,128)(2,1)S(1)} %get-tuple-element.57), channel_id=1, source_target_pairs={{0,2},{2,0},{1,3},{3,1},{4,6},{6,4},{5,7},{7,5},{8,10},{10,8},{9,1... | collective-permute-start | bytes 147464 | tf_op jit(solution)/shard_map/ppermute | solution.py:587
  34.9 6.5 %collective-permute-start.11 = (bf16[64,768]{1,0:T(8,128)(2,1)S(1)}, bf16[64,768]{1,0:T(8,128)(2,1)S(1)}, u32[]{:S(2)}, u32[]{:S(2)}) collective-permute-start(bf16[64,768]{1,0:T(8,128)(2,1)S(1)} %constant_dynamic-update-slice_fusion.refs_0_), channel_id=1, source_target_pairs={{0,2},{2,0},{1,3},{3,1},{4,6},{6,4},{5,7},{7,5},{8,10},{10,8},{9,1... | collective-permute-start | bytes 294920 | tf_op jit(solution)/shard_map/ppermute | solution.py:587
  41.1 1.4 %collective-permute-start.17 = (bf16[64,768]{1,0:T(8,128)(2,1)S(1)}, bf16[64,768]{1,0:T(8,128)(2,1)S(1)}, u32[]{:S(2)}, u32[]{:S(2)}) collective-permute-start(bf16[64,768]{1,0:T(8,128)(2,1)S(1)} %relay.5.refs_2_), channel_id=1, source_target_pairs={{0,2},{2,0},{1,3},{3,1},{4,6},{6,4},{5,7},{7,5},{8,10},{10,8},{9,1... | collective-permute-start | bytes 294920 | tf_op jit(solution)/shard_map/ppermute | solution.py:587
  50.4 1.5 %collective-permute-start.19 = (bf16[32,3072]{1,0:T(8,128)(2,1)S(1)}, bf16[32,3072]{1,0:T(8,128)(2,1)S(1)}, u32[]{:S(2)}, u32[]{:S(2)}) collective-permute-start(bf16[32,3072]{1,0:T(8,128)(2,1)S(1)} %get-tuple-element.74), channel_id=1, source_target_pairs={{0,2},{2,0},{1,3},{3,1},{4,6},{6,4},{5,7},{7,5},{8,10},{10,8},{9,1... | collective-permute-start | bytes 589832 | tf_op jit(solution)/shard_map/ppermute | solution.py:587
  50.7 1.5 %collective-permute-start.18 = (bf16[32,3072]{1,0:T(8,128)(2,1)S(1)}, bf16[32,3072]{1,0:T(8,128)(2,1)S(1)}, u32[]{:S(2)}, u32[]{:S(2)}) collective-permute-start(bf16[32,3072]{1,0:T(8,128)(2,1)S(1)} %get-tuple-element.73), channel_id=1, source_target_pairs={{0,2},{2,0},{1,3},{3,1},{4,6},{6,4},{5,7},{7,5},{8,10},{10,8},{9,1... | collective-permute-start | bytes 589832 | tf_op jit(solution)/shard_map/ppermute | solution.py:587
  52.3 8.7 %collective-permute-start.23 = (bf16[16,6144]{1,0:T(8,128)(2,1)S(1)}, bf16[16,6144]{1,0:T(8,128)(2,1)S(1)}, u32[]{:S(2)}, u32[]{:S(2)}) collective-permute-start(bf16[16,6144]{1,0:T(8,128)(2,1)S(1)} %get-tuple-element.82), channel_id=1, source_target_pairs={{0,1},{1,0},{2,3},{3,2},{4,5},{5,4},{6,7},{7,6},{8,9},{9,8},{10,11... | collective-permute-start | bytes 589832 | tf_op jit(solution)/shard_map/ppermute | solution.py:587
  53.1 6.0 %collective-permute-start.20 = (bf16[16,768]{1,0:T(8,128)(2,1)S(1)}, bf16[16,768]{1,0:T(8,128)(2,1)S(1)}, u32[]{:S(2)}, u32[]{:S(2)}) collective-permute-start(bf16[16,768]{1,0:T(8,128)(2,1)S(1)} %get-tuple-element.77), channel_id=1, source_target_pairs={{0,12},{4,8},{8,4},{12,0},{1,13},{5,9},{9,5},{13,1},{2,14},{6,10},... | collective-permute-start | bytes 73736 | tf_op jit(solution)/shard_map/ppermute | solution.py:587
  56.2 4.7 %collective-permute-start.21 = (bf16[16,768]{1,0:T(8,128)(2,1)S(1)}, bf16[16,768]{1,0:T(8,128)(2,1)S(1)}, u32[]{:S(2)}, u32[]{:S(2)}) collective-permute-start(bf16[16,768]{1,0:T(8,128)(2,1)S(1)} %get-tuple-element.78), channel_id=1, source_target_pairs={{0,8},{4,12},{8,0},{12,4},{1,9},{5,13},{9,1},{13,5},{2,10},{6,14},... | collective-permute-start | bytes 73736 | tf_op jit(solution)/shard_map/ppermute | solution.py:587
  56.2 4.7 %collective-permute-start.22 = (bf16[16,768]{1,0:T(8,128)(2,1)S(1)}, bf16[16,768]{1,0:T(8,128)(2,1)S(1)}, u32[]{:S(2)}, u32[]{:S(2)}) collective-permute-start(bf16[16,768]{1,0:T(8,128)(2,1)S(1)} %get-tuple-element.79), channel_id=1, source_target_pairs={{0,4},{4,0},{8,12},{12,8},{1,5},{5,1},{9,13},{13,9},{2,6},{6,2},{1... | collective-permute-start | bytes 73736 | tf_op jit(solution)/shard_map/ppermute | solution.py:587
  61.1 6.7 %collective-permute-start.24 = (bf16[8,3072]{1,0:T(8,128)(2,1)S(1)}, bf16[8,3072]{1,0:T(8,128)(2,1)S(1)}, u32[]{:S(2)}, u32[]{:S(2)}) collective-permute-start(bf16[8,3072]{1,0:T(8,128)(2,1)S(1)} %get-tuple-element.84), channel_id=1, source_target_pairs={{0,12},{4,8},{8,4},{12,0},{1,13},{5,9},{9,5},{13,1},{2,14},{6,10},... | collective-permute-start | bytes 147464 | tf_op jit(solution)/shard_map/ppermute | solution.py:587
  62.7 5.7 %collective-permute-start.25 = (bf16[8,3072]{1,0:T(8,128)(2,1)S(1)}, bf16[8,3072]{1,0:T(8,128)(2,1)S(1)}, u32[]{:S(2)}, u32[]{:S(2)}) collective-permute-start(bf16[8,3072]{1,0:T(8,128)(2,1)S(1)} %get-tuple-element.85), channel_id=1, source_target_pairs={{0,8},{4,12},{8,0},{12,4},{1,9},{5,13},{9,1},{13,5},{2,10},{6,14},... | collective-permute-start | bytes 147464 | tf_op jit(solution)/shard_map/ppermute | solution.py:587
  63.2 5.2 %collective-permute-start.26 = (bf16[8,3072]{1,0:T(8,128)(2,1)S(1)}, bf16[8,3072]{1,0:T(8,128)(2,1)S(1)}, u32[]{:S(2)}, u32[]{:S(2)}) collective-permute-start(bf16[8,3072]{1,0:T(8,128)(2,1)S(1)} %get-tuple-element.86), channel_id=1, source_target_pairs={{0,4},{4,0},{8,12},{12,8},{1,5},{5,1},{9,13},{13,9},{2,6},{6,2},{1... | collective-permute-start | bytes 147464 | tf_op jit(solution)/shard_map/ppermute | solution.py:587

commit v10 on v9

--- a/solution.py
+++ b/solution.py
@@ -305,7 +305,7 @@
             block = (expert ^ (first + d)) * 2 + (half ^ c)
             at = pl.ds(pl.multiple_of(block * columns, columns), columns)
             to = pl.ds(pl.multiple_of(block % 4 * columns, columns), columns)
-            turned_ref[to] = (x * gain_ref[:, at]).T.astype(BF16)
+            turned_ref[to] = (x * gain_ref[:, at]).astype(BF16).T
     return squares
 
 
@@ -323,8 +323,7 @@
     rest.start()
     squares_ref[...] = turn(turned_ref, gain_ref, pieces, 0, count)
     columns = half_of(gate_ref, 0)
-    for at in (slice(0, cut), slice(cut, gate_ref.shape[0])):
-        gate_sum_ref[at] = dot(gate_ref[at, columns], turned_ref[...])
+    gate_sum_ref[...] = dot(gate_ref[:, columns], turned_ref[...])
     up_sum_ref[:cut] = dot(up_ref[:, columns], turned_ref[...])
     rest.wait()
     up_sum_ref[cut:] = dot(up_rest_ref[:, columns], turned_ref[...])
@@ -332,7 +331,8 @@
 
 def expert_second_kernel(count, *refs):
     pieces, gain_ref, gate_ref, up_ref, up_rest_ref = refs[:4], *refs[4:8]
-    gate_sum_ref, up_sum_ref, squares_ref, down_hbm, hidden_ref, down_ref, turned_ref, sem = refs[8:]
+    gate_sum_ref, up_sum_ref, squares_ref, down_hbm, hidden_ref, down_ref = refs[8:14]
+    turned_ref, gate_value_ref, sem = refs[14:]
     units, width = gate_ref.shape
     cut = up_ref.shape[0]
     down = pltpu.make_async_copy(down_hbm, down_ref, sem)
@@ -341,8 +341,9 @@
     spread = jnp.sum(squares.T, axis=0, keepdims=True) / width
     scale = lax.rsqrt(spread + EPSILON)
     columns = half_of(gate_ref, 2)
+    gate_value_ref[...] = (gate_sum_ref[...] + dot(gate_ref[:, columns], turned_ref[...])) * scale
     for at, weight_ref in ((slice(0, cut), up_ref), (slice(cut, units), up_rest_ref)):
-        gate_value = (gate_sum_ref[at] + dot(gate_ref[at, columns], turned_ref[...])) * scale
+        gate_value = gate_value_ref[at]
         lifted = (up_sum_ref[at] + dot(weight_ref[:, columns], turned_ref[...])) * scale
         hidden = gate_value / (1.0 + jnp.exp(-gate_value)) * lifted
         hidden_ref[:, at] = hidden.T.astype(BF16)
@@ -416,7 +417,11 @@
             jax.ShapeDtypeStruct((2 * count, units), BF16),
             pltpu.VMEM((units, width), BF16),
         ],
-        scratch_shapes=[pltpu.VMEM((width // 2, 2 * count), BF16), pltpu.SemaphoreType.DMA],
+        scratch_shapes=[
+            pltpu.VMEM((width // 2, 2 * count), BF16),
+            pltpu.VMEM((units, 2 * count), F32),
+            pltpu.SemaphoreType.DMA,
+        ],
         compiler_params=limits(8),
         cost_estimate=cost(4 * units * width * count, 2 * units * width),
         name="experts_second",

time: 69.4 us -> 69.5 us (level)
  no operation moved by 1% of the time
where the time goes in v10:
time: 69.5 us; the launch traced here: 69.3 us
  Pallas kernels  30 us (43%)
  starting transfers between devices  26.4 us (38%)
  waiting for transfers between devices  12.7 us (18%)
    ppermute x27, starting transfers between devices, swap(): lax.ppermute(x, axis, [(i, i ^ by) for i in range(lax.axis_size(axis))])  26.4 us
    ppermute x27, waiting for transfers between devices, swap(): lax.ppermute(x, axis, [(i, i ^ by) for i in range(lax.axis_size(axis))])  12.7 us
    pallas_call x1, Pallas kernels, load(): pl.pallas_call(functools.partial(load_kernel, len(weights)), in_specs=[AN...  6.03 us
    pallas_call x1, Pallas kernels, expert_first(): pl.pallas_call(functools.partial(expert_first_kernel, count), in_specs=[V...  5.92 us
    pallas_call x1, Pallas kernels, expert_second(): pl.pallas_call(functools.partial(expert_second_kernel, count), in_specs=[...  5.23 us
    pallas_call x1, Pallas kernels, attend(): pl.pallas_call(functools.partial(attend_kernel, rows // requests, heads /...  3.76 us
    pallas_call x1, Pallas kernels, route(): pl.pallas_call(functools.partial(route_kernel, capacity, top), in_specs=[...  3.28 us
    pallas_call x2, Pallas kernels, expert_down(): pl.pallas_call(functools.partial(down_kernel, start, 512), in_specs=[VMEM...  2.71 us
  transfers between devices with their start and end apart: 27, of which 14 were waited for; matrix products, arithmetic and copies ran while one was open for 0% of the time, Pallas kernels for 24%

profile of v10, /device:TPU:0, one launch (start us, length us, event | category | flops | bytes accessed | tf_op | source)
XLA Modules:
  0.0 69.3 jit_solution(6720299789608954418)
XLA Ops:
  0.0 3.8 %attention.1 = (bf16[16,2944]{1,0:T(8,128)(2,1)S(1)}, bf16[16,2944]{1,0:T(8,128)(2,1)S(1)}, bf16[16,2944]{1,0:T(8,128)(2,1)S(1)}, bf16[16,2944]{1,0:T(8,128)(2,1)S(1)}) custom-call(f32[16]{0:T(128)} %decay_ref.1, s32[2,8]{1,0:T(2,128)} %bitcast.6, bf16[16,2048]{1,0:T(8,128)(2,1)} %q_ref.1, bf16[16,2048]{1,0:T(8,128)(2,1)} %k_ref.1, bf16[16,2048]{1,0:T(8,128)(2,1)} %v_ref.1, ...), custom_call_target="tpu_custom_call" | custom-call | tf_op jit(solution)/shard_map/attention/pallas_call | solution.py:111
  3.8 5.1 %collective-permute-start.1 = (bf16[16,2944]{1,0:T(8,128)(2,1)S(1)}, bf16[16,2944]{1,0:T(8,128)(2,1)S(1)}, u32[]{:S(2)}, u32[]{:S(2)}) collective-permute-start(bf16[16,2944]{1,0:T(8,128)(2,1)S(1)} %get-tuple-element.48), channel_id=1, source_target_pairs={{0,12},{4,8},{8,4},{12,0},{1,13},{5,9},{9,5},{13,1},{2,14},{6,10},... | collective-permute-start | bytes 282632 | tf_op jit(solution)/shard_map/ppermute | solution.py:592
  8.9 0.0 collective-permute-start.3
  8.9 0.6 collective-permute-start.5
  9.5 6.0 %load.1 = (bf16[16,2944]{1,0:T(8,128)(2,1)S(1)}, bf16[2048,768]{1,0:T(8,128)(2,1)S(1)}, f32[1,6144]{1,0:T(1,128)S(1)}, bf16[1152,6144]{1,0:T(8,128)(2,1)S(1)}) custom-call(bf16[16,2944]{1,0:T(8,128)(2,1)S(1)} %get-tuple-element.46.rows_hbm, bf16[2048,768]{1,0:T(8,128)(2,1)} %refs_0_.1, f32[1,6144]{1,0:T(1,128)} %bitcast.4, bf16[1152,6144]{1,0:T(8,128)(2,1)} %refs_2_.1), custom_call_target="tpu_custom_call" | custom-call | bytes 17326080 | tf_op jit(solution)/shard_map/load/pallas_call | solution.py:150
  15.6 0.1 collective-permute-start
  15.6 0.0 collective-permute-done.1.refs_2_
  15.7 0.5 collective-permute-start.2
  16.1 0.6 collective-permute-done.3.refs_4_
  16.8 0.0 collective-permute-start.4
  16.8 0.0 collective-permute-done.5.refs_6_
  16.8 0.5 collective-permute-start.6
  17.3 0.0 collective-permute-done.refs_1_
  17.3 0.0 collective-permute-done.2.refs_3_
  17.3 0.8 %collective-permute-done.4.refs_5_ = bf16[16,2944]{1,0:T(8,128)(2,1)S(1)} collective-permute-done((bf16[16,2944]{1,0:T(8,128)(2,1)S(1)}, bf16[16,2944]{1,0:T(8,128)(2,1)S(1)}, u32[]{:S(2)}, u32[]{:S(2)}) %collective-permute-start.4) | collective-permute-done | bytes 94240 | tf_op jit(solution)/shard_map/ppermute | solution.py:592
  18.1 0.2 collective-permute-done.6.refs_7_
  18.3 0.7 %projection.1 = (f32[64,768]{1,0:T(8,128)S(1)}, bf16[64,768]{1,0:T(8,128)(2,1)S(1)}) custom-call(bf16[16,2944]{1,0:T(8,128)(2,1)S(1)} %get-tuple-element.47.refs_0_, bf16[16,2944]{1,0:T(8,128)(2,1)S(1)} %collective-permute-done.refs_1_, bf16[16,2944]{1,0:T(8,128)(2,1)S(1)} %collective-permute-done.1.refs_2_, ...), custom_call_target="tpu_custom_call" | custom-call | tf_op jit(solution)/shard_map/projection/pallas_call | solution.py:187
  19.0 1.6 %collective-permute-start.7 = (bf16[64,768]{1,0:T(8,128)(2,1)S(1)}, bf16[64,768]{1,0:T(8,128)(2,1)S(1)}, u32[]{:S(2)}, u32[]{:S(2)}) collective-permute-start(bf16[64,768]{1,0:T(8,128)(2,1)S(1)} %get-tuple-element.53), channel_id=1, source_target_pairs={{0,1},{1,0},{2,3},{3,2},{4,5},{5,4},{6,7},{7,6},{8,9},{9,8},{10,11... | collective-permute-start | bytes 294920 | tf_op jit(solution)/shard_map/ppermute | solution.py:592
  20.5 3.3 %route.1 = (bf16[128,64]{1,0:T(8,128)(2,1)S(1)}, f32[64,768]{1,0:T(8,128)S(1)}, bf16[640,6144]{1,0:T(8,128)(2,1)S(1)}) custom-call(bf16[16,2944]{1,0:T(8,128)(2,1)S(1)} %get-tuple-element.47.refs_0_, bf16[16,2944]{1,0:T(8,128)(2,1)S(1)} %collective-permute-done.refs_1_, bf16[16,2944]{1,0:T(8,128)(2,1)S(1)} %collective-permute-done.1.refs_2_, ...), custom_call_target="tpu_custom_call" | custom-call | flops 1000000 | bytes 8000000 | tf_op jit(solution)/shard_map/route/pallas_call | solution.py:243
  23.8 0.3 collective-permute-done.7.got_ref
  24.1 0.2 pack.1
  24.3 0.8 %collective-permute-start.13 = (bf16[32,768]{1,0:T(8,128)(2,1)S(1)}, bf16[32,768]{1,0:T(8,128)(2,1)S(1)}, u32[]{:S(2)}, u32[]{:S(2)}) collective-permute-start(bf16[32,768]{1,0:T(8,128)(2,1)S(1)} %get-tuple-element.59.refs_0_), channel_id=1, source_target_pairs={{0,4},{4,0},{8,12},{12,8},{1,5},{5,1},{9,13},{13,9},{2,6},{6,2},{1... | collective-permute-start | bytes 147464 | tf_op jit(solution)/shard_map/ppermute | solution.py:592
  25.1 2.4 %collective-permute-start.10 = (bf16[32,768]{1,0:T(8,128)(2,1)S(1)}, bf16[32,768]{1,0:T(8,128)(2,1)S(1)}, u32[]{:S(2)}, u32[]{:S(2)}) collective-permute-start(bf16[32,768]{1,0:T(8,128)(2,1)S(1)} %relay.4), channel_id=1, source_target_pairs={{0,12},{4,8},{8,4},{12,0},{1,13},{5,9},{9,5},{13,1},{2,14},{6,10},... | collective-permute-start | bytes 147464 | tf_op jit(solution)/shard_map/ppermute | solution.py:592
  27.6 0.6 collective-permute-start.9
  28.2 0.3 collective-permute-done.13
  28.5 1.5 %collective-permute-start.15 = (bf16[64,768]{1,0:T(8,128)(2,1)S(1)}, bf16[64,768]{1,0:T(8,128)(2,1)S(1)}, u32[]{:S(2)}, u32[]{:S(2)}) collective-permute-start(bf16[64,768]{1,0:T(8,128)(2,1)S(1)} %constant_dynamic-update-slice_fusion.2.refs_0_), channel_id=1, source_target_pairs={{0,1},{1,0},{2,3},{3,2},{4,5},{5,4},{6,7},{7,6},{8,9},{9,8},{10,11... | collective-permute-start | bytes 294920 | tf_op jit(solution)/shard_map/ppermute | solution.py:592
  30.0 0.0 collective-permute-start.14
  30.0 2.7 %collective-permute-done.9 = bf16[32,768]{1,0:T(8,128)(2,1)S(1)} collective-permute-done((bf16[32,768]{1,0:T(8,128)(2,1)S(1)}, bf16[32,768]{1,0:T(8,128)(2,1)S(1)}, u32[]{:S(2)}, u32[]{:S(2)}) %collective-permute-start.9) | collective-permute-done | bytes 49184 | tf_op jit(solution)/shard_map/ppermute | solution.py:592
  32.7 0.4 collective-permute-done.15.refs_2_
  33.1 0.0 collective-permute-start.16
  33.1 1.6 %collective-permute-start.12 = (bf16[64,768]{1,0:T(8,128)(2,1)S(1)}, bf16[64,768]{1,0:T(8,128)(2,1)S(1)}, u32[]{:S(2)}, u32[]{:S(2)}) collective-permute-start(bf16[64,768]{1,0:T(8,128)(2,1)S(1)} %constant_dynamic-update-slice_fusion.refs_0_), channel_id=1, source_target_pairs={{0,1},{1,0},{2,3},{3,2},{4,5},{5,4},{6,7},{7,6},{8,9},{9,8},{10,11... | collective-permute-start | bytes 294920 | tf_op jit(solution)/shard_map/ppermute | solution.py:592
  34.6 0.2 collective-permute-start.8
  34.9 0.3 collective-permute-start.11
  35.2 0.0 collective-permute-done.14.refs_1_
  35.2 0.0 collective-permute-done.16.refs_3_
  35.2 5.9 %experts_first.1 = (f32[1152,64]{1,0:T(8,128)S(1)}, f32[1152,64]{1,0:T(8,128)S(1)}, f32[64,128]{1,0:T(8,128)S(1)}, bf16[512,6144]{1,0:T(8,128)(2,1)S(1)}) custom-call(bf16[64,768]{1,0:T(8,128)(2,1)S(1)} %constant_dynamic-update-slice_fusion.2.refs_0_, bf16[64,768]{1,0:T(8,128)(2,1)S(1)} %collective-permute-done.14.refs_1_, ...), custom_call_target="tpu_custom_call" | custom-call | flops 905969664 | bytes 14155776 | tf_op jit(solution)/shard_map/experts_first/pallas_call | solution.py:377
  41.1 0.0 collective-permute-done.8.refs_1_.cross_ref
  41.1 0.3 collective-permute-start.17
  41.4 0.0 collective-permute-done.11.refs_1_
  41.4 1.1 %collective-permute-done.17.refs_3_ = bf16[64,768]{1,0:T(8,128)(2,1)S(1)} collective-permute-done((bf16[64,768]{1,0:T(8,128)(2,1)S(1)}, bf16[64,768]{1,0:T(8,128)(2,1)S(1)}, u32[]{:S(2)}, u32[]{:S(2)}) %collective-permute-start.17) | collective-permute-done | bytes 98336 | tf_op jit(solution)/shard_map/ppermute | solution.py:592
  42.5 5.2 %experts_second.1 = (bf16[64,1152]{1,0:T(8,128)(2,1)S(1)}, bf16[1152,6144]{1,0:T(8,128)(2,1)S(1)}) custom-call(bf16[64,768]{1,0:T(8,128)(2,1)S(1)} %constant_dynamic-update-slice_fusion.refs_0_, bf16[64,768]{1,0:T(8,128)(2,1)S(1)} %collective-permute-done.11.refs_1_, bf16[64,768]{1,0:T(8,128)(2,1)S(1)} %relay.5.refs_2_, ...), custom_call_target="tpu_custom_call" | custom-call | flops 905969664 | bytes 14155776 | tf_op jit(solution)/shard_map/experts_second/pallas_call | solution.py:412
  47.7 1.4 %experts_down.3 = (f32[32,3072]{1,0:T(8,128)S(1)}, bf16[32,3072]{1,0:T(8,128)(2,1)S(1)}) custom-call(bf16[64,1152]{1,0:T(8,128)(2,1)S(1)} %get-tuple-element.69.hidden_ref, bf16[1152,6144]{1,0:T(8,128)(2,1)S(1)} %get-tuple-element.70.weight_ref), custom_call_target="tpu_custom_call" | custom-call | flops 905969664 | bytes 7077888 | tf_op jit(solution)/shard_map/experts_down/pallas_call | solution.py:432
  49.1 1.4 %experts_down.2 = (f32[32,3072]{1,0:T(8,128)S(1)}, bf16[32,3072]{1,0:T(8,128)(2,1)S(1)}) custom-call(bf16[64,1152]{1,0:T(8,128)(2,1)S(1)} %get-tuple-element.69.hidden_ref, bf16[1152,6144]{1,0:T(8,128)(2,1)S(1)} %get-tuple-element.70.weight_ref), custom_call_target="tpu_custom_call" | custom-call | flops 905969664 | bytes 7077888 | tf_op jit(solution)/shard_map/experts_down/pallas_call | solution.py:432
  50.5 0.3 collective-permute-start.19
  50.7 0.3 collective-permute-start.18
  51.0 0.9 %collective-permute-done.19.refs_3_ = bf16[32,3072]{1,0:T(8,128)(2,1)S(1)} collective-permute-done((bf16[32,3072]{1,0:T(8,128)(2,1)S(1)}, bf16[32,3072]{1,0:T(8,128)(2,1)S(1)}, u32[]{:S(2)}, u32[]{:S(2)}) %collective-permute-start.19) | collective-permute-done | bytes 196640 | tf_op jit(solution)/shard_map/ppermute | solution.py:592
  52.0 0.3 collective-permute-done.18.refs_2_
  52.3 0.1 chip_sum.1
  52.3 0.8 %collective-permute-start.23 = (bf16[16,6144]{1,0:T(8,128)(2,1)S(1)}, bf16[16,6144]{1,0:T(8,128)(2,1)S(1)}, u32[]{:S(2)}, u32[]{:S(2)}) collective-permute-start(bf16[16,6144]{1,0:T(8,128)(2,1)S(1)} %get-tuple-element.82), channel_id=1, source_target_pairs={{0,1},{1,0},{2,3},{3,2},{4,5},{5,4},{6,7},{7,6},{8,9},{9,8},{10,11... | collective-permute-start | bytes 589832 | tf_op jit(solution)/shard_map/ppermute | solution.py:592
  53.1 3.1 %collective-permute-start.20 = (bf16[16,768]{1,0:T(8,128)(2,1)S(1)}, bf16[16,768]{1,0:T(8,128)(2,1)S(1)}, u32[]{:S(2)}, u32[]{:S(2)}) collective-permute-start(bf16[16,768]{1,0:T(8,128)(2,1)S(1)} %get-tuple-element.77), channel_id=1, source_target_pairs={{0,12},{4,8},{8,4},{12,0},{1,13},{5,9},{9,5},{13,1},{2,14},{6,10},... | collective-permute-start | bytes 73736 | tf_op jit(solution)/shard_map/ppermute | solution.py:592
  56.3 1.3 %collective-permute-start.22 = (bf16[16,768]{1,0:T(8,128)(2,1)S(1)}, bf16[16,768]{1,0:T(8,128)(2,1)S(1)}, u32[]{:S(2)}, u32[]{:S(2)}) collective-permute-start(bf16[16,768]{1,0:T(8,128)(2,1)S(1)} %get-tuple-element.79), channel_id=1, source_target_pairs={{0,4},{4,0},{8,12},{12,8},{1,5},{5,1},{9,13},{13,9},{2,6},{6,2},{1... | collective-permute-start | bytes 73736 | tf_op jit(solution)/shard_map/ppermute | solution.py:592
  57.6 1.5 %collective-permute-done.20.refs_1_ = bf16[16,768]{1,0:T(8,128)(2,1)S(1)} collective-permute-done((bf16[16,768]{1,0:T(8,128)(2,1)S(1)}, bf16[16,768]{1,0:T(8,128)(2,1)S(1)}, u32[]{:S(2)}, u32[]{:S(2)}) %collective-permute-start.20) | collective-permute-done | bytes 24608 | tf_op jit(solution)/shard_map/ppermute | solution.py:592
  59.1 1.9 %collective-permute-done.21.refs_2_ = bf16[16,768]{1,0:T(8,128)(2,1)S(1)} collective-permute-done((bf16[16,768]{1,0:T(8,128)(2,1)S(1)}, bf16[16,768]{1,0:T(8,128)(2,1)S(1)}, u32[]{:S(2)}, u32[]{:S(2)}) %collective-permute-start.21) | collective-permute-done | bytes 24608 | tf_op jit(solution)/shard_map/ppermute | solution.py:592
  61.0 0.0 collective-permute-done.22.refs_3_
  61.0 0.0 collective-permute-done.23.got_ref
  61.0 0.1 pair_sum.1
  61.1 1.6 %collective-permute-start.24 = (bf16[8,3072]{1,0:T(8,128)(2,1)S(1)}, bf16[8,3072]{1,0:T(8,128)(2,1)S(1)}, u32[]{:S(2)}, u32[]{:S(2)}) collective-permute-start(bf16[8,3072]{1,0:T(8,128)(2,1)S(1)} %get-tuple-element.84), channel_id=1, source_target_pairs={{0,12},{4,8},{8,4},{12,0},{1,13},{5,9},{9,5},{13,1},{2,14},{6,10},... | collective-permute-start | bytes 147464 | tf_op jit(solution)/shard_map/ppermute | solution.py:592
  62.7 0.6 collective-permute-start.25
  63.3 2.3 %collective-permute-start.26 = (bf16[8,3072]{1,0:T(8,128)(2,1)S(1)}, bf16[8,3072]{1,0:T(8,128)(2,1)S(1)}, u32[]{:S(2)}, u32[]{:S(2)}) collective-permute-start(bf16[8,3072]{1,0:T(8,128)(2,1)S(1)} %get-tuple-element.86), channel_id=1, source_target_pairs={{0,4},{4,0},{8,12},{12,8},{1,5},{5,1},{9,13},{13,9},{2,6},{6,2},{1... | collective-permute-start | bytes 147464 | tf_op jit(solution)/shard_map/ppermute | solution.py:592
  65.6 1.1 %own_rows.1 = (f32[8,6144]{1,0:T(8,128)S(1)}, bf16[32,32]{1,0:T(8,128)(2,1)S(1)}) custom-call(s32[2,8]{1,0:T(2,128)} %bitcast.7, f32[2,8]{1,0:T(2,128)} %bitcast.8, bf16[8,6144]{1,0:T(8,128)(2,1)} %residual_ref.3, bf16[16,768]{1,0:T(8,128)(2,1)S(1)} %get-tuple-element.76.refs_0_, bf16[16,768]{1,0:T(8,128)(2,1)S(1)} %collective-permute-done.20.refs_1_, ...), custom_call_target="tpu_custom_call" | custom-call | flops 1000000 | bytes 1000000 | tf_op jit(solution)/shard_map/own_rows/pallas_call | solution.py:554
  66.7 1.1 %collective-permute-done.24.refs_1_ = bf16[8,3072]{1,0:T(8,128)(2,1)S(1)} collective-permute-done((bf16[8,3072]{1,0:T(8,128)(2,1)S(1)}, bf16[8,3072]{1,0:T(8,128)(2,1)S(1)}, u32[]{:S(2)}, u32[]{:S(2)}) %collective-permute-start.24) | collective-permute-done | bytes 49184 | tf_op jit(solution)/shard_map/ppermute | solution.py:592
  67.8 0.7 collective-permute-done.25.refs_2_
  68.4 0.0 collective-permute-done.26.refs_3_
  68.4 0.8 %finish.1 = bf16[8,6144]{1,0:T(8,128)(2,1)} custom-call(f32[8,6144]{1,0:T(8,128)S(1)} %get-tuple-element.80.combined_ref, bf16[32,32]{1,0:T(8,128)(2,1)S(1)} %get-tuple-element.81.weighting_ref, bf16[8,3072]{1,0:T(8,128)(2,1)S(1)} %get-tuple-element.83.refs_0_, bf16[8,3072]{1,0:T(8,128)(2,1)S(1)} %collective-permute-done.24.refs_1_, ...), custom_call_target="tpu_custom_call" | custom-call | tf_op jit(solution)/shard_map/finish/pallas_call | solution.py:581
  (11 shorter events, 0.1 us)
Async XLA Ops:
  3.8 11.9 %collective-permute-start.1 = (bf16[16,2944]{1,0:T(8,128)(2,1)S(1)}, bf16[16,2944]{1,0:T(8,128)(2,1)S(1)}, u32[]{:S(2)}, u32[]{:S(2)}) collective-permute-start(bf16[16,2944]{1,0:T(8,128)(2,1)S(1)} %get-tuple-element.48), channel_id=1, source_target_pairs={{0,12},{4,8},{8,4},{12,0},{1,13},{5,9},{9,5},{13,1},{2,14},{6,10},... | collective-permute-start | bytes 282632 | tf_op jit(solution)/shard_map/ppermute | solution.py:592
  8.9 7.9 %collective-permute-start.3 = (bf16[16,2944]{1,0:T(8,128)(2,1)S(1)}, bf16[16,2944]{1,0:T(8,128)(2,1)S(1)}, u32[]{:S(2)}, u32[]{:S(2)}) collective-permute-start(bf16[16,2944]{1,0:T(8,128)(2,1)S(1)} %get-tuple-element.49), channel_id=1, source_target_pairs={{0,8},{4,12},{8,0},{12,4},{1,9},{5,13},{9,1},{13,5},{2,10},{6,14},... | collective-permute-start | bytes 282632 | tf_op jit(solution)/shard_map/ppermute | solution.py:592
  8.9 7.9 %collective-permute-start.5 = (bf16[16,2944]{1,0:T(8,128)(2,1)S(1)}, bf16[16,2944]{1,0:T(8,128)(2,1)S(1)}, u32[]{:S(2)}, u32[]{:S(2)}) collective-permute-start(bf16[16,2944]{1,0:T(8,128)(2,1)S(1)} %get-tuple-element.50), channel_id=1, source_target_pairs={{0,4},{4,0},{8,12},{12,8},{1,5},{5,1},{9,13},{13,9},{2,6},{6,2},{1... | collective-permute-start | bytes 282632 | tf_op jit(solution)/shard_map/ppermute | solution.py:592
  15.6 1.7 %collective-permute-start = (bf16[16,2944]{1,0:T(8,128)(2,1)S(1)}, bf16[16,2944]{1,0:T(8,128)(2,1)S(1)}, u32[]{:S(2)}, u32[]{:S(2)}) collective-permute-start(bf16[16,2944]{1,0:T(8,128)(2,1)S(1)} %get-tuple-element.47.refs_0_), channel_id=1, source_target_pairs={{0,2},{2,0},{1,3},{3,1},{4,6},{6,4},{5,7},{7,5},{8,10},{10,8},{9,1... | collective-permute-start | bytes 282632 | tf_op jit(solution)/shard_map/ppermute | solution.py:592
  15.7 1.7 %collective-permute-start.2 = (bf16[16,2944]{1,0:T(8,128)(2,1)S(1)}, bf16[16,2944]{1,0:T(8,128)(2,1)S(1)}, u32[]{:S(2)}, u32[]{:S(2)}) collective-permute-start(bf16[16,2944]{1,0:T(8,128)(2,1)S(1)} %collective-permute-done.1.refs_2_), channel_id=1, source_target_pairs={{0,2},{2,0},{1,3},{3,1},{4,6},{6,4},{5,7},{7,5},{8,10},{10,8},{9,1... | collective-permute-start | bytes 282632 | tf_op jit(solution)/shard_map/ppermute | solution.py:592
  16.8 1.3 %collective-permute-start.4 = (bf16[16,2944]{1,0:T(8,128)(2,1)S(1)}, bf16[16,2944]{1,0:T(8,128)(2,1)S(1)}, u32[]{:S(2)}, u32[]{:S(2)}) collective-permute-start(bf16[16,2944]{1,0:T(8,128)(2,1)S(1)} %collective-permute-done.3.refs_4_), channel_id=1, source_target_pairs={{0,2},{2,0},{1,3},{3,1},{4,6},{6,4},{5,7},{7,5},{8,10},{10,8},{9,1... | collective-permute-start | bytes 282632 | tf_op jit(solution)/shard_map/ppermute | solution.py:592
  16.8 1.4 %collective-permute-start.6 = (bf16[16,2944]{1,0:T(8,128)(2,1)S(1)}, bf16[16,2944]{1,0:T(8,128)(2,1)S(1)}, u32[]{:S(2)}, u32[]{:S(2)}) collective-permute-start(bf16[16,2944]{1,0:T(8,128)(2,1)S(1)} %collective-permute-done.5.refs_6_), channel_id=1, source_target_pairs={{0,2},{2,0},{1,3},{3,1},{4,6},{6,4},{5,7},{7,5},{8,10},{10,8},{9,1... | collective-permute-start | bytes 282632 | tf_op jit(solution)/shard_map/ppermute | solution.py:592
  19.0 5.1 %collective-permute-start.7 = (bf16[64,768]{1,0:T(8,128)(2,1)S(1)}, bf16[64,768]{1,0:T(8,128)(2,1)S(1)}, u32[]{:S(2)}, u32[]{:S(2)}) collective-permute-start(bf16[64,768]{1,0:T(8,128)(2,1)S(1)} %get-tuple-element.53), channel_id=1, source_target_pairs={{0,1},{1,0},{2,3},{3,2},{4,5},{5,4},{6,7},{7,6},{8,9},{9,8},{10,11... | collective-permute-start | bytes 294920 | tf_op jit(solution)/shard_map/ppermute | solution.py:592
  24.3 4.2 %collective-permute-start.13 = (bf16[32,768]{1,0:T(8,128)(2,1)S(1)}, bf16[32,768]{1,0:T(8,128)(2,1)S(1)}, u32[]{:S(2)}, u32[]{:S(2)}) collective-permute-start(bf16[32,768]{1,0:T(8,128)(2,1)S(1)} %get-tuple-element.59.refs_0_), channel_id=1, source_target_pairs={{0,4},{4,0},{8,12},{12,8},{1,5},{5,1},{9,13},{13,9},{2,6},{6,2},{1... | collective-permute-start | bytes 147464 | tf_op jit(solution)/shard_map/ppermute | solution.py:592
  25.1 8.0 %collective-permute-start.10 = (bf16[32,768]{1,0:T(8,128)(2,1)S(1)}, bf16[32,768]{1,0:T(8,128)(2,1)S(1)}, u32[]{:S(2)}, u32[]{:S(2)}) collective-permute-start(bf16[32,768]{1,0:T(8,128)(2,1)S(1)} %relay.4), channel_id=1, source_target_pairs={{0,12},{4,8},{8,4},{12,0},{1,13},{5,9},{9,5},{13,1},{2,14},{6,10},... | collective-permute-start | bytes 147464 | tf_op jit(solution)/shard_map/ppermute | solution.py:592
  27.6 5.1 %collective-permute-start.9 = (bf16[32,768]{1,0:T(8,128)(2,1)S(1)}, bf16[32,768]{1,0:T(8,128)(2,1)S(1)}, u32[]{:S(2)}, u32[]{:S(2)}) collective-permute-start(bf16[32,768]{1,0:T(8,128)(2,1)S(1)} %relay.3), channel_id=1, source_target_pairs={{0,8},{4,12},{8,0},{12,4},{1,9},{5,13},{9,1},{13,5},{2,10},{6,14},... | collective-permute-start | bytes 147464 | tf_op jit(solution)/shard_map/ppermute | solution.py:592
  28.5 4.6 %collective-permute-start.15 = (bf16[64,768]{1,0:T(8,128)(2,1)S(1)}, bf16[64,768]{1,0:T(8,128)(2,1)S(1)}, u32[]{:S(2)}, u32[]{:S(2)}) collective-permute-start(bf16[64,768]{1,0:T(8,128)(2,1)S(1)} %constant_dynamic-update-slice_fusion.2.refs_0_), channel_id=1, source_target_pairs={{0,1},{1,0},{2,3},{3,2},{4,5},{5,4},{6,7},{7,6},{8,9},{9,8},{10,11... | collective-permute-start | bytes 294920 | tf_op jit(solution)/shard_map/ppermute | solution.py:592
  30.0 5.2 %collective-permute-start.14 = (bf16[64,768]{1,0:T(8,128)(2,1)S(1)}, bf16[64,768]{1,0:T(8,128)(2,1)S(1)}, u32[]{:S(2)}, u32[]{:S(2)}) collective-permute-start(bf16[64,768]{1,0:T(8,128)(2,1)S(1)} %constant_dynamic-update-slice_fusion.2.refs_0_), channel_id=1, source_target_pairs={{0,2},{2,0},{1,3},{3,1},{4,6},{6,4},{5,7},{7,5},{8,10},{10,8},{9,1... | collective-permute-start | bytes 294920 | tf_op jit(solution)/shard_map/ppermute | solution.py:592
  33.1 2.1 %collective-permute-start.16 = (bf16[64,768]{1,0:T(8,128)(2,1)S(1)}, bf16[64,768]{1,0:T(8,128)(2,1)S(1)}, u32[]{:S(2)}, u32[]{:S(2)}) collective-permute-start(bf16[64,768]{1,0:T(8,128)(2,1)S(1)} %collective-permute-done.15.refs_2_), channel_id=1, source_target_pairs={{0,2},{2,0},{1,3},{3,1},{4,6},{6,4},{5,7},{7,5},{8,10},{10,8},{9,1... | collective-permute-start | bytes 294920 | tf_op jit(solution)/shard_map/ppermute | solution.py:592
  33.1 8.0 %collective-permute-start.12 = (bf16[64,768]{1,0:T(8,128)(2,1)S(1)}, bf16[64,768]{1,0:T(8,128)(2,1)S(1)}, u32[]{:S(2)}, u32[]{:S(2)}) collective-permute-start(bf16[64,768]{1,0:T(8,128)(2,1)S(1)} %constant_dynamic-update-slice_fusion.refs_0_), channel_id=1, source_target_pairs={{0,1},{1,0},{2,3},{3,2},{4,5},{5,4},{6,7},{7,6},{8,9},{9,8},{10,11... | collective-permute-start | bytes 294920 | tf_op jit(solution)/shard_map/ppermute | solution.py:592
  34.6 6.4 %collective-permute-start.8 = (bf16[32,768]{1,0:T(8,128)(2,1)S(1)}, bf16[32,768]{1,0:T(8,128)(2,1)S(1)}, u32[]{:S(2)}, u32[]{:S(2)}) collective-permute-start(bf16[32,768]{1,0:T(8,128)(2,1)S(1)} %get-tuple-element.57), channel_id=1, source_target_pairs={{0,2},{2,0},{1,3},{3,1},{4,6},{6,4},{5,7},{7,5},{8,10},{10,8},{9,1... | collective-permute-start | bytes 147464 | tf_op jit(solution)/shard_map/ppermute | solution.py:592
  34.9 6.5 %collective-permute-start.11 = (bf16[64,768]{1,0:T(8,128)(2,1)S(1)}, bf16[64,768]{1,0:T(8,128)(2,1)S(1)}, u32[]{:S(2)}, u32[]{:S(2)}) collective-permute-start(bf16[64,768]{1,0:T(8,128)(2,1)S(1)} %constant_dynamic-update-slice_fusion.refs_0_), channel_id=1, source_target_pairs={{0,2},{2,0},{1,3},{3,1},{4,6},{6,4},{5,7},{7,5},{8,10},{10,8},{9,1... | collective-permute-start | bytes 294920 | tf_op jit(solution)/shard_map/ppermute | solution.py:592
  41.1 1.4 %collective-permute-start.17 = (bf16[64,768]{1,0:T(8,128)(2,1)S(1)}, bf16[64,768]{1,0:T(8,128)(2,1)S(1)}, u32[]{:S(2)}, u32[]{:S(2)}) collective-permute-start(bf16[64,768]{1,0:T(8,128)(2,1)S(1)} %relay.5.refs_2_), channel_id=1, source_target_pairs={{0,2},{2,0},{1,3},{3,1},{4,6},{6,4},{5,7},{7,5},{8,10},{10,8},{9,1... | collective-permute-start | bytes 294920 | tf_op jit(solution)/shard_map/ppermute | solution.py:592
  50.5 1.5 %collective-permute-start.19 = (bf16[32,3072]{1,0:T(8,128)(2,1)S(1)}, bf16[32,3072]{1,0:T(8,128)(2,1)S(1)}, u32[]{:S(2)}, u32[]{:S(2)}) collective-permute-start(bf16[32,3072]{1,0:T(8,128)(2,1)S(1)} %get-tuple-element.74), channel_id=1, source_target_pairs={{0,2},{2,0},{1,3},{3,1},{4,6},{6,4},{5,7},{7,5},{8,10},{10,8},{9,1... | collective-permute-start | bytes 589832 | tf_op jit(solution)/shard_map/ppermute | solution.py:592
  50.7 1.5 %collective-permute-start.18 = (bf16[32,3072]{1,0:T(8,128)(2,1)S(1)}, bf16[32,3072]{1,0:T(8,128)(2,1)S(1)}, u32[]{:S(2)}, u32[]{:S(2)}) collective-permute-start(bf16[32,3072]{1,0:T(8,128)(2,1)S(1)} %get-tuple-element.73), channel_id=1, source_target_pairs={{0,2},{2,0},{1,3},{3,1},{4,6},{6,4},{5,7},{7,5},{8,10},{10,8},{9,1... | collective-permute-start | bytes 589832 | tf_op jit(solution)/shard_map/ppermute | solution.py:592
  52.3 8.7 %collective-permute-start.23 = (bf16[16,6144]{1,0:T(8,128)(2,1)S(1)}, bf16[16,6144]{1,0:T(8,128)(2,1)S(1)}, u32[]{:S(2)}, u32[]{:S(2)}) collective-permute-start(bf16[16,6144]{1,0:T(8,128)(2,1)S(1)} %get-tuple-element.82), channel_id=1, source_target_pairs={{0,1},{1,0},{2,3},{3,2},{4,5},{5,4},{6,7},{7,6},{8,9},{9,8},{10,11... | collective-permute-start | bytes 589832 | tf_op jit(solution)/shard_map/ppermute | solution.py:592
  53.1 5.9 %collective-permute-start.20 = (bf16[16,768]{1,0:T(8,128)(2,1)S(1)}, bf16[16,768]{1,0:T(8,128)(2,1)S(1)}, u32[]{:S(2)}, u32[]{:S(2)}) collective-permute-start(bf16[16,768]{1,0:T(8,128)(2,1)S(1)} %get-tuple-element.77), channel_id=1, source_target_pairs={{0,12},{4,8},{8,4},{12,0},{1,13},{5,9},{9,5},{13,1},{2,14},{6,10},... | collective-permute-start | bytes 73736 | tf_op jit(solution)/shard_map/ppermute | solution.py:592
  56.3 4.7 %collective-permute-start.21 = (bf16[16,768]{1,0:T(8,128)(2,1)S(1)}, bf16[16,768]{1,0:T(8,128)(2,1)S(1)}, u32[]{:S(2)}, u32[]{:S(2)}) collective-permute-start(bf16[16,768]{1,0:T(8,128)(2,1)S(1)} %get-tuple-element.78), channel_id=1, source_target_pairs={{0,8},{4,12},{8,0},{12,4},{1,9},{5,13},{9,1},{13,5},{2,10},{6,14},... | collective-permute-start | bytes 73736 | tf_op jit(solution)/shard_map/ppermute | solution.py:592
  56.3 4.7 %collective-permute-start.22 = (bf16[16,768]{1,0:T(8,128)(2,1)S(1)}, bf16[16,768]{1,0:T(8,128)(2,1)S(1)}, u32[]{:S(2)}, u32[]{:S(2)}) collective-permute-start(bf16[16,768]{1,0:T(8,128)(2,1)S(1)} %get-tuple-element.79), channel_id=1, source_target_pairs={{0,4},{4,0},{8,12},{12,8},{1,5},{5,1},{9,13},{13,9},{2,6},{6,2},{1... | collective-permute-start | bytes 73736 | tf_op jit(solution)/shard_map/ppermute | solution.py:592
  61.1 6.7 %collective-permute-start.24 = (bf16[8,3072]{1,0:T(8,128)(2,1)S(1)}, bf16[8,3072]{1,0:T(8,128)(2,1)S(1)}, u32[]{:S(2)}, u32[]{:S(2)}) collective-permute-start(bf16[8,3072]{1,0:T(8,128)(2,1)S(1)} %get-tuple-element.84), channel_id=1, source_target_pairs={{0,12},{4,8},{8,4},{12,0},{1,13},{5,9},{9,5},{13,1},{2,14},{6,10},... | collective-permute-start | bytes 147464 | tf_op jit(solution)/shard_map/ppermute | solution.py:592
  62.7 5.7 %collective-permute-start.25 = (bf16[8,3072]{1,0:T(8,128)(2,1)S(1)}, bf16[8,3072]{1,0:T(8,128)(2,1)S(1)}, u32[]{:S(2)}, u32[]{:S(2)}) collective-permute-start(bf16[8,3072]{1,0:T(8,128)(2,1)S(1)} %get-tuple-element.85), channel_id=1, source_target_pairs={{0,8},{4,12},{8,0},{12,4},{1,9},{5,13},{9,1},{13,5},{2,10},{6,14},... | collective-permute-start | bytes 147464 | tf_op jit(solution)/shard_map/ppermute | solution.py:592
  63.3 5.2 %collective-permute-start.26 = (bf16[8,3072]{1,0:T(8,128)(2,1)S(1)}, bf16[8,3072]{1,0:T(8,128)(2,1)S(1)}, u32[]{:S(2)}, u32[]{:S(2)}) collective-permute-start(bf16[8,3072]{1,0:T(8,128)(2,1)S(1)} %get-tuple-element.86), channel_id=1, source_target_pairs={{0,4},{4,0},{8,12},{12,8},{1,5},{5,1},{9,13},{13,9},{2,6},{6,2},{1... | collective-permute-start | bytes 147464 | tf_op jit(solution)/shard_map/ppermute | solution.py:592

commit v11 on v10

--- a/solution.py
+++ b/solution.py
@@ -309,10 +309,17 @@
     return squares
 
 
-def half_of(ref, first):
-    width = ref.shape[1] // 2
-    which = (lax.axis_index("expert") ^ first) // 2
-    return pl.ds(pl.multiple_of(which * width, width), width)
+def meet(ref, at, turned_ref, first):
+    width = ref.shape[1] // 4
+    start = (lax.axis_index("expert") ^ first) // 2 * 2 * width
+    halves = [
+        dot(
+            ref[at, pl.ds(pl.multiple_of(start + h * width, width), width)],
+            turned_ref[h * width : (h + 1) * width],
+        )
+        for h in range(2)
+    ]
+    return halves[0] + halves[1]
 
 
 def expert_first_kernel(count, *refs):
@@ -322,11 +329,10 @@
     rest = pltpu.make_async_copy(up_hbm.at[cut:], up_rest_ref, sem)
     rest.start()
     squares_ref[...] = turn(turned_ref, gain_ref, pieces, 0, count)
-    columns = half_of(gate_ref, 0)
-    gate_sum_ref[...] = dot(gate_ref[:, columns], turned_ref[...])
-    up_sum_ref[:cut] = dot(up_ref[:, columns], turned_ref[...])
+    gate_sum_ref[...] = meet(gate_ref, slice(None), turned_ref, 0)
+    up_sum_ref[:cut] = meet(up_ref, slice(None), turned_ref, 0)
     rest.wait()
-    up_sum_ref[cut:] = dot(up_rest_ref[:, columns], turned_ref[...])
+    up_sum_ref[cut:] = meet(up_rest_ref, slice(None), turned_ref, 0)
 
 
 def expert_second_kernel(count, *refs):
@@ -340,11 +346,10 @@
     squares = squares_ref[...] + turn(turned_ref, gain_ref, pieces, 2, count)
     spread = jnp.sum(squares.T, axis=0, keepdims=True) / width
     scale = lax.rsqrt(spread + EPSILON)
-    columns = half_of(gate_ref, 2)
-    gate_value_ref[...] = (gate_sum_ref[...] + dot(gate_ref[:, columns], turned_ref[...])) * scale
+    gate_value_ref[...] = (gate_sum_ref[...] + meet(gate_ref, slice(None), turned_ref, 2)) * scale
     for at, weight_ref in ((slice(0, cut), up_ref), (slice(cut, units), up_rest_ref)):
         gate_value = gate_value_ref[at]
-        lifted = (up_sum_ref[at] + dot(weight_ref[:, columns], turned_ref[...])) * scale
+        lifted = (up_sum_ref[at] + meet(weight_ref, slice(None), turned_ref, 2)) * scale
         hidden = gate_value / (1.0 + jnp.exp(-gate_value)) * lifted
         hidden_ref[:, at] = hidden.T.astype(BF16)
     down.wait()

time: 69.5 us -> 72.3 us (1.040)
  Pallas kernels: 30 us -> 32.7 us
    pallas_call x1, Pallas kernels: 5.92 us -> 8.57 us  [expert_first(): pl.pallas_call(functools.partial(expert_first_kernel, count), in_specs=[V...]
  transfers between devices with their start and end apart: 27 -> 27, of which waited for: 14 -> 14; matrix products, arithmetic and copies ran while one was open for 0% -> 0% of each run, Pallas kernels for 24% -> 26%
where the time goes in v11:
time: 72.3 us; the launch traced here: 72 us
  Pallas kernels  32.7 us (45%)
  starting transfers between devices  26.4 us (37%)
  waiting for transfers between devices  12.8 us (18%)
    ppermute x27, starting transfers between devices, swap(): lax.ppermute(x, axis, [(i, i ^ by) for i in range(lax.axis_size(axis))])  26.4 us
    ppermute x27, waiting for transfers between devices, swap(): lax.ppermute(x, axis, [(i, i ^ by) for i in range(lax.axis_size(axis))])  12.8 us
    pallas_call x1, Pallas kernels, expert_first(): pl.pallas_call(functools.partial(expert_first_kernel, count), in_specs=[V...  8.57 us
    pallas_call x1, Pallas kernels, load(): pl.pallas_call(functools.partial(load_kernel, len(weights)), in_specs=[AN...  6.03 us
    pallas_call x1, Pallas kernels, expert_second(): pl.pallas_call(functools.partial(expert_second_kernel, count), in_specs=[...  5.32 us
    pallas_call x1, Pallas kernels, attend(): pl.pallas_call(functools.partial(attend_kernel, rows // requests, heads /...  3.76 us
    pallas_call x1, Pallas kernels, route(): pl.pallas_call(functools.partial(route_kernel, capacity, top), in_specs=[...  3.28 us
    pallas_call x2, Pallas kernels, expert_down(): pl.pallas_call(functools.partial(down_kernel, start, 512), in_specs=[VMEM...  2.73 us
  transfers between devices with their start and end apart: 27, of which 14 were waited for; matrix products, arithmetic and copies ran while one was open for 0% of the time, Pallas kernels for 26%

profile of v11, /device:TPU:0, one launch (start us, length us, event | category | flops | bytes accessed | tf_op | source)
XLA Modules:
  0.0 72.0 jit_solution(13455078476402974265)
XLA Ops:
  0.0 3.8 %attention.1 = (bf16[16,2944]{1,0:T(8,128)(2,1)S(1)}, bf16[16,2944]{1,0:T(8,128)(2,1)S(1)}, bf16[16,2944]{1,0:T(8,128)(2,1)S(1)}, bf16[16,2944]{1,0:T(8,128)(2,1)S(1)}) custom-call(f32[16]{0:T(128)} %decay_ref.1, s32[2,8]{1,0:T(2,128)} %bitcast.6, bf16[16,2048]{1,0:T(8,128)(2,1)} %q_ref.1, bf16[16,2048]{1,0:T(8,128)(2,1)} %k_ref.1, bf16[16,2048]{1,0:T(8,128)(2,1)} %v_ref.1, ...), custom_call_target="tpu_custom_call" | custom-call | tf_op jit(solution)/shard_map/attention/pallas_call | solution.py:111
  3.8 5.1 %collective-permute-start.1 = (bf16[16,2944]{1,0:T(8,128)(2,1)S(1)}, bf16[16,2944]{1,0:T(8,128)(2,1)S(1)}, u32[]{:S(2)}, u32[]{:S(2)}) collective-permute-start(bf16[16,2944]{1,0:T(8,128)(2,1)S(1)} %get-tuple-element.48), channel_id=1, source_target_pairs={{0,12},{4,8},{8,4},{12,0},{1,13},{5,9},{9,5},{13,1},{2,14},{6,10},... | collective-permute-start | bytes 282632 | tf_op jit(solution)/shard_map/ppermute | solution.py:597
  8.9 0.0 collective-permute-start.3
  8.9 0.6 collective-permute-start.5
  9.5 6.0 %load.1 = (bf16[16,2944]{1,0:T(8,128)(2,1)S(1)}, bf16[2048,768]{1,0:T(8,128)(2,1)S(1)}, f32[1,6144]{1,0:T(1,128)S(1)}, bf16[1152,6144]{1,0:T(8,128)(2,1)S(1)}) custom-call(bf16[16,2944]{1,0:T(8,128)(2,1)S(1)} %get-tuple-element.46.rows_hbm, bf16[2048,768]{1,0:T(8,128)(2,1)} %refs_0_.1, f32[1,6144]{1,0:T(1,128)} %bitcast.4, bf16[1152,6144]{1,0:T(8,128)(2,1)} %refs_2_.1), custom_call_target="tpu_custom_call" | custom-call | bytes 17326080 | tf_op jit(solution)/shard_map/load/pallas_call | solution.py:150
  15.6 0.1 collective-permute-start
  15.6 0.0 collective-permute-done.1.refs_2_
  15.7 0.5 collective-permute-start.2
  16.1 0.6 collective-permute-done.3.refs_4_
  16.8 0.0 collective-permute-start.4
  16.8 0.0 collective-permute-done.5.refs_6_
  16.8 0.5 collective-permute-start.6
  17.3 0.0 collective-permute-done.refs_1_
  17.3 0.0 collective-permute-done.2.refs_3_
  17.3 0.8 %collective-permute-done.4.refs_5_ = bf16[16,2944]{1,0:T(8,128)(2,1)S(1)} collective-permute-done((bf16[16,2944]{1,0:T(8,128)(2,1)S(1)}, bf16[16,2944]{1,0:T(8,128)(2,1)S(1)}, u32[]{:S(2)}, u32[]{:S(2)}) %collective-permute-start.4) | collective-permute-done | bytes 94240 | tf_op jit(solution)/shard_map/ppermute | solution.py:597
  18.1 0.2 collective-permute-done.6.refs_7_
  18.3 0.7 projection.1
  19.0 1.6 %collective-permute-start.7 = (bf16[64,768]{1,0:T(8,128)(2,1)S(1)}, bf16[64,768]{1,0:T(8,128)(2,1)S(1)}, u32[]{:S(2)}, u32[]{:S(2)}) collective-permute-start(bf16[64,768]{1,0:T(8,128)(2,1)S(1)} %get-tuple-element.53), channel_id=1, source_target_pairs={{0,1},{1,0},{2,3},{3,2},{4,5},{5,4},{6,7},{7,6},{8,9},{9,8},{10,11... | collective-permute-start | bytes 294920 | tf_op jit(solution)/shard_map/ppermute | solution.py:597
  20.5 3.3 %route.1 = (bf16[128,64]{1,0:T(8,128)(2,1)S(1)}, f32[64,768]{1,0:T(8,128)S(1)}, bf16[640,6144]{1,0:T(8,128)(2,1)S(1)}) custom-call(bf16[16,2944]{1,0:T(8,128)(2,1)S(1)} %get-tuple-element.47.refs_0_, bf16[16,2944]{1,0:T(8,128)(2,1)S(1)} %collective-permute-done.refs_1_, bf16[16,2944]{1,0:T(8,128)(2,1)S(1)} %collective-permute-done.1.refs_2_, ...), custom_call_target="tpu_custom_call" | custom-call | flops 1000000 | bytes 8000000 | tf_op jit(solution)/shard_map/route/pallas_call | solution.py:243
  23.8 0.3 collective-permute-done.7.got_ref
  24.1 0.2 pack.1
  24.3 0.8 %collective-permute-start.13 = (bf16[32,768]{1,0:T(8,128)(2,1)S(1)}, bf16[32,768]{1,0:T(8,128)(2,1)S(1)}, u32[]{:S(2)}, u32[]{:S(2)}) collective-permute-start(bf16[32,768]{1,0:T(8,128)(2,1)S(1)} %get-tuple-element.59.refs_0_), channel_id=1, source_target_pairs={{0,4},{4,0},{8,12},{12,8},{1,5},{5,1},{9,13},{13,9},{2,6},{6,2},{1... | collective-permute-start | bytes 147464 | tf_op jit(solution)/shard_map/ppermute | solution.py:597
  25.1 2.4 %collective-permute-start.10 = (bf16[32,768]{1,0:T(8,128)(2,1)S(1)}, bf16[32,768]{1,0:T(8,128)(2,1)S(1)}, u32[]{:S(2)}, u32[]{:S(2)}) collective-permute-start(bf16[32,768]{1,0:T(8,128)(2,1)S(1)} %relay.4), channel_id=1, source_target_pairs={{0,12},{4,8},{8,4},{12,0},{1,13},{5,9},{9,5},{13,1},{2,14},{6,10},... | collective-permute-start | bytes 147464 | tf_op jit(solution)/shard_map/ppermute | solution.py:597
  27.6 0.6 collective-permute-start.9
  28.2 0.3 collective-permute-done.13
  28.5 1.5 %collective-permute-start.15 = (bf16[64,768]{1,0:T(8,128)(2,1)S(1)}, bf16[64,768]{1,0:T(8,128)(2,1)S(1)}, u32[]{:S(2)}, u32[]{:S(2)}) collective-permute-start(bf16[64,768]{1,0:T(8,128)(2,1)S(1)} %constant_dynamic-update-slice_fusion.2.refs_0_), channel_id=1, source_target_pairs={{0,1},{1,0},{2,3},{3,2},{4,5},{5,4},{6,7},{7,6},{8,9},{9,8},{10,11... | collective-permute-start | bytes 294920 | tf_op jit(solution)/shard_map/ppermute | solution.py:597
  30.0 0.0 collective-permute-start.14
  30.0 2.7 %collective-permute-done.9 = bf16[32,768]{1,0:T(8,128)(2,1)S(1)} collective-permute-done((bf16[32,768]{1,0:T(8,128)(2,1)S(1)}, bf16[32,768]{1,0:T(8,128)(2,1)S(1)}, u32[]{:S(2)}, u32[]{:S(2)}) %collective-permute-start.9) | collective-permute-done | bytes 49184 | tf_op jit(solution)/shard_map/ppermute | solution.py:597
  32.7 0.4 collective-permute-done.15.refs_2_
  33.1 0.0 collective-permute-start.16
  33.1 0.0 collective-permute-done.10
  33.1 1.6 %collective-permute-start.12 = (bf16[64,768]{1,0:T(8,128)(2,1)S(1)}, bf16[64,768]{1,0:T(8,128)(2,1)S(1)}, u32[]{:S(2)}, u32[]{:S(2)}) collective-permute-start(bf16[64,768]{1,0:T(8,128)(2,1)S(1)} %constant_dynamic-update-slice_fusion.refs_0_), channel_id=1, source_target_pairs={{0,1},{1,0},{2,3},{3,2},{4,5},{5,4},{6,7},{7,6},{8,9},{9,8},{10,11... | collective-permute-start | bytes 294920 | tf_op jit(solution)/shard_map/ppermute | solution.py:597
  34.6 0.2 collective-permute-start.8
  34.9 0.3 collective-permute-start.11
  35.2 0.0 collective-permute-done.14.refs_1_
  35.2 0.0 collective-permute-done.16.refs_3_
  35.2 8.6 %experts_first.1 = (f32[1152,64]{1,0:T(8,128)S(1)}, f32[1152,64]{1,0:T(8,128)S(1)}, f32[64,128]{1,0:T(8,128)S(1)}, bf16[512,6144]{1,0:T(8,128)(2,1)S(1)}) custom-call(bf16[64,768]{1,0:T(8,128)(2,1)S(1)} %constant_dynamic-update-slice_fusion.2.refs_0_, bf16[64,768]{1,0:T(8,128)(2,1)S(1)} %collective-permute-done.14.refs_1_, ...), custom_call_target="tpu_custom_call" | custom-call | flops 905969664 | bytes 14155776 | tf_op jit(solution)/shard_map/experts_first/pallas_call | solution.py:382
  43.7 0.0 collective-permute-done.8.refs_1_.cross_ref
  43.8 0.0 collective-permute-done.12.rows_ref
  43.8 0.3 collective-permute-start.17
  44.1 0.0 collective-permute-done.11.refs_1_
  44.1 1.1 %collective-permute-done.17.refs_3_ = bf16[64,768]{1,0:T(8,128)(2,1)S(1)} collective-permute-done((bf16[64,768]{1,0:T(8,128)(2,1)S(1)}, bf16[64,768]{1,0:T(8,128)(2,1)S(1)}, u32[]{:S(2)}, u32[]{:S(2)}) %collective-permute-start.17) | collective-permute-done | bytes 98336 | tf_op jit(solution)/shard_map/ppermute | solution.py:597
  45.2 5.3 %experts_second.1 = (bf16[64,1152]{1,0:T(8,128)(2,1)S(1)}, bf16[1152,6144]{1,0:T(8,128)(2,1)S(1)}) custom-call(bf16[64,768]{1,0:T(8,128)(2,1)S(1)} %constant_dynamic-update-slice_fusion.refs_0_, bf16[64,768]{1,0:T(8,128)(2,1)S(1)} %collective-permute-done.11.refs_1_, bf16[64,768]{1,0:T(8,128)(2,1)S(1)} %relay.5.refs_2_, ...), custom_call_target="tpu_custom_call" | custom-call | flops 905969664 | bytes 14155776 | tf_op jit(solution)/shard_map/experts_second/pallas_call | solution.py:417
  50.5 1.4 %experts_down.3 = (f32[32,3072]{1,0:T(8,128)S(1)}, bf16[32,3072]{1,0:T(8,128)(2,1)S(1)}) custom-call(bf16[64,1152]{1,0:T(8,128)(2,1)S(1)} %get-tuple-element.69.hidden_ref, bf16[1152,6144]{1,0:T(8,128)(2,1)S(1)} %get-tuple-element.70.weight_ref), custom_call_target="tpu_custom_call" | custom-call | flops 905969664 | bytes 7077888 | tf_op jit(solution)/shard_map/experts_down/pallas_call | solution.py:437
  51.9 1.4 %experts_down.2 = (f32[32,3072]{1,0:T(8,128)S(1)}, bf16[32,3072]{1,0:T(8,128)(2,1)S(1)}) custom-call(bf16[64,1152]{1,0:T(8,128)(2,1)S(1)} %get-tuple-element.69.hidden_ref, bf16[1152,6144]{1,0:T(8,128)(2,1)S(1)} %get-tuple-element.70.weight_ref), custom_call_target="tpu_custom_call" | custom-call | flops 905969664 | bytes 7077888 | tf_op jit(solution)/shard_map/experts_down/pallas_call | solution.py:437
  53.2 0.3 collective-permute-start.19
  53.5 0.3 collective-permute-start.18
  53.8 0.9 %collective-permute-done.19.refs_3_ = bf16[32,3072]{1,0:T(8,128)(2,1)S(1)} collective-permute-done((bf16[32,3072]{1,0:T(8,128)(2,1)S(1)}, bf16[32,3072]{1,0:T(8,128)(2,1)S(1)}, u32[]{:S(2)}, u32[]{:S(2)}) %collective-permute-start.19) | collective-permute-done | bytes 196640 | tf_op jit(solution)/shard_map/ppermute | solution.py:597
  54.7 0.3 collective-permute-done.18.refs_2_
  55.0 0.1 chip_sum.1
  55.1 0.7 %collective-permute-start.23 = (bf16[16,6144]{1,0:T(8,128)(2,1)S(1)}, bf16[16,6144]{1,0:T(8,128)(2,1)S(1)}, u32[]{:S(2)}, u32[]{:S(2)}) collective-permute-start(bf16[16,6144]{1,0:T(8,128)(2,1)S(1)} %get-tuple-element.82), channel_id=1, source_target_pairs={{0,1},{1,0},{2,3},{3,2},{4,5},{5,4},{6,7},{7,6},{8,9},{9,8},{10,11... | collective-permute-start | bytes 589832 | tf_op jit(solution)/shard_map/ppermute | solution.py:597
  55.8 3.2 %collective-permute-start.20 = (bf16[16,768]{1,0:T(8,128)(2,1)S(1)}, bf16[16,768]{1,0:T(8,128)(2,1)S(1)}, u32[]{:S(2)}, u32[]{:S(2)}) collective-permute-start(bf16[16,768]{1,0:T(8,128)(2,1)S(1)} %get-tuple-element.77), channel_id=1, source_target_pairs={{0,12},{4,8},{8,4},{12,0},{1,13},{5,9},{9,5},{13,1},{2,14},{6,10},... | collective-permute-start | bytes 73736 | tf_op jit(solution)/shard_map/ppermute | solution.py:597
  59.0 1.3 %collective-permute-start.22 = (bf16[16,768]{1,0:T(8,128)(2,1)S(1)}, bf16[16,768]{1,0:T(8,128)(2,1)S(1)}, u32[]{:S(2)}, u32[]{:S(2)}) collective-permute-start(bf16[16,768]{1,0:T(8,128)(2,1)S(1)} %get-tuple-element.79), channel_id=1, source_target_pairs={{0,4},{4,0},{8,12},{12,8},{1,5},{5,1},{9,13},{13,9},{2,6},{6,2},{1... | collective-permute-start | bytes 73736 | tf_op jit(solution)/shard_map/ppermute | solution.py:597
  60.3 1.5 %collective-permute-done.20.refs_1_ = bf16[16,768]{1,0:T(8,128)(2,1)S(1)} collective-permute-done((bf16[16,768]{1,0:T(8,128)(2,1)S(1)}, bf16[16,768]{1,0:T(8,128)(2,1)S(1)}, u32[]{:S(2)}, u32[]{:S(2)}) %collective-permute-start.20) | collective-permute-done | bytes 24608 | tf_op jit(solution)/shard_map/ppermute | solution.py:597
  61.8 1.9 %collective-permute-done.21.refs_2_ = bf16[16,768]{1,0:T(8,128)(2,1)S(1)} collective-permute-done((bf16[16,768]{1,0:T(8,128)(2,1)S(1)}, bf16[16,768]{1,0:T(8,128)(2,1)S(1)}, u32[]{:S(2)}, u32[]{:S(2)}) %collective-permute-start.21) | collective-permute-done | bytes 24608 | tf_op jit(solution)/shard_map/ppermute | solution.py:597
  63.7 0.0 collective-permute-done.23.got_ref
  63.7 0.1 pair_sum.1
  63.8 1.6 %collective-permute-start.24 = (bf16[8,3072]{1,0:T(8,128)(2,1)S(1)}, bf16[8,3072]{1,0:T(8,128)(2,1)S(1)}, u32[]{:S(2)}, u32[]{:S(2)}) collective-permute-start(bf16[8,3072]{1,0:T(8,128)(2,1)S(1)} %get-tuple-element.84), channel_id=1, source_target_pairs={{0,12},{4,8},{8,4},{12,0},{1,13},{5,9},{9,5},{13,1},{2,14},{6,10},... | collective-permute-start | bytes 147464 | tf_op jit(solution)/shard_map/ppermute | solution.py:597
  65.5 0.6 collective-permute-start.25
  66.0 2.3 %collective-permute-start.26 = (bf16[8,3072]{1,0:T(8,128)(2,1)S(1)}, bf16[8,3072]{1,0:T(8,128)(2,1)S(1)}, u32[]{:S(2)}, u32[]{:S(2)}) collective-permute-start(bf16[8,3072]{1,0:T(8,128)(2,1)S(1)} %get-tuple-element.86), channel_id=1, source_target_pairs={{0,4},{4,0},{8,12},{12,8},{1,5},{5,1},{9,13},{13,9},{2,6},{6,2},{1... | collective-permute-start | bytes 147464 | tf_op jit(solution)/shard_map/ppermute | solution.py:597
  68.3 1.1 %own_rows.1 = (f32[8,6144]{1,0:T(8,128)S(1)}, bf16[32,32]{1,0:T(8,128)(2,1)S(1)}) custom-call(s32[2,8]{1,0:T(2,128)} %bitcast.7, f32[2,8]{1,0:T(2,128)} %bitcast.8, bf16[8,6144]{1,0:T(8,128)(2,1)} %residual_ref.3, bf16[16,768]{1,0:T(8,128)(2,1)S(1)} %get-tuple-element.76.refs_0_, bf16[16,768]{1,0:T(8,128)(2,1)S(1)} %collective-permute-done.20.refs_1_, ...), custom_call_target="tpu_custom_call" | custom-call | flops 1000000 | bytes 1000000 | tf_op jit(solution)/shard_map/own_rows/pallas_call | solution.py:559
  69.4 1.0 %collective-permute-done.24.refs_1_ = bf16[8,3072]{1,0:T(8,128)(2,1)S(1)} collective-permute-done((bf16[8,3072]{1,0:T(8,128)(2,1)S(1)}, bf16[8,3072]{1,0:T(8,128)(2,1)S(1)}, u32[]{:S(2)}, u32[]{:S(2)}) %collective-permute-start.24) | collective-permute-done | bytes 49184 | tf_op jit(solution)/shard_map/ppermute | solution.py:597
  70.4 0.8 %collective-permute-done.25.refs_2_ = bf16[8,3072]{1,0:T(8,128)(2,1)S(1)} collective-permute-done((bf16[8,3072]{1,0:T(8,128)(2,1)S(1)}, bf16[8,3072]{1,0:T(8,128)(2,1)S(1)}, u32[]{:S(2)}, u32[]{:S(2)}) %collective-permute-start.25) | collective-permute-done | bytes 49184 | tf_op jit(solution)/shard_map/ppermute | solution.py:597
  71.2 0.8 %finish.1 = bf16[8,6144]{1,0:T(8,128)(2,1)} custom-call(f32[8,6144]{1,0:T(8,128)S(1)} %get-tuple-element.80.combined_ref, bf16[32,32]{1,0:T(8,128)(2,1)S(1)} %get-tuple-element.81.weighting_ref, bf16[8,3072]{1,0:T(8,128)(2,1)S(1)} %get-tuple-element.83.refs_0_, bf16[8,3072]{1,0:T(8,128)(2,1)S(1)} %collective-permute-done.24.refs_1_, ...), custom_call_target="tpu_custom_call" | custom-call | tf_op jit(solution)/shard_map/finish/pallas_call | solution.py:586
  (11 shorter events, 0.1 us)
Async XLA Ops:
  3.8 11.9 %collective-permute-start.1 = (bf16[16,2944]{1,0:T(8,128)(2,1)S(1)}, bf16[16,2944]{1,0:T(8,128)(2,1)S(1)}, u32[]{:S(2)}, u32[]{:S(2)}) collective-permute-start(bf16[16,2944]{1,0:T(8,128)(2,1)S(1)} %get-tuple-element.48), channel_id=1, source_target_pairs={{0,12},{4,8},{8,4},{12,0},{1,13},{5,9},{9,5},{13,1},{2,14},{6,10},... | collective-permute-start | bytes 282632 | tf_op jit(solution)/shard_map/ppermute | solution.py:597
  8.9 7.9 %collective-permute-start.3 = (bf16[16,2944]{1,0:T(8,128)(2,1)S(1)}, bf16[16,2944]{1,0:T(8,128)(2,1)S(1)}, u32[]{:S(2)}, u32[]{:S(2)}) collective-permute-start(bf16[16,2944]{1,0:T(8,128)(2,1)S(1)} %get-tuple-element.49), channel_id=1, source_target_pairs={{0,8},{4,12},{8,0},{12,4},{1,9},{5,13},{9,1},{13,5},{2,10},{6,14},... | collective-permute-start | bytes 282632 | tf_op jit(solution)/shard_map/ppermute | solution.py:597
  8.9 7.9 %collective-permute-start.5 = (bf16[16,2944]{1,0:T(8,128)(2,1)S(1)}, bf16[16,2944]{1,0:T(8,128)(2,1)S(1)}, u32[]{:S(2)}, u32[]{:S(2)}) collective-permute-start(bf16[16,2944]{1,0:T(8,128)(2,1)S(1)} %get-tuple-element.50), channel_id=1, source_target_pairs={{0,4},{4,0},{8,12},{12,8},{1,5},{5,1},{9,13},{13,9},{2,6},{6,2},{1... | collective-permute-start | bytes 282632 | tf_op jit(solution)/shard_map/ppermute | solution.py:597
  15.6 1.7 %collective-permute-start = (bf16[16,2944]{1,0:T(8,128)(2,1)S(1)}, bf16[16,2944]{1,0:T(8,128)(2,1)S(1)}, u32[]{:S(2)}, u32[]{:S(2)}) collective-permute-start(bf16[16,2944]{1,0:T(8,128)(2,1)S(1)} %get-tuple-element.47.refs_0_), channel_id=1, source_target_pairs={{0,2},{2,0},{1,3},{3,1},{4,6},{6,4},{5,7},{7,5},{8,10},{10,8},{9,1... | collective-permute-start | bytes 282632 | tf_op jit(solution)/shard_map/ppermute | solution.py:597
  15.7 1.7 %collective-permute-start.2 = (bf16[16,2944]{1,0:T(8,128)(2,1)S(1)}, bf16[16,2944]{1,0:T(8,128)(2,1)S(1)}, u32[]{:S(2)}, u32[]{:S(2)}) collective-permute-start(bf16[16,2944]{1,0:T(8,128)(2,1)S(1)} %collective-permute-done.1.refs_2_), channel_id=1, source_target_pairs={{0,2},{2,0},{1,3},{3,1},{4,6},{6,4},{5,7},{7,5},{8,10},{10,8},{9,1... | collective-permute-start | bytes 282632 | tf_op jit(solution)/shard_map/ppermute | solution.py:597
  16.8 1.3 %collective-permute-start.4 = (bf16[16,2944]{1,0:T(8,128)(2,1)S(1)}, bf16[16,2944]{1,0:T(8,128)(2,1)S(1)}, u32[]{:S(2)}, u32[]{:S(2)}) collective-permute-start(bf16[16,2944]{1,0:T(8,128)(2,1)S(1)} %collective-permute-done.3.refs_4_), channel_id=1, source_target_pairs={{0,2},{2,0},{1,3},{3,1},{4,6},{6,4},{5,7},{7,5},{8,10},{10,8},{9,1... | collective-permute-start | bytes 282632 | tf_op jit(solution)/shard_map/ppermute | solution.py:597
  16.8 1.4 %collective-permute-start.6 = (bf16[16,2944]{1,0:T(8,128)(2,1)S(1)}, bf16[16,2944]{1,0:T(8,128)(2,1)S(1)}, u32[]{:S(2)}, u32[]{:S(2)}) collective-permute-start(bf16[16,2944]{1,0:T(8,128)(2,1)S(1)} %collective-permute-done.5.refs_6_), channel_id=1, source_target_pairs={{0,2},{2,0},{1,3},{3,1},{4,6},{6,4},{5,7},{7,5},{8,10},{10,8},{9,1... | collective-permute-start | bytes 282632 | tf_op jit(solution)/shard_map/ppermute | solution.py:597
  19.0 5.1 %collective-permute-start.7 = (bf16[64,768]{1,0:T(8,128)(2,1)S(1)}, bf16[64,768]{1,0:T(8,128)(2,1)S(1)}, u32[]{:S(2)}, u32[]{:S(2)}) collective-permute-start(bf16[64,768]{1,0:T(8,128)(2,1)S(1)} %get-tuple-element.53), channel_id=1, source_target_pairs={{0,1},{1,0},{2,3},{3,2},{4,5},{5,4},{6,7},{7,6},{8,9},{9,8},{10,11... | collective-permute-start | bytes 294920 | tf_op jit(solution)/shard_map/ppermute | solution.py:597
  24.3 4.2 %collective-permute-start.13 = (bf16[32,768]{1,0:T(8,128)(2,1)S(1)}, bf16[32,768]{1,0:T(8,128)(2,1)S(1)}, u32[]{:S(2)}, u32[]{:S(2)}) collective-permute-start(bf16[32,768]{1,0:T(8,128)(2,1)S(1)} %get-tuple-element.59.refs_0_), channel_id=1, source_target_pairs={{0,4},{4,0},{8,12},{12,8},{1,5},{5,1},{9,13},{13,9},{2,6},{6,2},{1... | collective-permute-start | bytes 147464 | tf_op jit(solution)/shard_map/ppermute | solution.py:597
  25.1 8.0 %collective-permute-start.10 = (bf16[32,768]{1,0:T(8,128)(2,1)S(1)}, bf16[32,768]{1,0:T(8,128)(2,1)S(1)}, u32[]{:S(2)}, u32[]{:S(2)}) collective-permute-start(bf16[32,768]{1,0:T(8,128)(2,1)S(1)} %relay.4), channel_id=1, source_target_pairs={{0,12},{4,8},{8,4},{12,0},{1,13},{5,9},{9,5},{13,1},{2,14},{6,10},... | collective-permute-start | bytes 147464 | tf_op jit(solution)/shard_map/ppermute | solution.py:597
  27.6 5.1 %collective-permute-start.9 = (bf16[32,768]{1,0:T(8,128)(2,1)S(1)}, bf16[32,768]{1,0:T(8,128)(2,1)S(1)}, u32[]{:S(2)}, u32[]{:S(2)}) collective-permute-start(bf16[32,768]{1,0:T(8,128)(2,1)S(1)} %relay.3), channel_id=1, source_target_pairs={{0,8},{4,12},{8,0},{12,4},{1,9},{5,13},{9,1},{13,5},{2,10},{6,14},... | collective-permute-start | bytes 147464 | tf_op jit(solution)/shard_map/ppermute | solution.py:597
  28.5 4.6 %collective-permute-start.15 = (bf16[64,768]{1,0:T(8,128)(2,1)S(1)}, bf16[64,768]{1,0:T(8,128)(2,1)S(1)}, u32[]{:S(2)}, u32[]{:S(2)}) collective-permute-start(bf16[64,768]{1,0:T(8,128)(2,1)S(1)} %constant_dynamic-update-slice_fusion.2.refs_0_), channel_id=1, source_target_pairs={{0,1},{1,0},{2,3},{3,2},{4,5},{5,4},{6,7},{7,6},{8,9},{9,8},{10,11... | collective-permute-start | bytes 294920 | tf_op jit(solution)/shard_map/ppermute | solution.py:597
  30.0 5.2 %collective-permute-start.14 = (bf16[64,768]{1,0:T(8,128)(2,1)S(1)}, bf16[64,768]{1,0:T(8,128)(2,1)S(1)}, u32[]{:S(2)}, u32[]{:S(2)}) collective-permute-start(bf16[64,768]{1,0:T(8,128)(2,1)S(1)} %constant_dynamic-update-slice_fusion.2.refs_0_), channel_id=1, source_target_pairs={{0,2},{2,0},{1,3},{3,1},{4,6},{6,4},{5,7},{7,5},{8,10},{10,8},{9,1... | collective-permute-start | bytes 294920 | tf_op jit(solution)/shard_map/ppermute | solution.py:597
  33.1 2.1 %collective-permute-start.16 = (bf16[64,768]{1,0:T(8,128)(2,1)S(1)}, bf16[64,768]{1,0:T(8,128)(2,1)S(1)}, u32[]{:S(2)}, u32[]{:S(2)}) collective-permute-start(bf16[64,768]{1,0:T(8,128)(2,1)S(1)} %collective-permute-done.15.refs_2_), channel_id=1, source_target_pairs={{0,2},{2,0},{1,3},{3,1},{4,6},{6,4},{5,7},{7,5},{8,10},{10,8},{9,1... | collective-permute-start | bytes 294920 | tf_op jit(solution)/shard_map/ppermute | solution.py:597
  33.1 10.7 %collective-permute-start.12 = (bf16[64,768]{1,0:T(8,128)(2,1)S(1)}, bf16[64,768]{1,0:T(8,128)(2,1)S(1)}, u32[]{:S(2)}, u32[]{:S(2)}) collective-permute-start(bf16[64,768]{1,0:T(8,128)(2,1)S(1)} %constant_dynamic-update-slice_fusion.refs_0_), channel_id=1, source_target_pairs={{0,1},{1,0},{2,3},{3,2},{4,5},{5,4},{6,7},{7,6},{8,9},{9,8},{10,11... | collective-permute-start | bytes 294920 | tf_op jit(solution)/shard_map/ppermute | solution.py:597
  34.6 9.1 %collective-permute-start.8 = (bf16[32,768]{1,0:T(8,128)(2,1)S(1)}, bf16[32,768]{1,0:T(8,128)(2,1)S(1)}, u32[]{:S(2)}, u32[]{:S(2)}) collective-permute-start(bf16[32,768]{1,0:T(8,128)(2,1)S(1)} %get-tuple-element.57), channel_id=1, source_target_pairs={{0,2},{2,0},{1,3},{3,1},{4,6},{6,4},{5,7},{7,5},{8,10},{10,8},{9,1... | collective-permute-start | bytes 147464 | tf_op jit(solution)/shard_map/ppermute | solution.py:597
  34.9 9.2 %collective-permute-start.11 = (bf16[64,768]{1,0:T(8,128)(2,1)S(1)}, bf16[64,768]{1,0:T(8,128)(2,1)S(1)}, u32[]{:S(2)}, u32[]{:S(2)}) collective-permute-start(bf16[64,768]{1,0:T(8,128)(2,1)S(1)} %constant_dynamic-update-slice_fusion.refs_0_), channel_id=1, source_target_pairs={{0,2},{2,0},{1,3},{3,1},{4,6},{6,4},{5,7},{7,5},{8,10},{10,8},{9,1... | collective-permute-start | bytes 294920 | tf_op jit(solution)/shard_map/ppermute | solution.py:597
  43.8 1.4 %collective-permute-start.17 = (bf16[64,768]{1,0:T(8,128)(2,1)S(1)}, bf16[64,768]{1,0:T(8,128)(2,1)S(1)}, u32[]{:S(2)}, u32[]{:S(2)}) collective-permute-start(bf16[64,768]{1,0:T(8,128)(2,1)S(1)} %relay.5.refs_2_), channel_id=1, source_target_pairs={{0,2},{2,0},{1,3},{3,1},{4,6},{6,4},{5,7},{7,5},{8,10},{10,8},{9,1... | collective-permute-start | bytes 294920 | tf_op jit(solution)/shard_map/ppermute | solution.py:597
  53.2 1.5 %collective-permute-start.19 = (bf16[32,3072]{1,0:T(8,128)(2,1)S(1)}, bf16[32,3072]{1,0:T(8,128)(2,1)S(1)}, u32[]{:S(2)}, u32[]{:S(2)}) collective-permute-start(bf16[32,3072]{1,0:T(8,128)(2,1)S(1)} %get-tuple-element.74), channel_id=1, source_target_pairs={{0,2},{2,0},{1,3},{3,1},{4,6},{6,4},{5,7},{7,5},{8,10},{10,8},{9,1... | collective-permute-start | bytes 589832 | tf_op jit(solution)/shard_map/ppermute | solution.py:597
  53.5 1.5 %collective-permute-start.18 = (bf16[32,3072]{1,0:T(8,128)(2,1)S(1)}, bf16[32,3072]{1,0:T(8,128)(2,1)S(1)}, u32[]{:S(2)}, u32[]{:S(2)}) collective-permute-start(bf16[32,3072]{1,0:T(8,128)(2,1)S(1)} %get-tuple-element.73), channel_id=1, source_target_pairs={{0,2},{2,0},{1,3},{3,1},{4,6},{6,4},{5,7},{7,5},{8,10},{10,8},{9,1... | collective-permute-start | bytes 589832 | tf_op jit(solution)/shard_map/ppermute | solution.py:597
  55.1 8.7 %collective-permute-start.23 = (bf16[16,6144]{1,0:T(8,128)(2,1)S(1)}, bf16[16,6144]{1,0:T(8,128)(2,1)S(1)}, u32[]{:S(2)}, u32[]{:S(2)}) collective-permute-start(bf16[16,6144]{1,0:T(8,128)(2,1)S(1)} %get-tuple-element.82), channel_id=1, source_target_pairs={{0,1},{1,0},{2,3},{3,2},{4,5},{5,4},{6,7},{7,6},{8,9},{9,8},{10,11... | collective-permute-start | bytes 589832 | tf_op jit(solution)/shard_map/ppermute | solution.py:597
  55.8 6.0 %collective-permute-start.20 = (bf16[16,768]{1,0:T(8,128)(2,1)S(1)}, bf16[16,768]{1,0:T(8,128)(2,1)S(1)}, u32[]{:S(2)}, u32[]{:S(2)}) collective-permute-start(bf16[16,768]{1,0:T(8,128)(2,1)S(1)} %get-tuple-element.77), channel_id=1, source_target_pairs={{0,12},{4,8},{8,4},{12,0},{1,13},{5,9},{9,5},{13,1},{2,14},{6,10},... | collective-permute-start | bytes 73736 | tf_op jit(solution)/shard_map/ppermute | solution.py:597
  59.0 4.7 %collective-permute-start.21 = (bf16[16,768]{1,0:T(8,128)(2,1)S(1)}, bf16[16,768]{1,0:T(8,128)(2,1)S(1)}, u32[]{:S(2)}, u32[]{:S(2)}) collective-permute-start(bf16[16,768]{1,0:T(8,128)(2,1)S(1)} %get-tuple-element.78), channel_id=1, source_target_pairs={{0,8},{4,12},{8,0},{12,4},{1,9},{5,13},{9,1},{13,5},{2,10},{6,14},... | collective-permute-start | bytes 73736 | tf_op jit(solution)/shard_map/ppermute | solution.py:597
  59.0 4.7 %collective-permute-start.22 = (bf16[16,768]{1,0:T(8,128)(2,1)S(1)}, bf16[16,768]{1,0:T(8,128)(2,1)S(1)}, u32[]{:S(2)}, u32[]{:S(2)}) collective-permute-start(bf16[16,768]{1,0:T(8,128)(2,1)S(1)} %get-tuple-element.79), channel_id=1, source_target_pairs={{0,4},{4,0},{8,12},{12,8},{1,5},{5,1},{9,13},{13,9},{2,6},{6,2},{1... | collective-permute-start | bytes 73736 | tf_op jit(solution)/shard_map/ppermute | solution.py:597
  63.8 6.6 %collective-permute-start.24 = (bf16[8,3072]{1,0:T(8,128)(2,1)S(1)}, bf16[8,3072]{1,0:T(8,128)(2,1)S(1)}, u32[]{:S(2)}, u32[]{:S(2)}) collective-permute-start(bf16[8,3072]{1,0:T(8,128)(2,1)S(1)} %get-tuple-element.84), channel_id=1, source_target_pairs={{0,12},{4,8},{8,4},{12,0},{1,13},{5,9},{9,5},{13,1},{2,14},{6,10},... | collective-permute-start | bytes 147464 | tf_op jit(solution)/shard_map/ppermute | solution.py:597
  65.5 5.7 %collective-permute-start.25 = (bf16[8,3072]{1,0:T(8,128)(2,1)S(1)}, bf16[8,3072]{1,0:T(8,128)(2,1)S(1)}, u32[]{:S(2)}, u32[]{:S(2)}) collective-permute-start(bf16[8,3072]{1,0:T(8,128)(2,1)S(1)} %get-tuple-element.85), channel_id=1, source_target_pairs={{0,8},{4,12},{8,0},{12,4},{1,9},{5,13},{9,1},{13,5},{2,10},{6,14},... | collective-permute-start | bytes 147464 | tf_op jit(solution)/shard_map/ppermute | solution.py:597
  66.0 5.2 %collective-permute-start.26 = (bf16[8,3072]{1,0:T(8,128)(2,1)S(1)}, bf16[8,3072]{1,0:T(8,128)(2,1)S(1)}, u32[]{:S(2)}, u32[]{:S(2)}) collective-permute-start(bf16[8,3072]{1,0:T(8,128)(2,1)S(1)} %get-tuple-element.86), channel_id=1, source_target_pairs={{0,4},{4,0},{8,12},{12,8},{1,5},{5,1},{9,13},{13,9},{2,6},{6,2},{1... | collective-permute-start | bytes 147464 | tf_op jit(solution)/shard_map/ppermute | solution.py:597

commit v12 on v10

--- a/solution.py
+++ b/solution.py
@@ -323,10 +323,10 @@
     rest.start()
     squares_ref[...] = turn(turned_ref, gain_ref, pieces, 0, count)
     columns = half_of(gate_ref, 0)
-    gate_sum_ref[...] = dot(gate_ref[:, columns], turned_ref[...])
-    up_sum_ref[:cut] = dot(up_ref[:, columns], turned_ref[...])
     rest.wait()
-    up_sum_ref[cut:] = dot(up_rest_ref[:, columns], turned_ref[...])
+    for at, weight_ref in ((slice(0, cut), up_ref), (slice(cut, gate_ref.shape[0]), up_rest_ref)):
+        gate_sum_ref[at] = dot(gate_ref[at, columns], turned_ref[...])
+        up_sum_ref[at] = dot(weight_ref[:, columns], turned_ref[...])
 
 
 def expert_second_kernel(count, *refs):

time: 69.5 us -> 70.3 us (1.012)
  Pallas kernels: 30 us -> 30.8 us
    pallas_call x1, Pallas kernels: 5.92 us -> 6.73 us  [expert_first(): pl.pallas_call(functools.partial(expert_first_kernel, count), in_specs=[V...]
where the time goes in v12:
time: 70.3 us; the launch traced here: 70.1 us
  Pallas kernels  30.8 us (44%)
  starting transfers between devices  26.4 us (38%)
  waiting for transfers between devices  12.7 us (18%)
    ppermute x27, starting transfers between devices, swap(): lax.ppermute(x, axis, [(i, i ^ by) for i in range(lax.axis_size(axis))])  26.4 us
    ppermute x27, waiting for transfers between devices, swap(): lax.ppermute(x, axis, [(i, i ^ by) for i in range(lax.axis_size(axis))])  12.7 us
    pallas_call x1, Pallas kernels, expert_first(): pl.pallas_call(functools.partial(expert_first_kernel, count), in_specs=[V...  6.73 us
    pallas_call x1, Pallas kernels, load(): pl.pallas_call(functools.partial(load_kernel, len(weights)), in_specs=[AN...  6.03 us
    pallas_call x1, Pallas kernels, expert_second(): pl.pallas_call(functools.partial(expert_second_kernel, count), in_specs=[...  5.23 us
    pallas_call x1, Pallas kernels, attend(): pl.pallas_call(functools.partial(attend_kernel, rows // requests, heads /...  3.76 us
    pallas_call x1, Pallas kernels, route(): pl.pallas_call(functools.partial(route_kernel, capacity, top), in_specs=[...  3.28 us
    pallas_call x2, Pallas kernels, expert_down(): pl.pallas_call(functools.partial(down_kernel, start, 512), in_specs=[VMEM...  2.71 us
  transfers between devices with their start and end apart: 27, of which 14 were waited for; matrix products, arithmetic and copies ran while one was open for 0% of the time, Pallas kernels for 24%

profile of v12, /device:TPU:0, one launch (start us, length us, event | category | flops | bytes accessed | tf_op | source)
XLA Modules:
  0.0 70.1 jit_solution(13955530893782804312)
XLA Ops:
  0.0 3.8 %attention.1 = (bf16[16,2944]{1,0:T(8,128)(2,1)S(1)}, bf16[16,2944]{1,0:T(8,128)(2,1)S(1)}, bf16[16,2944]{1,0:T(8,128)(2,1)S(1)}, bf16[16,2944]{1,0:T(8,128)(2,1)S(1)}) custom-call(f32[16]{0:T(128)} %decay_ref.1, s32[2,8]{1,0:T(2,128)} %bitcast.6, bf16[16,2048]{1,0:T(8,128)(2,1)} %q_ref.1, bf16[16,2048]{1,0:T(8,128)(2,1)} %k_ref.1, bf16[16,2048]{1,0:T(8,128)(2,1)} %v_ref.1, ...), custom_call_target="tpu_custom_call" | custom-call | tf_op jit(solution)/shard_map/attention/pallas_call | solution.py:111
  3.8 5.1 %collective-permute-start.1 = (bf16[16,2944]{1,0:T(8,128)(2,1)S(1)}, bf16[16,2944]{1,0:T(8,128)(2,1)S(1)}, u32[]{:S(2)}, u32[]{:S(2)}) collective-permute-start(bf16[16,2944]{1,0:T(8,128)(2,1)S(1)} %get-tuple-element.48), channel_id=1, source_target_pairs={{0,12},{4,8},{8,4},{12,0},{1,13},{5,9},{9,5},{13,1},{2,14},{6,10},... | collective-permute-start | bytes 282632 | tf_op jit(solution)/shard_map/ppermute | solution.py:592
  8.9 0.0 collective-permute-start.3
  8.9 0.6 collective-permute-start.5
  9.5 6.0 %load.1 = (bf16[16,2944]{1,0:T(8,128)(2,1)S(1)}, bf16[2048,768]{1,0:T(8,128)(2,1)S(1)}, f32[1,6144]{1,0:T(1,128)S(1)}, bf16[1152,6144]{1,0:T(8,128)(2,1)S(1)}) custom-call(bf16[16,2944]{1,0:T(8,128)(2,1)S(1)} %get-tuple-element.46.rows_hbm, bf16[2048,768]{1,0:T(8,128)(2,1)} %refs_0_.1, f32[1,6144]{1,0:T(1,128)} %bitcast.4, bf16[1152,6144]{1,0:T(8,128)(2,1)} %refs_2_.1), custom_call_target="tpu_custom_call" | custom-call | bytes 17326080 | tf_op jit(solution)/shard_map/load/pallas_call | solution.py:150
  15.6 0.1 collective-permute-start
  15.6 0.0 collective-permute-done.1.refs_2_
  15.7 0.5 collective-permute-start.2
  16.1 0.6 collective-permute-done.3.refs_4_
  16.8 0.0 collective-permute-start.4
  16.8 0.0 collective-permute-done.5.refs_6_
  16.8 0.5 collective-permute-start.6
  17.3 0.0 collective-permute-done.refs_1_
  17.3 0.0 collective-permute-done.2.refs_3_
  17.3 0.8 %collective-permute-done.4.refs_5_ = bf16[16,2944]{1,0:T(8,128)(2,1)S(1)} collective-permute-done((bf16[16,2944]{1,0:T(8,128)(2,1)S(1)}, bf16[16,2944]{1,0:T(8,128)(2,1)S(1)}, u32[]{:S(2)}, u32[]{:S(2)}) %collective-permute-start.4) | collective-permute-done | bytes 94240 | tf_op jit(solution)/shard_map/ppermute | solution.py:592
  18.1 0.2 collective-permute-done.6.refs_7_
  18.3 0.7 %projection.1 = (f32[64,768]{1,0:T(8,128)S(1)}, bf16[64,768]{1,0:T(8,128)(2,1)S(1)}) custom-call(bf16[16,2944]{1,0:T(8,128)(2,1)S(1)} %get-tuple-element.47.refs_0_, bf16[16,2944]{1,0:T(8,128)(2,1)S(1)} %collective-permute-done.refs_1_, bf16[16,2944]{1,0:T(8,128)(2,1)S(1)} %collective-permute-done.1.refs_2_, ...), custom_call_target="tpu_custom_call" | custom-call | tf_op jit(solution)/shard_map/projection/pallas_call | solution.py:187
  19.0 1.6 %collective-permute-start.7 = (bf16[64,768]{1,0:T(8,128)(2,1)S(1)}, bf16[64,768]{1,0:T(8,128)(2,1)S(1)}, u32[]{:S(2)}, u32[]{:S(2)}) collective-permute-start(bf16[64,768]{1,0:T(8,128)(2,1)S(1)} %get-tuple-element.53), channel_id=1, source_target_pairs={{0,1},{1,0},{2,3},{3,2},{4,5},{5,4},{6,7},{7,6},{8,9},{9,8},{10,11... | collective-permute-start | bytes 294920 | tf_op jit(solution)/shard_map/ppermute | solution.py:592
  20.5 3.3 %route.1 = (bf16[128,64]{1,0:T(8,128)(2,1)S(1)}, f32[64,768]{1,0:T(8,128)S(1)}, bf16[640,6144]{1,0:T(8,128)(2,1)S(1)}) custom-call(bf16[16,2944]{1,0:T(8,128)(2,1)S(1)} %get-tuple-element.47.refs_0_, bf16[16,2944]{1,0:T(8,128)(2,1)S(1)} %collective-permute-done.refs_1_, bf16[16,2944]{1,0:T(8,128)(2,1)S(1)} %collective-permute-done.1.refs_2_, ...), custom_call_target="tpu_custom_call" | custom-call | flops 1000000 | bytes 8000000 | tf_op jit(solution)/shard_map/route/pallas_call | solution.py:243
  23.8 0.3 collective-permute-done.7.got_ref
  24.1 0.2 pack.1
  24.3 0.8 %collective-permute-start.13 = (bf16[32,768]{1,0:T(8,128)(2,1)S(1)}, bf16[32,768]{1,0:T(8,128)(2,1)S(1)}, u32[]{:S(2)}, u32[]{:S(2)}) collective-permute-start(bf16[32,768]{1,0:T(8,128)(2,1)S(1)} %get-tuple-element.59.refs_0_), channel_id=1, source_target_pairs={{0,4},{4,0},{8,12},{12,8},{1,5},{5,1},{9,13},{13,9},{2,6},{6,2},{1... | collective-permute-start | bytes 147464 | tf_op jit(solution)/shard_map/ppermute | solution.py:592
  25.1 2.4 %collective-permute-start.10 = (bf16[32,768]{1,0:T(8,128)(2,1)S(1)}, bf16[32,768]{1,0:T(8,128)(2,1)S(1)}, u32[]{:S(2)}, u32[]{:S(2)}) collective-permute-start(bf16[32,768]{1,0:T(8,128)(2,1)S(1)} %relay.4), channel_id=1, source_target_pairs={{0,12},{4,8},{8,4},{12,0},{1,13},{5,9},{9,5},{13,1},{2,14},{6,10},... | collective-permute-start | bytes 147464 | tf_op jit(solution)/shard_map/ppermute | solution.py:592
  27.6 0.6 collective-permute-start.9
  28.2 0.3 collective-permute-done.13
  28.5 1.5 %collective-permute-start.15 = (bf16[64,768]{1,0:T(8,128)(2,1)S(1)}, bf16[64,768]{1,0:T(8,128)(2,1)S(1)}, u32[]{:S(2)}, u32[]{:S(2)}) collective-permute-start(bf16[64,768]{1,0:T(8,128)(2,1)S(1)} %constant_dynamic-update-slice_fusion.2.refs_0_), channel_id=1, source_target_pairs={{0,1},{1,0},{2,3},{3,2},{4,5},{5,4},{6,7},{7,6},{8,9},{9,8},{10,11... | collective-permute-start | bytes 294920 | tf_op jit(solution)/shard_map/ppermute | solution.py:592
  30.0 0.0 collective-permute-start.14
  30.0 2.7 %collective-permute-done.9 = bf16[32,768]{1,0:T(8,128)(2,1)S(1)} collective-permute-done((bf16[32,768]{1,0:T(8,128)(2,1)S(1)}, bf16[32,768]{1,0:T(8,128)(2,1)S(1)}, u32[]{:S(2)}, u32[]{:S(2)}) %collective-permute-start.9) | collective-permute-done | bytes 49184 | tf_op jit(solution)/shard_map/ppermute | solution.py:592
  32.7 0.4 collective-permute-done.15.refs_2_
  33.1 0.0 collective-permute-start.16
  33.1 0.0 collective-permute-done.10
  33.1 1.6 %collective-permute-start.12 = (bf16[64,768]{1,0:T(8,128)(2,1)S(1)}, bf16[64,768]{1,0:T(8,128)(2,1)S(1)}, u32[]{:S(2)}, u32[]{:S(2)}) collective-permute-start(bf16[64,768]{1,0:T(8,128)(2,1)S(1)} %constant_dynamic-update-slice_fusion.refs_0_), channel_id=1, source_target_pairs={{0,1},{1,0},{2,3},{3,2},{4,5},{5,4},{6,7},{7,6},{8,9},{9,8},{10,11... | collective-permute-start | bytes 294920 | tf_op jit(solution)/shard_map/ppermute | solution.py:592
  34.6 0.2 collective-permute-start.8
  34.9 0.3 collective-permute-start.11
  35.2 0.0 collective-permute-done.14.refs_1_
  35.2 0.0 collective-permute-done.16.refs_3_
  35.2 6.7 %experts_first.1 = (f32[1152,64]{1,0:T(8,128)S(1)}, f32[1152,64]{1,0:T(8,128)S(1)}, f32[64,128]{1,0:T(8,128)S(1)}, bf16[512,6144]{1,0:T(8,128)(2,1)S(1)}) custom-call(bf16[64,768]{1,0:T(8,128)(2,1)S(1)} %constant_dynamic-update-slice_fusion.2.refs_0_, bf16[64,768]{1,0:T(8,128)(2,1)S(1)} %collective-permute-done.14.refs_1_, ...), custom_call_target="tpu_custom_call" | custom-call | flops 905969664 | bytes 14155776 | tf_op jit(solution)/shard_map/experts_first/pallas_call | solution.py:377
  41.9 0.0 collective-permute-done.8.refs_1_.cross_ref
  41.9 0.0 collective-permute-done.12.rows_ref
  41.9 0.3 collective-permute-start.17
  42.2 1.1 %collective-permute-done.17.refs_3_ = bf16[64,768]{1,0:T(8,128)(2,1)S(1)} collective-permute-done((bf16[64,768]{1,0:T(8,128)(2,1)S(1)}, bf16[64,768]{1,0:T(8,128)(2,1)S(1)}, u32[]{:S(2)}, u32[]{:S(2)}) %collective-permute-start.17) | collective-permute-done | bytes 98336 | tf_op jit(solution)/shard_map/ppermute | solution.py:592
  43.3 5.2 %experts_second.1 = (bf16[64,1152]{1,0:T(8,128)(2,1)S(1)}, bf16[1152,6144]{1,0:T(8,128)(2,1)S(1)}) custom-call(bf16[64,768]{1,0:T(8,128)(2,1)S(1)} %constant_dynamic-update-slice_fusion.refs_0_, bf16[64,768]{1,0:T(8,128)(2,1)S(1)} %collective-permute-done.11.refs_1_, bf16[64,768]{1,0:T(8,128)(2,1)S(1)} %relay.5.refs_2_, ...), custom_call_target="tpu_custom_call" | custom-call | flops 905969664 | bytes 14155776 | tf_op jit(solution)/shard_map/experts_second/pallas_call | solution.py:412
  48.5 1.4 %experts_down.3 = (f32[32,3072]{1,0:T(8,128)S(1)}, bf16[32,3072]{1,0:T(8,128)(2,1)S(1)}) custom-call(bf16[64,1152]{1,0:T(8,128)(2,1)S(1)} %get-tuple-element.69.hidden_ref, bf16[1152,6144]{1,0:T(8,128)(2,1)S(1)} %get-tuple-element.70.weight_ref), custom_call_target="tpu_custom_call" | custom-call | flops 905969664 | bytes 7077888 | tf_op jit(solution)/shard_map/experts_down/pallas_call | solution.py:432
  49.9 1.4 %experts_down.2 = (f32[32,3072]{1,0:T(8,128)S(1)}, bf16[32,3072]{1,0:T(8,128)(2,1)S(1)}) custom-call(bf16[64,1152]{1,0:T(8,128)(2,1)S(1)} %get-tuple-element.69.hidden_ref, bf16[1152,6144]{1,0:T(8,128)(2,1)S(1)} %get-tuple-element.70.weight_ref), custom_call_target="tpu_custom_call" | custom-call | flops 905969664 | bytes 7077888 | tf_op jit(solution)/shard_map/experts_down/pallas_call | solution.py:432
  51.3 0.3 collective-permute-start.19
  51.6 0.3 collective-permute-start.18
  51.9 0.9 %collective-permute-done.19.refs_3_ = bf16[32,3072]{1,0:T(8,128)(2,1)S(1)} collective-permute-done((bf16[32,3072]{1,0:T(8,128)(2,1)S(1)}, bf16[32,3072]{1,0:T(8,128)(2,1)S(1)}, u32[]{:S(2)}, u32[]{:S(2)}) %collective-permute-start.19) | collective-permute-done | bytes 196640 | tf_op jit(solution)/shard_map/ppermute | solution.py:592
  52.8 0.3 collective-permute-done.18.refs_2_
  53.1 0.1 chip_sum.1
  53.1 0.8 %collective-permute-start.23 = (bf16[16,6144]{1,0:T(8,128)(2,1)S(1)}, bf16[16,6144]{1,0:T(8,128)(2,1)S(1)}, u32[]{:S(2)}, u32[]{:S(2)}) collective-permute-start(bf16[16,6144]{1,0:T(8,128)(2,1)S(1)} %get-tuple-element.82), channel_id=1, source_target_pairs={{0,1},{1,0},{2,3},{3,2},{4,5},{5,4},{6,7},{7,6},{8,9},{9,8},{10,11... | collective-permute-start | bytes 589832 | tf_op jit(solution)/shard_map/ppermute | solution.py:592
  53.9 3.2 %collective-permute-start.20 = (bf16[16,768]{1,0:T(8,128)(2,1)S(1)}, bf16[16,768]{1,0:T(8,128)(2,1)S(1)}, u32[]{:S(2)}, u32[]{:S(2)}) collective-permute-start(bf16[16,768]{1,0:T(8,128)(2,1)S(1)} %get-tuple-element.77), channel_id=1, source_target_pairs={{0,12},{4,8},{8,4},{12,0},{1,13},{5,9},{9,5},{13,1},{2,14},{6,10},... | collective-permute-start | bytes 73736 | tf_op jit(solution)/shard_map/ppermute | solution.py:592
  57.1 0.0 collective-permute-start.21
  57.1 1.3 %collective-permute-start.22 = (bf16[16,768]{1,0:T(8,128)(2,1)S(1)}, bf16[16,768]{1,0:T(8,128)(2,1)S(1)}, u32[]{:S(2)}, u32[]{:S(2)}) collective-permute-start(bf16[16,768]{1,0:T(8,128)(2,1)S(1)} %get-tuple-element.79), channel_id=1, source_target_pairs={{0,4},{4,0},{8,12},{12,8},{1,5},{5,1},{9,13},{13,9},{2,6},{6,2},{1... | collective-permute-start | bytes 73736 | tf_op jit(solution)/shard_map/ppermute | solution.py:592
  58.4 1.5 %collective-permute-done.20.refs_1_ = bf16[16,768]{1,0:T(8,128)(2,1)S(1)} collective-permute-done((bf16[16,768]{1,0:T(8,128)(2,1)S(1)}, bf16[16,768]{1,0:T(8,128)(2,1)S(1)}, u32[]{:S(2)}, u32[]{:S(2)}) %collective-permute-start.20) | collective-permute-done | bytes 24608 | tf_op jit(solution)/shard_map/ppermute | solution.py:592
  59.9 1.9 %collective-permute-done.21.refs_2_ = bf16[16,768]{1,0:T(8,128)(2,1)S(1)} collective-permute-done((bf16[16,768]{1,0:T(8,128)(2,1)S(1)}, bf16[16,768]{1,0:T(8,128)(2,1)S(1)}, u32[]{:S(2)}, u32[]{:S(2)}) %collective-permute-start.21) | collective-permute-done | bytes 24608 | tf_op jit(solution)/shard_map/ppermute | solution.py:592
  61.8 0.1 pair_sum.1
  61.9 1.6 %collective-permute-start.24 = (bf16[8,3072]{1,0:T(8,128)(2,1)S(1)}, bf16[8,3072]{1,0:T(8,128)(2,1)S(1)}, u32[]{:S(2)}, u32[]{:S(2)}) collective-permute-start(bf16[8,3072]{1,0:T(8,128)(2,1)S(1)} %get-tuple-element.84), channel_id=1, source_target_pairs={{0,12},{4,8},{8,4},{12,0},{1,13},{5,9},{9,5},{13,1},{2,14},{6,10},... | collective-permute-start | bytes 147464 | tf_op jit(solution)/shard_map/ppermute | solution.py:592
  63.5 0.6 collective-permute-start.25
  64.1 2.3 %collective-permute-start.26 = (bf16[8,3072]{1,0:T(8,128)(2,1)S(1)}, bf16[8,3072]{1,0:T(8,128)(2,1)S(1)}, u32[]{:S(2)}, u32[]{:S(2)}) collective-permute-start(bf16[8,3072]{1,0:T(8,128)(2,1)S(1)} %get-tuple-element.86), channel_id=1, source_target_pairs={{0,4},{4,0},{8,12},{12,8},{1,5},{5,1},{9,13},{13,9},{2,6},{6,2},{1... | collective-permute-start | bytes 147464 | tf_op jit(solution)/shard_map/ppermute | solution.py:592
  66.4 1.1 %own_rows.1 = (f32[8,6144]{1,0:T(8,128)S(1)}, bf16[32,32]{1,0:T(8,128)(2,1)S(1)}) custom-call(s32[2,8]{1,0:T(2,128)} %bitcast.7, f32[2,8]{1,0:T(2,128)} %bitcast.8, bf16[8,6144]{1,0:T(8,128)(2,1)} %residual_ref.3, bf16[16,768]{1,0:T(8,128)(2,1)S(1)} %get-tuple-element.76.refs_0_, bf16[16,768]{1,0:T(8,128)(2,1)S(1)} %collective-permute-done.20.refs_1_, ...), custom_call_target="tpu_custom_call" | custom-call | flops 1000000 | bytes 1000000 | tf_op jit(solution)/shard_map/own_rows/pallas_call | solution.py:554
  67.5 1.1 %collective-permute-done.24.refs_1_ = bf16[8,3072]{1,0:T(8,128)(2,1)S(1)} collective-permute-done((bf16[8,3072]{1,0:T(8,128)(2,1)S(1)}, bf16[8,3072]{1,0:T(8,128)(2,1)S(1)}, u32[]{:S(2)}, u32[]{:S(2)}) %collective-permute-start.24) | collective-permute-done | bytes 49184 | tf_op jit(solution)/shard_map/ppermute | solution.py:592
  68.6 0.7 collective-permute-done.25.refs_2_
  69.2 0.0 collective-permute-done.26.refs_3_
  69.2 0.8 %finish.1 = bf16[8,6144]{1,0:T(8,128)(2,1)} custom-call(f32[8,6144]{1,0:T(8,128)S(1)} %get-tuple-element.80.combined_ref, bf16[32,32]{1,0:T(8,128)(2,1)S(1)} %get-tuple-element.81.weighting_ref, bf16[8,3072]{1,0:T(8,128)(2,1)S(1)} %get-tuple-element.83.refs_0_, bf16[8,3072]{1,0:T(8,128)(2,1)S(1)} %collective-permute-done.24.refs_1_, ...), custom_call_target="tpu_custom_call" | custom-call | tf_op jit(solution)/shard_map/finish/pallas_call | solution.py:581
  (11 shorter events, 0.1 us)
Async XLA Ops:
  3.8 11.9 %collective-permute-start.1 = (bf16[16,2944]{1,0:T(8,128)(2,1)S(1)}, bf16[16,2944]{1,0:T(8,128)(2,1)S(1)}, u32[]{:S(2)}, u32[]{:S(2)}) collective-permute-start(bf16[16,2944]{1,0:T(8,128)(2,1)S(1)} %get-tuple-element.48), channel_id=1, source_target_pairs={{0,12},{4,8},{8,4},{12,0},{1,13},{5,9},{9,5},{13,1},{2,14},{6,10},... | collective-permute-start | bytes 282632 | tf_op jit(solution)/shard_map/ppermute | solution.py:592
  8.9 7.9 %collective-permute-start.3 = (bf16[16,2944]{1,0:T(8,128)(2,1)S(1)}, bf16[16,2944]{1,0:T(8,128)(2,1)S(1)}, u32[]{:S(2)}, u32[]{:S(2)}) collective-permute-start(bf16[16,2944]{1,0:T(8,128)(2,1)S(1)} %get-tuple-element.49), channel_id=1, source_target_pairs={{0,8},{4,12},{8,0},{12,4},{1,9},{5,13},{9,1},{13,5},{2,10},{6,14},... | collective-permute-start | bytes 282632 | tf_op jit(solution)/shard_map/ppermute | solution.py:592
  8.9 7.9 %collective-permute-start.5 = (bf16[16,2944]{1,0:T(8,128)(2,1)S(1)}, bf16[16,2944]{1,0:T(8,128)(2,1)S(1)}, u32[]{:S(2)}, u32[]{:S(2)}) collective-permute-start(bf16[16,2944]{1,0:T(8,128)(2,1)S(1)} %get-tuple-element.50), channel_id=1, source_target_pairs={{0,4},{4,0},{8,12},{12,8},{1,5},{5,1},{9,13},{13,9},{2,6},{6,2},{1... | collective-permute-start | bytes 282632 | tf_op jit(solution)/shard_map/ppermute | solution.py:592
  15.6 1.7 %collective-permute-start = (bf16[16,2944]{1,0:T(8,128)(2,1)S(1)}, bf16[16,2944]{1,0:T(8,128)(2,1)S(1)}, u32[]{:S(2)}, u32[]{:S(2)}) collective-permute-start(bf16[16,2944]{1,0:T(8,128)(2,1)S(1)} %get-tuple-element.47.refs_0_), channel_id=1, source_target_pairs={{0,2},{2,0},{1,3},{3,1},{4,6},{6,4},{5,7},{7,5},{8,10},{10,8},{9,1... | collective-permute-start | bytes 282632 | tf_op jit(solution)/shard_map/ppermute | solution.py:592
  15.7 1.7 %collective-permute-start.2 = (bf16[16,2944]{1,0:T(8,128)(2,1)S(1)}, bf16[16,2944]{1,0:T(8,128)(2,1)S(1)}, u32[]{:S(2)}, u32[]{:S(2)}) collective-permute-start(bf16[16,2944]{1,0:T(8,128)(2,1)S(1)} %collective-permute-done.1.refs_2_), channel_id=1, source_target_pairs={{0,2},{2,0},{1,3},{3,1},{4,6},{6,4},{5,7},{7,5},{8,10},{10,8},{9,1... | collective-permute-start | bytes 282632 | tf_op jit(solution)/shard_map/ppermute | solution.py:592
  16.8 1.3 %collective-permute-start.4 = (bf16[16,2944]{1,0:T(8,128)(2,1)S(1)}, bf16[16,2944]{1,0:T(8,128)(2,1)S(1)}, u32[]{:S(2)}, u32[]{:S(2)}) collective-permute-start(bf16[16,2944]{1,0:T(8,128)(2,1)S(1)} %collective-permute-done.3.refs_4_), channel_id=1, source_target_pairs={{0,2},{2,0},{1,3},{3,1},{4,6},{6,4},{5,7},{7,5},{8,10},{10,8},{9,1... | collective-permute-start | bytes 282632 | tf_op jit(solution)/shard_map/ppermute | solution.py:592
  16.8 1.4 %collective-permute-start.6 = (bf16[16,2944]{1,0:T(8,128)(2,1)S(1)}, bf16[16,2944]{1,0:T(8,128)(2,1)S(1)}, u32[]{:S(2)}, u32[]{:S(2)}) collective-permute-start(bf16[16,2944]{1,0:T(8,128)(2,1)S(1)} %collective-permute-done.5.refs_6_), channel_id=1, source_target_pairs={{0,2},{2,0},{1,3},{3,1},{4,6},{6,4},{5,7},{7,5},{8,10},{10,8},{9,1... | collective-permute-start | bytes 282632 | tf_op jit(solution)/shard_map/ppermute | solution.py:592
  19.0 5.1 %collective-permute-start.7 = (bf16[64,768]{1,0:T(8,128)(2,1)S(1)}, bf16[64,768]{1,0:T(8,128)(2,1)S(1)}, u32[]{:S(2)}, u32[]{:S(2)}) collective-permute-start(bf16[64,768]{1,0:T(8,128)(2,1)S(1)} %get-tuple-element.53), channel_id=1, source_target_pairs={{0,1},{1,0},{2,3},{3,2},{4,5},{5,4},{6,7},{7,6},{8,9},{9,8},{10,11... | collective-permute-start | bytes 294920 | tf_op jit(solution)/shard_map/ppermute | solution.py:592
  24.3 4.2 %collective-permute-start.13 = (bf16[32,768]{1,0:T(8,128)(2,1)S(1)}, bf16[32,768]{1,0:T(8,128)(2,1)S(1)}, u32[]{:S(2)}, u32[]{:S(2)}) collective-permute-start(bf16[32,768]{1,0:T(8,128)(2,1)S(1)} %get-tuple-element.59.refs_0_), channel_id=1, source_target_pairs={{0,4},{4,0},{8,12},{12,8},{1,5},{5,1},{9,13},{13,9},{2,6},{6,2},{1... | collective-permute-start | bytes 147464 | tf_op jit(solution)/shard_map/ppermute | solution.py:592
  25.1 8.0 %collective-permute-start.10 = (bf16[32,768]{1,0:T(8,128)(2,1)S(1)}, bf16[32,768]{1,0:T(8,128)(2,1)S(1)}, u32[]{:S(2)}, u32[]{:S(2)}) collective-permute-start(bf16[32,768]{1,0:T(8,128)(2,1)S(1)} %relay.4), channel_id=1, source_target_pairs={{0,12},{4,8},{8,4},{12,0},{1,13},{5,9},{9,5},{13,1},{2,14},{6,10},... | collective-permute-start | bytes 147464 | tf_op jit(solution)/shard_map/ppermute | solution.py:592
  27.6 5.1 %collective-permute-start.9 = (bf16[32,768]{1,0:T(8,128)(2,1)S(1)}, bf16[32,768]{1,0:T(8,128)(2,1)S(1)}, u32[]{:S(2)}, u32[]{:S(2)}) collective-permute-start(bf16[32,768]{1,0:T(8,128)(2,1)S(1)} %relay.3), channel_id=1, source_target_pairs={{0,8},{4,12},{8,0},{12,4},{1,9},{5,13},{9,1},{13,5},{2,10},{6,14},... | collective-permute-start | bytes 147464 | tf_op jit(solution)/shard_map/ppermute | solution.py:592
  28.5 4.6 %collective-permute-start.15 = (bf16[64,768]{1,0:T(8,128)(2,1)S(1)}, bf16[64,768]{1,0:T(8,128)(2,1)S(1)}, u32[]{:S(2)}, u32[]{:S(2)}) collective-permute-start(bf16[64,768]{1,0:T(8,128)(2,1)S(1)} %constant_dynamic-update-slice_fusion.2.refs_0_), channel_id=1, source_target_pairs={{0,1},{1,0},{2,3},{3,2},{4,5},{5,4},{6,7},{7,6},{8,9},{9,8},{10,11... | collective-permute-start | bytes 294920 | tf_op jit(solution)/shard_map/ppermute | solution.py:592
  30.0 5.2 %collective-permute-start.14 = (bf16[64,768]{1,0:T(8,128)(2,1)S(1)}, bf16[64,768]{1,0:T(8,128)(2,1)S(1)}, u32[]{:S(2)}, u32[]{:S(2)}) collective-permute-start(bf16[64,768]{1,0:T(8,128)(2,1)S(1)} %constant_dynamic-update-slice_fusion.2.refs_0_), channel_id=1, source_target_pairs={{0,2},{2,0},{1,3},{3,1},{4,6},{6,4},{5,7},{7,5},{8,10},{10,8},{9,1... | collective-permute-start | bytes 294920 | tf_op jit(solution)/shard_map/ppermute | solution.py:592
  33.1 2.1 %collective-permute-start.16 = (bf16[64,768]{1,0:T(8,128)(2,1)S(1)}, bf16[64,768]{1,0:T(8,128)(2,1)S(1)}, u32[]{:S(2)}, u32[]{:S(2)}) collective-permute-start(bf16[64,768]{1,0:T(8,128)(2,1)S(1)} %collective-permute-done.15.refs_2_), channel_id=1, source_target_pairs={{0,2},{2,0},{1,3},{3,1},{4,6},{6,4},{5,7},{7,5},{8,10},{10,8},{9,1... | collective-permute-start | bytes 294920 | tf_op jit(solution)/shard_map/ppermute | solution.py:592
  33.1 8.8 %collective-permute-start.12 = (bf16[64,768]{1,0:T(8,128)(2,1)S(1)}, bf16[64,768]{1,0:T(8,128)(2,1)S(1)}, u32[]{:S(2)}, u32[]{:S(2)}) collective-permute-start(bf16[64,768]{1,0:T(8,128)(2,1)S(1)} %constant_dynamic-update-slice_fusion.refs_0_), channel_id=1, source_target_pairs={{0,1},{1,0},{2,3},{3,2},{4,5},{5,4},{6,7},{7,6},{8,9},{9,8},{10,11... | collective-permute-start | bytes 294920 | tf_op jit(solution)/shard_map/ppermute | solution.py:592
  34.6 7.3 %collective-permute-start.8 = (bf16[32,768]{1,0:T(8,128)(2,1)S(1)}, bf16[32,768]{1,0:T(8,128)(2,1)S(1)}, u32[]{:S(2)}, u32[]{:S(2)}) collective-permute-start(bf16[32,768]{1,0:T(8,128)(2,1)S(1)} %get-tuple-element.57), channel_id=1, source_target_pairs={{0,2},{2,0},{1,3},{3,1},{4,6},{6,4},{5,7},{7,5},{8,10},{10,8},{9,1... | collective-permute-start | bytes 147464 | tf_op jit(solution)/shard_map/ppermute | solution.py:592
  34.9 7.4 %collective-permute-start.11 = (bf16[64,768]{1,0:T(8,128)(2,1)S(1)}, bf16[64,768]{1,0:T(8,128)(2,1)S(1)}, u32[]{:S(2)}, u32[]{:S(2)}) collective-permute-start(bf16[64,768]{1,0:T(8,128)(2,1)S(1)} %constant_dynamic-update-slice_fusion.refs_0_), channel_id=1, source_target_pairs={{0,2},{2,0},{1,3},{3,1},{4,6},{6,4},{5,7},{7,5},{8,10},{10,8},{9,1... | collective-permute-start | bytes 294920 | tf_op jit(solution)/shard_map/ppermute | solution.py:592
  41.9 1.4 %collective-permute-start.17 = (bf16[64,768]{1,0:T(8,128)(2,1)S(1)}, bf16[64,768]{1,0:T(8,128)(2,1)S(1)}, u32[]{:S(2)}, u32[]{:S(2)}) collective-permute-start(bf16[64,768]{1,0:T(8,128)(2,1)S(1)} %relay.5.refs_2_), channel_id=1, source_target_pairs={{0,2},{2,0},{1,3},{3,1},{4,6},{6,4},{5,7},{7,5},{8,10},{10,8},{9,1... | collective-permute-start | bytes 294920 | tf_op jit(solution)/shard_map/ppermute | solution.py:592
  51.3 1.5 %collective-permute-start.19 = (bf16[32,3072]{1,0:T(8,128)(2,1)S(1)}, bf16[32,3072]{1,0:T(8,128)(2,1)S(1)}, u32[]{:S(2)}, u32[]{:S(2)}) collective-permute-start(bf16[32,3072]{1,0:T(8,128)(2,1)S(1)} %get-tuple-element.74), channel_id=1, source_target_pairs={{0,2},{2,0},{1,3},{3,1},{4,6},{6,4},{5,7},{7,5},{8,10},{10,8},{9,1... | collective-permute-start | bytes 589832 | tf_op jit(solution)/shard_map/ppermute | solution.py:592
  51.6 1.5 %collective-permute-start.18 = (bf16[32,3072]{1,0:T(8,128)(2,1)S(1)}, bf16[32,3072]{1,0:T(8,128)(2,1)S(1)}, u32[]{:S(2)}, u32[]{:S(2)}) collective-permute-start(bf16[32,3072]{1,0:T(8,128)(2,1)S(1)} %get-tuple-element.73), channel_id=1, source_target_pairs={{0,2},{2,0},{1,3},{3,1},{4,6},{6,4},{5,7},{7,5},{8,10},{10,8},{9,1... | collective-permute-start | bytes 589832 | tf_op jit(solution)/shard_map/ppermute | solution.py:592
  53.1 8.7 %collective-permute-start.23 = (bf16[16,6144]{1,0:T(8,128)(2,1)S(1)}, bf16[16,6144]{1,0:T(8,128)(2,1)S(1)}, u32[]{:S(2)}, u32[]{:S(2)}) collective-permute-start(bf16[16,6144]{1,0:T(8,128)(2,1)S(1)} %get-tuple-element.82), channel_id=1, source_target_pairs={{0,1},{1,0},{2,3},{3,2},{4,5},{5,4},{6,7},{7,6},{8,9},{9,8},{10,11... | collective-permute-start | bytes 589832 | tf_op jit(solution)/shard_map/ppermute | solution.py:592
  53.9 6.0 %collective-permute-start.20 = (bf16[16,768]{1,0:T(8,128)(2,1)S(1)}, bf16[16,768]{1,0:T(8,128)(2,1)S(1)}, u32[]{:S(2)}, u32[]{:S(2)}) collective-permute-start(bf16[16,768]{1,0:T(8,128)(2,1)S(1)} %get-tuple-element.77), channel_id=1, source_target_pairs={{0,12},{4,8},{8,4},{12,0},{1,13},{5,9},{9,5},{13,1},{2,14},{6,10},... | collective-permute-start | bytes 73736 | tf_op jit(solution)/shard_map/ppermute | solution.py:592
  57.1 4.7 %collective-permute-start.21 = (bf16[16,768]{1,0:T(8,128)(2,1)S(1)}, bf16[16,768]{1,0:T(8,128)(2,1)S(1)}, u32[]{:S(2)}, u32[]{:S(2)}) collective-permute-start(bf16[16,768]{1,0:T(8,128)(2,1)S(1)} %get-tuple-element.78), channel_id=1, source_target_pairs={{0,8},{4,12},{8,0},{12,4},{1,9},{5,13},{9,1},{13,5},{2,10},{6,14},... | collective-permute-start | bytes 73736 | tf_op jit(solution)/shard_map/ppermute | solution.py:592
  57.1 4.7 %collective-permute-start.22 = (bf16[16,768]{1,0:T(8,128)(2,1)S(1)}, bf16[16,768]{1,0:T(8,128)(2,1)S(1)}, u32[]{:S(2)}, u32[]{:S(2)}) collective-permute-start(bf16[16,768]{1,0:T(8,128)(2,1)S(1)} %get-tuple-element.79), channel_id=1, source_target_pairs={{0,4},{4,0},{8,12},{12,8},{1,5},{5,1},{9,13},{13,9},{2,6},{6,2},{1... | collective-permute-start | bytes 73736 | tf_op jit(solution)/shard_map/ppermute | solution.py:592
  61.9 6.7 %collective-permute-start.24 = (bf16[8,3072]{1,0:T(8,128)(2,1)S(1)}, bf16[8,3072]{1,0:T(8,128)(2,1)S(1)}, u32[]{:S(2)}, u32[]{:S(2)}) collective-permute-start(bf16[8,3072]{1,0:T(8,128)(2,1)S(1)} %get-tuple-element.84), channel_id=1, source_target_pairs={{0,12},{4,8},{8,4},{12,0},{1,13},{5,9},{9,5},{13,1},{2,14},{6,10},... | collective-permute-start | bytes 147464 | tf_op jit(solution)/shard_map/ppermute | solution.py:592
  63.5 5.7 %collective-permute-start.25 = (bf16[8,3072]{1,0:T(8,128)(2,1)S(1)}, bf16[8,3072]{1,0:T(8,128)(2,1)S(1)}, u32[]{:S(2)}, u32[]{:S(2)}) collective-permute-start(bf16[8,3072]{1,0:T(8,128)(2,1)S(1)} %get-tuple-element.85), channel_id=1, source_target_pairs={{0,8},{4,12},{8,0},{12,4},{1,9},{5,13},{9,1},{13,5},{2,10},{6,14},... | collective-permute-start | bytes 147464 | tf_op jit(solution)/shard_map/ppermute | solution.py:592
  64.1 5.2 %collective-permute-start.26 = (bf16[8,3072]{1,0:T(8,128)(2,1)S(1)}, bf16[8,3072]{1,0:T(8,128)(2,1)S(1)}, u32[]{:S(2)}, u32[]{:S(2)}) collective-permute-start(bf16[8,3072]{1,0:T(8,128)(2,1)S(1)} %get-tuple-element.86), channel_id=1, source_target_pairs={{0,4},{4,0},{8,12},{12,8},{1,5},{5,1},{9,13},{13,9},{2,6},{6,2},{1... | collective-permute-start | bytes 147464 | tf_op jit(solution)/shard_map/ppermute | solution.py:592
